TPU v7x, 32 devices: a whole 2x2x4 slice. The times are simulated.
32 devices in a mesh: row: 8 (over z, core), col: 4 (over y, x).
Axes of the slice: x: 2, y: 2, z: 4, core: 2. Of those that a mesh axis runs over, the one named last changes fastest.
Arguments:
- embed: bfloat16 [1024, 1024], P(('row', 'col')), may hold values from -0.1875 to 0.1875
- positives: int32 [1024, 4], P('row'), may hold values from 0 to 1023, as said below
- placement: int32 [1024], replicated, may hold values from 0 to 1023, as said below
Outputs:
- embed_grad: float32 [1024, 1024], P(('row', 'col'))
Inputs may be any that keep to these rules, and one draw needn't show every extreme that they name: `positives`: each row names 4 different entities, none of them the entity placed at that row's position. `placement`: a permutation of the entity ids.
All inputs are finite; a program needn't handle non-finite values.
Results may differ from a plain program's by a relative error of at most 0.003.
Values may be sent and summed in bfloat16 or wider, within the bound.
No kernel may reach another device: no remote copies, remote signals or barrier semaphores. Data moves between devices by JAX's collectives and lax.ppermute only.
A program may use at most 64 MiB of HBM per device.

v0:
```python
import jax
import jax.numpy as jnp
from jax import lax
from jax.sharding import PartitionSpec as P

logistic_sharpness = 0.02


def positive_rank(matching_pair_affinity_lines):
    affinity_differences = (
        matching_pair_affinity_lines[:, None, :] - matching_pair_affinity_lines[:, :, None]
    ) / logistic_sharpness
    return 0.5 + jnp.sum(jax.nn.sigmoid(affinity_differences), axis=2)


def coefficients(matching_pair_affinity_lines, ranks, slopes, total):
    prank, pullback = jax.vjp(positive_rank, matching_pair_affinity_lines)
    factor = 1.0 / (matching_pair_affinity_lines.shape[1] * total)
    smoothed_ordering_slope = prank / (ranks * ranks) * factor
    prank_grad = -factor / ranks
    pulled = pullback(prank_grad)[0]
    ordering_coefficient_vector = smoothed_ordering_slope / logistic_sharpness
    extra = pulled - ordering_coefficient_vector * slopes
    return (ordering_coefficient_vector, extra)


def sigmoid_sums(cosine_affinity_matrix, matching_pair_affinity_lines, allowed):
    counts = []
    slopes = []
    for element_location in range(matching_pair_affinity_lines.shape[1]):
        difference_before_squash = jax.nn.sigmoid(
            (
                cosine_affinity_matrix
                - matching_pair_affinity_lines[:, element_location : element_location + 1]
            )
            / logistic_sharpness
        )
        counts.append(jnp.sum(jnp.where(allowed, difference_before_squash, 0.0), axis=1))
        slopes.append(
            jnp.sum(
                jnp.where(
                    allowed, difference_before_squash * (1.0 - difference_before_squash), 0.0
                ),
                axis=1,
            )
        )
    return (jnp.stack(counts, axis=1), jnp.stack(slopes, axis=1))


def score_grads(
    cosine_affinity_matrix,
    matching_pair_affinity_lines,
    allowed,
    column_pos,
    targets,
    ordering_coefficient_vector,
    extra,
):
    dense = jnp.zeros(cosine_affinity_matrix.shape, jnp.float32)
    for element_location in range(matching_pair_affinity_lines.shape[1]):
        difference_before_squash = jax.nn.sigmoid(
            (
                cosine_affinity_matrix
                - matching_pair_affinity_lines[:, element_location : element_location + 1]
            )
            / logistic_sharpness
        )
        dense = dense + ordering_coefficient_vector[
            :, element_location : element_location + 1
        ] * jnp.where(allowed, difference_before_squash * (1.0 - difference_before_squash), 0.0)
    for element_location in range(matching_pair_affinity_lines.shape[1]):
        dense = dense + jnp.where(
            column_pos[None, :] == targets[:, element_location : element_location + 1],
            extra[:, element_location : element_location + 1],
            0.0,
        )
    return dense.astype(jnp.bfloat16)


def body(embed, positives, placement):
    shard = embed.shape[0]
    row_count = lax.axis_size("row")
    col_count = lax.axis_size("col")
    total = shard * row_count * col_count
    row_id = lax.axis_index("row")
    col_id = lax.axis_index("col")
    anchors = lax.all_gather(embed, "col", axis=0, tiled=True)
    candidates = lax.all_gather(embed, "row", axis=0, tiled=True)
    anchor_width = anchors.shape[0]
    targets = jnp.take(placement, positives)
    own = row_id * anchor_width + jnp.arange(anchor_width, dtype=jnp.int32)
    local = jnp.arange(candidates.shape[0], dtype=jnp.int32)
    column_pos = local // shard * anchor_width + col_id * shard + local % shard
    allowed = column_pos[None, :] != own[:, None]
    cosine_affinity_matrix = jnp.einsum(
        "ad,kd->ak", anchors, candidates, preferred_element_type=jnp.float32
    )
    columns = []
    for element_location in range(targets.shape[1]):
        found = column_pos[None, :] == targets[:, element_location : element_location + 1]
        columns.append(jnp.sum(jnp.where(found, cosine_affinity_matrix, 0.0), axis=1))
    pos_part = jnp.stack(columns, axis=1)
    matching_pair_affinity_lines = lax.psum(pos_part, "col")
    count_part, slope_part = sigmoid_sums(
        cosine_affinity_matrix, matching_pair_affinity_lines, allowed
    )
    count_sum, slope_sum = lax.psum((count_part, slope_part), "col")
    ordering_coefficient_vector, extra = coefficients(
        matching_pair_affinity_lines, 0.5 + count_sum, slope_sum, total
    )
    grad_tile = score_grads(
        cosine_affinity_matrix,
        matching_pair_affinity_lines,
        allowed,
        column_pos,
        targets,
        ordering_coefficient_vector,
        extra,
    )
    part = grad_tile
    grad_anchor = lax.psum_scatter(
        jnp.dot(part, candidates, preferred_element_type=jnp.float32),
        "col",
        scatter_dimension=0,
        tiled=True,
    )
    part = grad_tile
    grad_candidate = lax.psum_scatter(
        lax.dot_general(
            part, anchors, (((0,), (0,)), ((), ())), preferred_element_type=jnp.float32
        ),
        "row",
        scatter_dimension=0,
        tiled=True,
    )
    return grad_anchor + grad_candidate


def solution(mesh):
    return jax.shard_map(
        body,
        mesh=mesh,
        in_specs=(P(("row", "col"), None), P("row", None), P()),
        out_specs=P(("row", "col"), None),
        check_vma=False,
    )
```

profile of v0, /device:TPU:0, one launch (start us, length us, event | category | flops | bytes accessed | tf_op | source)
XLA Modules:
  0.0 124.3 jit_solution(1618321457621587863)
XLA Ops:
  6.5 0.0 copy-start
  6.5 0.0 reduce-scatter.3.cloned.1.call-start
  6.5 0.0 copy-start.1
  6.5 10.8 %all_gather.6 = bf16[128,1024]{1,0:T(8,128)(2,1)S(1)} all-gather(bf16[32,1024]{1,0:T(8,128)(2,1)} %param.3), channel_id=1, replica_groups=mesh['row'=8,'col'=4] {'col'}, dimensions={0}, use_global_device_ids=true | all-gather | bytes 327680 | tf_op jit(solution)/shard_map/all_gather | solution.py:87
  17.4 0.0 copy-done.1
  17.4 15.4 %all_gather.7 = bf16[256,1024]{1,0:T(8,128)(2,1)S(1)} all-gather(bf16[32,1024]{1,0:T(8,128)(2,1)S(1)} %copy-done.1), channel_id=1, replica_groups=mesh['row'=8,'col'=4] {'row'}, dimensions={0}, use_global_device_ids=true | all-gather | bytes 589824 | tf_op jit(solution)/shard_map/all_gather | solution.py:88
  32.8 0.0 copy-start.2
  32.8 0.7 copy-done.2
  33.5 0.1 copy.28
  33.6 0.1 reshape.42
  33.7 0.0 copy-done
  33.7 2.3 %gather_fusion = s32[512]{0:T(512)S(1)} fusion(s32[1024]{0:T(1024)S(1)} %copy-done, s32[1024]{0:T(1024)S(1)} %pad_clamp_fusion), kind=kCustom, calls=%fused_computation | custom fusion | bytes 6144 | tf_op jit(solution)/shard_map/jit(_take)/gather | solution.py:90
  36.0 0.1 reshape.41
  36.1 0.1 copy.29
  36.2 0.4 fusion
  36.7 8.9 %psum.21 = f32[128,4]{0,1:T(4,128)S(1)} all-reduce(f32[128,4]{0,1:T(4,128)S(1)} %pad_maximum_fusion), channel_id=1, replica_groups=mesh['row'=8,'col'=4] {'col'}, use_global_device_ids=true, to_apply=%region_4.5 | all-reduce | flops 512 | bytes 4096 | tf_op jit(solution)/shard_map/psum | solution.py:103
  45.6 0.4 fusion.13
  46.1 8.6 %all-reduce = (f32[128,4]{0,1:T(4,128)S(1)}, f32[128,4]{0,1:T(4,128)S(1)}) all-reduce(f32[128,4]{0,1:T(4,128)S(1)} %get-tuple-element.51, f32[128,4]{0,1:T(4,128)S(1)} %get-tuple-element.52), channel_id=1, replica_groups=mesh['row'=8,'col'=4] {'col'}, use_global_device_ids=true, to_apply=%region_10.11 | all-reduce | flops 1024 | bytes 8192 | tf_op jit(solution)/shard_map/psum | solution.py:107
  54.8 0.3 fusion.5
  55.1 1.1 fusion.29
  56.2 0.0 reduce-scatter.3.cloned.1.call-update
  56.2 0.0 reduce-scatter.5.cloned.1.call-start
  56.2 1.3 %fusion.30 = f32[256,1024]{1,0:T(8,128)} fusion(bf16[128,256]{1,0:T(8,128)(2,1)S(1)} %fusion.5, bf16[128,1024]{1,0:T(8,128)(2,1)S(1)} %all_gather.6), kind=kOutput, calls=%fused_computation.87 | convolution fusion | flops 67108864 | bytes 1376256 | tf_op jit(solution)/shard_map/dot_general | solution.py:129
  57.5 0.0 reduce-scatter.5.cloned.1.call-update
  57.6 23.3 %reduce-scatter.3.cloned.1.call-done = f32[32,1024]{1,0:T(8,128)} async-done(((f32[128,1024]{1,0:T(8,128)}), f32[32,1024]{1,0:T(8,128)}) %reduce-scatter.3.cloned.1.call-update) | async-done | bytes 131088 | tf_op jit(solution)/shard_map/reduce_scatter | solution.py:121
  80.9 34.9 %reduce-scatter.5.cloned.1.call-done = f32[32,1024]{1,0:T(8,128)} async-done(((f32[256,1024]{1,0:T(8,128)}), f32[32,1024]{1,0:T(8,128)}) %reduce-scatter.5.cloned.1.call-update) | async-done | bytes 131088 | tf_op jit(solution)/shard_map/reduce_scatter | solution.py:128
  115.8 1.6 %add.131 = f32[32,1024]{1,0:T(8,128)} add(f32[32,1024]{1,0:T(8,128)} %reduce-scatter.3.cloned.1.call-done, f32[32,1024]{1,0:T(8,128)} %reduce-scatter.5.cloned.1.call-done) | non-fusion elementwise | flops 32768 | bytes 393216 | tf_op jit(solution)/shard_map/add | solution.py:136
  (14 shorter events, 0.2 us)
Async XLA Ops:
  6.5 27.2 %copy-start = (s32[1024]{0:T(1024)S(1)}, s32[1024]{0:T(1024)}, u32[]{:S(2)}) copy-start(s32[1024]{0:T(1024)} %param.5) | copy-start | bytes 12292
  6.5 74.3 %reduce-scatter.3.cloned.1.call-start = ((), (), s32[]{:S(2)}) async-start(), calls=%async_computation.2 | async-start | bytes 655360 | tf_op jit(solution)/shard_map/reduce_scatter | solution.py:121
  6.5 10.8 %copy-start.1 = (bf16[32,1024]{1,0:T(8,128)(2,1)S(1)}, bf16[32,1024]{1,0:T(8,128)(2,1)}, u32[]{:S(2)}) copy-start(bf16[32,1024]{1,0:T(8,128)(2,1)} %param.3) | copy-start | bytes 196612
  32.8 0.7 copy-start.2
  56.2 59.6 %reduce-scatter.5.cloned.1.call-start = ((), (), s32[]{:S(2)}) async-start(), calls=%async_computation.3 | async-start | bytes 1179648 | tf_op jit(solution)/shard_map/reduce_scatter | solution.py:128
Sparse Core Ops, SparseCore 0:
  56.3 24.5 reduce-scatter.2
  83.2 32.5 reduce-scatter.4
where the time goes:
time: 125 us; the launch traced here: 124 us
  waiting for transfers between devices  58.3 us (47%)
  blocking collectives  43.8 us (35%)
  between operations  13.5 us (11%)
  local copies, waits for them, and re-layouts  3.39 us (3%)
  matrix products  2.8 us (2%)
  other arithmetic  2.46 us (2%)
    reduce_scatter x1, waiting for transfers between devices, body(): lax.psum_scatter(lax.dot_general(part, anchors, (((0,), (0,)), ((), ())),...  34.9 us
    reduce_scatter x1, waiting for transfers between devices, body(): lax.psum_scatter(jnp.dot(part, candidates, preferred_element_type=jnp.flo...  23.3 us
    all_gather x1, blocking collectives, body(): candidates = lax.all_gather(embed, 'row', axis=0, tiled=True)  15.4 us
    all_gather x1, blocking collectives, body(): anchors = lax.all_gather(embed, 'col', axis=0, tiled=True)  10.8 us
    psum x1, blocking collectives, body(): matching_pair_affinity_lines = lax.psum(pos_part, 'col')  8.93 us
    psum x1, blocking collectives, body(): count_sum, slope_sum = lax.psum((count_part, slope_part), 'col')  8.64 us
  transfers between devices with their start and end apart: 2, of which 2 were waited for; matrix products, arithmetic and copies ran while one was open for 1% of the time, Pallas kernels for 0%

commit v1 on v0

v1 whole, which is shorter than its diff:
```python
import functools

import jax
import jax.numpy as jnp
from jax import lax
from jax.experimental import pallas as pl
from jax.experimental.pallas import tpu as pltpu
from jax.sharding import PartitionSpec as P

logistic_sharpness = 0.02
half_scale = 0.5 / logistic_sharpness
masked = -1e30
lane_block = 256
row_chunk = 64


def fold_rows(values):
    return jnp.sum(values.reshape(values.shape[0] // 8, 8, values.shape[1]), axis=0)


def lookup_rows(table_ref, ids):
    high = ids // 128
    low = ids % 128
    found = jnp.zeros(ids.shape, jnp.int32)
    for line in range(table_ref.shape[0]):
        entries = jnp.broadcast_to(table_ref[line : line + 1, :], ids.shape)
        picked = jnp.take_along_axis(entries, low, axis=1)
        found = jnp.where(high == line, picked, found)
    return found


def kernel(shard, width, pos_count, base_ref, packed_ref, table_ref, out_ref, score_ref, own_ref, stat_ref):
    total = packed_ref.shape[0]
    base = pl.multiple_of(base_ref[0], shard)
    embed_ref = packed_ref.at[:, 0:width]
    place = lax.broadcasted_iota(jnp.int32, (16, 128), 0)
    eye = (place == lax.broadcasted_iota(jnp.int32, (16, 128), 1)).astype(jnp.bfloat16)

    def target_step(block, carry):
        begin = pl.multiple_of(block * 128, 128)
        parts = lax.dot_general(
            eye,
            packed_ref[pl.ds(begin, 128), width : width + 128],
            (((1,), (1,)), ((), ())),
            preferred_element_type=jnp.float32,
        ).astype(jnp.int32)
        ids = parts[0:8, :] * 256 + parts[8:16, :]
        stat_ref[0:8, pl.ds(begin, 128)] = lookup_rows(table_ref, ids).astype(jnp.float32)
        return carry

    lax.fori_loop(0, total // 128, target_step, 0)

    def block_step(block, carry):
        start = pl.multiple_of(block * lane_block, lane_block)
        anchors = embed_ref[pl.ds(start, lane_block), :]
        targets = stat_ref[0:pos_count, pl.ds(start, lane_block)].astype(jnp.int32)
        index = lax.broadcasted_iota(jnp.int32, (row_chunk, lane_block), 0)
        lane = lax.broadcasted_iota(jnp.int32, (row_chunk, lane_block), 1)

        def score_step(chunk, sums):
            row = pl.multiple_of(chunk * row_chunk, row_chunk)
            scores = half_scale * lax.dot_general(
                embed_ref[pl.ds(row, row_chunk), :],
                anchors,
                (((1,), (1,)), ((), ())),
                preferred_element_type=jnp.float32,
            )
            scores = jnp.where(index + (row - start) == lane, masked, scores)
            score_ref[pl.ds(row, row_chunk), :] = scores
            return tuple(
                sums[m]
                + fold_rows(jnp.where(index == targets[m : m + 1, :] - row, scores, 0.0))
                for m in range(pos_count)
            )

        zero = jnp.zeros((8, lane_block), jnp.float32)
        sums = lax.fori_loop(0, total // row_chunk, score_step, (zero,) * pos_count)
        pos = [jnp.sum(part, axis=0, keepdims=True) for part in sums]

        def rank_step(chunk, sums):
            row = pl.multiple_of(chunk * row_chunk, row_chunk)
            scores = score_ref[pl.ds(row, row_chunk), :]
            out = []
            for m in range(pos_count):
                bent = jnp.tanh(scores - pos[m])
                out.append(sums[2 * m] + fold_rows(bent))
                out.append(sums[2 * m + 1] + fold_rows(bent * bent))
            return tuple(out)

        sums = lax.fori_loop(0, total // row_chunk, rank_step, (zero,) * (2 * pos_count))
        ranks = []
        slopes = []
        for m in range(pos_count):
            ranks.append(0.5 + 0.5 * (total + jnp.sum(sums[2 * m], axis=0, keepdims=True)))
            slopes.append(0.25 * (total - jnp.sum(sums[2 * m + 1], axis=0, keepdims=True)))
        own_ref[:, pl.ds(start, lane_block)] = score_ref[pl.ds(base, shard), :]

        factor = 1.0 / (pos_count * total)
        pulls = [-factor / ranks[m] for m in range(pos_count)]
        for m in range(pos_count):
            prank = 1.0
            pulled = 0.0
            for q in range(pos_count):
                if q != m:
                    bent = jnp.tanh(pos[q] - pos[m])
                    prank = prank + 0.5 * (1.0 + bent)
                    pulled = pulled + (pulls[q] - pulls[m]) * (0.25 * (1.0 - bent * bent))
            weight = prank / (ranks[m] * ranks[m]) * (factor / logistic_sharpness)
            extra = pulled / logistic_sharpness - weight * slopes[m]
            stat_ref[8 + m : 9 + m, pl.ds(start, lane_block)] = pos[m]
            stat_ref[16 + m : 17 + m, pl.ds(start, lane_block)] = 0.25 * weight
            stat_ref[24 + m : 25 + m, pl.ds(start, lane_block)] = extra
        return carry

    lax.fori_loop(0, total // lane_block, block_step, 0)

    scores = own_ref[...]
    lane = lax.broadcasted_iota(jnp.int32, (shard, total), 1)
    line = lax.broadcasted_iota(jnp.int32, (shard, total), 0) + base
    own_lane = pl.multiple_of(base // 128 * 128, 128)
    near = lax.broadcasted_iota(jnp.int32, (shard, 128), 1) + own_lane
    chosen = near == lax.broadcasted_iota(jnp.int32, (shard, 128), 0) + base

    def column(k):
        values = stat_ref[k : k + 1, pl.ds(own_lane, 128)]
        return jnp.sum(jnp.where(chosen, values, 0.0), axis=1, keepdims=True)

    grads = [jnp.zeros((shard, total), jnp.float32) for _ in range(2)]
    for m in range(pos_count):
        bent = jnp.tanh(scores - stat_ref[8 + m : 9 + m, :])
        grads[0] = grads[0] + stat_ref[16 + m : 17 + m, :] * (1.0 - bent * bent)
        bent = jnp.tanh(scores - column(8 + m))
        grads[1] = grads[1] + column(16 + m) * (1.0 - bent * bent)
    for m in range(pos_count):
        found = line == stat_ref[m : m + 1, :].astype(jnp.int32)
        grads[0] = grads[0] + jnp.where(found, stat_ref[24 + m : 25 + m, :], 0.0)
        found = lane == column(m).astype(jnp.int32)
        grads[1] = grads[1] + jnp.where(found, column(24 + m), 0.0)
    both = jnp.concatenate(grads, axis=0).astype(jnp.bfloat16)
    product = jnp.dot(both, embed_ref[...], preferred_element_type=jnp.float32)
    out_ref[...] = product[:shard, :] + product[shard:, :]


def body(embed, positives, placement):
    shard, width = embed.shape
    axes = ("row", "col")
    total = shard * lax.axis_size(axes)
    pos_count = positives.shape[1]
    ids = lax.dynamic_slice_in_dim(positives, lax.axis_index("col") * shard, shard, 0)
    tail = jnp.zeros((shard, 128), jnp.bfloat16)
    tail = tail.at[:, 0:pos_count].set((ids // 256).astype(jnp.bfloat16))
    tail = tail.at[:, 8 : 8 + pos_count].set((ids % 256).astype(jnp.bfloat16))
    packed = lax.all_gather(jnp.concatenate([embed, tail], axis=1), axes, axis=0, tiled=True)
    base = (lax.axis_index(axes) * shard).astype(jnp.int32).reshape(1)
    vmem = pl.BlockSpec(memory_space=pltpu.VMEM)
    return pl.pallas_call(
        functools.partial(kernel, shard, width, pos_count),
        out_shape=jax.ShapeDtypeStruct((shard, width), jnp.float32),
        in_specs=[pl.BlockSpec(memory_space=pltpu.SMEM), vmem, vmem],
        out_specs=vmem,
        scratch_shapes=[
            pltpu.VMEM((total, lane_block), jnp.float32),
            pltpu.VMEM((shard, total), jnp.float32),
            pltpu.VMEM((32, total), jnp.float32),
        ],
        compiler_params=pltpu.CompilerParams(vmem_limit_bytes=48 * 1024 * 1024),
        cost_estimate=pl.CostEstimate(
            flops=2 * total * total * width,
            bytes_accessed=2 * total * width,
            transcendentals=4 * total * total,
        ),
    )(base, packed, placement.reshape(-1, 128))


def solution(mesh):
    return jax.shard_map(
        body,
        mesh=mesh,
        in_specs=(P(("row", "col"), None), P("row", None), P()),
        out_specs=P(("row", "col"), None),
        check_vma=False,
    )
```

time: 125 us -> 109 us (0.87)
  blocking collectives: 43.8 us -> 0 us
  Pallas kernels: 0 us -> 28.3 us
  matrix products: 2.8 us -> 0 us
  waiting for transfers between devices: 58.3 us -> 60.1 us
  other arithmetic: 2.46 us -> 4.08 us
    all_gather x0 -> x1, waiting for transfers between devices: none -> 60.1 us  [body(): lax.all_gather(jnp.concatenate([embed, tail], axis=1), axes, axis=0, tile...]
    reduce_scatter x2 -> x0, waiting for transfers between devices: 58.2 us -> none  [the longest x1 34.9 us: body(): lax.psum_scatter(lax.dot_general(part, anchors, (((0,), (0,)), ((), ())),...]
    pallas_call x0 -> x1, Pallas kernels: none -> 28.3 us  [body(): pl.pallas_call(functools.partial(kernel, shard, width, pos_count), out_sh...]
    all_gather x2 -> x0, blocking collectives: 26.3 us -> none  [the longest x1 15.4 us: body(): candidates = lax.all_gather(embed, 'row', axis=0, tiled=True)]
    psum x2 -> x0, blocking collectives: 17.6 us -> none  [the longest x1 8.93 us: body(): matching_pair_affinity_lines = lax.psum(pos_part, 'col')]
    dot_general x3 -> x0, matrix products: 2.8 us -> none  [the longest x1 1.31 us: body(): lax.dot_general(part, anchors, (((0,), (0,)), ((), ())), preferred_elemen...]
    another operation x2 -> x3, other arithmetic: 0.02 us -> 2.6 us  [the longest x1 0.01 us: sigmoid_sums(): return (jnp.stack(counts, axis=1), jnp.stack(slopes, axis=1))]
    gather x3 -> x0, local copies, waits for them, and re-layouts: 2.45 us -> none  [body(): targets = jnp.take(placement, positives)]
  transfers between devices with their start and end apart: 2 -> 1, of which waited for: 2 -> 1; matrix products, arithmetic and copies ran while one was open for 1% -> 0% of each run, Pallas kernels for 0% -> 0%
where the time goes in v1:
time: 109 us
  waiting for transfers between devices  60.1 us (55%)
  Pallas kernels  28.3 us (26%)
  between operations  13.4 us (12%)
  other arithmetic  4.08 us (4%)
  local copies, waits for them, and re-layouts  2.82 us (3%)
    all_gather x1, waiting for transfers between devices, body(): lax.all_gather(jnp.concatenate([embed, tail], axis=1), axes, axis=0, tile...  60.1 us
    pallas_call x1, Pallas kernels, body(): pl.pallas_call(functools.partial(kernel, shard, width, pos_count), out_sh...  28.3 us
    another operation x3, other arithmetic  2.6 us
    unnamed x7, local copies, waits for them, and re-layouts  2.45 us
  transfers between devices with their start and end apart: 1, of which 1 were waited for; matrix products, arithmetic and copies ran while one was open for 0% of the time, Pallas kernels for 0%

profile of v1, /device:TPU:0, one launch (start us, length us, event | category | flops | bytes accessed | tf_op | source)
XLA Modules:
  0.0 108.7 jit_solution(2577073779516823251)
XLA Ops:
  6.5 0.0 copy-start
  6.5 0.0 all-gather.2.cloned.1.call-start
  6.5 0.7 compare_reduce_fusion.1
  7.2 0.6 compare_reduce_fusion
  7.8 0.0 copy-done
  7.8 0.1 constant_dynamic-slice_fusion
  7.9 0.1 copy.5
  8.0 1.3 %fusion.4 = (bf16[32,4]{1,0:T(8,128)(2,1)S(1)}, bf16[32,4]{1,0:T(8,128)(2,1)S(1)}) fusion(s32[32,4]{1,0:T(8,128)S(1)} %copy.5, pred[]{:T(512)} %compare_reduce_fusion, pred[]{:T(512)} %compare_reduce_fusion.1), kind=kLoop, calls=%fused_computation.11 | loop fusion | flops 2944 | bytes 1026 | tf_op jit(solution)/shard_map/select.3
  9.3 0.3 scatter.9
  9.6 1.5 %pad_maximum_fusion = bf16[32,1152]{1,0:T(8,128)(2,1)} fusion(bf16[32,128]{1,0:T(8,128)(2,1)S(1)} %scatter.9, bf16[32,1024]{1,0:T(8,128)(2,1)} %param.7), kind=kLoop, calls=%fused_computation | loop fusion | flops 147456 | bytes 147456 | tf_op jit(solution)/shard_map/concatenate | solution.py:153
  11.1 0.0 all-gather.2.cloned.1.call-update
  11.1 60.1 %all-gather.2.cloned.1.call-done.packed_ref = bf16[1024,1152]{1,0:T(8,128)(2,1)} async-done(((bf16[32,1152]{1,0:T(8,128)(2,1)}), bf16[1024,1152]{1,0:T(8,128)(2,1)}) %all-gather.2.cloned.1.call-update) | async-done | bytes 2359312 | tf_op jit(solution)/shard_map/all_gather | solution.py:153
  71.3 0.0 copy-start.1
  71.3 1.7 %copy-done.1 = bf16[1024,1152]{1,0:T(8,128)(2,1)S(1)} copy-done((bf16[1024,1152]{1,0:T(8,128)(2,1)S(1)}, bf16[1024,1152]{1,0:T(8,128)(2,1)}, u32[]{:S(2)}) %copy-start.1) | copy-done | bytes 2359320
  72.9 0.0 copy-start.2
  72.9 0.7 copy-done.2
  73.6 28.3 %shard_map.37 = f32[32,1024]{1,0:T(8,128)} custom-call(s32[1]{0:T(128)} %bitcast.base_ref, bf16[1024,1152]{1,0:T(8,128)(2,1)S(1)} %copy-done.1, s32[8,128]{1,0:T(8,128)S(1)} %bitcast.2), custom_call_target="tpu_custom_call" | custom-call | flops 2147483648 | bytes 2097152 | tf_op jit(solution)/shard_map/pallas_call | solution.py:156
  (1 shorter events, 0.0 us)
Async XLA Ops:
  6.5 1.3 %copy-start = (s32[128,4]{0,1:T(4,128)S(1)}, s32[128,4]{0,1:T(4,128)}, u32[]{:S(2)}) copy-start(s32[128,4]{0,1:T(4,128)} %param.8) | copy-start | bytes 6148
  6.5 64.7 %all-gather.2.cloned.1.call-start = ((), (), s32[]{:S(2)}) async-start(), calls=%async_computation | async-start | bytes 2433024 | tf_op jit(solution)/shard_map/all_gather | solution.py:153
  71.3 1.7 %copy-start.1 = (bf16[1024,1152]{1,0:T(8,128)(2,1)S(1)}, bf16[1024,1152]{1,0:T(8,128)(2,1)}, u32[]{:S(2)}) copy-start(bf16[1024,1152]{1,0:T(8,128)(2,1)} %all-gather.2.cloned.1.call-done.packed_ref) | copy-start | bytes 7077892
  72.9 0.7 copy-start.2
Sparse Core Ops, SparseCore 0:
  11.3 59.9 all-gather.1

commit v2 on v1

v2 whole, which is shorter than its diff:
```python
import functools

import jax
import jax.numpy as jnp
from jax import lax
from jax.experimental import pallas as pl
from jax.experimental.pallas import tpu as pltpu
from jax.sharding import PartitionSpec as P

logistic_sharpness = 0.02
half_scale = 0.5 / logistic_sharpness
masked = -1e30
lane_block = 256
row_chunk = 256


def fold_rows(values):
    return jnp.sum(values.reshape(values.shape[0] // 8, 8, values.shape[1]), axis=0)


def lookup(table_ref, ids):
    low = ids % 128
    high = ids // 128
    found = jnp.zeros(ids.shape, jnp.int32)
    for line in range(table_ref.shape[0]):
        entries = jnp.broadcast_to(table_ref[line : line + 1, :], ids.shape)
        found = jnp.where(high == line, jnp.take_along_axis(entries, low, axis=1), found)
    return found


def kernel(cols, levels, shard, pos_count, *refs):
    place_ref, table_ref = refs[:2]
    lines = 2 * levels
    ids_refs = refs[2 : 2 + lines]
    blocks = refs[2 + lines : 2 + lines + 2 * cols]
    out_ref, embed_ref, score_ref, own_ref, target_ref, stat_ref, sems = refs[2 + lines + 2 * cols :]
    total = embed_ref.shape[0]
    me = place_ref[0]
    my_col = place_ref[1]

    copies = []
    for p in range(cols):
        for c in range(2):
            for d in range(levels):
                copies.append(
                    pltpu.make_async_copy(
                        blocks[p * 2 + c].at[d * shard : (d + 1) * shard, :],
                        embed_ref.at[pl.ds(((d * 2 + c) * cols + p) * shard, shard), :],
                        sems.at[len(copies)],
                    )
                )
    for copy in copies:
        copy.start()

    group = cols * shard
    for line in range(lines):
        for begin in range(0, group, 128):
            ids = ids_refs[line][:, begin : begin + 128]
            ids = jnp.concatenate([ids, ids], axis=0)
            found = lookup(table_ref, ids) ^ me
            lane = lax.broadcasted_iota(jnp.int32, found.shape, 1)
            found = jnp.take_along_axis(found, lane ^ (my_col % 128), axis=1)
            start = line * group + (begin ^ (my_col - my_col % 128))
            target_ref[:, pl.ds(pl.multiple_of(start, 128), 128)] = found
    for copy in copies:
        copy.wait()

    pair = lane_block // 128

    def score_chunk(anchors, start, buffer, chunk, picked):
        row = pl.multiple_of(chunk * row_chunk, row_chunk)
        scores = half_scale * lax.dot_general(
            embed_ref[pl.ds(row, row_chunk), :],
            anchors,
            (((1,), (1,)), ((), ())),
            preferred_element_type=jnp.float32,
        )
        index = lax.broadcasted_iota(jnp.int32, (row_chunk, lane_block), 0)
        lane = lax.broadcasted_iota(jnp.int32, (row_chunk, lane_block), 1)
        scores = jnp.where(index + (row - start) == lane, masked, scores)
        score_ref[buffer, pl.ds(row, row_chunk), :] = scores
        picked = list(picked)
        for half in range(pair):
            targets = target_ref[:, pl.ds(pl.multiple_of(start + half * 128, 128), 128)]
            near = (targets - row) >> 3
            sub = targets & 7
            for step in range(row_chunk // 8):
                tile = scores[step * 8 : (step + 1) * 8, half * 128 : (half + 1) * 128]
                tile = jnp.take_along_axis(tile, sub, axis=0)
                picked[half] = jnp.where(near == step, tile, picked[half])
        return tuple(picked)

    def rank_chunk(pos, buffer, chunk, sums):
        row = pl.multiple_of(chunk * row_chunk, row_chunk)
        sums = list(sums)
        for part in range(row_chunk // 64):
            scores = score_ref[buffer, pl.ds(row + part * 64, 64), :]
            for m in range(pos_count):
                bent = jnp.tanh(scores - pos[m])
                sums[2 * m] = sums[2 * m] + fold_rows(bent)
                sums[2 * m + 1] = sums[2 * m + 1] + fold_rows(bent * bent)
        return tuple(sums)

    chunks = total // row_chunk
    nothing = (jnp.zeros((8, 128), jnp.float32),) * pair
    zero = (jnp.zeros((8, lane_block), jnp.float32),) * (2 * pos_count)

    def split(picked):
        wide = jnp.concatenate(picked, axis=1)
        return tuple(wide[m : m + 1, :] for m in range(pos_count))

    def finish(start, buffer, pos, sums):
        ranks = []
        slopes = []
        for m in range(pos_count):
            ranks.append(0.5 + 0.5 * (total + jnp.sum(sums[2 * m], axis=0, keepdims=True)))
            slopes.append(0.25 * (total - jnp.sum(sums[2 * m + 1], axis=0, keepdims=True)))
        own_ref[:, pl.ds(start, lane_block)] = score_ref[buffer, 0:shard, :]
        factor = 1.0 / (pos_count * total)
        pulls = [-factor / ranks[m] for m in range(pos_count)]
        for m in range(pos_count):
            prank = 1.0
            pulled = 0.0
            for q in range(pos_count):
                if q != m:
                    bent = jnp.tanh(pos[q] - pos[m])
                    prank = prank + 0.5 * (1.0 + bent)
                    pulled = pulled + (pulls[q] - pulls[m]) * (0.25 * (1.0 - bent * bent))
            weight = prank / (ranks[m] * ranks[m]) * (factor / logistic_sharpness)
            extra = pulled / logistic_sharpness - weight * slopes[m]
            stat_ref[m : m + 1, pl.ds(start, lane_block)] = pos[m]
            stat_ref[8 + m : 9 + m, pl.ds(start, lane_block)] = 0.25 * weight
            stat_ref[16 + m : 17 + m, pl.ds(start, lane_block)] = extra

    first = embed_ref[0:lane_block, :]
    picked = lax.fori_loop(
        0, chunks, lambda chunk, have: score_chunk(first, 0, 0, chunk, have), nothing
    )

    def block_step(block, pos):
        start = pl.multiple_of(block * lane_block, lane_block)
        buffer = lax.rem(block, 2)
        following = pl.multiple_of(start + lane_block, lane_block)
        anchors = embed_ref[pl.ds(following, lane_block), :]

        def both(chunk, carry):
            picked, sums = carry
            picked = score_chunk(anchors, following, 1 - buffer, chunk, picked)
            return picked, rank_chunk(pos, buffer, chunk, sums)

        picked, sums = lax.fori_loop(0, chunks, both, (nothing, zero))
        finish(start, buffer, pos, sums)
        return split(picked)

    last = total // lane_block - 1
    pos = lax.fori_loop(0, last, block_step, split(picked))
    sums = lax.fori_loop(
        0, chunks, lambda chunk, have: rank_chunk(pos, last % 2, chunk, have), zero
    )
    finish(last * lane_block, last % 2, pos, sums)

    scores = own_ref[...]
    lane = lax.broadcasted_iota(jnp.int32, (shard, total), 1)
    line = lax.broadcasted_iota(jnp.int32, (shard, total), 0)
    columns = jnp.transpose(
        jnp.concatenate(
            [stat_ref[:, 0:128], target_ref[:, 0:128].astype(jnp.float32)], axis=0
        )
    )[0:shard, :]
    grads = [jnp.zeros((shard, total), jnp.float32) for _ in range(2)]
    for m in range(pos_count):
        bent = jnp.tanh(scores - stat_ref[m : m + 1, :])
        grads[0] = grads[0] + stat_ref[8 + m : 9 + m, :] * (1.0 - bent * bent)
        bent = jnp.tanh(scores - columns[:, m : m + 1])
        grads[1] = grads[1] + columns[:, 8 + m : 9 + m] * (1.0 - bent * bent)
    for m in range(pos_count):
        found = line == target_ref[m : m + 1, :]
        grads[0] = grads[0] + jnp.where(found, stat_ref[16 + m : 17 + m, :], 0.0)
        found = lane == columns[:, 24 + m : 25 + m].astype(jnp.int32)
        grads[1] = grads[1] + jnp.where(found, columns[:, 16 + m : 17 + m], 0.0)
    both = jnp.concatenate(grads, axis=0).astype(jnp.bfloat16)
    product = jnp.dot(both, embed_ref[...], preferred_element_type=jnp.float32)
    out_ref[...] = product[:shard, :] + product[shard:, :]


def body(embed, positives, placement):
    shard, width = embed.shape
    axes = ("row", "col")
    rows = lax.axis_size("row")
    cols = lax.axis_size("col")
    levels = rows // 2
    total = shard * rows * cols
    pos_count = positives.shape[1]

    def swap(array, axis, mask):
        size = lax.axis_size(axis)
        return lax.ppermute(array, axis, [(i, i ^ mask) for i in range(size)])

    tall = jnp.concatenate(
        [embed] + [swap(embed, "row", 2 * d) for d in range(1, levels)], axis=0
    )
    ids = positives.T
    ids = [ids] + [swap(ids, "row", line) for line in range(1, rows)]
    plane = [tall] + [swap(tall, "col", p) for p in range(1, cols)]
    blocks = []
    for part in plane:
        blocks += [part, swap(part, "row", 1)]

    place = jnp.stack([lax.axis_index(axes) * shard, lax.axis_index("col") * shard])
    vmem = pl.BlockSpec(memory_space=pltpu.VMEM)
    return pl.pallas_call(
        functools.partial(kernel, cols, levels, shard, pos_count),
        out_shape=jax.ShapeDtypeStruct((shard, width), jnp.float32),
        in_specs=[pl.BlockSpec(memory_space=pltpu.SMEM), vmem]
        + [vmem] * rows
        + [pl.BlockSpec(memory_space=pl.ANY)] * (2 * cols),
        out_specs=vmem,
        scratch_shapes=[
            pltpu.VMEM((total, width), jnp.bfloat16),
            pltpu.VMEM((2, total, lane_block), jnp.float32),
            pltpu.VMEM((shard, total), jnp.float32),
            pltpu.VMEM((8, total), jnp.int32),
            pltpu.VMEM((24, total), jnp.float32),
            pltpu.SemaphoreType.DMA((rows * cols,)),
        ],
        compiler_params=pltpu.CompilerParams(vmem_limit_bytes=50 * 1024 * 1024),
        cost_estimate=pl.CostEstimate(
            flops=2 * total * total * width,
            bytes_accessed=2 * total * width,
            transcendentals=4 * total * total,
        ),
    )(place.astype(jnp.int32), placement.reshape(-1, 128), *ids, *blocks)


def solution(mesh):
    return jax.shard_map(
        body,
        mesh=mesh,
        in_specs=(P(("row", "col"), None), P("row", None), P()),
        out_specs=P(("row", "col"), None),
        check_vma=False,
    )
```

time: 109 us -> 66 us (0.61)
  waiting for transfers between devices: 60.1 us -> 37.7 us
  Pallas kernels: 28.3 us -> 14.1 us
  between operations: 13.4 us -> 0.06 us
  starting transfers between devices: 0.01 us -> 13 us
  other arithmetic: 4.08 us -> 0.07 us
  local copies, waits for them, and re-layouts: 2.82 us -> 0.94 us
    all_gather x1 -> x0, waiting for transfers between devices: 60.1 us -> none  [body(): lax.all_gather(jnp.concatenate([embed, tail], axis=1), axes, axis=0, tile...]
    ppermute x0 -> x17, waiting for transfers between devices: none -> 37.7 us  [swap(): return lax.ppermute(array, axis, [(i, i ^ mask) for i in range(size)])]
    pallas_call x1, Pallas kernels: 28.3 us -> 14.1 us  [body(): pl.pallas_call(functools.partial(kernel, cols, levels, shard, pos_count),...]
    ppermute x0 -> x17, starting transfers between devices: none -> 13 us  [swap(): return lax.ppermute(array, axis, [(i, i ^ mask) for i in range(size)])]
    another operation x3 -> x1, other arithmetic: 2.6 us -> 0.07 us  [body(): jnp.stack([lax.axis_index(axes) * shard, lax.axis_index('col') * shard])]
    unnamed x7, local copies, waits for them, and re-layouts: 2.45 us -> 0.93 us
    concatenate x1 -> x0, other arithmetic: 1.48 us -> none  [body(): jnp.concatenate([embed, tail], axis=1)]
  transfers between devices with their start and end apart: 1 -> 17, of which waited for: 1 -> 12; matrix products, arithmetic and copies ran while one was open for 0% -> 2% of each run, Pallas kernels for 0% -> 0%
where the time goes in v2:
time: 66 us; the launch traced here: 65.9 us
  waiting for transfers between devices  37.7 us (57%)
  Pallas kernels  14.1 us (21%)
  starting transfers between devices  13 us (20%)
  local copies, waits for them, and re-layouts  0.94 us (1%)
    ppermute x17, waiting for transfers between devices, swap(): return lax.ppermute(array, axis, [(i, i ^ mask) for i in range(size)])  37.7 us
    pallas_call x1, Pallas kernels, body(): pl.pallas_call(functools.partial(kernel, cols, levels, shard, pos_count),...  14.1 us
    ppermute x17, starting transfers between devices, swap(): return lax.ppermute(array, axis, [(i, i ^ mask) for i in range(size)])  13 us
  transfers between devices with their start and end apart: 17, of which 12 were waited for; matrix products, arithmetic and copies ran while one was open for 2% of the time, Pallas kernels for 0%

profile of v2, /device:TPU:0, one launch (start us, length us, event | category | flops | bytes accessed | tf_op | source)
XLA Modules:
  0.0 65.9 jit_solution(16627566542568998546)
XLA Ops:
  0.0 4.0 %collective-permute-start.8 = (bf16[32,1024]{1,0:T(8,128)(2,1)}, bf16[32,1024]{1,0:T(8,128)(2,1)S(1)}, u32[]{:S(2)}, u32[]{:S(2)}) collective-permute-start(bf16[32,1024]{1,0:T(8,128)(2,1)} %param.3), channel_id=1, source_target_pairs={{0,16},{4,20},{8,24},{12,28},{16,0},{20,4},{24,8},{28,12},{1,17},{... | collective-permute-start | bytes 196616 | tf_op jit(solution)/shard_map/ppermute | solution.py:197
  4.0 1.6 %collective-permute-start.7 = (bf16[32,1024]{1,0:T(8,128)(2,1)}, bf16[32,1024]{1,0:T(8,128)(2,1)S(1)}, u32[]{:S(2)}, u32[]{:S(2)}) collective-permute-start(bf16[32,1024]{1,0:T(8,128)(2,1)} %param.3), channel_id=1, source_target_pairs={{0,8},{4,12},{8,0},{12,4},{16,24},{20,28},{24,16},{28,20},{1,9},{5... | collective-permute-start | bytes 196616 | tf_op jit(solution)/shard_map/ppermute | solution.py:197
  5.6 0.0 collective-permute-start.9
  5.6 0.9 %constant_dynamic-update-slice_fusion.3 = bf16[128,1024]{1,0:T(8,128)(2,1)S(1)} fusion(bf16[32,1024]{1,0:T(8,128)(2,1)} %param.3), kind=kLoop, calls=%fused_computation.3 | loop fusion | bytes 131072
  6.5 2.0 %collective-permute-done.7 = bf16[32,1024]{1,0:T(8,128)(2,1)S(1)} collective-permute-done((bf16[32,1024]{1,0:T(8,128)(2,1)}, bf16[32,1024]{1,0:T(8,128)(2,1)S(1)}, u32[]{:S(2)}, u32[]{:S(2)}) %collective-permute-start.7) | collective-permute-done | bytes 65568 | tf_op jit(solution)/shard_map/ppermute | solution.py:197
  8.5 0.0 collective-permute-done.8
  8.5 0.0 copy-start.1
  8.6 3.3 %collective-permute-done.9 = bf16[32,1024]{1,0:T(8,128)(2,1)S(1)} collective-permute-done((bf16[32,1024]{1,0:T(8,128)(2,1)}, bf16[32,1024]{1,0:T(8,128)(2,1)S(1)}, u32[]{:S(2)}, u32[]{:S(2)}) %collective-permute-start.9) | collective-permute-done | bytes 65568 | tf_op jit(solution)/shard_map/ppermute | solution.py:197
  11.9 2.4 %collective-permute-start.15 = (bf16[128,1024]{1,0:T(8,128)(2,1)S(1)}, bf16[128,1024]{1,0:T(8,128)(2,1)S(1)}, u32[]{:S(2)}, u32[]{:S(2)}) collective-permute-start(bf16[128,1024]{1,0:T(8,128)(2,1)S(1)} %constant_dynamic-update-slice_fusion.refs_10_), channel_id=1, source_target_pairs={{0,3},{1,2},{2,1},{3,0},{4,7},{5,6},{6,5},{7,4},{8,11},{9,10},{10,... | collective-permute-start | bytes 786440 | tf_op jit(solution)/shard_map/ppermute | solution.py:197
  14.3 0.5 collective-permute-start.13
  14.8 0.5 collective-permute-start.11
  15.4 0.0 collective-permute-start.10
  15.4 6.7 %collective-permute-done.15.refs_16_ = bf16[128,1024]{1,0:T(8,128)(2,1)S(1)} collective-permute-done((bf16[128,1024]{1,0:T(8,128)(2,1)S(1)}, bf16[128,1024]{1,0:T(8,128)(2,1)S(1)}, u32[]{:S(2)}, u32[]{:S(2)}) %collective-permute-start.15) | collective-permute-done | bytes 262176 | tf_op jit(solution)/shard_map/ppermute | solution.py:197
  22.0 0.0 collective-permute-start.16
  22.0 2.8 %collective-permute-done.13.refs_14_ = bf16[128,1024]{1,0:T(8,128)(2,1)S(1)} collective-permute-done((bf16[128,1024]{1,0:T(8,128)(2,1)S(1)}, bf16[128,1024]{1,0:T(8,128)(2,1)S(1)}, u32[]{:S(2)}, u32[]{:S(2)}) %collective-permute-start.13) | collective-permute-done | bytes 262176 | tf_op jit(solution)/shard_map/ppermute | solution.py:197
  24.9 0.0 collective-permute-start.14
  24.9 0.1 collective-permute-done.11.refs_12_
  25.0 0.4 collective-permute-start.12
  25.4 0.0 copy-done.1
  25.4 1.6 %collective-permute-start.6 = (s32[4,128]{1,0:T(4,128)S(1)}, s32[4,128]{1,0:T(4,128)S(1)}, u32[]{:S(2)}, u32[]{:S(2)}) collective-permute-start(s32[4,128]{1,0:T(4,128)S(1)} %bitcast.5), channel_id=1, source_target_pairs={{0,28},{4,24},{8,20},{12,16},{16,12},{20,8},{24,4},{28,0},{1,29},{... | collective-permute-start | bytes 6152 | tf_op jit(solution)/shard_map/ppermute | solution.py:197
  27.0 3.2 %collective-permute-done.6.refs_9_ = s32[4,128]{1,0:T(4,128)S(1)} collective-permute-done((s32[4,128]{1,0:T(4,128)S(1)}, s32[4,128]{1,0:T(4,128)S(1)}, u32[]{:S(2)}, u32[]{:S(2)}) %collective-permute-start.6) | collective-permute-done | bytes 2080 | tf_op jit(solution)/shard_map/ppermute | solution.py:197
  30.2 1.9 %collective-permute-start.5 = (s32[4,128]{1,0:T(4,128)S(1)}, s32[4,128]{1,0:T(4,128)S(1)}, u32[]{:S(2)}, u32[]{:S(2)}) collective-permute-start(s32[4,128]{1,0:T(4,128)S(1)} %bitcast.6), channel_id=1, source_target_pairs={{0,24},{4,28},{8,16},{12,20},{16,8},{20,12},{24,0},{28,4},{1,25},{... | collective-permute-start | bytes 6152 | tf_op jit(solution)/shard_map/ppermute | solution.py:197
  32.1 3.5 %collective-permute-done.5.refs_8_ = s32[4,128]{1,0:T(4,128)S(1)} collective-permute-done((s32[4,128]{1,0:T(4,128)S(1)}, s32[4,128]{1,0:T(4,128)S(1)}, u32[]{:S(2)}, u32[]{:S(2)}) %collective-permute-start.5) | collective-permute-done | bytes 2080 | tf_op jit(solution)/shard_map/ppermute | solution.py:197
  35.6 0.0 collective-permute-start.4
  35.6 3.9 %collective-permute-done.4.refs_7_ = s32[4,128]{1,0:T(4,128)S(1)} collective-permute-done((s32[4,128]{1,0:T(4,128)S(1)}, s32[4,128]{1,0:T(4,128)S(1)}, u32[]{:S(2)}, u32[]{:S(2)}) %collective-permute-start.4) | collective-permute-done | bytes 2080 | tf_op jit(solution)/shard_map/ppermute | solution.py:197
  39.5 0.0 collective-permute-start.3
  39.5 4.5 %collective-permute-done.3.refs_6_ = s32[4,128]{1,0:T(4,128)S(1)} collective-permute-done((s32[4,128]{1,0:T(4,128)S(1)}, s32[4,128]{1,0:T(4,128)S(1)}, u32[]{:S(2)}, u32[]{:S(2)}) %collective-permute-start.3) | collective-permute-done | bytes 2080 | tf_op jit(solution)/shard_map/ppermute | solution.py:197
  44.0 0.0 collective-permute-start.2
  44.0 3.0 %collective-permute-done.2.refs_5_ = s32[4,128]{1,0:T(4,128)S(1)} collective-permute-done((s32[4,128]{1,0:T(4,128)S(1)}, s32[4,128]{1,0:T(4,128)S(1)}, u32[]{:S(2)}, u32[]{:S(2)}) %collective-permute-start.2) | collective-permute-done | bytes 2080 | tf_op jit(solution)/shard_map/ppermute | solution.py:197
  47.0 0.0 collective-permute-start.1
  47.0 0.0 copy-start
  47.0 3.6 %collective-permute-done.1.refs_4_ = s32[4,128]{1,0:T(4,128)S(1)} collective-permute-done((s32[4,128]{1,0:T(4,128)S(1)}, s32[4,128]{1,0:T(4,128)S(1)}, u32[]{:S(2)}, u32[]{:S(2)}) %collective-permute-start.1) | collective-permute-done | bytes 2080 | tf_op jit(solution)/shard_map/ppermute | solution.py:197
  50.6 0.0 collective-permute-start
  50.6 0.1 pad_add_fusion.refs_0_
  50.6 1.1 %collective-permute-done.refs_3_ = s32[4,128]{1,0:T(4,128)S(1)} collective-permute-done((s32[4,128]{1,0:T(4,128)S(1)}, s32[4,128]{1,0:T(4,128)S(1)}, u32[]{:S(2)}, u32[]{:S(2)}) %collective-permute-start) | collective-permute-done | bytes 2080 | tf_op jit(solution)/shard_map/ppermute | solution.py:197
  51.7 0.0 collective-permute-done.10.refs_11_
  51.7 0.0 collective-permute-done.16.refs_17_
  51.7 0.0 collective-permute-done.14.refs_15_
  51.7 0.0 collective-permute-done.12.refs_13_
  51.7 0.0 copy-done
  51.7 14.1 %shard_map.37 = f32[32,1024]{1,0:T(8,128)} custom-call(s32[2]{0:T(128)S(1)} %pad_add_fusion.refs_0_, s32[8,128]{1,0:T(8,128)S(1)} %bitcast.4, s32[4,128]{1,0:T(4,128)S(1)} %bitcast.12, s32[4,128]{1,0:T(4,128)S(1)} %collective-permute-done.refs_3_, s32[4,128]{1,0:T(4,128)S(1)} %collective-permute-done.1.refs_4_, s32[4,128]{1,0:T(4,128)S(1)} %collective-permute-done.2.refs_5_, ...), custom_call_target="tpu_custom_call" | custom-call | flops 2147483648 | bytes 2097152 | tf_op jit(solution)/shard_map/pallas_call | solution.py:211
  (3 shorter events, 0.0 us)
Async XLA Ops:
  0.0 8.5 %collective-permute-start.8 = (bf16[32,1024]{1,0:T(8,128)(2,1)}, bf16[32,1024]{1,0:T(8,128)(2,1)S(1)}, u32[]{:S(2)}, u32[]{:S(2)}) collective-permute-start(bf16[32,1024]{1,0:T(8,128)(2,1)} %param.3), channel_id=1, source_target_pairs={{0,16},{4,20},{8,24},{12,28},{16,0},{20,4},{24,8},{28,12},{1,17},{... | collective-permute-start | bytes 196616 | tf_op jit(solution)/shard_map/ppermute | solution.py:197
  4.0 4.5 %collective-permute-start.7 = (bf16[32,1024]{1,0:T(8,128)(2,1)}, bf16[32,1024]{1,0:T(8,128)(2,1)S(1)}, u32[]{:S(2)}, u32[]{:S(2)}) collective-permute-start(bf16[32,1024]{1,0:T(8,128)(2,1)} %param.3), channel_id=1, source_target_pairs={{0,8},{4,12},{8,0},{12,4},{16,24},{20,28},{24,16},{28,20},{1,9},{5... | collective-permute-start | bytes 196616 | tf_op jit(solution)/shard_map/ppermute | solution.py:197
  5.6 6.3 %collective-permute-start.9 = (bf16[32,1024]{1,0:T(8,128)(2,1)}, bf16[32,1024]{1,0:T(8,128)(2,1)S(1)}, u32[]{:S(2)}, u32[]{:S(2)}) collective-permute-start(bf16[32,1024]{1,0:T(8,128)(2,1)} %param.3), channel_id=1, source_target_pairs={{0,24},{4,28},{8,16},{12,20},{16,8},{20,12},{24,0},{28,4},{1,25},{... | collective-permute-start | bytes 196616 | tf_op jit(solution)/shard_map/ppermute | solution.py:197
  8.5 16.8 %copy-start.1 = (s32[128,4]{0,1:T(4,128)S(1)}, s32[128,4]{0,1:T(4,128)}, u32[]{:S(2)}) copy-start(s32[128,4]{0,1:T(4,128)} %param.4) | copy-start | bytes 6148
  11.9 10.2 %collective-permute-start.15 = (bf16[128,1024]{1,0:T(8,128)(2,1)S(1)}, bf16[128,1024]{1,0:T(8,128)(2,1)S(1)}, u32[]{:S(2)}, u32[]{:S(2)}) collective-permute-start(bf16[128,1024]{1,0:T(8,128)(2,1)S(1)} %constant_dynamic-update-slice_fusion.refs_10_), channel_id=1, source_target_pairs={{0,3},{1,2},{2,1},{3,0},{4,7},{5,6},{6,5},{7,4},{8,11},{9,10},{10,... | collective-permute-start | bytes 786440 | tf_op jit(solution)/shard_map/ppermute | solution.py:197
  14.3 10.5 %collective-permute-start.13 = (bf16[128,1024]{1,0:T(8,128)(2,1)S(1)}, bf16[128,1024]{1,0:T(8,128)(2,1)S(1)}, u32[]{:S(2)}, u32[]{:S(2)}) collective-permute-start(bf16[128,1024]{1,0:T(8,128)(2,1)S(1)} %constant_dynamic-update-slice_fusion.refs_10_), channel_id=1, source_target_pairs={{0,2},{1,3},{2,0},{3,1},{4,6},{5,7},{6,4},{7,5},{8,10},{9,11},{10,... | collective-permute-start | bytes 786440 | tf_op jit(solution)/shard_map/ppermute | solution.py:197
  14.8 10.1 %collective-permute-start.11 = (bf16[128,1024]{1,0:T(8,128)(2,1)S(1)}, bf16[128,1024]{1,0:T(8,128)(2,1)S(1)}, u32[]{:S(2)}, u32[]{:S(2)}) collective-permute-start(bf16[128,1024]{1,0:T(8,128)(2,1)S(1)} %constant_dynamic-update-slice_fusion.refs_10_), channel_id=1, source_target_pairs={{0,1},{1,0},{2,3},{3,2},{4,5},{5,4},{6,7},{7,6},{8,9},{9,8},{10,11... | collective-permute-start | bytes 786440 | tf_op jit(solution)/shard_map/ppermute | solution.py:197
  15.4 36.3 %collective-permute-start.10 = (bf16[128,1024]{1,0:T(8,128)(2,1)S(1)}, bf16[128,1024]{1,0:T(8,128)(2,1)S(1)}, u32[]{:S(2)}, u32[]{:S(2)}) collective-permute-start(bf16[128,1024]{1,0:T(8,128)(2,1)S(1)} %constant_dynamic-update-slice_fusion.refs_10_), channel_id=1, source_target_pairs={{0,4},{4,0},{8,12},{12,8},{16,20},{20,16},{24,28},{28,24},{1,5},{5... | collective-permute-start | bytes 786440 | tf_op jit(solution)/shard_map/ppermute | solution.py:197
  22.0 29.7 %collective-permute-start.16 = (bf16[128,1024]{1,0:T(8,128)(2,1)S(1)}, bf16[128,1024]{1,0:T(8,128)(2,1)S(1)}, u32[]{:S(2)}, u32[]{:S(2)}) collective-permute-start(bf16[128,1024]{1,0:T(8,128)(2,1)S(1)} %collective-permute-done.15.refs_16_), channel_id=1, source_target_pairs={{0,4},{4,0},{8,12},{12,8},{16,20},{20,16},{24,28},{28,24},{1,5},{5... | collective-permute-start | bytes 786440 | tf_op jit(solution)/shard_map/ppermute | solution.py:197
  24.9 26.9 %collective-permute-start.14 = (bf16[128,1024]{1,0:T(8,128)(2,1)S(1)}, bf16[128,1024]{1,0:T(8,128)(2,1)S(1)}, u32[]{:S(2)}, u32[]{:S(2)}) collective-permute-start(bf16[128,1024]{1,0:T(8,128)(2,1)S(1)} %collective-permute-done.13.refs_14_), channel_id=1, source_target_pairs={{0,4},{4,0},{8,12},{12,8},{16,20},{20,16},{24,28},{28,24},{1,5},{5... | collective-permute-start | bytes 786440 | tf_op jit(solution)/shard_map/ppermute | solution.py:197
  25.0 26.8 %collective-permute-start.12 = (bf16[128,1024]{1,0:T(8,128)(2,1)S(1)}, bf16[128,1024]{1,0:T(8,128)(2,1)S(1)}, u32[]{:S(2)}, u32[]{:S(2)}) collective-permute-start(bf16[128,1024]{1,0:T(8,128)(2,1)S(1)} %collective-permute-done.11.refs_12_), channel_id=1, source_target_pairs={{0,4},{4,0},{8,12},{12,8},{16,20},{20,16},{24,28},{28,24},{1,5},{5... | collective-permute-start | bytes 786440 | tf_op jit(solution)/shard_map/ppermute | solution.py:197
  25.4 4.8 %collective-permute-start.6 = (s32[4,128]{1,0:T(4,128)S(1)}, s32[4,128]{1,0:T(4,128)S(1)}, u32[]{:S(2)}, u32[]{:S(2)}) collective-permute-start(s32[4,128]{1,0:T(4,128)S(1)} %bitcast.5), channel_id=1, source_target_pairs={{0,28},{4,24},{8,20},{12,16},{16,12},{20,8},{24,4},{28,0},{1,29},{... | collective-permute-start | bytes 6152 | tf_op jit(solution)/shard_map/ppermute | solution.py:197
  30.2 5.4 %collective-permute-start.5 = (s32[4,128]{1,0:T(4,128)S(1)}, s32[4,128]{1,0:T(4,128)S(1)}, u32[]{:S(2)}, u32[]{:S(2)}) collective-permute-start(s32[4,128]{1,0:T(4,128)S(1)} %bitcast.6), channel_id=1, source_target_pairs={{0,24},{4,28},{8,16},{12,20},{16,8},{20,12},{24,0},{28,4},{1,25},{... | collective-permute-start | bytes 6152 | tf_op jit(solution)/shard_map/ppermute | solution.py:197
  35.6 3.9 %collective-permute-start.4 = (s32[4,128]{1,0:T(4,128)S(1)}, s32[4,128]{1,0:T(4,128)S(1)}, u32[]{:S(2)}, u32[]{:S(2)}) collective-permute-start(s32[4,128]{1,0:T(4,128)S(1)} %bitcast.7), channel_id=1, source_target_pairs={{0,20},{4,16},{8,28},{12,24},{16,4},{20,0},{24,12},{28,8},{1,21},{... | collective-permute-start | bytes 6152 | tf_op jit(solution)/shard_map/ppermute | solution.py:197
  39.5 4.5 %collective-permute-start.3 = (s32[4,128]{1,0:T(4,128)S(1)}, s32[4,128]{1,0:T(4,128)S(1)}, u32[]{:S(2)}, u32[]{:S(2)}) collective-permute-start(s32[4,128]{1,0:T(4,128)S(1)} %bitcast.8), channel_id=1, source_target_pairs={{0,16},{4,20},{8,24},{12,28},{16,0},{20,4},{24,8},{28,12},{1,17},{... | collective-permute-start | bytes 6152 | tf_op jit(solution)/shard_map/ppermute | solution.py:197
  44.0 3.0 %collective-permute-start.2 = (s32[4,128]{1,0:T(4,128)S(1)}, s32[4,128]{1,0:T(4,128)S(1)}, u32[]{:S(2)}, u32[]{:S(2)}) collective-permute-start(s32[4,128]{1,0:T(4,128)S(1)} %bitcast.9), channel_id=1, source_target_pairs={{0,12},{4,8},{8,4},{12,0},{16,28},{20,24},{24,20},{28,16},{1,13},{... | collective-permute-start | bytes 6152 | tf_op jit(solution)/shard_map/ppermute | solution.py:197
  47.0 3.6 %collective-permute-start.1 = (s32[4,128]{1,0:T(4,128)S(1)}, s32[4,128]{1,0:T(4,128)S(1)}, u32[]{:S(2)}, u32[]{:S(2)}) collective-permute-start(s32[4,128]{1,0:T(4,128)S(1)} %bitcast.10), channel_id=1, source_target_pairs={{0,8},{4,12},{8,0},{12,4},{16,24},{20,28},{24,16},{28,20},{1,9},{5... | collective-permute-start | bytes 6152 | tf_op jit(solution)/shard_map/ppermute | solution.py:197
  47.0 4.8 %copy-start = (s32[1024]{0:T(1024)S(1)}, s32[1024]{0:T(1024)}, u32[]{:S(2)}) copy-start(s32[1024]{0:T(1024)} %param.5) | copy-start | bytes 12292
  50.6 1.2 %collective-permute-start = (s32[4,128]{1,0:T(4,128)S(1)}, s32[4,128]{1,0:T(4,128)S(1)}, u32[]{:S(2)}, u32[]{:S(2)}) collective-permute-start(s32[4,128]{1,0:T(4,128)S(1)} %bitcast.11), channel_id=1, source_target_pairs={{0,4},{4,0},{8,12},{12,8},{16,20},{20,16},{24,28},{28,24},{1,5},{5... | collective-permute-start | bytes 6152 | tf_op jit(solution)/shard_map/ppermute | solution.py:197

commit v3 on v2

v3 whole, which is shorter than its diff:
```python
import functools

import jax
import jax.numpy as jnp
from jax import lax
from jax.experimental import pallas as pl
from jax.experimental.pallas import tpu as pltpu
from jax.sharding import PartitionSpec as P

logistic_sharpness = 0.02
half_scale = 0.5 / logistic_sharpness
masked = -1e30


def fold_rows(values):
    return jnp.sum(values.reshape(values.shape[0] // 8, 8, values.shape[1]), axis=0)


def lookup(table_ref, ids):
    low = ids % 128
    high = ids // 128
    found = jnp.zeros(ids.shape, jnp.int32)
    for line in range(table_ref.shape[0]):
        entries = jnp.broadcast_to(table_ref[line : line + 1, :], ids.shape)
        found = jnp.where(high == line, jnp.take_along_axis(entries, low, axis=1), found)
    return found


def kernel(cols, levels, shard, pos_count, lane_block, layout, *refs):
    place_ref, table_ref = refs[:2]
    ids_refs = refs[2:4]
    pieces = refs[4 : 4 + len(layout)]
    out_ref, embed_ref, score_ref, own_ref, target_ref, stat_ref = refs[4 + len(layout) :]
    total = embed_ref.shape[0]
    me = place_ref[0]
    my_col = place_ref[1]
    pair = lane_block // 128
    row_chunk = min(512, total)

    for piece, slots in zip(pieces, layout):
        for spot, slot in enumerate(slots):
            embed_ref[slot * shard : (slot + 1) * shard, :] = piece[spot * shard : (spot + 1) * shard, :]

    group = cols * shard
    for line in range(2 * levels):
        for begin in range(0, group, 128):
            level = line // 2 * pos_count
            ids = ids_refs[line % 2][level : level + pos_count, begin : begin + 128]
            ids = jnp.concatenate([ids, ids], axis=0)
            found = lookup(table_ref, ids) ^ me
            lane = lax.broadcasted_iota(jnp.int32, found.shape, 1)
            found = jnp.take_along_axis(found, lane ^ (my_col % 128), axis=1)
            start = line * group + (begin ^ (my_col - my_col % 128))
            target_ref[:, pl.ds(pl.multiple_of(start, 128), 128)] = found

    def score_chunk(anchors, start, buffer, chunk, picked):
        row = pl.multiple_of(chunk * row_chunk, row_chunk)
        scores = half_scale * lax.dot_general(
            embed_ref[pl.ds(row, row_chunk), :],
            anchors,
            (((1,), (1,)), ((), ())),
            preferred_element_type=jnp.float32,
        )
        score_ref[buffer, pl.ds(row, row_chunk), :] = scores
        picked = list(picked)
        for half in range(pair):
            targets = target_ref[:, pl.ds(pl.multiple_of(start + half * 128, 128), 128)]
            near = (targets - row) >> 3
            sub = targets & 7
            for step in range(row_chunk // 8):
                tile = scores[step * 8 : (step + 1) * 8, half * 128 : (half + 1) * 128]
                tile = jnp.take_along_axis(tile, sub, axis=0)
                picked[half] = jnp.where(near == step, tile, picked[half])
        return tuple(picked)

    def rank_chunk(pos, buffer, chunk, sums):
        row = pl.multiple_of(chunk * row_chunk, row_chunk)
        sums = list(sums)
        for half in range(pair):
            for part in range(row_chunk // 32):
                scores = score_ref[buffer, pl.ds(row + part * 32, 32), half * 128 : (half + 1) * 128]
                for m in range(pos_count):
                    at = (half * pos_count + m) * 2
                    bent = jnp.tanh(scores - pos[half][m])
                    sums[at] = sums[at] + fold_rows(bent)
                    sums[at + 1] = sums[at + 1] + fold_rows(bent * bent)
        return tuple(sums)

    chunks = total // row_chunk
    nothing = (jnp.zeros((8, 128), jnp.float32),) * pair
    zero = (jnp.zeros((8, 128), jnp.float32),) * (2 * pos_count * pair)

    def split(start, buffer, picked):
        inside = (buffer, pl.ds(start, lane_block), slice(None))
        index = lax.broadcasted_iota(jnp.int32, (lane_block, lane_block), 0)
        lane = lax.broadcasted_iota(jnp.int32, (lane_block, lane_block), 1)
        score_ref[inside] = jnp.where(index == lane, masked, score_ref[inside])
        return tuple(tuple(part[m : m + 1, :] for m in range(pos_count)) for part in picked)

    def finish(start, buffer, pos, sums):
        factor = 1.0 / (pos_count * total)
        for half in range(pair):
            lanes = pl.ds(pl.multiple_of(start + half * 128, 128), 128)
            spot = pos[half]
            ranks = []
            slopes = []
            for m in range(pos_count):
                at = (half * pos_count + m) * 2
                ranks.append(0.5 + 0.5 * (total + jnp.sum(sums[at], axis=0, keepdims=True)))
                slopes.append(0.25 * (total - jnp.sum(sums[at + 1], axis=0, keepdims=True)))
            own_ref[:, lanes] = score_ref[buffer, 0:shard, half * 128 : (half + 1) * 128]
            pulls = [-factor / ranks[m] for m in range(pos_count)]
            for m in range(pos_count):
                prank = 1.0
                pulled = 0.0
                for q in range(pos_count):
                    if q != m:
                        bent = jnp.tanh(spot[q] - spot[m])
                        prank = prank + 0.5 * (1.0 + bent)
                        pulled = pulled + (pulls[q] - pulls[m]) * (0.25 * (1.0 - bent * bent))
                weight = prank / (ranks[m] * ranks[m]) * (factor / logistic_sharpness)
                extra = pulled / logistic_sharpness - weight * slopes[m]
                stat_ref[m : m + 1, lanes] = spot[m]
                stat_ref[8 + m : 9 + m, lanes] = 0.25 * weight
                stat_ref[16 + m : 17 + m, lanes] = extra

    first = embed_ref[0:lane_block, :]
    picked = lax.fori_loop(
        0, chunks, lambda chunk, have: score_chunk(first, 0, 0, chunk, have), nothing
    )

    def block_step(block, pos):
        start = pl.multiple_of(block * lane_block, lane_block)
        buffer = lax.rem(block, 2)
        following = pl.multiple_of(start + lane_block, lane_block)
        anchors = embed_ref[pl.ds(following, lane_block), :]

        def both(chunk, carry):
            picked, sums = carry
            picked = score_chunk(anchors, following, 1 - buffer, chunk, picked)
            return picked, rank_chunk(pos, buffer, chunk, sums)

        picked, sums = lax.fori_loop(0, chunks, both, (nothing, zero))
        finish(start, buffer, pos, sums)
        return split(following, 1 - buffer, picked)

    last = total // lane_block - 1
    pos = lax.fori_loop(0, last, block_step, split(0, 0, picked))
    sums = lax.fori_loop(
        0, chunks, lambda chunk, have: rank_chunk(pos, last % 2, chunk, have), zero
    )
    finish(last * lane_block, last % 2, pos, sums)

    scores = own_ref[...]
    lane = lax.broadcasted_iota(jnp.int32, (shard, total), 1)
    line = lax.broadcasted_iota(jnp.int32, (shard, total), 0)
    columns = jnp.transpose(
        jnp.concatenate(
            [stat_ref[:, 0:128], target_ref[:, 0:128].astype(jnp.float32)], axis=0
        )
    )[0:shard, :]
    grads = [jnp.zeros((shard, total), jnp.float32) for _ in range(2)]
    for m in range(pos_count):
        bent = jnp.tanh(scores - stat_ref[m : m + 1, :])
        grads[0] = grads[0] + stat_ref[8 + m : 9 + m, :] * (1.0 - bent * bent)
        bent = jnp.tanh(scores - columns[:, m : m + 1])
        grads[1] = grads[1] + columns[:, 8 + m : 9 + m] * (1.0 - bent * bent)
    for m in range(pos_count):
        found = line == target_ref[m : m + 1, :]
        grads[0] = grads[0] + jnp.where(found, stat_ref[16 + m : 17 + m, :], 0.0)
        found = lane == columns[:, 24 + m : 25 + m].astype(jnp.int32)
        grads[1] = grads[1] + jnp.where(found, columns[:, 16 + m : 17 + m], 0.0)
    both = jnp.concatenate(grads, axis=0).astype(jnp.bfloat16)
    product = jnp.dot(both, embed_ref[...], preferred_element_type=jnp.float32)
    out_ref[...] = product[:shard, :] + product[shard:, :]


def body(embed, positives, placement):
    shard, width = embed.shape
    axes = ("row", "col")
    rows = lax.axis_size("row")
    cols = lax.axis_size("col")
    levels = rows // 2
    total = shard * rows * cols
    pos_count = positives.shape[1]
    lane_block = 256 if total <= 4096 else 128

    def swap(array, axis, mask):
        size = lax.axis_size(axis)
        return lax.ppermute(array, axis, [(i, i ^ mask) for i in range(size)])

    tall = jnp.concatenate(
        [embed] + [swap(embed, "row", 2 * d) for d in range(1, levels)], axis=0
    )
    ids = positives.T
    ids = jnp.concatenate([ids] + [swap(ids, "row", 2 * d) for d in range(1, levels)], axis=0)
    tall, ids = lax.optimization_barrier((tall, ids))

    half = levels // 2 * shard
    plane = {0: [tall]}
    for p in range(1, cols):
        low, high = p & -p, 1 << (p.bit_length() - 1)
        if low == high:
            plane[p] = [swap(tall, "col", p)]
        else:
            first, second = plane[p ^ low], plane[p ^ high]
            first = first[0][:half] if len(first) == 1 else first[0]
            second = second[0][half:] if len(second) == 1 else second[1]
            plane[p] = [swap(first, "col", low), swap(second, "col", high)]

    pieces = []
    layout = []
    for p in range(cols):
        level = 0
        for part in plane[p]:
            count = part.shape[0] // shard
            for c in range(2):
                pieces.append(part if c == 0 else swap(part, "row", 1))
                layout.append([((level + d) * 2 + c) * cols + p for d in range(count)])
            level += count

    place = jnp.stack([lax.axis_index(axes) * shard, lax.axis_index("col") * shard])
    vmem = pl.BlockSpec(memory_space=pltpu.VMEM)
    return pl.pallas_call(
        functools.partial(kernel, cols, levels, shard, pos_count, lane_block, layout),
        out_shape=jax.ShapeDtypeStruct((shard, width), jnp.float32),
        in_specs=[pl.BlockSpec(memory_space=pltpu.SMEM)] + [vmem] * (3 + len(pieces)),
        out_specs=vmem,
        scratch_shapes=[
            pltpu.VMEM((total, width), jnp.bfloat16),
            pltpu.VMEM((2, total, lane_block), jnp.float32),
            pltpu.VMEM((shard, total), jnp.float32),
            pltpu.VMEM((8, total), jnp.int32),
            pltpu.VMEM((24, total), jnp.float32),
        ],
        compiler_params=pltpu.CompilerParams(vmem_limit_bytes=4 * total * width + 8 * total * lane_block + (8 << 20)),
        cost_estimate=pl.CostEstimate(
            flops=2 * total * total * width,
            bytes_accessed=2 * total * width,
            transcendentals=4 * total * total,
        ),
    )(
        place.astype(jnp.int32),
        placement.reshape(-1, 128),
        ids,
        swap(ids, "row", 1),
        *pieces,
    )


def solution(mesh):
    return jax.shard_map(
        body,
        mesh=mesh,
        in_specs=(P(("row", "col"), None), P("row", None), P()),
        out_specs=P(("row", "col"), None),
        check_vma=False,
    )
```

time: 66 us -> 43.3 us (0.66)
  waiting for transfers between devices: 37.7 us -> 15.6 us
  Pallas kernels: 14.1 us -> 9.26 us
  starting transfers between devices: 13 us -> 16.5 us
  other arithmetic: 0.07 us -> 1.62 us
  local copies, waits for them, and re-layouts: 0.94 us -> 0.02 us
    ppermute x17 -> x16, waiting for transfers between devices: 37.7 us -> 15.6 us  [swap(): return lax.ppermute(array, axis, [(i, i ^ mask) for i in range(size)])]
    pallas_call x1, Pallas kernels: 14.1 us -> 9.26 us  [body(): pl.pallas_call(functools.partial(kernel, cols, levels, shard, pos_count,...]
    ppermute x17 -> x16, starting transfers between devices: 13 us -> 16.5 us  [swap(): return lax.ppermute(array, axis, [(i, i ^ mask) for i in range(size)])]
    concatenate x0 -> x2, other arithmetic: none -> 1.55 us  [the longest x1 0.86 us: body(): jnp.concatenate([embed] + [swap(embed, 'row', 2 * d) for d in range(1, le...]
    unnamed x7 -> x2, local copies, waits for them, and re-layouts: 0.93 us -> 0.01 us
  transfers between devices with their start and end apart: 17 -> 16, of which waited for: 12 -> 7; matrix products, arithmetic and copies ran while one was open for 2% -> 2% of each run, Pallas kernels for 0% -> 0%
where the time goes in v3:
time: 43.3 us; the launch traced here: 43.1 us
  starting transfers between devices  16.5 us (38%)
  waiting for transfers between devices  15.6 us (36%)
  Pallas kernels  9.26 us (21%)
  other arithmetic  1.62 us (4%)
    ppermute x16, starting transfers between devices, swap(): return lax.ppermute(array, axis, [(i, i ^ mask) for i in range(size)])  16.5 us
    ppermute x16, waiting for transfers between devices, swap(): return lax.ppermute(array, axis, [(i, i ^ mask) for i in range(size)])  15.6 us
    pallas_call x1, Pallas kernels, body(): pl.pallas_call(functools.partial(kernel, cols, levels, shard, pos_count,...  9.26 us
  transfers between devices with their start and end apart: 16, of which 7 were waited for; matrix products, arithmetic and copies ran while one was open for 2% of the time, Pallas kernels for 0%

profile of v3, /device:TPU:0, one launch (start us, length us, event | category | flops | bytes accessed | tf_op | source)
XLA Modules:
  0.0 43.1 jit_solution(362057563482907381)
XLA Ops:
  0.0 5.0 %collective-permute-start.5 = (s32[4,128]{1,0:T(4,128)}, s32[4,128]{1,0:T(4,128)S(1)}, u32[]{:S(2)}, u32[]{:S(2)}) collective-permute-start(s32[4,128]{1,0:T(4,128)} %bitcast.5), channel_id=1, source_target_pairs={{0,24},{4,28},{8,16},{12,20},{16,8},{20,12},{24,0},{28,4},{1,25},{... | collective-permute-start | bytes 6152 | tf_op jit(solution)/shard_map/ppermute | solution.py:190
  5.0 0.0 collective-permute-start.4
  5.1 0.6 %collective-permute-start.3 = (s32[4,128]{1,0:T(4,128)}, s32[4,128]{1,0:T(4,128)S(1)}, u32[]{:S(2)}, u32[]{:S(2)}) collective-permute-start(s32[4,128]{1,0:T(4,128)} %bitcast.7), channel_id=1, source_target_pairs={{0,8},{4,12},{8,0},{12,4},{16,24},{20,28},{24,16},{28,20},{1,9},{5... | collective-permute-start | bytes 6152 | tf_op jit(solution)/shard_map/ppermute | solution.py:190
  5.6 2.4 %collective-permute-start.1 = (bf16[32,1024]{1,0:T(8,128)(2,1)}, bf16[32,1024]{1,0:T(8,128)(2,1)S(1)}, u32[]{:S(2)}, u32[]{:S(2)}) collective-permute-start(bf16[32,1024]{1,0:T(8,128)(2,1)} %param.3), channel_id=1, source_target_pairs={{0,16},{4,20},{8,24},{12,28},{16,0},{20,4},{24,8},{28,12},{1,17},{... | collective-permute-start | bytes 196616 | tf_op jit(solution)/shard_map/ppermute | solution.py:190
  8.0 2.0 %collective-permute-start = (bf16[32,1024]{1,0:T(8,128)(2,1)}, bf16[32,1024]{1,0:T(8,128)(2,1)S(1)}, u32[]{:S(2)}, u32[]{:S(2)}) collective-permute-start(bf16[32,1024]{1,0:T(8,128)(2,1)} %param.3), channel_id=1, source_target_pairs={{0,8},{4,12},{8,0},{12,4},{16,24},{20,28},{24,16},{28,20},{1,9},{5... | collective-permute-start | bytes 196616 | tf_op jit(solution)/shard_map/ppermute | solution.py:190
  10.0 0.0 collective-permute-done.5
  10.0 0.6 %collective-permute-start.2 = (bf16[32,1024]{1,0:T(8,128)(2,1)}, bf16[32,1024]{1,0:T(8,128)(2,1)S(1)}, u32[]{:S(2)}, u32[]{:S(2)}) collective-permute-start(bf16[32,1024]{1,0:T(8,128)(2,1)} %param.3), channel_id=1, source_target_pairs={{0,24},{4,28},{8,16},{12,20},{16,8},{20,12},{24,0},{28,4},{1,25},{... | collective-permute-start | bytes 196616 | tf_op jit(solution)/shard_map/ppermute | solution.py:190
  10.6 0.0 collective-permute-done.4
  10.6 0.0 collective-permute-done.3
  10.7 0.7 %pad_add_fusion.refs_2_ = s32[16,128]{1,0:T(8,128)S(1)} fusion(s32[4,128]{1,0:T(4,128)S(1)} %collective-permute-done.5, s32[4,128]{1,0:T(4,128)S(1)} %collective-permute-done.4, s32[4,128]{1,0:T(4,128)S(1)} %collective-permute-done.3, s32[4,128]{1,0:T(4,128)} %bitcast.8), kind=kLoop, calls=%fused_computation.1 | loop fusion | flops 6144 | bytes 16384 | tf_op jit(solution)/shard_map/concatenate | solution.py:196
  11.3 0.0 collective-permute-done.1
  11.3 1.1 %collective-permute-done = bf16[32,1024]{1,0:T(8,128)(2,1)S(1)} collective-permute-done((bf16[32,1024]{1,0:T(8,128)(2,1)}, bf16[32,1024]{1,0:T(8,128)(2,1)S(1)}, u32[]{:S(2)}, u32[]{:S(2)}) %collective-permute-start) | collective-permute-done | bytes 65568 | tf_op jit(solution)/shard_map/ppermute | solution.py:190
  12.5 3.8 %collective-permute-done.2 = bf16[32,1024]{1,0:T(8,128)(2,1)S(1)} collective-permute-done((bf16[32,1024]{1,0:T(8,128)(2,1)}, bf16[32,1024]{1,0:T(8,128)(2,1)S(1)}, u32[]{:S(2)}, u32[]{:S(2)}) %collective-permute-start.2) | collective-permute-done | bytes 65568 | tf_op jit(solution)/shard_map/ppermute | solution.py:190
  16.3 0.9 %pad_maximum_fusion.refs_4_ = bf16[128,1024]{1,0:T(8,128)(2,1)S(1)} fusion(bf16[32,1024]{1,0:T(8,128)(2,1)S(1)} %collective-permute-done.2, bf16[32,1024]{1,0:T(8,128)(2,1)S(1)} %collective-permute-done.1, bf16[32,1024]{1,0:T(8,128)(2,1)S(1)} %collective-permute-done, bf16[32,1024]{1,0:T(8,128)(2,1)} %param.3), kind=kLoop, calls=%fused_computation | loop fusion | flops 1048576 | bytes 524288 | tf_op jit(solution)/shard_map/concatenate | solution.py:192
  17.1 1.6 %collective-permute-start.10 = (bf16[128,1024]{1,0:T(8,128)(2,1)S(1)}, bf16[128,1024]{1,0:T(8,128)(2,1)S(1)}, u32[]{:S(2)}, u32[]{:S(2)}) collective-permute-start(bf16[128,1024]{1,0:T(8,128)(2,1)S(1)} %pad_maximum_fusion.refs_4_), channel_id=1, source_target_pairs={{0,2},{1,3},{2,0},{3,1},{4,6},{5,7},{6,4},{7,5},{8,10},{9,11},{10,... | collective-permute-start | bytes 786440 | tf_op jit(solution)/shard_map/ppermute | solution.py:190
  18.7 1.5 %collective-permute-start.8 = (bf16[128,1024]{1,0:T(8,128)(2,1)S(1)}, bf16[128,1024]{1,0:T(8,128)(2,1)S(1)}, u32[]{:S(2)}, u32[]{:S(2)}) collective-permute-start(bf16[128,1024]{1,0:T(8,128)(2,1)S(1)} %pad_maximum_fusion.refs_4_), channel_id=1, source_target_pairs={{0,1},{1,0},{2,3},{3,2},{4,5},{5,4},{6,7},{7,6},{8,9},{9,8},{10,11... | collective-permute-start | bytes 786440 | tf_op jit(solution)/shard_map/ppermute | solution.py:190
  20.2 0.0 collective-permute-start.6
  20.2 0.5 %collective-permute-start.7 = (bf16[128,1024]{1,0:T(8,128)(2,1)S(1)}, bf16[128,1024]{1,0:T(8,128)(2,1)S(1)}, u32[]{:S(2)}, u32[]{:S(2)}) collective-permute-start(bf16[128,1024]{1,0:T(8,128)(2,1)S(1)} %pad_maximum_fusion.refs_4_), channel_id=1, source_target_pairs={{0,4},{4,0},{8,12},{12,8},{16,20},{20,16},{24,28},{28,24},{1,5},{5... | collective-permute-start | bytes 786440 | tf_op jit(solution)/shard_map/ppermute | solution.py:190
  20.7 2.8 %collective-permute-done.10.refs_8_ = bf16[128,1024]{1,0:T(8,128)(2,1)S(1)} collective-permute-done((bf16[128,1024]{1,0:T(8,128)(2,1)S(1)}, bf16[128,1024]{1,0:T(8,128)(2,1)S(1)}, u32[]{:S(2)}, u32[]{:S(2)}) %collective-permute-start.10) | collective-permute-done | bytes 262176 | tf_op jit(solution)/shard_map/ppermute | solution.py:190
  23.6 1.6 %collective-permute-start.12 = (bf16[64,1024]{1,0:T(8,128)(2,1)S(1)}, bf16[64,1024]{1,0:T(8,128)(2,1)S(1)}, u32[]{:S(2)}, u32[]{:S(2)}) collective-permute-start(bf16[64,1024]{1,0:T(8,128)(2,1)S(1)} %slice.8), channel_id=1, source_target_pairs={{0,1},{1,0},{2,3},{3,2},{4,5},{5,4},{6,7},{7,6},{8,9},{9,8},{10,11... | collective-permute-start | bytes 393224 | tf_op jit(solution)/shard_map/ppermute | solution.py:190
  25.1 0.0 collective-permute-start.11
  25.2 1.4 %collective-permute-done.8.refs_6_ = bf16[128,1024]{1,0:T(8,128)(2,1)S(1)} collective-permute-done((bf16[128,1024]{1,0:T(8,128)(2,1)S(1)}, bf16[128,1024]{1,0:T(8,128)(2,1)S(1)}, u32[]{:S(2)}, u32[]{:S(2)}) %collective-permute-start.8) | collective-permute-done | bytes 262176 | tf_op jit(solution)/shard_map/ppermute | solution.py:190
  26.5 0.1 collective-permute-start.9
  26.6 0.0 collective-permute-done.6.refs_3_
  26.6 0.7 %collective-permute-start.14 = (bf16[64,1024]{1,0:T(8,128)(2,1)S(1)}, bf16[64,1024]{1,0:T(8,128)(2,1)S(1)}, u32[]{:S(2)}, u32[]{:S(2)}) collective-permute-start(bf16[64,1024]{1,0:T(8,128)(2,1)S(1)} %slice.9), channel_id=1, source_target_pairs={{0,2},{1,3},{2,0},{3,1},{4,6},{5,7},{6,4},{7,5},{8,10},{9,11},{10,... | collective-permute-start | bytes 393224 | tf_op jit(solution)/shard_map/ppermute | solution.py:190
  27.3 1.4 %collective-permute-done.12.refs_10_ = bf16[64,1024]{1,0:T(8,128)(2,1)S(1)} collective-permute-done((bf16[64,1024]{1,0:T(8,128)(2,1)S(1)}, bf16[64,1024]{1,0:T(8,128)(2,1)S(1)}, u32[]{:S(2)}, u32[]{:S(2)}) %collective-permute-start.12) | collective-permute-done | bytes 131104 | tf_op jit(solution)/shard_map/ppermute | solution.py:190
  28.6 0.0 collective-permute-start.13
  28.6 3.9 %collective-permute-done.14.refs_12_ = bf16[64,1024]{1,0:T(8,128)(2,1)S(1)} collective-permute-done((bf16[64,1024]{1,0:T(8,128)(2,1)S(1)}, bf16[64,1024]{1,0:T(8,128)(2,1)S(1)}, u32[]{:S(2)}, u32[]{:S(2)}) %collective-permute-start.14) | collective-permute-done | bytes 131104 | tf_op jit(solution)/shard_map/ppermute | solution.py:190
  32.5 0.0 collective-permute-start.15
  32.5 0.0 copy-start
  32.5 0.1 pad_add_fusion.1.refs_0_
  32.6 0.0 collective-permute-done.7.refs_5_
  32.6 0.0 collective-permute-done.11.refs_9_
  32.6 0.0 collective-permute-done.9.refs_7_
  32.6 0.0 collective-permute-done.13.refs_11_
  32.6 1.2 %collective-permute-done.15.refs_13_ = bf16[64,1024]{1,0:T(8,128)(2,1)S(1)} collective-permute-done((bf16[64,1024]{1,0:T(8,128)(2,1)S(1)}, bf16[64,1024]{1,0:T(8,128)(2,1)S(1)}, u32[]{:S(2)}, u32[]{:S(2)}) %collective-permute-start.15) | collective-permute-done | bytes 131104 | tf_op jit(solution)/shard_map/ppermute | solution.py:190
  33.9 0.0 copy-done
  33.9 9.3 %shard_map.37 = f32[32,1024]{1,0:T(8,128)} custom-call(s32[2]{0:T(128)S(1)} %pad_add_fusion.1.refs_0_, s32[8,128]{1,0:T(8,128)S(1)} %bitcast.4, s32[16,128]{1,0:T(8,128)S(1)} %pad_add_fusion.refs_2_, s32[16,128]{1,0:T(8,128)S(1)} %collective-permute-done.6.refs_3_, bf16[128,1024]{1,0:T(8,128)(2,1)S(1)} %pad_maximum_fusion.refs_4_, ...), custom_call_target="tpu_custom_call" | custom-call | flops 2147483648 | bytes 2097152 | tf_op jit(solution)/shard_map/pallas_call | solution.py:224
  (2 shorter events, 0.0 us)
Async XLA Ops:
  0.0 10.0 %collective-permute-start.5 = (s32[4,128]{1,0:T(4,128)}, s32[4,128]{1,0:T(4,128)S(1)}, u32[]{:S(2)}, u32[]{:S(2)}) collective-permute-start(s32[4,128]{1,0:T(4,128)} %bitcast.5), channel_id=1, source_target_pairs={{0,24},{4,28},{8,16},{12,20},{16,8},{20,12},{24,0},{28,4},{1,25},{... | collective-permute-start | bytes 6152 | tf_op jit(solution)/shard_map/ppermute | solution.py:190
  5.0 5.6 %collective-permute-start.4 = (s32[4,128]{1,0:T(4,128)}, s32[4,128]{1,0:T(4,128)S(1)}, u32[]{:S(2)}, u32[]{:S(2)}) collective-permute-start(s32[4,128]{1,0:T(4,128)} %bitcast.6), channel_id=1, source_target_pairs={{0,16},{4,20},{8,24},{12,28},{16,0},{20,4},{24,8},{28,12},{1,17},{... | collective-permute-start | bytes 6152 | tf_op jit(solution)/shard_map/ppermute | solution.py:190
  5.1 5.6 %collective-permute-start.3 = (s32[4,128]{1,0:T(4,128)}, s32[4,128]{1,0:T(4,128)S(1)}, u32[]{:S(2)}, u32[]{:S(2)}) collective-permute-start(s32[4,128]{1,0:T(4,128)} %bitcast.7), channel_id=1, source_target_pairs={{0,8},{4,12},{8,0},{12,4},{16,24},{20,28},{24,16},{28,20},{1,9},{5... | collective-permute-start | bytes 6152 | tf_op jit(solution)/shard_map/ppermute | solution.py:190
  5.6 5.7 %collective-permute-start.1 = (bf16[32,1024]{1,0:T(8,128)(2,1)}, bf16[32,1024]{1,0:T(8,128)(2,1)S(1)}, u32[]{:S(2)}, u32[]{:S(2)}) collective-permute-start(bf16[32,1024]{1,0:T(8,128)(2,1)} %param.3), channel_id=1, source_target_pairs={{0,16},{4,20},{8,24},{12,28},{16,0},{20,4},{24,8},{28,12},{1,17},{... | collective-permute-start | bytes 196616 | tf_op jit(solution)/shard_map/ppermute | solution.py:190
  8.0 4.5 %collective-permute-start = (bf16[32,1024]{1,0:T(8,128)(2,1)}, bf16[32,1024]{1,0:T(8,128)(2,1)S(1)}, u32[]{:S(2)}, u32[]{:S(2)}) collective-permute-start(bf16[32,1024]{1,0:T(8,128)(2,1)} %param.3), channel_id=1, source_target_pairs={{0,8},{4,12},{8,0},{12,4},{16,24},{20,28},{24,16},{28,20},{1,9},{5... | collective-permute-start | bytes 196616 | tf_op jit(solution)/shard_map/ppermute | solution.py:190
  10.0 6.3 %collective-permute-start.2 = (bf16[32,1024]{1,0:T(8,128)(2,1)}, bf16[32,1024]{1,0:T(8,128)(2,1)S(1)}, u32[]{:S(2)}, u32[]{:S(2)}) collective-permute-start(bf16[32,1024]{1,0:T(8,128)(2,1)} %param.3), channel_id=1, source_target_pairs={{0,24},{4,28},{8,16},{12,20},{16,8},{20,12},{24,0},{28,4},{1,25},{... | collective-permute-start | bytes 196616 | tf_op jit(solution)/shard_map/ppermute | solution.py:190
  17.1 6.4 %collective-permute-start.10 = (bf16[128,1024]{1,0:T(8,128)(2,1)S(1)}, bf16[128,1024]{1,0:T(8,128)(2,1)S(1)}, u32[]{:S(2)}, u32[]{:S(2)}) collective-permute-start(bf16[128,1024]{1,0:T(8,128)(2,1)S(1)} %pad_maximum_fusion.refs_4_), channel_id=1, source_target_pairs={{0,2},{1,3},{2,0},{3,1},{4,6},{5,7},{6,4},{7,5},{8,10},{9,11},{10,... | collective-permute-start | bytes 786440 | tf_op jit(solution)/shard_map/ppermute | solution.py:190
  18.7 7.8 %collective-permute-start.8 = (bf16[128,1024]{1,0:T(8,128)(2,1)S(1)}, bf16[128,1024]{1,0:T(8,128)(2,1)S(1)}, u32[]{:S(2)}, u32[]{:S(2)}) collective-permute-start(bf16[128,1024]{1,0:T(8,128)(2,1)S(1)} %pad_maximum_fusion.refs_4_), channel_id=1, source_target_pairs={{0,1},{1,0},{2,3},{3,2},{4,5},{5,4},{6,7},{7,6},{8,9},{9,8},{10,11... | collective-permute-start | bytes 786440 | tf_op jit(solution)/shard_map/ppermute | solution.py:190
  20.2 6.4 %collective-permute-start.6 = (s32[16,128]{1,0:T(8,128)S(1)}, s32[16,128]{1,0:T(8,128)S(1)}, u32[]{:S(2)}, u32[]{:S(2)}) collective-permute-start(s32[16,128]{1,0:T(8,128)S(1)} %pad_add_fusion.refs_2_), channel_id=1, source_target_pairs={{0,4},{4,0},{8,12},{12,8},{16,20},{20,16},{24,28},{28,24},{1,5},{5... | collective-permute-start | bytes 24584 | tf_op jit(solution)/shard_map/ppermute | solution.py:190
  20.2 12.4 %collective-permute-start.7 = (bf16[128,1024]{1,0:T(8,128)(2,1)S(1)}, bf16[128,1024]{1,0:T(8,128)(2,1)S(1)}, u32[]{:S(2)}, u32[]{:S(2)}) collective-permute-start(bf16[128,1024]{1,0:T(8,128)(2,1)S(1)} %pad_maximum_fusion.refs_4_), channel_id=1, source_target_pairs={{0,4},{4,0},{8,12},{12,8},{16,20},{20,16},{24,28},{28,24},{1,5},{5... | collective-permute-start | bytes 786440 | tf_op jit(solution)/shard_map/ppermute | solution.py:190
  23.6 5.0 %collective-permute-start.12 = (bf16[64,1024]{1,0:T(8,128)(2,1)S(1)}, bf16[64,1024]{1,0:T(8,128)(2,1)S(1)}, u32[]{:S(2)}, u32[]{:S(2)}) collective-permute-start(bf16[64,1024]{1,0:T(8,128)(2,1)S(1)} %slice.8), channel_id=1, source_target_pairs={{0,1},{1,0},{2,3},{3,2},{4,5},{5,4},{6,7},{7,6},{8,9},{9,8},{10,11... | collective-permute-start | bytes 393224 | tf_op jit(solution)/shard_map/ppermute | solution.py:190
  25.1 7.5 %collective-permute-start.11 = (bf16[128,1024]{1,0:T(8,128)(2,1)S(1)}, bf16[128,1024]{1,0:T(8,128)(2,1)S(1)}, u32[]{:S(2)}, u32[]{:S(2)}) collective-permute-start(bf16[128,1024]{1,0:T(8,128)(2,1)S(1)} %collective-permute-done.10.refs_8_), channel_id=1, source_target_pairs={{0,4},{4,0},{8,12},{12,8},{16,20},{20,16},{24,28},{28,24},{1,5},{5... | collective-permute-start | bytes 786440 | tf_op jit(solution)/shard_map/ppermute | solution.py:190
  26.5 6.1 %collective-permute-start.9 = (bf16[128,1024]{1,0:T(8,128)(2,1)S(1)}, bf16[128,1024]{1,0:T(8,128)(2,1)S(1)}, u32[]{:S(2)}, u32[]{:S(2)}) collective-permute-start(bf16[128,1024]{1,0:T(8,128)(2,1)S(1)} %collective-permute-done.8.refs_6_), channel_id=1, source_target_pairs={{0,4},{4,0},{8,12},{12,8},{16,20},{20,16},{24,28},{28,24},{1,5},{5... | collective-permute-start | bytes 786440 | tf_op jit(solution)/shard_map/ppermute | solution.py:190
  26.6 5.9 %collective-permute-start.14 = (bf16[64,1024]{1,0:T(8,128)(2,1)S(1)}, bf16[64,1024]{1,0:T(8,128)(2,1)S(1)}, u32[]{:S(2)}, u32[]{:S(2)}) collective-permute-start(bf16[64,1024]{1,0:T(8,128)(2,1)S(1)} %slice.9), channel_id=1, source_target_pairs={{0,2},{1,3},{2,0},{3,1},{4,6},{5,7},{6,4},{7,5},{8,10},{9,11},{10,... | collective-permute-start | bytes 393224 | tf_op jit(solution)/shard_map/ppermute | solution.py:190
  28.6 4.0 %collective-permute-start.13 = (bf16[64,1024]{1,0:T(8,128)(2,1)S(1)}, bf16[64,1024]{1,0:T(8,128)(2,1)S(1)}, u32[]{:S(2)}, u32[]{:S(2)}) collective-permute-start(bf16[64,1024]{1,0:T(8,128)(2,1)S(1)} %collective-permute-done.12.refs_10_), channel_id=1, source_target_pairs={{0,4},{4,0},{8,12},{12,8},{16,20},{20,16},{24,28},{28,24},{1,5},{5... | collective-permute-start | bytes 393224 | tf_op jit(solution)/shard_map/ppermute | solution.py:190
  32.5 1.3 %collective-permute-start.15 = (bf16[64,1024]{1,0:T(8,128)(2,1)S(1)}, bf16[64,1024]{1,0:T(8,128)(2,1)S(1)}, u32[]{:S(2)}, u32[]{:S(2)}) collective-permute-start(bf16[64,1024]{1,0:T(8,128)(2,1)S(1)} %collective-permute-done.14.refs_12_), channel_id=1, source_target_pairs={{0,4},{4,0},{8,12},{12,8},{16,20},{20,16},{24,28},{28,24},{1,5},{5... | collective-permute-start | bytes 393224 | tf_op jit(solution)/shard_map/ppermute | solution.py:190
  32.5 1.3 %copy-start = (s32[1024]{0:T(1024)S(1)}, s32[1024]{0:T(1024)}, u32[]{:S(2)}) copy-start(s32[1024]{0:T(1024)} %param.5) | copy-start | bytes 12292

commit v4 on v3

--- a/solution.py
+++ b/solution.py
@@ -26,7 +26,7 @@
     return found
 
 
-def kernel(cols, levels, shard, pos_count, lane_block, layout, *refs):
+def kernel(cols, order, shard, pos_count, lane_block, layout, *refs):
     place_ref, table_ref = refs[:2]
     ids_refs = refs[2:4]
     pieces = refs[4 : 4 + len(layout)]
@@ -42,9 +42,9 @@
             embed_ref[slot * shard : (slot + 1) * shard, :] = piece[spot * shard : (spot + 1) * shard, :]
 
     group = cols * shard
-    for line in range(2 * levels):
+    for line in range(2 * len(order)):
         for begin in range(0, group, 128):
-            level = line // 2 * pos_count
+            level = order.index(line // 2) * pos_count
             ids = ids_refs[line % 2][level : level + pos_count, begin : begin + 128]
             ids = jnp.concatenate([ids, ids], axis=0)
             found = lookup(table_ref, ids) ^ me
@@ -189,40 +189,65 @@
         size = lax.axis_size(axis)
         return lax.ppermute(array, axis, [(i, i ^ mask) for i in range(size)])
 
-    tall = jnp.concatenate(
-        [embed] + [swap(embed, "row", 2 * d) for d in range(1, levels)], axis=0
-    )
-    ids = positives.T
-    ids = jnp.concatenate([ids] + [swap(ids, "row", 2 * d) for d in range(1, levels)], axis=0)
-    tall, ids = lax.optimization_barrier((tall, ids))
+    order = [0]
+    bits = [1 << b for b in reversed(range(levels.bit_length() - 1))]
+    line = [swap(embed, "row", 2 * d) for d in range(1, levels)]
+
+    def spread(ids):
+        if bits:
+            bit = bits.pop(0)
+            order.extend([d ^ bit for d in order])
+            return (jnp.concatenate([ids[0], swap(ids[0], "row", 2 * bit)], axis=0),)
+        if len(ids) == 1:
+            return (ids[0], swap(ids[0], "row", 1))
+        return ids
+
+    ids = spread((positives.T,))
+    line, ids = lax.optimization_barrier((line, ids))
+    tall = jnp.concatenate([embed] + line, axis=0)
 
     half = levels // 2 * shard
     plane = {0: [tall]}
-    for p in range(1, cols):
-        low, high = p & -p, 1 << (p.bit_length() - 1)
-        if low == high:
-            plane[p] = [swap(tall, "col", p)]
-        else:
-            first, second = plane[p ^ low], plane[p ^ high]
-            first = first[0][:half] if len(first) == 1 else first[0]
-            second = second[0][half:] if len(second) == 1 else second[1]
-            plane[p] = [swap(first, "col", low), swap(second, "col", high)]
+    other = {}
+    fresh = [0]
+    for weight in range(1, (cols - 1).bit_count() + 1):
+        coming = [p for p in range(1, cols) if p.bit_count() == weight]
+        for p in coming:
+            low, high = p & -p, 1 << (p.bit_length() - 1)
+            if low == high:
+                plane[p] = [swap(tall, "col", p)]
+            else:
+                first, second = plane[p ^ low], plane[p ^ high]
+                first = first[0][:half] if len(first) == 1 else first[0]
+                second = second[0][half:] if len(second) == 1 else second[1]
+                plane[p] = [swap(first, "col", low), swap(second, "col", high)]
+        ids = spread(ids)
+        ready, ids = lax.optimization_barrier(([plane[p] for p in fresh], ids))
+        for p, parts in zip(fresh, ready):
+            other[p] = [swap(part, "row", 1) for part in parts]
+        fresh = coming
+        if weight < (cols - 1).bit_count():
+            plane, other, ids = lax.optimization_barrier((plane, other, ids))
+    while bits or len(ids) == 1:
+        ids = spread(ids)
+    for p in fresh:
+        other[p] = [swap(part, "row", 1) for part in plane[p]]
 
     pieces = []
     layout = []
     for p in range(cols):
-        level = 0
-        for part in plane[p]:
-            count = part.shape[0] // shard
-            for c in range(2):
-                pieces.append(part if c == 0 else swap(part, "row", 1))
+        for c, parts in enumerate((plane[p], other[p])):
+            level = 0
+            for part in parts:
+                count = part.shape[0] // shard
+                pieces.append(part)
                 layout.append([((level + d) * 2 + c) * cols + p for d in range(count)])
-            level += count
+                level += count
 
     place = jnp.stack([lax.axis_index(axes) * shard, lax.axis_index("col") * shard])
     vmem = pl.BlockSpec(memory_space=pltpu.VMEM)
     return pl.pallas_call(
-        functools.partial(kernel, cols, levels, shard, pos_count, lane_block, layout),
+        functools.partial(kernel, cols, order, shard, pos_count, lane_block, layout),
         out_shape=jax.ShapeDtypeStruct((shard, width), jnp.float32),
         in_specs=[pl.BlockSpec(memory_space=pltpu.SMEM)] + [vmem] * (3 + len(pieces)),
         out_specs=vmem,
@@ -242,8 +267,7 @@
     )(
         place.astype(jnp.int32),
         placement.reshape(-1, 128),
-        ids,
-        swap(ids, "row", 1),
+        *ids,
         *pieces,
     )
 

time: 43.3 us -> 38.6 us (0.89)
  starting transfers between devices: 16.5 us -> 13.9 us
  other arithmetic: 1.62 us -> 0.08 us
  waiting for transfers between devices: 15.6 us -> 14.2 us
  local copies, waits for them, and re-layouts: 0.02 us -> 0.89 us
    ppermute x16 -> x15, starting transfers between devices: 16.5 us -> 13.9 us  [swap(): return lax.ppermute(array, axis, [(i, i ^ mask) for i in range(size)])]
    concatenate x2, other arithmetic: 1.55 us -> 0.01 us  [spread(): return (jnp.concatenate([ids[0], swap(ids[0], 'row', 2 * bit)], axis=0),)]
    ppermute x16 -> x15, waiting for transfers between devices: 15.6 us -> 14.2 us  [swap(): return lax.ppermute(array, axis, [(i, i ^ mask) for i in range(size)])]
    unnamed x2 -> x7, local copies, waits for them, and re-layouts: 0.01 us -> 0.86 us
  transfers between devices with their start and end apart: 16 -> 15, of which waited for: 7 -> 8; matrix products, arithmetic and copies ran while one was open for 2% -> 3% of each run, Pallas kernels for 0% -> 0%
where the time goes in v4:
time: 38.6 us; the launch traced here: 38.4 us
  waiting for transfers between devices  14.2 us (37%)
  starting transfers between devices  13.9 us (36%)
  Pallas kernels  9.28 us (24%)
  local copies, waits for them, and re-layouts  0.89 us (2%)
    ppermute x15, waiting for transfers between devices, swap(): return lax.ppermute(array, axis, [(i, i ^ mask) for i in range(size)])  14.2 us
    ppermute x15, starting transfers between devices, swap(): return lax.ppermute(array, axis, [(i, i ^ mask) for i in range(size)])  13.9 us
    pallas_call x1, Pallas kernels, body(): pl.pallas_call(functools.partial(kernel, cols, order, shard, pos_count, l...  9.28 us
    unnamed x7, local copies, waits for them, and re-layouts  0.86 us
  transfers between devices with their start and end apart: 15, of which 8 were waited for; matrix products, arithmetic and copies ran while one was open for 3% of the time, Pallas kernels for 0%

profile of v4, /device:TPU:0, one launch (start us, length us, event | category | flops | bytes accessed | tf_op | source)
XLA Modules:
  0.0 38.4 jit_solution(13613432891504418836)
XLA Ops:
  0.0 4.0 %collective-permute-start.1 = (bf16[32,1024]{1,0:T(8,128)(2,1)}, bf16[32,1024]{1,0:T(8,128)(2,1)S(1)}, u32[]{:S(2)}, u32[]{:S(2)}) collective-permute-start(bf16[32,1024]{1,0:T(8,128)(2,1)} %param.3), channel_id=1, source_target_pairs={{0,16},{4,20},{8,24},{12,28},{16,0},{20,4},{24,8},{28,12},{1,17},{... | collective-permute-start | bytes 196616 | tf_op jit(solution)/shard_map/ppermute | solution.py:190
  4.0 1.6 %collective-permute-start = (bf16[32,1024]{1,0:T(8,128)(2,1)}, bf16[32,1024]{1,0:T(8,128)(2,1)S(1)}, u32[]{:S(2)}, u32[]{:S(2)}) collective-permute-start(bf16[32,1024]{1,0:T(8,128)(2,1)} %param.3), channel_id=1, source_target_pairs={{0,8},{4,12},{8,0},{12,4},{16,24},{20,28},{24,16},{28,20},{1,9},{5... | collective-permute-start | bytes 196616 | tf_op jit(solution)/shard_map/ppermute | solution.py:190
  5.6 0.0 collective-permute-start.2
  5.6 0.0 copy-start.1
  5.6 1.9 %collective-permute-start.3 = (s32[4,128]{1,0:T(4,128)}, s32[4,128]{1,0:T(4,128)S(1)}, u32[]{:S(2)}, u32[]{:S(2)}) collective-permute-start(s32[4,128]{1,0:T(4,128)} %bitcast.5), channel_id=1, source_target_pairs={{0,16},{4,20},{8,24},{12,28},{16,0},{20,4},{24,8},{28,12},{1,17},{... | collective-permute-start | bytes 6152 | tf_op jit(solution)/shard_map/ppermute | solution.py:190
  7.5 0.8 %constant_dynamic-update-slice_fusion.3 = bf16[128,1024]{1,0:T(8,128)(2,1)S(1)} fusion(bf16[32,1024]{1,0:T(8,128)(2,1)} %param.3), kind=kLoop, calls=%fused_computation.3 | loop fusion | bytes 131072
  8.4 2.3 %collective-permute-done.3 = s32[4,128]{1,0:T(4,128)S(1)} collective-permute-done((s32[4,128]{1,0:T(4,128)}, s32[4,128]{1,0:T(4,128)S(1)}, u32[]{:S(2)}, u32[]{:S(2)}) %collective-permute-start.3) | collective-permute-done | bytes 2080 | tf_op jit(solution)/shard_map/ppermute | solution.py:190
  10.7 0.0 copy-done.1
  10.7 0.0 collective-permute-done.1
  10.7 0.0 collective-permute-done
  10.8 1.1 %collective-permute-done.2 = bf16[32,1024]{1,0:T(8,128)(2,1)S(1)} collective-permute-done((bf16[32,1024]{1,0:T(8,128)(2,1)}, bf16[32,1024]{1,0:T(8,128)(2,1)S(1)}, u32[]{:S(2)}, u32[]{:S(2)}) %collective-permute-start.2) | collective-permute-done | bytes 65568 | tf_op jit(solution)/shard_map/ppermute | solution.py:190
  11.9 0.7 %collective-permute-start.6 = (s32[8,128]{1,0:T(8,128)S(1)}, s32[8,128]{1,0:T(8,128)S(1)}, u32[]{:S(2)}, u32[]{:S(2)}) collective-permute-start(s32[8,128]{1,0:T(8,128)S(1)} %pad_add_fusion.1), channel_id=1, source_target_pairs={{0,8},{4,12},{8,0},{12,4},{16,24},{20,28},{24,16},{28,20},{1,9},{5... | collective-permute-start | bytes 12296 | tf_op jit(solution)/shard_map/ppermute | solution.py:190
  12.6 1.6 %collective-permute-start.5 = (bf16[128,1024]{1,0:T(8,128)(2,1)S(1)}, bf16[128,1024]{1,0:T(8,128)(2,1)S(1)}, u32[]{:S(2)}, u32[]{:S(2)}) collective-permute-start(bf16[128,1024]{1,0:T(8,128)(2,1)S(1)} %constant_dynamic-update-slice_fusion.refs_4_), channel_id=1, source_target_pairs={{0,2},{1,3},{2,0},{3,1},{4,6},{5,7},{6,4},{7,5},{8,10},{9,11},{10,... | collective-permute-start | bytes 786440 | tf_op jit(solution)/shard_map/ppermute | solution.py:190
  14.2 1.5 %collective-permute-start.4 = (bf16[128,1024]{1,0:T(8,128)(2,1)S(1)}, bf16[128,1024]{1,0:T(8,128)(2,1)S(1)}, u32[]{:S(2)}, u32[]{:S(2)}) collective-permute-start(bf16[128,1024]{1,0:T(8,128)(2,1)S(1)} %constant_dynamic-update-slice_fusion.refs_4_), channel_id=1, source_target_pairs={{0,1},{1,0},{2,3},{3,2},{4,5},{5,4},{6,7},{7,6},{8,9},{9,8},{10,11... | collective-permute-start | bytes 786440 | tf_op jit(solution)/shard_map/ppermute | solution.py:190
  15.7 0.0 collective-permute-done.6
  15.7 0.0 collective-permute-start.7
  15.7 3.4 %collective-permute-done.5.refs_8_ = bf16[128,1024]{1,0:T(8,128)(2,1)S(1)} collective-permute-done((bf16[128,1024]{1,0:T(8,128)(2,1)S(1)}, bf16[128,1024]{1,0:T(8,128)(2,1)S(1)}, u32[]{:S(2)}, u32[]{:S(2)}) %collective-permute-start.5) | collective-permute-done | bytes 262176 | tf_op jit(solution)/shard_map/ppermute | solution.py:190
  19.1 1.5 %collective-permute-done.4.refs_6_ = bf16[128,1024]{1,0:T(8,128)(2,1)S(1)} collective-permute-done((bf16[128,1024]{1,0:T(8,128)(2,1)S(1)}, bf16[128,1024]{1,0:T(8,128)(2,1)S(1)}, u32[]{:S(2)}, u32[]{:S(2)}) %collective-permute-start.4) | collective-permute-done | bytes 262176 | tf_op jit(solution)/shard_map/ppermute | solution.py:190
  20.6 0.0 collective-permute-done.7.refs_5_
  20.6 0.0 collective-permute-start.8
  20.6 1.6 %collective-permute-start.11 = (bf16[64,1024]{1,0:T(8,128)(2,1)S(1)}, bf16[64,1024]{1,0:T(8,128)(2,1)S(1)}, u32[]{:S(2)}, u32[]{:S(2)}) collective-permute-start(bf16[64,1024]{1,0:T(8,128)(2,1)S(1)} %slice.6), channel_id=1, source_target_pairs={{0,1},{1,0},{2,3},{3,2},{4,5},{5,4},{6,7},{7,6},{8,9},{9,8},{10,11... | collective-permute-start | bytes 393224 | tf_op jit(solution)/shard_map/ppermute | solution.py:190
  22.2 0.5 %collective-permute-start.12 = (bf16[64,1024]{1,0:T(8,128)(2,1)S(1)}, bf16[64,1024]{1,0:T(8,128)(2,1)S(1)}, u32[]{:S(2)}, u32[]{:S(2)}) collective-permute-start(bf16[64,1024]{1,0:T(8,128)(2,1)S(1)} %slice.7), channel_id=1, source_target_pairs={{0,2},{1,3},{2,0},{3,1},{4,6},{5,7},{6,4},{7,5},{8,10},{9,11},{10,... | collective-permute-start | bytes 393224 | tf_op jit(solution)/shard_map/ppermute | solution.py:190
  22.7 0.0 collective-permute-done.8.refs_3_
  22.7 0.0 collective-permute-start.9
  22.7 0.5 %collective-permute-start.10 = (bf16[128,1024]{1,0:T(8,128)(2,1)S(1)}, bf16[128,1024]{1,0:T(8,128)(2,1)S(1)}, u32[]{:S(2)}, u32[]{:S(2)}) collective-permute-start(bf16[128,1024]{1,0:T(8,128)(2,1)S(1)} %collective-permute-done.5.refs_8_), channel_id=1, source_target_pairs={{0,4},{4,0},{8,12},{12,8},{16,20},{20,16},{24,28},{28,24},{1,5},{5... | collective-permute-start | bytes 786440 | tf_op jit(solution)/shard_map/ppermute | solution.py:190
  23.2 3.4 %collective-permute-done.11.refs_10_ = bf16[64,1024]{1,0:T(8,128)(2,1)S(1)} collective-permute-done((bf16[64,1024]{1,0:T(8,128)(2,1)S(1)}, bf16[64,1024]{1,0:T(8,128)(2,1)S(1)}, u32[]{:S(2)}, u32[]{:S(2)}) %collective-permute-start.11) | collective-permute-done | bytes 131104 | tf_op jit(solution)/shard_map/ppermute | solution.py:190
  26.6 0.0 collective-permute-start.13
  26.6 1.2 %collective-permute-done.12.refs_11_ = bf16[64,1024]{1,0:T(8,128)(2,1)S(1)} collective-permute-done((bf16[64,1024]{1,0:T(8,128)(2,1)S(1)}, bf16[64,1024]{1,0:T(8,128)(2,1)S(1)}, u32[]{:S(2)}, u32[]{:S(2)}) %collective-permute-start.12) | collective-permute-done | bytes 131104 | tf_op jit(solution)/shard_map/ppermute | solution.py:190
  27.8 0.0 collective-permute-start.14
  27.8 0.0 copy-start
  27.8 0.1 pad_add_fusion.2.refs_0_
  27.9 0.1 collective-permute-done.13.refs_12_
  27.9 1.2 %collective-permute-done.14.refs_13_ = bf16[64,1024]{1,0:T(8,128)(2,1)S(1)} collective-permute-done((bf16[64,1024]{1,0:T(8,128)(2,1)S(1)}, bf16[64,1024]{1,0:T(8,128)(2,1)S(1)}, u32[]{:S(2)}, u32[]{:S(2)}) %collective-permute-start.14) | collective-permute-done | bytes 131104 | tf_op jit(solution)/shard_map/ppermute | solution.py:190
  29.1 0.0 collective-permute-done.9.refs_7_
  29.1 0.0 collective-permute-done.10.refs_9_
  29.2 0.0 copy-done
  29.2 9.3 %shard_map.37 = f32[32,1024]{1,0:T(8,128)} custom-call(s32[2]{0:T(128)S(1)} %pad_add_fusion.2.refs_0_, s32[8,128]{1,0:T(8,128)S(1)} %bitcast.4, s32[16,128]{1,0:T(8,128)S(1)} %pad_add_fusion.refs_2_, s32[16,128]{1,0:T(8,128)S(1)} %collective-permute-done.8.refs_3_, bf16[128,1024]{1,0:T(8,128)(2,1)S(1)} %constant_dynamic-update-slice_fusion.refs_4_, ...), custom_call_target="tpu_custom_call" | custom-call | flops 2147483648 | bytes 2097152 | tf_op jit(solution)/shard_map/pallas_call | solution.py:249
  (7 shorter events, 0.0 us)
Async XLA Ops:
  0.0 10.7 %collective-permute-start.1 = (bf16[32,1024]{1,0:T(8,128)(2,1)}, bf16[32,1024]{1,0:T(8,128)(2,1)S(1)}, u32[]{:S(2)}, u32[]{:S(2)}) collective-permute-start(bf16[32,1024]{1,0:T(8,128)(2,1)} %param.3), channel_id=1, source_target_pairs={{0,16},{4,20},{8,24},{12,28},{16,0},{20,4},{24,8},{28,12},{1,17},{... | collective-permute-start | bytes 196616 | tf_op jit(solution)/shard_map/ppermute | solution.py:190
  4.0 6.7 %collective-permute-start = (bf16[32,1024]{1,0:T(8,128)(2,1)}, bf16[32,1024]{1,0:T(8,128)(2,1)S(1)}, u32[]{:S(2)}, u32[]{:S(2)}) collective-permute-start(bf16[32,1024]{1,0:T(8,128)(2,1)} %param.3), channel_id=1, source_target_pairs={{0,8},{4,12},{8,0},{12,4},{16,24},{20,28},{24,16},{28,20},{1,9},{5... | collective-permute-start | bytes 196616 | tf_op jit(solution)/shard_map/ppermute | solution.py:190
  5.6 6.3 %collective-permute-start.2 = (bf16[32,1024]{1,0:T(8,128)(2,1)}, bf16[32,1024]{1,0:T(8,128)(2,1)S(1)}, u32[]{:S(2)}, u32[]{:S(2)}) collective-permute-start(bf16[32,1024]{1,0:T(8,128)(2,1)} %param.3), channel_id=1, source_target_pairs={{0,24},{4,28},{8,16},{12,20},{16,8},{20,12},{24,0},{28,4},{1,25},{... | collective-permute-start | bytes 196616 | tf_op jit(solution)/shard_map/ppermute | solution.py:190
  5.6 5.1 %copy-start.1 = (s32[128,4]{0,1:T(4,128)S(1)}, s32[128,4]{0,1:T(4,128)}, u32[]{:S(2)}) copy-start(s32[128,4]{0,1:T(4,128)} %param.4) | copy-start | bytes 6148
  5.6 5.1 %collective-permute-start.3 = (s32[4,128]{1,0:T(4,128)}, s32[4,128]{1,0:T(4,128)S(1)}, u32[]{:S(2)}, u32[]{:S(2)}) collective-permute-start(s32[4,128]{1,0:T(4,128)} %bitcast.5), channel_id=1, source_target_pairs={{0,16},{4,20},{8,24},{12,28},{16,0},{20,4},{24,8},{28,12},{1,17},{... | collective-permute-start | bytes 6152 | tf_op jit(solution)/shard_map/ppermute | solution.py:190
  11.9 3.8 %collective-permute-start.6 = (s32[8,128]{1,0:T(8,128)S(1)}, s32[8,128]{1,0:T(8,128)S(1)}, u32[]{:S(2)}, u32[]{:S(2)}) collective-permute-start(s32[8,128]{1,0:T(8,128)S(1)} %pad_add_fusion.1), channel_id=1, source_target_pairs={{0,8},{4,12},{8,0},{12,4},{16,24},{20,28},{24,16},{28,20},{1,9},{5... | collective-permute-start | bytes 12296 | tf_op jit(solution)/shard_map/ppermute | solution.py:190
  12.6 6.5 %collective-permute-start.5 = (bf16[128,1024]{1,0:T(8,128)(2,1)S(1)}, bf16[128,1024]{1,0:T(8,128)(2,1)S(1)}, u32[]{:S(2)}, u32[]{:S(2)}) collective-permute-start(bf16[128,1024]{1,0:T(8,128)(2,1)S(1)} %constant_dynamic-update-slice_fusion.refs_4_), channel_id=1, source_target_pairs={{0,2},{1,3},{2,0},{3,1},{4,6},{5,7},{6,4},{7,5},{8,10},{9,11},{10,... | collective-permute-start | bytes 786440 | tf_op jit(solution)/shard_map/ppermute | solution.py:190
  14.2 6.4 %collective-permute-start.4 = (bf16[128,1024]{1,0:T(8,128)(2,1)S(1)}, bf16[128,1024]{1,0:T(8,128)(2,1)S(1)}, u32[]{:S(2)}, u32[]{:S(2)}) collective-permute-start(bf16[128,1024]{1,0:T(8,128)(2,1)S(1)} %constant_dynamic-update-slice_fusion.refs_4_), channel_id=1, source_target_pairs={{0,1},{1,0},{2,3},{3,2},{4,5},{5,4},{6,7},{7,6},{8,9},{9,8},{10,11... | collective-permute-start | bytes 786440 | tf_op jit(solution)/shard_map/ppermute | solution.py:190
  15.7 4.9 %collective-permute-start.7 = (bf16[128,1024]{1,0:T(8,128)(2,1)S(1)}, bf16[128,1024]{1,0:T(8,128)(2,1)S(1)}, u32[]{:S(2)}, u32[]{:S(2)}) collective-permute-start(bf16[128,1024]{1,0:T(8,128)(2,1)S(1)} %constant_dynamic-update-slice_fusion.refs_4_), channel_id=1, source_target_pairs={{0,4},{4,0},{8,12},{12,8},{16,20},{20,16},{24,28},{28,24},{1,5},{5... | collective-permute-start | bytes 786440 | tf_op jit(solution)/shard_map/ppermute | solution.py:190
  20.6 2.1 %collective-permute-start.8 = (s32[16,128]{1,0:T(8,128)S(1)}, s32[16,128]{1,0:T(8,128)S(1)}, u32[]{:S(2)}, u32[]{:S(2)}) collective-permute-start(s32[16,128]{1,0:T(8,128)S(1)} %pad_add_fusion.refs_2_), channel_id=1, source_target_pairs={{0,4},{4,0},{8,12},{12,8},{16,20},{20,16},{24,28},{28,24},{1,5},{5... | collective-permute-start | bytes 24584 | tf_op jit(solution)/shard_map/ppermute | solution.py:190
  20.6 6.0 %collective-permute-start.11 = (bf16[64,1024]{1,0:T(8,128)(2,1)S(1)}, bf16[64,1024]{1,0:T(8,128)(2,1)S(1)}, u32[]{:S(2)}, u32[]{:S(2)}) collective-permute-start(bf16[64,1024]{1,0:T(8,128)(2,1)S(1)} %slice.6), channel_id=1, source_target_pairs={{0,1},{1,0},{2,3},{3,2},{4,5},{5,4},{6,7},{7,6},{8,9},{9,8},{10,11... | collective-permute-start | bytes 393224 | tf_op jit(solution)/shard_map/ppermute | solution.py:190
  22.2 5.6 %collective-permute-start.12 = (bf16[64,1024]{1,0:T(8,128)(2,1)S(1)}, bf16[64,1024]{1,0:T(8,128)(2,1)S(1)}, u32[]{:S(2)}, u32[]{:S(2)}) collective-permute-start(bf16[64,1024]{1,0:T(8,128)(2,1)S(1)} %slice.7), channel_id=1, source_target_pairs={{0,2},{1,3},{2,0},{3,1},{4,6},{5,7},{6,4},{7,5},{8,10},{9,11},{10,... | collective-permute-start | bytes 393224 | tf_op jit(solution)/shard_map/ppermute | solution.py:190
  22.7 6.5 %collective-permute-start.9 = (bf16[128,1024]{1,0:T(8,128)(2,1)S(1)}, bf16[128,1024]{1,0:T(8,128)(2,1)S(1)}, u32[]{:S(2)}, u32[]{:S(2)}) collective-permute-start(bf16[128,1024]{1,0:T(8,128)(2,1)S(1)} %collective-permute-done.4.refs_6_), channel_id=1, source_target_pairs={{0,4},{4,0},{8,12},{12,8},{16,20},{20,16},{24,28},{28,24},{1,5},{5... | collective-permute-start | bytes 786440 | tf_op jit(solution)/shard_map/ppermute | solution.py:190
  22.7 6.5 %collective-permute-start.10 = (bf16[128,1024]{1,0:T(8,128)(2,1)S(1)}, bf16[128,1024]{1,0:T(8,128)(2,1)S(1)}, u32[]{:S(2)}, u32[]{:S(2)}) collective-permute-start(bf16[128,1024]{1,0:T(8,128)(2,1)S(1)} %collective-permute-done.5.refs_8_), channel_id=1, source_target_pairs={{0,4},{4,0},{8,12},{12,8},{16,20},{20,16},{24,28},{28,24},{1,5},{5... | collective-permute-start | bytes 786440 | tf_op jit(solution)/shard_map/ppermute | solution.py:190
  26.6 1.3 %collective-permute-start.13 = (bf16[64,1024]{1,0:T(8,128)(2,1)S(1)}, bf16[64,1024]{1,0:T(8,128)(2,1)S(1)}, u32[]{:S(2)}, u32[]{:S(2)}) collective-permute-start(bf16[64,1024]{1,0:T(8,128)(2,1)S(1)} %collective-permute-done.11.refs_10_), channel_id=1, source_target_pairs={{0,4},{4,0},{8,12},{12,8},{16,20},{20,16},{24,28},{28,24},{1,5},{5... | collective-permute-start | bytes 393224 | tf_op jit(solution)/shard_map/ppermute | solution.py:190
  27.8 1.3 %collective-permute-start.14 = (bf16[64,1024]{1,0:T(8,128)(2,1)S(1)}, bf16[64,1024]{1,0:T(8,128)(2,1)S(1)}, u32[]{:S(2)}, u32[]{:S(2)}) collective-permute-start(bf16[64,1024]{1,0:T(8,128)(2,1)S(1)} %collective-permute-done.12.refs_11_), channel_id=1, source_target_pairs={{0,4},{4,0},{8,12},{12,8},{16,20},{20,16},{24,28},{28,24},{1,5},{5... | collective-permute-start | bytes 393224 | tf_op jit(solution)/shard_map/ppermute | solution.py:190
  27.8 1.4 %copy-start = (s32[1024]{0:T(1024)S(1)}, s32[1024]{0:T(1024)}, u32[]{:S(2)}) copy-start(s32[1024]{0:T(1024)} %param.5) | copy-start | bytes 12292

commit v5 on v3

--- a/solution.py
+++ b/solution.py
@@ -26,26 +26,46 @@
     return found
 
 
-def kernel(cols, levels, shard, pos_count, lane_block, layout, *refs):
-    place_ref, table_ref = refs[:2]
-    ids_refs = refs[2:4]
-    pieces = refs[4 : 4 + len(layout)]
-    out_ref, embed_ref, score_ref, own_ref, target_ref, stat_ref = refs[4 + len(layout) :]
+def kernel(
+    order,
+    shard,
+    pos_count,
+    lane_block,
+    place_ref,
+    table_ref,
+    own_ids_ref,
+    other_ids_ref,
+    own_rows_ref,
+    other_rows_ref,
+    out_ref,
+    embed_ref,
+    score_ref,
+    own_ref,
+    target_ref,
+    stat_ref,
+):
     total = embed_ref.shape[0]
     me = place_ref[0]
-    my_col = place_ref[1]
+    my_col = place_ref[1] * shard
+    cols = own_rows_ref.shape[0]
+    ids_refs = (own_ids_ref, other_ids_ref)
     pair = lane_block // 128
     row_chunk = min(512, total)
 
-    for piece, slots in zip(pieces, layout):
-        for spot, slot in enumerate(slots):
-            embed_ref[slot * shard : (slot + 1) * shard, :] = piece[spot * shard : (spot + 1) * shard, :]
+    for q in range(cols):
+        p = q ^ place_ref[1]
+        for c, rows_ref in enumerate((own_rows_ref, other_rows_ref)):
+            for d in range(len(order)):
+                start = ((d * 2 + c) * cols + p) * shard
+                embed_ref[pl.ds(pl.multiple_of(start, shard), shard), :] = rows_ref[
+                    q, d * shard : (d + 1) * shard, :
+                ]
 
     group = cols * shard
-    for line in range(2 * levels):
+    for line in range(2 * len(order)):
         for begin in range(0, group, 128):
-            level = line // 2 * pos_count
-            ids = ids_refs[line % 2][level : level + pos_count, begin : begin + 128]
+            at = order.index(line // 2) * pos_count
+            ids = ids_refs[line % 2][at : at + pos_count, begin : begin + 128]
             ids = jnp.concatenate([ids, ids], axis=0)
             found = lookup(table_ref, ids) ^ me
             lane = lax.broadcasted_iota(jnp.int32, found.shape, 1)
@@ -189,42 +209,34 @@
         size = lax.axis_size(axis)
         return lax.ppermute(array, axis, [(i, i ^ mask) for i in range(size)])
 
-    tall = jnp.concatenate(
-        [embed] + [swap(embed, "row", 2 * d) for d in range(1, levels)], axis=0
-    )
+    order = [0]
+    bits = [1 << b for b in reversed(range(levels.bit_length() - 1))]
+    line = [swap(embed, "row", 2 * d) for d in range(1, levels)]
     ids = positives.T
-    ids = jnp.concatenate([ids] + [swap(ids, "row", 2 * d) for d in range(1, levels)], axis=0)
-    tall, ids = lax.optimization_barrier((tall, ids))
-
-    half = levels // 2 * shard
-    plane = {0: [tall]}
-    for p in range(1, cols):
-        low, high = p & -p, 1 << (p.bit_length() - 1)
-        if low == high:
-            plane[p] = [swap(tall, "col", p)]
-        else:
-            first, second = plane[p ^ low], plane[p ^ high]
-            first = first[0][:half] if len(first) == 1 else first[0]
-            second = second[0][half:] if len(second) == 1 else second[1]
-            plane[p] = [swap(first, "col", low), swap(second, "col", high)]
-
-    pieces = []
-    layout = []
-    for p in range(cols):
-        level = 0
-        for part in plane[p]:
-            count = part.shape[0] // shard
-            for c in range(2):
-                pieces.append(part if c == 0 else swap(part, "row", 1))
-                layout.append([((level + d) * 2 + c) * cols + p for d in range(count)])
-            level += count
-
-    place = jnp.stack([lax.axis_index(axes) * shard, lax.axis_index("col") * shard])
+
+    def spread(ids):
+        bit = bits.pop(0)
+        order.extend([d ^ bit for d in order])
+        return jnp.concatenate([ids, swap(ids, "row", 2 * bit)], axis=0)
+
+    if bits:
+        ids = spread(ids)
+    line, ids = lax.optimization_barrier((line, ids))
+    tall = jnp.concatenate([embed] + line, axis=0)
+
+    wide = jnp.broadcast_to(tall[None], (cols, *tall.shape))
+    wide = lax.all_to_all(wide, "col", 0, 0)
+    while bits:
+        ids = spread(ids)
+    wide, ids = lax.optimization_barrier((wide, ids))
+    pieces = [ids, swap(ids, "row", 1), wide, swap(wide, "row", 1)]
+
+    place = jnp.stack([lax.axis_index(axes) * shard, lax.axis_index("col")])
     vmem = pl.BlockSpec(memory_space=pltpu.VMEM)
     return pl.pallas_call(
-        functools.partial(kernel, cols, levels, shard, pos_count, lane_block, layout),
+        functools.partial(kernel, order, shard, pos_count, lane_block),
         out_shape=jax.ShapeDtypeStruct((shard, width), jnp.float32),
-        in_specs=[pl.BlockSpec(memory_space=pltpu.SMEM)] + [vmem] * (3 + len(pieces)),
+        in_specs=[pl.BlockSpec(memory_space=pltpu.SMEM)] + [vmem] * (1 + len(pieces)),
         out_specs=vmem,
         scratch_shapes=[
             pltpu.VMEM((total, width), jnp.bfloat16),
@@ -233,7 +245,7 @@
             pltpu.VMEM((8, total), jnp.int32),
             pltpu.VMEM((24, total), jnp.float32),
         ],
-        compiler_params=pltpu.CompilerParams(vmem_limit_bytes=4 * total * width + 8 * total * lane_block + (8 << 20)),
+        compiler_params=pltpu.CompilerParams(vmem_limit_bytes=4 * total * width + 8 * total * lane_block + (16 << 20)),
         cost_estimate=pl.CostEstimate(
             flops=2 * total * total * width,
             bytes_accessed=2 * total * width,
@@ -242,8 +254,6 @@
     )(
         place.astype(jnp.int32),
         placement.reshape(-1, 128),
-        ids,
-        swap(ids, "row", 1),
         *pieces,
     )
 

time: 43.3 us -> 42.8 us (0.988)
  starting transfers between devices: 16.5 us -> 13.8 us
  waiting for transfers between devices: 15.6 us -> 16.7 us
  local copies, waits for them, and re-layouts: 0.02 us -> 1.1 us
    all_to_all x0 -> x1, waiting for transfers between devices: none -> 8.54 us  [body(): wide = lax.all_to_all(wide, 'col', 0, 0)]
    ppermute x16 -> x7, waiting for transfers between devices: 15.6 us -> 8.13 us  [swap(): return lax.ppermute(array, axis, [(i, i ^ mask) for i in range(size)])]
    ppermute x16 -> x7, starting transfers between devices: 16.5 us -> 10.1 us  [swap(): return lax.ppermute(array, axis, [(i, i ^ mask) for i in range(size)])]
    all_to_all x0 -> x1, starting transfers between devices: none -> 3.72 us  [body(): wide = lax.all_to_all(wide, 'col', 0, 0)]
    broadcast_in_dim x0 -> x1, local copies, waits for them, and re-layouts: none -> 1.09 us  [body(): wide = jnp.broadcast_to(tall[None], (cols, *tall.shape))]
    concatenate x2 -> x3, other arithmetic: 1.55 us -> 1.55 us  [the longest x1 0.86 us: body(): tall = jnp.concatenate([embed] + line, axis=0)]
  transfers between devices with their start and end apart: 16 -> 8, of which waited for: 7 -> 5; matrix products, arithmetic and copies ran while one was open for 2% -> 2% of each run, Pallas kernels for 0% -> 0%
where the time goes in v5:
time: 42.8 us; the launch traced here: 42.5 us
  waiting for transfers between devices  16.7 us (39%)
  starting transfers between devices  13.8 us (32%)
  Pallas kernels  9.34 us (22%)
  other arithmetic  1.62 us (4%)
  local copies, waits for them, and re-layouts  1.1 us (3%)
    ppermute x7, starting transfers between devices, swap(): return lax.ppermute(array, axis, [(i, i ^ mask) for i in range(size)])  10.1 us
    pallas_call x1, Pallas kernels, body(): pl.pallas_call(functools.partial(kernel, order, shard, pos_count, lane_bl...  9.34 us
    all_to_all x1, waiting for transfers between devices, body(): wide = lax.all_to_all(wide, 'col', 0, 0)  8.54 us
    ppermute x7, waiting for transfers between devices, swap(): return lax.ppermute(array, axis, [(i, i ^ mask) for i in range(size)])  8.13 us
    all_to_all x1, starting transfers between devices, body(): wide = lax.all_to_all(wide, 'col', 0, 0)  3.72 us
    broadcast_in_dim x1, local copies, waits for them, and re-layouts, body(): wide = jnp.broadcast_to(tall[None], (cols, *tall.shape))  1.09 us
    concatenate x1, other arithmetic, body(): tall = jnp.concatenate([embed] + line, axis=0)  0.86 us
  transfers between devices with their start and end apart: 8, of which 5 were waited for; matrix products, arithmetic and copies ran while one was open for 2% of the time, Pallas kernels for 0%

profile of v5, /device:TPU:0, one launch (start us, length us, event | category | flops | bytes accessed | tf_op | source)
XLA Modules:
  0.0 42.5 jit_solution(6232152353560162050)
XLA Ops:
  0.0 4.0 %collective-permute-start.3 = (s32[4,128]{1,0:T(4,128)}, s32[4,128]{1,0:T(4,128)S(1)}, u32[]{:S(2)}, u32[]{:S(2)}) collective-permute-start(s32[4,128]{1,0:T(4,128)} %bitcast.5), channel_id=1, source_target_pairs={{0,16},{4,20},{8,24},{12,28},{16,0},{20,4},{24,8},{28,12},{1,17},{... | collective-permute-start | bytes 6152 | tf_op jit(solution)/shard_map/ppermute | solution.py:210
  4.0 0.0 collective-permute-start.1
  4.1 1.9 %collective-permute-start = (bf16[32,1024]{1,0:T(8,128)(2,1)}, bf16[32,1024]{1,0:T(8,128)(2,1)S(1)}, u32[]{:S(2)}, u32[]{:S(2)}) collective-permute-start(bf16[32,1024]{1,0:T(8,128)(2,1)} %param.3), channel_id=1, source_target_pairs={{0,8},{4,12},{8,0},{12,4},{16,24},{20,28},{24,16},{28,20},{1,9},{5... | collective-permute-start | bytes 196616 | tf_op jit(solution)/shard_map/ppermute | solution.py:210
  6.0 2.5 %collective-permute-start.2 = (bf16[32,1024]{1,0:T(8,128)(2,1)}, bf16[32,1024]{1,0:T(8,128)(2,1)S(1)}, u32[]{:S(2)}, u32[]{:S(2)}) collective-permute-start(bf16[32,1024]{1,0:T(8,128)(2,1)} %param.3), channel_id=1, source_target_pairs={{0,24},{4,28},{8,16},{12,20},{16,8},{20,12},{24,0},{28,4},{1,25},{... | collective-permute-start | bytes 196616 | tf_op jit(solution)/shard_map/ppermute | solution.py:210
  8.4 0.0 collective-permute-done.3
  8.4 0.7 %pad_add_fusion.1 = s32[8,128]{1,0:T(8,128)S(1)} fusion(s32[4,128]{1,0:T(4,128)S(1)} %collective-permute-done.3, s32[4,128]{1,0:T(4,128)} %bitcast.6), kind=kLoop, calls=%fused_computation.2 | loop fusion | flops 1024 | bytes 8192 | tf_op jit(solution)/shard_map/concatenate | solution.py:220
  9.1 2.7 %collective-permute-done.1 = bf16[32,1024]{1,0:T(8,128)(2,1)S(1)} collective-permute-done((bf16[32,1024]{1,0:T(8,128)(2,1)}, bf16[32,1024]{1,0:T(8,128)(2,1)S(1)}, u32[]{:S(2)}, u32[]{:S(2)}) %collective-permute-start.1) | collective-permute-done | bytes 65568 | tf_op jit(solution)/shard_map/ppermute | solution.py:210
  11.8 0.0 collective-permute-done
  11.8 0.8 %collective-permute-done.2 = bf16[32,1024]{1,0:T(8,128)(2,1)S(1)} collective-permute-done((bf16[32,1024]{1,0:T(8,128)(2,1)}, bf16[32,1024]{1,0:T(8,128)(2,1)S(1)}, u32[]{:S(2)}, u32[]{:S(2)}) %collective-permute-start.2) | collective-permute-done | bytes 65568 | tf_op jit(solution)/shard_map/ppermute | solution.py:210
  12.7 0.9 %pad_maximum_fusion = bf16[128,1024]{1,0:T(8,128)(2,1)S(1)} fusion(bf16[32,1024]{1,0:T(8,128)(2,1)S(1)} %collective-permute-done.2, bf16[32,1024]{1,0:T(8,128)(2,1)S(1)} %collective-permute-done.1, bf16[32,1024]{1,0:T(8,128)(2,1)S(1)} %collective-permute-done, bf16[32,1024]{1,0:T(8,128)(2,1)} %param.3), kind=kLoop, calls=%fused_computation | loop fusion | flops 1048576 | bytes 524288 | tf_op jit(solution)/shard_map/concatenate | solution.py:225
  13.5 1.1 %broadcast_in_dim.2 = bf16[4,128,1024]{2,1,0:T(8,128)(2,1)} broadcast(bf16[128,1024]{1,0:T(8,128)(2,1)S(1)} %pad_maximum_fusion), dimensions={1,2} | broadcast | bytes 1310720 | tf_op jit(solution)/shard_map/broadcast_in_dim | solution.py:227
  14.6 3.7 %all-to-all-start = ((bf16[4,128,1024]{2,1,0:T(8,128)(2,1)}), bf16[4,128,1024]{2,1,0:T(8,128)(2,1)S(1)}, u32[]{:S(2)}, u32[]{:S(2)}) async-start(bf16[4,128,1024]{2,1,0:T(8,128)(2,1)} %broadcast_in_dim.2), calls=%async_computation | async-start | bytes 2097152 | tf_op jit(solution)/shard_map/all_to_all | solution.py:228
  18.3 1.1 %collective-permute-start.4 = (s32[8,128]{1,0:T(8,128)S(1)}, s32[8,128]{1,0:T(8,128)S(1)}, u32[]{:S(2)}, u32[]{:S(2)}) collective-permute-start(s32[8,128]{1,0:T(8,128)S(1)} %pad_add_fusion.1), channel_id=1, source_target_pairs={{0,8},{4,12},{8,0},{12,4},{16,24},{20,28},{24,16},{28,20},{1,9},{5... | collective-permute-start | bytes 12296 | tf_op jit(solution)/shard_map/ppermute | solution.py:210
  19.5 2.5 %collective-permute-done.4 = s32[8,128]{1,0:T(8,128)S(1)} collective-permute-done((s32[8,128]{1,0:T(8,128)S(1)}, s32[8,128]{1,0:T(8,128)S(1)}, u32[]{:S(2)}, u32[]{:S(2)}) %collective-permute-start.4) | collective-permute-done | bytes 4128 | tf_op jit(solution)/shard_map/ppermute | solution.py:210
  21.9 8.5 %all-to-all-done.own_rows_ref = bf16[4,128,1024]{2,1,0:T(8,128)(2,1)S(1)} async-done(((bf16[4,128,1024]{2,1,0:T(8,128)(2,1)}), bf16[4,128,1024]{2,1,0:T(8,128)(2,1)S(1)}, u32[]{:S(2)}, u32[]{:S(2)}) %all-to-all-start) | async-done | bytes 1048608 | tf_op jit(solution)/shard_map/all_to_all | solution.py:228
  30.5 0.0 collective-permute-start.6
  30.5 0.0 copy-start
  30.5 0.5 %collective-permute-start.5 = (s32[16,128]{1,0:T(8,128)S(1)}, s32[16,128]{1,0:T(8,128)S(1)}, u32[]{:S(2)}, u32[]{:S(2)}) collective-permute-start(s32[16,128]{1,0:T(8,128)S(1)} %pad_add_fusion.own_ids_ref), channel_id=1, source_target_pairs={{0,4},{4,0},{8,12},{12,8},{16,20},{20,16},{24,28},{28,24},{1,5},{5... | collective-permute-start | bytes 24584 | tf_op jit(solution)/shard_map/ppermute | solution.py:210
  31.0 0.1 pad_add_fusion.2.place_ref
  31.1 2.1 %collective-permute-done.5.other_ids_ref = s32[16,128]{1,0:T(8,128)S(1)} collective-permute-done((s32[16,128]{1,0:T(8,128)S(1)}, s32[16,128]{1,0:T(8,128)S(1)}, u32[]{:S(2)}, u32[]{:S(2)}) %collective-permute-start.5) | collective-permute-done | bytes 8224 | tf_op jit(solution)/shard_map/ppermute | solution.py:210
  33.2 0.0 collective-permute-done.6.other_rows_ref
  33.2 0.0 copy-done
  33.2 9.3 %shard_map.37 = f32[32,1024]{1,0:T(8,128)} custom-call(s32[2]{0:T(128)S(1)} %pad_add_fusion.2.place_ref, s32[8,128]{1,0:T(8,128)S(1)} %bitcast.4, s32[16,128]{1,0:T(8,128)S(1)} %pad_add_fusion.own_ids_ref, s32[16,128]{1,0:T(8,128)S(1)} %collective-permute-done.5.other_ids_ref, bf16[4,128,1024]{2,1,0:T(8,128)(2,1)S(1)} %all-to-all-done.own_rows_ref, ...), custom_call_target="tpu_custom_call" | custom-call | flops 2147483648 | bytes 2097152 | tf_op jit(solution)/shard_map/pallas_call | solution.py:236
  (1 shorter events, 0.0 us)
Async XLA Ops:
  0.0 8.4 %collective-permute-start.3 = (s32[4,128]{1,0:T(4,128)}, s32[4,128]{1,0:T(4,128)S(1)}, u32[]{:S(2)}, u32[]{:S(2)}) collective-permute-start(s32[4,128]{1,0:T(4,128)} %bitcast.5), channel_id=1, source_target_pairs={{0,16},{4,20},{8,24},{12,28},{16,0},{20,4},{24,8},{28,12},{1,17},{... | collective-permute-start | bytes 6152 | tf_op jit(solution)/shard_map/ppermute | solution.py:210
  4.0 7.8 %collective-permute-start.1 = (bf16[32,1024]{1,0:T(8,128)(2,1)}, bf16[32,1024]{1,0:T(8,128)(2,1)S(1)}, u32[]{:S(2)}, u32[]{:S(2)}) collective-permute-start(bf16[32,1024]{1,0:T(8,128)(2,1)} %param.3), channel_id=1, source_target_pairs={{0,16},{4,20},{8,24},{12,28},{16,0},{20,4},{24,8},{28,12},{1,17},{... | collective-permute-start | bytes 196616 | tf_op jit(solution)/shard_map/ppermute | solution.py:210
  4.1 7.8 %collective-permute-start = (bf16[32,1024]{1,0:T(8,128)(2,1)}, bf16[32,1024]{1,0:T(8,128)(2,1)S(1)}, u32[]{:S(2)}, u32[]{:S(2)}) collective-permute-start(bf16[32,1024]{1,0:T(8,128)(2,1)} %param.3), channel_id=1, source_target_pairs={{0,8},{4,12},{8,0},{12,4},{16,24},{20,28},{24,16},{28,20},{1,9},{5... | collective-permute-start | bytes 196616 | tf_op jit(solution)/shard_map/ppermute | solution.py:210
  6.0 6.7 %collective-permute-start.2 = (bf16[32,1024]{1,0:T(8,128)(2,1)}, bf16[32,1024]{1,0:T(8,128)(2,1)S(1)}, u32[]{:S(2)}, u32[]{:S(2)}) collective-permute-start(bf16[32,1024]{1,0:T(8,128)(2,1)} %param.3), channel_id=1, source_target_pairs={{0,24},{4,28},{8,16},{12,20},{16,8},{20,12},{24,0},{28,4},{1,25},{... | collective-permute-start | bytes 196616 | tf_op jit(solution)/shard_map/ppermute | solution.py:210
  14.6 15.9 %all-to-all-start = ((bf16[4,128,1024]{2,1,0:T(8,128)(2,1)}), bf16[4,128,1024]{2,1,0:T(8,128)(2,1)S(1)}, u32[]{:S(2)}, u32[]{:S(2)}) async-start(bf16[4,128,1024]{2,1,0:T(8,128)(2,1)} %broadcast_in_dim.2), calls=%async_computation | async-start | bytes 2097152 | tf_op jit(solution)/shard_map/all_to_all | solution.py:228
  18.3 3.6 %collective-permute-start.4 = (s32[8,128]{1,0:T(8,128)S(1)}, s32[8,128]{1,0:T(8,128)S(1)}, u32[]{:S(2)}, u32[]{:S(2)}) collective-permute-start(s32[8,128]{1,0:T(8,128)S(1)} %pad_add_fusion.1), channel_id=1, source_target_pairs={{0,8},{4,12},{8,0},{12,4},{16,24},{20,28},{24,16},{28,20},{1,9},{5... | collective-permute-start | bytes 12296 | tf_op jit(solution)/shard_map/ppermute | solution.py:210
  30.5 2.7 %collective-permute-start.6 = (bf16[4,128,1024]{2,1,0:T(8,128)(2,1)S(1)}, bf16[4,128,1024]{2,1,0:T(8,128)(2,1)S(1)}, u32[]{:S(2)}, u32[]{:S(2)}) collective-permute-start(bf16[4,128,1024]{2,1,0:T(8,128)(2,1)S(1)} %all-to-all-done.own_rows_ref), channel_id=1, source_target_pairs={{0,4},{4,0},{8,12},{12,8},{16,20},{20,16},{24,28},{28,24},{1,5},{5... | collective-permute-start | bytes 3145736 | tf_op jit(solution)/shard_map/ppermute | solution.py:210
  30.5 2.7 %copy-start = (s32[1024]{0:T(1024)S(1)}, s32[1024]{0:T(1024)}, u32[]{:S(2)}) copy-start(s32[1024]{0:T(1024)} %param.5) | copy-start | bytes 12292
  30.5 2.7 %collective-permute-start.5 = (s32[16,128]{1,0:T(8,128)S(1)}, s32[16,128]{1,0:T(8,128)S(1)}, u32[]{:S(2)}, u32[]{:S(2)}) collective-permute-start(s32[16,128]{1,0:T(8,128)S(1)} %pad_add_fusion.own_ids_ref), channel_id=1, source_target_pairs={{0,4},{4,0},{8,12},{12,8},{16,20},{20,16},{24,28},{28,24},{1,5},{5... | collective-permute-start | bytes 24584 | tf_op jit(solution)/shard_map/ppermute | solution.py:210

commit v6 on v4

--- a/solution.py
+++ b/solution.py
@@ -37,9 +37,11 @@
     pair = lane_block // 128
     row_chunk = min(512, total)
 
-    for piece, slots in zip(pieces, layout):
-        for spot, slot in enumerate(slots):
-            embed_ref[slot * shard : (slot + 1) * shard, :] = piece[spot * shard : (spot + 1) * shard, :]
+    for piece, (level, count, c, p, mirrored) in zip(pieces, layout):
+        p = jnp.where(place_ref[2] == c, p, mirrored)
+        for d in range(count):
+            start = pl.multiple_of((((level + d) * 2 + c) * cols + p) * shard, shard)
+            embed_ref[pl.ds(start, shard), :] = piece[d * shard : (d + 1) * shard, :]
 
     group = cols * shard
     for line in range(2 * len(order)):
@@ -189,49 +191,54 @@
         size = lax.axis_size(axis)
         return lax.ppermute(array, axis, [(i, i ^ mask) for i in range(size)])
 
+    width_bits = cols.bit_length() - 1
+    mirror = [sum(((p >> b) & 1) << (width_bits - 1 - b) for b in range(width_bits)) for p in range(cols)]
+
+    def hop(array, p):
+        pairs = []
+        for row in range(rows):
+            for col in range(cols):
+                peer = col ^ (mirror[p] if row % 2 else p)
+                pairs.append((row * cols + col, row * cols + peer))
+        return lax.ppermute(array, axes, pairs)
+
     order = [0]
     bits = [1 << b for b in reversed(range(levels.bit_length() - 1))]
+
+    def spread(ids):
+        if not bits:
+            return ids
+        bit = bits.pop(0)
+        order.extend([d ^ bit for d in order])
+        return jnp.concatenate([ids, swap(ids, "row", 2 * bit)], axis=0)
+
     line = [swap(embed, "row", 2 * d) for d in range(1, levels)]
-
-    def spread(ids):
-        if bits:
-            bit = bits.pop(0)
-            order.extend([d ^ bit for d in order])
-            return (jnp.concatenate([ids[0], swap(ids[0], "row", 2 * bit)], axis=0),)
-        if len(ids) == 1:
-            return (ids[0], swap(ids[0], "row", 1))
-        return ids
-
-    ids = spread((positives.T,))
+    ids = spread(positives.T)
     line, ids = lax.optimization_barrier((line, ids))
     tall = jnp.concatenate([embed] + line, axis=0)
 
     half = levels // 2 * shard
     plane = {0: [tall]}
-    other = {}
-    fresh = [0]
-    for weight in range(1, (cols - 1).bit_count() + 1):
-        coming = [p for p in range(1, cols) if p.bit_count() == weight]
-        for p in coming:
-            low, high = p & -p, 1 << (p.bit_length() - 1)
-            if low == high:
-                plane[p] = [swap(tall, "col", p)]
-            else:
-                first, second = plane[p ^ low], plane[p ^ high]
+    for weight in range(1, width_bits + 1):
+        for p in range(cols):
+            if p.bit_count() == weight:
+                low, high = p & -p, 1 << (p.bit_length() - 1)
+                if low == high:
+                    plane[p] = [hop(tall, p)]
+                    continue
+                first, second = plane[p ^ high], plane[p ^ low]
                 first = first[0][:half] if len(first) == 1 else first[0]
                 second = second[0][half:] if len(second) == 1 else second[1]
-                plane[p] = [swap(first, "col", low), swap(second, "col", high)]
+                plane[p] = [hop(first, high), hop(second, low)]
+    while bits:
         ids = spread(ids)
-        ready, ids = lax.optimization_barrier(([plane[p] for p in fresh], ids))
-        for p, parts in zip(fresh, ready):
-            other[p] = [swap(part, "row", 1) for part in parts]
-        fresh = coming
-        if weight < (cols - 1).bit_count():
-            plane, other, ids = lax.optimization_barrier((plane, other, ids))
-    while bits or len(ids) == 1:
-        ids = spread(ids)
-    for p in fresh:
-        other[p] = [swap(part, "row", 1) for part in plane[p]]
+
+    far = plane[cols - 1]
+    near = {p: plane[p] for p in range(cols - 1)}
+    near, far[0], ids = lax.optimization_barrier((near, far[0], ids))
+    plane = {**near, cols - 1: far}
+    other = {p: [swap(part, "row", 1) for part in plane[p]] for p in range(cols)}
+    ids = (ids, swap(ids, "row", 1))
 
     pieces = []
     layout = []
@@ -241,10 +248,12 @@
             for part in parts:
                 count = part.shape[0] // shard
                 pieces.append(part)
-                layout.append([((level + d) * 2 + c) * cols + p for d in range(count)])
+                layout.append((level, count, c, p, mirror[p]))
                 level += count
 
-    place = jnp.stack([lax.axis_index(axes) * shard, lax.axis_index("col") * shard])
+    place = jnp.stack(
+        [lax.axis_index(axes) * shard, lax.axis_index("col") * shard, lax.axis_index("row") % 2]
+    )
     vmem = pl.BlockSpec(memory_space=pltpu.VMEM)
     return pl.pallas_call(
         functools.partial(kernel, cols, order, shard, pos_count, lane_block, layout),
@@ -258,7 +267,7 @@
             pltpu.VMEM((8, total), jnp.int32),
             pltpu.VMEM((24, total), jnp.float32),
         ],
-        compiler_params=pltpu.CompilerParams(vmem_limit_bytes=4 * total * width + 8 * total * lane_block + (8 << 20)),
+        compiler_params=pltpu.CompilerParams(vmem_limit_bytes=4 * total * width + 8 * total * lane_block + (16 << 20)),
         cost_estimate=pl.CostEstimate(
             flops=2 * total * total * width,
             bytes_accessed=2 * total * width,

time: 38.6 us -> 40.9 us (1.060)
  waiting for transfers between devices: 14.2 us -> 15.9 us
  starting transfers between devices: 13.9 us -> 14.5 us
    ppermute x0 -> x4, waiting for transfers between devices: none -> 8.53 us  [hop(): return lax.ppermute(array, axes, pairs)]
    ppermute x15 -> x11, waiting for transfers between devices: 14.2 us -> 7.37 us  [swap(): return lax.ppermute(array, axis, [(i, i ^ mask) for i in range(size)])]
    ppermute x0 -> x4, starting transfers between devices: none -> 4.7 us  [hop(): return lax.ppermute(array, axes, pairs)]
    ppermute x15 -> x11, starting transfers between devices: 13.9 us -> 9.8 us  [swap(): return lax.ppermute(array, axis, [(i, i ^ mask) for i in range(size)])]
  transfers between devices with their start and end apart: 15 -> 15, of which waited for: 8 -> 7; matrix products, arithmetic and copies ran while one was open for 3% -> 2% of each run, Pallas kernels for 0% -> 0%
where the time goes in v6:
time: 40.9 us; the launch traced here: 40.7 us
  waiting for transfers between devices  15.9 us (39%)
  starting transfers between devices  14.5 us (35%)
  Pallas kernels  9.29 us (23%)
  local copies, waits for them, and re-layouts  0.89 us (2%)
    ppermute x11, starting transfers between devices, swap(): return lax.ppermute(array, axis, [(i, i ^ mask) for i in range(size)])  9.8 us
    pallas_call x1, Pallas kernels, body(): pl.pallas_call(functools.partial(kernel, cols, order, shard, pos_count, l...  9.29 us
    ppermute x4, waiting for transfers between devices, hop(): return lax.ppermute(array, axes, pairs)  8.53 us
    ppermute x11, waiting for transfers between devices, swap(): return lax.ppermute(array, axis, [(i, i ^ mask) for i in range(size)])  7.37 us
    ppermute x4, starting transfers between devices, hop(): return lax.ppermute(array, axes, pairs)  4.7 us
    unnamed x7, local copies, waits for them, and re-layouts  0.86 us
  transfers between devices with their start and end apart: 15, of which 7 were waited for; matrix products, arithmetic and copies ran while one was open for 2% of the time, Pallas kernels for 0%

profile of v6, /device:TPU:0, one launch (start us, length us, event | category | flops | bytes accessed | tf_op | source)
XLA Modules:
  0.0 40.7 jit_solution(6438131191094883758)
XLA Ops:
  0.0 4.0 %collective-permute-start.1 = (bf16[32,1024]{1,0:T(8,128)(2,1)}, bf16[32,1024]{1,0:T(8,128)(2,1)S(1)}, u32[]{:S(2)}, u32[]{:S(2)}) collective-permute-start(bf16[32,1024]{1,0:T(8,128)(2,1)} %param.3), channel_id=1, source_target_pairs={{0,16},{4,20},{8,24},{12,28},{16,0},{20,4},{24,8},{28,12},{1,17},{... | collective-permute-start | bytes 196616 | tf_op jit(solution)/shard_map/ppermute | solution.py:192
  4.0 1.6 %collective-permute-start = (bf16[32,1024]{1,0:T(8,128)(2,1)}, bf16[32,1024]{1,0:T(8,128)(2,1)S(1)}, u32[]{:S(2)}, u32[]{:S(2)}) collective-permute-start(bf16[32,1024]{1,0:T(8,128)(2,1)} %param.3), channel_id=1, source_target_pairs={{0,8},{4,12},{8,0},{12,4},{16,24},{20,28},{24,16},{28,20},{1,9},{5... | collective-permute-start | bytes 196616 | tf_op jit(solution)/shard_map/ppermute | solution.py:192
  5.6 0.0 collective-permute-start.2
  5.6 0.0 copy-start.1
  5.6 1.9 %collective-permute-start.3 = (s32[4,128]{1,0:T(4,128)}, s32[4,128]{1,0:T(4,128)S(1)}, u32[]{:S(2)}, u32[]{:S(2)}) collective-permute-start(s32[4,128]{1,0:T(4,128)} %bitcast.6), channel_id=1, source_target_pairs={{0,16},{4,20},{8,24},{12,28},{16,0},{20,4},{24,8},{28,12},{1,17},{... | collective-permute-start | bytes 6152 | tf_op jit(solution)/shard_map/ppermute | solution.py:192
  7.5 0.8 %constant_dynamic-update-slice_fusion.3 = bf16[128,1024]{1,0:T(8,128)(2,1)S(1)} fusion(bf16[32,1024]{1,0:T(8,128)(2,1)} %param.3), kind=kLoop, calls=%fused_computation.3 | loop fusion | bytes 131072
  8.4 2.3 %collective-permute-done.3 = s32[4,128]{1,0:T(4,128)S(1)} collective-permute-done((s32[4,128]{1,0:T(4,128)}, s32[4,128]{1,0:T(4,128)S(1)}, u32[]{:S(2)}, u32[]{:S(2)}) %collective-permute-start.3) | collective-permute-done | bytes 2080 | tf_op jit(solution)/shard_map/ppermute | solution.py:192
  10.7 0.0 copy-done.1
  10.7 0.0 collective-permute-done.1
  10.7 0.0 collective-permute-done
  10.8 1.1 %collective-permute-done.2 = bf16[32,1024]{1,0:T(8,128)(2,1)S(1)} collective-permute-done((bf16[32,1024]{1,0:T(8,128)(2,1)}, bf16[32,1024]{1,0:T(8,128)(2,1)S(1)}, u32[]{:S(2)}, u32[]{:S(2)}) %collective-permute-start.2) | collective-permute-done | bytes 65568 | tf_op jit(solution)/shard_map/ppermute | solution.py:192
  11.9 1.6 %collective-permute-start.4 = (bf16[128,1024]{1,0:T(8,128)(2,1)S(1)}, bf16[128,1024]{1,0:T(8,128)(2,1)S(1)}, u32[]{:S(2)}, u32[]{:S(2)}) collective-permute-start(bf16[128,1024]{1,0:T(8,128)(2,1)S(1)} %constant_dynamic-update-slice_fusion.refs_4_), channel_id=1, source_target_pairs={{0,1},{1,0},{2,3},{3,2},{4,6},{5,7},{6,4},{7,5},{8,9},{9,8},{10,11... | collective-permute-start | bytes 786440 | tf_op jit(solution)/shard_map/ppermute | solution.py:203
  13.5 1.5 %collective-permute-start.5 = (bf16[128,1024]{1,0:T(8,128)(2,1)S(1)}, bf16[128,1024]{1,0:T(8,128)(2,1)S(1)}, u32[]{:S(2)}, u32[]{:S(2)}) collective-permute-start(bf16[128,1024]{1,0:T(8,128)(2,1)S(1)} %constant_dynamic-update-slice_fusion.refs_4_), channel_id=1, source_target_pairs={{0,2},{1,3},{2,0},{3,1},{4,5},{5,4},{6,7},{7,6},{8,10},{9,11},{10,... | collective-permute-start | bytes 786440 | tf_op jit(solution)/shard_map/ppermute | solution.py:203
  15.0 6.1 %collective-permute-done.4.refs_6_ = bf16[128,1024]{1,0:T(8,128)(2,1)S(1)} collective-permute-done((bf16[128,1024]{1,0:T(8,128)(2,1)S(1)}, bf16[128,1024]{1,0:T(8,128)(2,1)S(1)}, u32[]{:S(2)}, u32[]{:S(2)}) %collective-permute-start.4) | collective-permute-done | bytes 262176 | tf_op jit(solution)/shard_map/ppermute | solution.py:203
  21.1 0.1 collective-permute-start.6
  21.2 0.7 %collective-permute-start.7 = (s32[8,128]{1,0:T(8,128)S(1)}, s32[8,128]{1,0:T(8,128)S(1)}, u32[]{:S(2)}, u32[]{:S(2)}) collective-permute-start(s32[8,128]{1,0:T(8,128)S(1)} %pad_add_fusion.1), channel_id=1, source_target_pairs={{0,8},{4,12},{8,0},{12,4},{16,24},{20,28},{24,16},{28,20},{1,9},{5... | collective-permute-start | bytes 12296 | tf_op jit(solution)/shard_map/ppermute | solution.py:192
  21.9 2.9 %collective-permute-done.7 = s32[8,128]{1,0:T(8,128)S(1)} collective-permute-done((s32[8,128]{1,0:T(8,128)S(1)}, s32[8,128]{1,0:T(8,128)S(1)}, u32[]{:S(2)}, u32[]{:S(2)}) %collective-permute-start.7) | collective-permute-done | bytes 4128 | tf_op jit(solution)/shard_map/ppermute | solution.py:192
  24.8 0.0 collective-permute-done.5.refs_8_
  24.9 1.6 %collective-permute-start.12 = (bf16[64,1024]{1,0:T(8,128)(2,1)S(1)}, bf16[64,1024]{1,0:T(8,128)(2,1)S(1)}, u32[]{:S(2)}, u32[]{:S(2)}) collective-permute-start(bf16[64,1024]{1,0:T(8,128)(2,1)S(1)} %slice.9), channel_id=1, source_target_pairs={{0,1},{1,0},{2,3},{3,2},{4,6},{5,7},{6,4},{7,5},{8,9},{9,8},{10,11... | collective-permute-start | bytes 393224 | tf_op jit(solution)/shard_map/ppermute | solution.py:203
  26.4 0.0 collective-permute-done.6.refs_10_
  26.4 0.0 collective-permute-start.9
  26.4 0.5 %collective-permute-start.10 = (bf16[128,1024]{1,0:T(8,128)(2,1)S(1)}, bf16[128,1024]{1,0:T(8,128)(2,1)S(1)}, u32[]{:S(2)}, u32[]{:S(2)}) collective-permute-start(bf16[128,1024]{1,0:T(8,128)(2,1)S(1)} %collective-permute-done.4.refs_6_), channel_id=1, source_target_pairs={{0,4},{4,0},{8,12},{12,8},{16,20},{20,16},{24,28},{28,24},{1,5},{5... | collective-permute-start | bytes 786440 | tf_op jit(solution)/shard_map/ppermute | solution.py:192
  26.9 0.0 collective-permute-start.11
  26.9 0.5 %collective-permute-start.8 = (s32[16,128]{1,0:T(8,128)S(1)}, s32[16,128]{1,0:T(8,128)S(1)}, u32[]{:S(2)}, u32[]{:S(2)}) collective-permute-start(s32[16,128]{1,0:T(8,128)S(1)} %pad_add_fusion.refs_2_), channel_id=1, source_target_pairs={{0,4},{4,0},{8,12},{12,8},{16,20},{20,16},{24,28},{28,24},{1,5},{5... | collective-permute-start | bytes 24584 | tf_op jit(solution)/shard_map/ppermute | solution.py:192
  27.4 2.5 %collective-permute-done.12.refs_11_ = bf16[64,1024]{1,0:T(8,128)(2,1)S(1)} collective-permute-done((bf16[64,1024]{1,0:T(8,128)(2,1)S(1)}, bf16[64,1024]{1,0:T(8,128)(2,1)S(1)}, u32[]{:S(2)}, u32[]{:S(2)}) %collective-permute-start.12) | collective-permute-done | bytes 131104 | tf_op jit(solution)/shard_map/ppermute | solution.py:203
  29.9 0.0 collective-permute-start.14
  29.9 0.0 collective-permute-done.8.refs_3_
  29.9 0.5 %collective-permute-start.13 = (bf16[64,1024]{1,0:T(8,128)(2,1)S(1)}, bf16[64,1024]{1,0:T(8,128)(2,1)S(1)}, u32[]{:S(2)}, u32[]{:S(2)}) collective-permute-start(bf16[64,1024]{1,0:T(8,128)(2,1)S(1)} %collective-permute-done.6.refs_10_), channel_id=1, source_target_pairs={{0,4},{4,0},{8,12},{12,8},{16,20},{20,16},{24,28},{28,24},{1,5},{5... | collective-permute-start | bytes 393224 | tf_op jit(solution)/shard_map/ppermute | solution.py:192
  30.4 0.0 copy-start
  30.4 0.1 pad_add_fusion.2.refs_0_
  30.5 0.8 %collective-permute-done.14.refs_13_ = bf16[64,1024]{1,0:T(8,128)(2,1)S(1)} collective-permute-done((bf16[64,1024]{1,0:T(8,128)(2,1)S(1)}, bf16[64,1024]{1,0:T(8,128)(2,1)S(1)}, u32[]{:S(2)}, u32[]{:S(2)}) %collective-permute-start.14) | collective-permute-done | bytes 131104 | tf_op jit(solution)/shard_map/ppermute | solution.py:192
  31.2 0.2 collective-permute-done.13.refs_12_
  31.4 0.0 collective-permute-done.9.refs_5_
  31.4 0.0 collective-permute-done.10.refs_7_
  31.4 0.0 collective-permute-done.11.refs_9_
  31.4 0.0 copy-done
  31.4 9.3 %shard_map.37 = f32[32,1024]{1,0:T(8,128)} custom-call(s32[3]{0:T(128)S(1)} %pad_add_fusion.2.refs_0_, s32[8,128]{1,0:T(8,128)S(1)} %bitcast.5, s32[16,128]{1,0:T(8,128)S(1)} %pad_add_fusion.refs_2_, s32[16,128]{1,0:T(8,128)S(1)} %collective-permute-done.8.refs_3_, bf16[128,1024]{1,0:T(8,128)(2,1)S(1)} %constant_dynamic-update-slice_fusion.refs_4_, ...), custom_call_target="tpu_custom_call" | custom-call | flops 2147483648 | bytes 2097152 | tf_op jit(solution)/shard_map/pallas_call | solution.py:258
  (7 shorter events, 0.0 us)
Async XLA Ops:
  0.0 10.7 %collective-permute-start.1 = (bf16[32,1024]{1,0:T(8,128)(2,1)}, bf16[32,1024]{1,0:T(8,128)(2,1)S(1)}, u32[]{:S(2)}, u32[]{:S(2)}) collective-permute-start(bf16[32,1024]{1,0:T(8,128)(2,1)} %param.3), channel_id=1, source_target_pairs={{0,16},{4,20},{8,24},{12,28},{16,0},{20,4},{24,8},{28,12},{1,17},{... | collective-permute-start | bytes 196616 | tf_op jit(solution)/shard_map/ppermute | solution.py:192
  4.0 6.7 %collective-permute-start = (bf16[32,1024]{1,0:T(8,128)(2,1)}, bf16[32,1024]{1,0:T(8,128)(2,1)S(1)}, u32[]{:S(2)}, u32[]{:S(2)}) collective-permute-start(bf16[32,1024]{1,0:T(8,128)(2,1)} %param.3), channel_id=1, source_target_pairs={{0,8},{4,12},{8,0},{12,4},{16,24},{20,28},{24,16},{28,20},{1,9},{5... | collective-permute-start | bytes 196616 | tf_op jit(solution)/shard_map/ppermute | solution.py:192
  5.6 6.3 %collective-permute-start.2 = (bf16[32,1024]{1,0:T(8,128)(2,1)}, bf16[32,1024]{1,0:T(8,128)(2,1)S(1)}, u32[]{:S(2)}, u32[]{:S(2)}) collective-permute-start(bf16[32,1024]{1,0:T(8,128)(2,1)} %param.3), channel_id=1, source_target_pairs={{0,24},{4,28},{8,16},{12,20},{16,8},{20,12},{24,0},{28,4},{1,25},{... | collective-permute-start | bytes 196616 | tf_op jit(solution)/shard_map/ppermute | solution.py:192
  5.6 5.1 %copy-start.1 = (s32[128,4]{0,1:T(4,128)S(1)}, s32[128,4]{0,1:T(4,128)}, u32[]{:S(2)}) copy-start(s32[128,4]{0,1:T(4,128)} %param.4) | copy-start | bytes 6148
  5.6 5.1 %collective-permute-start.3 = (s32[4,128]{1,0:T(4,128)}, s32[4,128]{1,0:T(4,128)S(1)}, u32[]{:S(2)}, u32[]{:S(2)}) collective-permute-start(s32[4,128]{1,0:T(4,128)} %bitcast.6), channel_id=1, source_target_pairs={{0,16},{4,20},{8,24},{12,28},{16,0},{20,4},{24,8},{28,12},{1,17},{... | collective-permute-start | bytes 6152 | tf_op jit(solution)/shard_map/ppermute | solution.py:192
  11.9 9.1 %collective-permute-start.4 = (bf16[128,1024]{1,0:T(8,128)(2,1)S(1)}, bf16[128,1024]{1,0:T(8,128)(2,1)S(1)}, u32[]{:S(2)}, u32[]{:S(2)}) collective-permute-start(bf16[128,1024]{1,0:T(8,128)(2,1)S(1)} %constant_dynamic-update-slice_fusion.refs_4_), channel_id=1, source_target_pairs={{0,1},{1,0},{2,3},{3,2},{4,6},{5,7},{6,4},{7,5},{8,9},{9,8},{10,11... | collective-permute-start | bytes 786440 | tf_op jit(solution)/shard_map/ppermute | solution.py:203
  13.5 11.4 %collective-permute-start.5 = (bf16[128,1024]{1,0:T(8,128)(2,1)S(1)}, bf16[128,1024]{1,0:T(8,128)(2,1)S(1)}, u32[]{:S(2)}, u32[]{:S(2)}) collective-permute-start(bf16[128,1024]{1,0:T(8,128)(2,1)S(1)} %constant_dynamic-update-slice_fusion.refs_4_), channel_id=1, source_target_pairs={{0,2},{1,3},{2,0},{3,1},{4,5},{5,4},{6,7},{7,6},{8,10},{9,11},{10,... | collective-permute-start | bytes 786440 | tf_op jit(solution)/shard_map/ppermute | solution.py:203
  21.1 5.3 %collective-permute-start.6 = (bf16[64,1024]{1,0:T(8,128)(2,1)S(1)}, bf16[64,1024]{1,0:T(8,128)(2,1)S(1)}, u32[]{:S(2)}, u32[]{:S(2)}) collective-permute-start(bf16[64,1024]{1,0:T(8,128)(2,1)S(1)} %slice.8), channel_id=1, source_target_pairs={{0,2},{1,3},{2,0},{3,1},{4,5},{5,4},{6,7},{7,6},{8,10},{9,11},{10,... | collective-permute-start | bytes 393224 | tf_op jit(solution)/shard_map/ppermute | solution.py:203
  21.2 3.7 %collective-permute-start.7 = (s32[8,128]{1,0:T(8,128)S(1)}, s32[8,128]{1,0:T(8,128)S(1)}, u32[]{:S(2)}, u32[]{:S(2)}) collective-permute-start(s32[8,128]{1,0:T(8,128)S(1)} %pad_add_fusion.1), channel_id=1, source_target_pairs={{0,8},{4,12},{8,0},{12,4},{16,24},{20,28},{24,16},{28,20},{1,9},{5... | collective-permute-start | bytes 12296 | tf_op jit(solution)/shard_map/ppermute | solution.py:192
  24.9 5.0 %collective-permute-start.12 = (bf16[64,1024]{1,0:T(8,128)(2,1)S(1)}, bf16[64,1024]{1,0:T(8,128)(2,1)S(1)}, u32[]{:S(2)}, u32[]{:S(2)}) collective-permute-start(bf16[64,1024]{1,0:T(8,128)(2,1)S(1)} %slice.9), channel_id=1, source_target_pairs={{0,1},{1,0},{2,3},{3,2},{4,6},{5,7},{6,4},{7,5},{8,9},{9,8},{10,11... | collective-permute-start | bytes 393224 | tf_op jit(solution)/shard_map/ppermute | solution.py:203
  26.4 5.0 %collective-permute-start.9 = (bf16[128,1024]{1,0:T(8,128)(2,1)S(1)}, bf16[128,1024]{1,0:T(8,128)(2,1)S(1)}, u32[]{:S(2)}, u32[]{:S(2)}) collective-permute-start(bf16[128,1024]{1,0:T(8,128)(2,1)S(1)} %constant_dynamic-update-slice_fusion.refs_4_), channel_id=1, source_target_pairs={{0,4},{4,0},{8,12},{12,8},{16,20},{20,16},{24,28},{28,24},{1,5},{5... | collective-permute-start | bytes 786440 | tf_op jit(solution)/shard_map/ppermute | solution.py:192
  26.4 5.0 %collective-permute-start.10 = (bf16[128,1024]{1,0:T(8,128)(2,1)S(1)}, bf16[128,1024]{1,0:T(8,128)(2,1)S(1)}, u32[]{:S(2)}, u32[]{:S(2)}) collective-permute-start(bf16[128,1024]{1,0:T(8,128)(2,1)S(1)} %collective-permute-done.4.refs_6_), channel_id=1, source_target_pairs={{0,4},{4,0},{8,12},{12,8},{16,20},{20,16},{24,28},{28,24},{1,5},{5... | collective-permute-start | bytes 786440 | tf_op jit(solution)/shard_map/ppermute | solution.py:192
  26.9 4.5 %collective-permute-start.11 = (bf16[128,1024]{1,0:T(8,128)(2,1)S(1)}, bf16[128,1024]{1,0:T(8,128)(2,1)S(1)}, u32[]{:S(2)}, u32[]{:S(2)}) collective-permute-start(bf16[128,1024]{1,0:T(8,128)(2,1)S(1)} %collective-permute-done.5.refs_8_), channel_id=1, source_target_pairs={{0,4},{4,0},{8,12},{12,8},{16,20},{20,16},{24,28},{28,24},{1,5},{5... | collective-permute-start | bytes 786440 | tf_op jit(solution)/shard_map/ppermute | solution.py:192
  26.9 3.0 %collective-permute-start.8 = (s32[16,128]{1,0:T(8,128)S(1)}, s32[16,128]{1,0:T(8,128)S(1)}, u32[]{:S(2)}, u32[]{:S(2)}) collective-permute-start(s32[16,128]{1,0:T(8,128)S(1)} %pad_add_fusion.refs_2_), channel_id=1, source_target_pairs={{0,4},{4,0},{8,12},{12,8},{16,20},{20,16},{24,28},{28,24},{1,5},{5... | collective-permute-start | bytes 24584 | tf_op jit(solution)/shard_map/ppermute | solution.py:192
  29.9 1.3 %collective-permute-start.14 = (bf16[64,1024]{1,0:T(8,128)(2,1)S(1)}, bf16[64,1024]{1,0:T(8,128)(2,1)S(1)}, u32[]{:S(2)}, u32[]{:S(2)}) collective-permute-start(bf16[64,1024]{1,0:T(8,128)(2,1)S(1)} %collective-permute-done.12.refs_11_), channel_id=1, source_target_pairs={{0,4},{4,0},{8,12},{12,8},{16,20},{20,16},{24,28},{28,24},{1,5},{5... | collective-permute-start | bytes 393224 | tf_op jit(solution)/shard_map/ppermute | solution.py:192
  29.9 1.5 %collective-permute-start.13 = (bf16[64,1024]{1,0:T(8,128)(2,1)S(1)}, bf16[64,1024]{1,0:T(8,128)(2,1)S(1)}, u32[]{:S(2)}, u32[]{:S(2)}) collective-permute-start(bf16[64,1024]{1,0:T(8,128)(2,1)S(1)} %collective-permute-done.6.refs_10_), channel_id=1, source_target_pairs={{0,4},{4,0},{8,12},{12,8},{16,20},{20,16},{24,28},{28,24},{1,5},{5... | collective-permute-start | bytes 393224 | tf_op jit(solution)/shard_map/ppermute | solution.py:192
  30.4 1.0 %copy-start = (s32[1024]{0:T(1024)S(1)}, s32[1024]{0:T(1024)}, u32[]{:S(2)}) copy-start(s32[1024]{0:T(1024)} %param.5) | copy-start | bytes 12292

commit v7 on v3

--- a/solution.py
+++ b/solution.py
@@ -26,7 +26,7 @@
     return found
 
 
-def kernel(cols, levels, shard, pos_count, lane_block, layout, *refs):
+def kernel(cols, order, shard, pos_count, lane_block, layout, *refs):
     place_ref, table_ref = refs[:2]
     ids_refs = refs[2:4]
     pieces = refs[4 : 4 + len(layout)]
@@ -42,9 +42,9 @@
             embed_ref[slot * shard : (slot + 1) * shard, :] = piece[spot * shard : (spot + 1) * shard, :]
 
     group = cols * shard
-    for line in range(2 * levels):
+    for line in range(2 * len(order)):
         for begin in range(0, group, 128):
-            level = line // 2 * pos_count
+            level = order.index(line // 2) * pos_count
             ids = ids_refs[line % 2][level : level + pos_count, begin : begin + 128]
             ids = jnp.concatenate([ids, ids], axis=0)
             found = lookup(table_ref, ids) ^ me
@@ -64,13 +64,25 @@
         score_ref[buffer, pl.ds(row, row_chunk), :] = scores
         picked = list(picked)
         for half in range(pair):
-            targets = target_ref[:, pl.ds(pl.multiple_of(start + half * 128, 128), 128)]
-            near = (targets - row) >> 3
-            sub = targets & 7
-            for step in range(row_chunk // 8):
-                tile = scores[step * 8 : (step + 1) * 8, half * 128 : (half + 1) * 128]
-                tile = jnp.take_along_axis(tile, sub, axis=0)
-                picked[half] = jnp.where(near == step, tile, picked[half])
+            lanes = slice(half * 128, (half + 1) * 128)
+            for m in range(pos_count):
+                target = jnp.broadcast_to(
+                    target_ref[m : m + 1, pl.ds(pl.multiple_of(start + half * 128, 128), 128)],
+                    (8, 128),
+                )
+                odd = [(target & (8 << b)) != 0 for b in range(3)]
+                near = (target - row) >> 6
+                at = half * pos_count + m
+                for step in range(row_chunk // 64):
+                    tiles = [
+                        scores[step * 64 + k * 8 : step * 64 + (k + 1) * 8, lanes] for k in range(8)
+                    ]
+                    for b in range(3):
+                        tiles = [
+                            jnp.where(odd[b], tiles[2 * k + 1], tiles[2 * k])
+                            for k in range(len(tiles) // 2)
+                        ]
+                    picked[at] = jnp.where(near == step, tiles[0], picked[at])
         return tuple(picked)
 
     def rank_chunk(pos, buffer, chunk, sums):
@@ -87,7 +99,7 @@
         return tuple(sums)
 
     chunks = total // row_chunk
-    nothing = (jnp.zeros((8, 128), jnp.float32),) * pair
+    nothing = (jnp.zeros((8, 128), jnp.float32),) * (pair * pos_count)
     zero = (jnp.zeros((8, 128), jnp.float32),) * (2 * pos_count * pair)
 
     def split(start, buffer, picked):
@@ -95,7 +107,22 @@
         index = lax.broadcasted_iota(jnp.int32, (lane_block, lane_block), 0)
         lane = lax.broadcasted_iota(jnp.int32, (lane_block, lane_block), 1)
         score_ref[inside] = jnp.where(index == lane, masked, score_ref[inside])
-        return tuple(tuple(part[m : m + 1, :] for m in range(pos_count)) for part in picked)
+        sub = lax.broadcasted_iota(jnp.int32, (8, 128), 0)
+        pos = []
+        for half in range(pair):
+            targets = target_ref[:, pl.ds(pl.multiple_of(start + half * 128, 128), 128)]
+            parts = picked[half * pos_count : (half + 1) * pos_count]
+            pos.append(
+                tuple(
+                    jnp.sum(
+                        jnp.where(sub == (targets[m : m + 1, :] & 7), parts[m], 0.0),
+                        axis=0,
+                        keepdims=True,
+                    )
+                    for m in range(pos_count)
+                )
+            )
+        return tuple(pos)
 
     def finish(start, buffer, pos, sums):
         factor = 1.0 / (pos_count * total)
@@ -189,40 +216,46 @@
         size = lax.axis_size(axis)
         return lax.ppermute(array, axis, [(i, i ^ mask) for i in range(size)])
 
-    tall = jnp.concatenate(
-        [embed] + [swap(embed, "row", 2 * d) for d in range(1, levels)], axis=0
-    )
-    ids = positives.T
-    ids = jnp.concatenate([ids] + [swap(ids, "row", 2 * d) for d in range(1, levels)], axis=0)
-    tall, ids = lax.optimization_barrier((tall, ids))
-
-    half = levels // 2 * shard
-    plane = {0: [tall]}
-    for p in range(1, cols):
-        low, high = p & -p, 1 << (p.bit_length() - 1)
-        if low == high:
-            plane[p] = [swap(tall, "col", p)]
-        else:
-            first, second = plane[p ^ low], plane[p ^ high]
-            first = first[0][:half] if len(first) == 1 else first[0]
-            second = second[0][half:] if len(second) == 1 else second[1]
-            plane[p] = [swap(first, "col", low), swap(second, "col", high)]
+    def join(parts):
+        return parts[0] if len(parts) == 1 else jnp.concatenate(parts, axis=0)
+
+    bits = [1 << b for b in reversed(range(levels.bit_length() - 1))]
+    order = [0]
+    steps = list(bits)
+
+    def spread(ids):
+        if not steps:
+            return ids
+        bit = steps.pop(0)
+        order.extend([d ^ bit for d in order])
+        return jnp.concatenate([ids, swap(ids, "row", 2 * bit)], axis=0)
+
+    line = {0: embed}
+    for bit in bits:
+        line.update({d ^ bit: swap(line[d], "row", 2 * bit) for d in line})
+    ids = spread(positives.T)
+    line, ids = lax.optimization_barrier((line, ids))
+    tall = join([line[d] for d in range(levels)])
+
+    plane = {0: tall}
+    plane.update({p: swap(tall, "col", p) for p in range(1, cols)})
+    while steps:
+        ids = spread(ids)
+    plane, ids = lax.optimization_barrier((plane, ids))
+
+    ids = (ids, swap(ids, "row", 1))
 
     pieces = []
     layout = []
     for p in range(cols):
-        level = 0
-        for part in plane[p]:
-            count = part.shape[0] // shard
-            for c in range(2):
-                pieces.append(part if c == 0 else swap(part, "row", 1))
-                layout.append([((level + d) * 2 + c) * cols + p for d in range(count)])
-            level += count
+        for c, part in enumerate((plane[p], swap(plane[p], "row", 1))):
+            pieces.append(part)
+            layout.append([(d * 2 + c) * cols + p for d in range(levels)])
 
     place = jnp.stack([lax.axis_index(axes) * shard, lax.axis_index("col") * shard])
     vmem = pl.BlockSpec(memory_space=pltpu.VMEM)
     return pl.pallas_call(
-        functools.partial(kernel, cols, levels, shard, pos_count, lane_block, layout),
+        functools.partial(kernel, cols, order, shard, pos_count, lane_block, layout),
         out_shape=jax.ShapeDtypeStruct((shard, width), jnp.float32),
         in_specs=[pl.BlockSpec(memory_space=pltpu.SMEM)] + [vmem] * (3 + len(pieces)),
         out_specs=vmem,
@@ -233,7 +266,7 @@
             pltpu.VMEM((8, total), jnp.int32),
             pltpu.VMEM((24, total), jnp.float32),
         ],
-        compiler_params=pltpu.CompilerParams(vmem_limit_bytes=4 * total * width + 8 * total * lane_block + (8 << 20)),
+        compiler_params=pltpu.CompilerParams(vmem_limit_bytes=4 * total * width + 8 * total * lane_block + (16 << 20)),
         cost_estimate=pl.CostEstimate(
             flops=2 * total * total * width,
             bytes_accessed=2 * total * width,
@@ -242,8 +275,7 @@
     )(
         place.astype(jnp.int32),
         placement.reshape(-1, 128),
-        ids,
-        swap(ids, "row", 1),
+        *ids,
         *pieces,
     )
 

time: 43.3 us -> 37.5 us (0.87)
  starting transfers between devices: 16.5 us -> 12.1 us
  waiting for transfers between devices: 15.6 us -> 14.2 us
  other arithmetic: 1.62 us -> 0.77 us
  local copies, waits for them, and re-layouts: 0.02 us -> 0.87 us
    ppermute x16 -> x13, starting transfers between devices: 16.5 us -> 12.1 us  [swap(): return lax.ppermute(array, axis, [(i, i ^ mask) for i in range(size)])]
    ppermute x16 -> x13, waiting for transfers between devices: 15.6 us -> 14.2 us  [swap(): return lax.ppermute(array, axis, [(i, i ^ mask) for i in range(size)])]
    concatenate x2, other arithmetic: 1.55 us -> 0.69 us  [spread(): return jnp.concatenate([ids, swap(ids, 'row', 2 * bit)], axis=0)]
    unnamed x2 -> x5, local copies, waits for them, and re-layouts: 0.01 us -> 0.86 us
  transfers between devices with their start and end apart: 16 -> 13, of which waited for: 7 -> 8; matrix products, arithmetic and copies ran while one was open for 2% -> 2% of each run, Pallas kernels for 0% -> 0%
where the time goes in v7:
time: 37.5 us; the launch traced here: 37.3 us
  waiting for transfers between devices  14.2 us (38%)
  starting transfers between devices  12.1 us (32%)
  Pallas kernels  9.43 us (25%)
  local copies, waits for them, and re-layouts  0.87 us (2%)
  other arithmetic  0.77 us (2%)
    ppermute x13, waiting for transfers between devices, swap(): return lax.ppermute(array, axis, [(i, i ^ mask) for i in range(size)])  14.2 us
    ppermute x13, starting transfers between devices, swap(): return lax.ppermute(array, axis, [(i, i ^ mask) for i in range(size)])  12.1 us
    pallas_call x1, Pallas kernels, body(): pl.pallas_call(functools.partial(kernel, cols, order, shard, pos_count, l...  9.43 us
    unnamed x5, local copies, waits for them, and re-layouts  0.86 us
  transfers between devices with their start and end apart: 13, of which 8 were waited for; matrix products, arithmetic and copies ran while one was open for 2% of the time, Pallas kernels for 0%

profile of v7, /device:TPU:0, one launch (start us, length us, event | category | flops | bytes accessed | tf_op | source)
XLA Modules:
  0.0 37.3 jit_solution(14279413385889284471)
XLA Ops:
  0.0 4.0 %collective-permute-start.1 = (bf16[32,1024]{1,0:T(8,128)(2,1)}, bf16[32,1024]{1,0:T(8,128)(2,1)S(1)}, u32[]{:S(2)}, u32[]{:S(2)}) collective-permute-start(bf16[32,1024]{1,0:T(8,128)(2,1)} %param.3), channel_id=1, source_target_pairs={{0,16},{4,20},{8,24},{12,28},{16,0},{20,4},{24,8},{28,12},{1,17},{... | collective-permute-start | bytes 196616 | tf_op jit(solution)/shard_map/ppermute | solution.py:217
  4.0 0.0 collective-permute-start.3
  4.1 1.9 %collective-permute-start = (bf16[32,1024]{1,0:T(8,128)(2,1)}, bf16[32,1024]{1,0:T(8,128)(2,1)S(1)}, u32[]{:S(2)}, u32[]{:S(2)}) collective-permute-start(bf16[32,1024]{1,0:T(8,128)(2,1)} %param.3), channel_id=1, source_target_pairs={{0,8},{4,12},{8,0},{12,4},{16,24},{20,28},{24,16},{28,20},{1,9},{5... | collective-permute-start | bytes 196616 | tf_op jit(solution)/shard_map/ppermute | solution.py:217
  6.0 1.9 %collective-permute-done.1 = bf16[32,1024]{1,0:T(8,128)(2,1)S(1)} collective-permute-done((bf16[32,1024]{1,0:T(8,128)(2,1)}, bf16[32,1024]{1,0:T(8,128)(2,1)S(1)}, u32[]{:S(2)}, u32[]{:S(2)}) %collective-permute-start.1) | collective-permute-done | bytes 65568 | tf_op jit(solution)/shard_map/ppermute | solution.py:217
  7.9 0.8 %collective-permute-start.2 = (bf16[32,1024]{1,0:T(8,128)(2,1)S(1)}, bf16[32,1024]{1,0:T(8,128)(2,1)S(1)}, u32[]{:S(2)}, u32[]{:S(2)}) collective-permute-start(bf16[32,1024]{1,0:T(8,128)(2,1)S(1)} %collective-permute-done.1), channel_id=1, source_target_pairs={{0,8},{4,12},{8,0},{12,4},{16,24},{20,28},{24,16},{28,20},{1,9},{5... | collective-permute-start | bytes 196616 | tf_op jit(solution)/shard_map/ppermute | solution.py:217
  8.7 0.1 collective-permute-done.3
  8.7 0.7 %pad_add_fusion.1 = s32[8,128]{1,0:T(8,128)S(1)} fusion(s32[4,128]{1,0:T(4,128)S(1)} %collective-permute-done.3, s32[4,128]{1,0:T(4,128)} %bitcast.6), kind=kLoop, calls=%fused_computation.5 | loop fusion | flops 1024 | bytes 8192 | tf_op jit(solution)/shard_map/concatenate | solution.py:231
  9.4 0.0 collective-permute-done
  9.4 2.7 %collective-permute-done.2 = bf16[32,1024]{1,0:T(8,128)(2,1)S(1)} collective-permute-done((bf16[32,1024]{1,0:T(8,128)(2,1)S(1)}, bf16[32,1024]{1,0:T(8,128)(2,1)S(1)}, u32[]{:S(2)}, u32[]{:S(2)}) %collective-permute-start.2) | collective-permute-done | bytes 65568 | tf_op jit(solution)/shard_map/ppermute | solution.py:217
  12.2 0.8 %constant_dynamic-update-slice_fusion.3 = bf16[128,1024]{1,0:T(8,128)(2,1)S(1)} fusion(bf16[32,1024]{1,0:T(8,128)(2,1)} %param.3), kind=kLoop, calls=%fused_computation.3 | loop fusion | bytes 131072
  13.0 2.7 %collective-permute-start.6 = (bf16[128,1024]{1,0:T(8,128)(2,1)S(1)}, bf16[128,1024]{1,0:T(8,128)(2,1)S(1)}, u32[]{:S(2)}, u32[]{:S(2)}) collective-permute-start(bf16[128,1024]{1,0:T(8,128)(2,1)S(1)} %constant_dynamic-update-slice_fusion.refs_4_), channel_id=1, source_target_pairs={{0,3},{1,2},{2,1},{3,0},{4,7},{5,6},{6,5},{7,4},{8,11},{9,10},{10,... | collective-permute-start | bytes 786440 | tf_op jit(solution)/shard_map/ppermute | solution.py:217
  15.8 0.5 %collective-permute-start.5 = (bf16[128,1024]{1,0:T(8,128)(2,1)S(1)}, bf16[128,1024]{1,0:T(8,128)(2,1)S(1)}, u32[]{:S(2)}, u32[]{:S(2)}) collective-permute-start(bf16[128,1024]{1,0:T(8,128)(2,1)S(1)} %constant_dynamic-update-slice_fusion.refs_4_), channel_id=1, source_target_pairs={{0,2},{1,3},{2,0},{3,1},{4,6},{5,7},{6,4},{7,5},{8,10},{9,11},{10,... | collective-permute-start | bytes 786440 | tf_op jit(solution)/shard_map/ppermute | solution.py:217
  16.3 0.3 collective-permute-start.4
  16.6 0.8 %collective-permute-start.7 = (s32[8,128]{1,0:T(8,128)S(1)}, s32[8,128]{1,0:T(8,128)S(1)}, u32[]{:S(2)}, u32[]{:S(2)}) collective-permute-start(s32[8,128]{1,0:T(8,128)S(1)} %pad_add_fusion.1), channel_id=1, source_target_pairs={{0,8},{4,12},{8,0},{12,4},{16,24},{20,28},{24,16},{28,20},{1,9},{5... | collective-permute-start | bytes 12296 | tf_op jit(solution)/shard_map/ppermute | solution.py:217
  17.4 2.8 %collective-permute-done.7 = s32[8,128]{1,0:T(8,128)S(1)} collective-permute-done((s32[8,128]{1,0:T(8,128)S(1)}, s32[8,128]{1,0:T(8,128)S(1)}, u32[]{:S(2)}, u32[]{:S(2)}) %collective-permute-start.7) | collective-permute-done | bytes 4128 | tf_op jit(solution)/shard_map/ppermute | solution.py:217
  20.2 2.0 %collective-permute-done.6.refs_10_ = bf16[128,1024]{1,0:T(8,128)(2,1)S(1)} collective-permute-done((bf16[128,1024]{1,0:T(8,128)(2,1)S(1)}, bf16[128,1024]{1,0:T(8,128)(2,1)S(1)}, u32[]{:S(2)}, u32[]{:S(2)}) %collective-permute-start.6) | collective-permute-done | bytes 262176 | tf_op jit(solution)/shard_map/ppermute | solution.py:217
  22.2 2.7 %collective-permute-done.5.refs_8_ = bf16[128,1024]{1,0:T(8,128)(2,1)S(1)} collective-permute-done((bf16[128,1024]{1,0:T(8,128)(2,1)S(1)}, bf16[128,1024]{1,0:T(8,128)(2,1)S(1)}, u32[]{:S(2)}, u32[]{:S(2)}) %collective-permute-start.5) | collective-permute-done | bytes 262176 | tf_op jit(solution)/shard_map/ppermute | solution.py:217
  24.9 0.3 collective-permute-done.4.refs_6_
  25.2 0.0 collective-permute-start.9
  25.2 0.5 %collective-permute-start.10 = (bf16[128,1024]{1,0:T(8,128)(2,1)S(1)}, bf16[128,1024]{1,0:T(8,128)(2,1)S(1)}, u32[]{:S(2)}, u32[]{:S(2)}) collective-permute-start(bf16[128,1024]{1,0:T(8,128)(2,1)S(1)} %collective-permute-done.4.refs_6_), channel_id=1, source_target_pairs={{0,4},{4,0},{8,12},{12,8},{16,20},{20,16},{24,28},{28,24},{1,5},{5... | collective-permute-start | bytes 786440 | tf_op jit(solution)/shard_map/ppermute | solution.py:217
  25.7 0.0 collective-permute-start.11
  25.7 0.5 %collective-permute-start.12 = (bf16[128,1024]{1,0:T(8,128)(2,1)S(1)}, bf16[128,1024]{1,0:T(8,128)(2,1)S(1)}, u32[]{:S(2)}, u32[]{:S(2)}) collective-permute-start(bf16[128,1024]{1,0:T(8,128)(2,1)S(1)} %collective-permute-done.6.refs_10_), channel_id=1, source_target_pairs={{0,4},{4,0},{8,12},{12,8},{16,20},{20,16},{24,28},{28,24},{1,5},{5... | collective-permute-start | bytes 786440 | tf_op jit(solution)/shard_map/ppermute | solution.py:217
  26.2 0.0 copy-start
  26.2 0.0 collective-permute-start.8
  26.2 0.1 pad_add_fusion.2.refs_0_
  26.3 1.6 %collective-permute-done.8.refs_3_ = s32[16,128]{1,0:T(8,128)S(1)} collective-permute-done((s32[16,128]{1,0:T(8,128)S(1)}, s32[16,128]{1,0:T(8,128)S(1)}, u32[]{:S(2)}, u32[]{:S(2)}) %collective-permute-start.8) | collective-permute-done | bytes 8224 | tf_op jit(solution)/shard_map/ppermute | solution.py:217
  27.9 0.0 collective-permute-done.9.refs_5_
  27.9 0.0 collective-permute-done.10.refs_7_
  27.9 0.0 collective-permute-done.11.refs_9_
  27.9 0.0 collective-permute-done.12.refs_11_
  27.9 0.0 copy-done
  27.9 9.4 %shard_map.37 = f32[32,1024]{1,0:T(8,128)} custom-call(s32[2]{0:T(128)S(1)} %pad_add_fusion.2.refs_0_, s32[8,128]{1,0:T(8,128)S(1)} %bitcast.4, s32[16,128]{1,0:T(8,128)S(1)} %pad_add_fusion.refs_2_, s32[16,128]{1,0:T(8,128)S(1)} %collective-permute-done.8.refs_3_, bf16[128,1024]{1,0:T(8,128)(2,1)S(1)} %constant_dynamic-update-slice_fusion.refs_4_, ...), custom_call_target="tpu_custom_call" | custom-call | flops 2147483648 | bytes 2097152 | tf_op jit(solution)/shard_map/pallas_call | solution.py:257
  (4 shorter events, 0.0 us)
Async XLA Ops:
  0.0 7.9 %collective-permute-start.1 = (bf16[32,1024]{1,0:T(8,128)(2,1)}, bf16[32,1024]{1,0:T(8,128)(2,1)S(1)}, u32[]{:S(2)}, u32[]{:S(2)}) collective-permute-start(bf16[32,1024]{1,0:T(8,128)(2,1)} %param.3), channel_id=1, source_target_pairs={{0,16},{4,20},{8,24},{12,28},{16,0},{20,4},{24,8},{28,12},{1,17},{... | collective-permute-start | bytes 196616 | tf_op jit(solution)/shard_map/ppermute | solution.py:217
  4.0 4.7 %collective-permute-start.3 = (s32[4,128]{1,0:T(4,128)}, s32[4,128]{1,0:T(4,128)S(1)}, u32[]{:S(2)}, u32[]{:S(2)}) collective-permute-start(s32[4,128]{1,0:T(4,128)} %bitcast.5), channel_id=1, source_target_pairs={{0,16},{4,20},{8,24},{12,28},{16,0},{20,4},{24,8},{28,12},{1,17},{... | collective-permute-start | bytes 6152 | tf_op jit(solution)/shard_map/ppermute | solution.py:217
  4.1 5.4 %collective-permute-start = (bf16[32,1024]{1,0:T(8,128)(2,1)}, bf16[32,1024]{1,0:T(8,128)(2,1)S(1)}, u32[]{:S(2)}, u32[]{:S(2)}) collective-permute-start(bf16[32,1024]{1,0:T(8,128)(2,1)} %param.3), channel_id=1, source_target_pairs={{0,8},{4,12},{8,0},{12,4},{16,24},{20,28},{24,16},{28,20},{1,9},{5... | collective-permute-start | bytes 196616 | tf_op jit(solution)/shard_map/ppermute | solution.py:217
  7.9 4.3 %collective-permute-start.2 = (bf16[32,1024]{1,0:T(8,128)(2,1)S(1)}, bf16[32,1024]{1,0:T(8,128)(2,1)S(1)}, u32[]{:S(2)}, u32[]{:S(2)}) collective-permute-start(bf16[32,1024]{1,0:T(8,128)(2,1)S(1)} %collective-permute-done.1), channel_id=1, source_target_pairs={{0,8},{4,12},{8,0},{12,4},{16,24},{20,28},{24,16},{28,20},{1,9},{5... | collective-permute-start | bytes 196616 | tf_op jit(solution)/shard_map/ppermute | solution.py:217
  13.0 9.2 %collective-permute-start.6 = (bf16[128,1024]{1,0:T(8,128)(2,1)S(1)}, bf16[128,1024]{1,0:T(8,128)(2,1)S(1)}, u32[]{:S(2)}, u32[]{:S(2)}) collective-permute-start(bf16[128,1024]{1,0:T(8,128)(2,1)S(1)} %constant_dynamic-update-slice_fusion.refs_4_), channel_id=1, source_target_pairs={{0,3},{1,2},{2,1},{3,0},{4,7},{5,6},{6,5},{7,4},{8,11},{9,10},{10,... | collective-permute-start | bytes 786440 | tf_op jit(solution)/shard_map/ppermute | solution.py:217
  15.8 9.1 %collective-permute-start.5 = (bf16[128,1024]{1,0:T(8,128)(2,1)S(1)}, bf16[128,1024]{1,0:T(8,128)(2,1)S(1)}, u32[]{:S(2)}, u32[]{:S(2)}) collective-permute-start(bf16[128,1024]{1,0:T(8,128)(2,1)S(1)} %constant_dynamic-update-slice_fusion.refs_4_), channel_id=1, source_target_pairs={{0,2},{1,3},{2,0},{3,1},{4,6},{5,7},{6,4},{7,5},{8,10},{9,11},{10,... | collective-permute-start | bytes 786440 | tf_op jit(solution)/shard_map/ppermute | solution.py:217
  16.3 8.9 %collective-permute-start.4 = (bf16[128,1024]{1,0:T(8,128)(2,1)S(1)}, bf16[128,1024]{1,0:T(8,128)(2,1)S(1)}, u32[]{:S(2)}, u32[]{:S(2)}) collective-permute-start(bf16[128,1024]{1,0:T(8,128)(2,1)S(1)} %constant_dynamic-update-slice_fusion.refs_4_), channel_id=1, source_target_pairs={{0,1},{1,0},{2,3},{3,2},{4,5},{5,4},{6,7},{7,6},{8,9},{9,8},{10,11... | collective-permute-start | bytes 786440 | tf_op jit(solution)/shard_map/ppermute | solution.py:217
  16.6 3.6 %collective-permute-start.7 = (s32[8,128]{1,0:T(8,128)S(1)}, s32[8,128]{1,0:T(8,128)S(1)}, u32[]{:S(2)}, u32[]{:S(2)}) collective-permute-start(s32[8,128]{1,0:T(8,128)S(1)} %pad_add_fusion.1), channel_id=1, source_target_pairs={{0,8},{4,12},{8,0},{12,4},{16,24},{20,28},{24,16},{28,20},{1,9},{5... | collective-permute-start | bytes 12296 | tf_op jit(solution)/shard_map/ppermute | solution.py:217
  25.2 2.7 %collective-permute-start.9 = (bf16[128,1024]{1,0:T(8,128)(2,1)S(1)}, bf16[128,1024]{1,0:T(8,128)(2,1)S(1)}, u32[]{:S(2)}, u32[]{:S(2)}) collective-permute-start(bf16[128,1024]{1,0:T(8,128)(2,1)S(1)} %constant_dynamic-update-slice_fusion.refs_4_), channel_id=1, source_target_pairs={{0,4},{4,0},{8,12},{12,8},{16,20},{20,16},{24,28},{28,24},{1,5},{5... | collective-permute-start | bytes 786440 | tf_op jit(solution)/shard_map/ppermute | solution.py:217
  25.2 2.7 %collective-permute-start.10 = (bf16[128,1024]{1,0:T(8,128)(2,1)S(1)}, bf16[128,1024]{1,0:T(8,128)(2,1)S(1)}, u32[]{:S(2)}, u32[]{:S(2)}) collective-permute-start(bf16[128,1024]{1,0:T(8,128)(2,1)S(1)} %collective-permute-done.4.refs_6_), channel_id=1, source_target_pairs={{0,4},{4,0},{8,12},{12,8},{16,20},{20,16},{24,28},{28,24},{1,5},{5... | collective-permute-start | bytes 786440 | tf_op jit(solution)/shard_map/ppermute | solution.py:217
  25.7 2.2 %collective-permute-start.11 = (bf16[128,1024]{1,0:T(8,128)(2,1)S(1)}, bf16[128,1024]{1,0:T(8,128)(2,1)S(1)}, u32[]{:S(2)}, u32[]{:S(2)}) collective-permute-start(bf16[128,1024]{1,0:T(8,128)(2,1)S(1)} %collective-permute-done.5.refs_8_), channel_id=1, source_target_pairs={{0,4},{4,0},{8,12},{12,8},{16,20},{20,16},{24,28},{28,24},{1,5},{5... | collective-permute-start | bytes 786440 | tf_op jit(solution)/shard_map/ppermute | solution.py:217
  25.7 2.2 %collective-permute-start.12 = (bf16[128,1024]{1,0:T(8,128)(2,1)S(1)}, bf16[128,1024]{1,0:T(8,128)(2,1)S(1)}, u32[]{:S(2)}, u32[]{:S(2)}) collective-permute-start(bf16[128,1024]{1,0:T(8,128)(2,1)S(1)} %collective-permute-done.6.refs_10_), channel_id=1, source_target_pairs={{0,4},{4,0},{8,12},{12,8},{16,20},{20,16},{24,28},{28,24},{1,5},{5... | collective-permute-start | bytes 786440 | tf_op jit(solution)/shard_map/ppermute | solution.py:217
  26.2 1.7 %copy-start = (s32[1024]{0:T(1024)S(1)}, s32[1024]{0:T(1024)}, u32[]{:S(2)}) copy-start(s32[1024]{0:T(1024)} %param.5) | copy-start | bytes 12292
  26.2 1.6 %collective-permute-start.8 = (s32[16,128]{1,0:T(8,128)S(1)}, s32[16,128]{1,0:T(8,128)S(1)}, u32[]{:S(2)}, u32[]{:S(2)}) collective-permute-start(s32[16,128]{1,0:T(8,128)S(1)} %pad_add_fusion.refs_2_), channel_id=1, source_target_pairs={{0,4},{4,0},{8,12},{12,8},{16,20},{20,16},{24,28},{28,24},{1,5},{5... | collective-permute-start | bytes 24584 | tf_op jit(solution)/shard_map/ppermute | solution.py:217

commit v8 on v7

--- a/solution.py
+++ b/solution.py
@@ -35,7 +35,7 @@
     me = place_ref[0]
     my_col = place_ref[1]
     pair = lane_block // 128
-    row_chunk = min(512, total)
+    row_chunk = min(1024, total)
 
     for piece, slots in zip(pieces, layout):
         for spot, slot in enumerate(slots):
@@ -230,12 +230,12 @@
         order.extend([d ^ bit for d in order])
         return jnp.concatenate([ids, swap(ids, "row", 2 * bit)], axis=0)
 
-    line = {0: embed}
-    for bit in bits:
-        line.update({d ^ bit: swap(line[d], "row", 2 * bit) for d in line})
+    line = [swap(embed, "row", 2 * d) for d in range(1, levels)]
+    mine = {0: embed}
+    mine.update({p: swap(embed, "col", p) for p in range(1, cols)})
     ids = spread(positives.T)
-    line, ids = lax.optimization_barrier((line, ids))
-    tall = join([line[d] for d in range(levels)])
+    line, mine, ids = lax.optimization_barrier((line, mine, ids))
+    tall = join(line)
 
     plane = {0: tall}
     plane.update({p: swap(tall, "col", p) for p in range(1, cols)})
@@ -244,13 +244,13 @@
     plane, ids = lax.optimization_barrier((plane, ids))
 
     ids = (ids, swap(ids, "row", 1))
-
-    pieces = []
-    layout = []
+    near = join([mine[p] for p in range(cols)])
+    pieces = [near, swap(near, "row", 1)]
+    layout = [[c * cols + p for p in range(cols)] for c in range(2)]
     for p in range(cols):
         for c, part in enumerate((plane[p], swap(plane[p], "row", 1))):
             pieces.append(part)
-            layout.append([(d * 2 + c) * cols + p for d in range(levels)])
+            layout.append([(d * 2 + c) * cols + p for d in range(1, levels)])
 
     place = jnp.stack([lax.axis_index(axes) * shard, lax.axis_index("col") * shard])
     vmem = pl.BlockSpec(memory_space=pltpu.VMEM)

time: 37.5 us -> 37.4 us (level)
  starting transfers between devices: 12.1 us -> 17.4 us
  waiting for transfers between devices: 14.2 us -> 10.1 us
  local copies, waits for them, and re-layouts: 0.87 us -> 0.05 us
  Pallas kernels: 9.43 us -> 8.81 us
    ppermute x13 -> x17, starting transfers between devices: 12.1 us -> 17.4 us  [swap(): return lax.ppermute(array, axis, [(i, i ^ mask) for i in range(size)])]
    ppermute x13 -> x17, waiting for transfers between devices: 14.2 us -> 10.1 us  [swap(): return lax.ppermute(array, axis, [(i, i ^ mask) for i in range(size)])]
    unnamed x5 -> x9, local copies, waits for them, and re-layouts: 0.86 us -> 0.04 us
    pallas_call x1, Pallas kernels: 9.43 us -> 8.81 us  [body(): pl.pallas_call(functools.partial(kernel, cols, order, shard, pos_count, l...]
  transfers between devices with their start and end apart: 13 -> 17, of which waited for: 8 -> 11; matrix products, arithmetic and copies ran while one was open for 2% -> 2% of each run, Pallas kernels for 0% -> 0%
where the time goes in v8:
time: 37.4 us; the launch traced here: 37.2 us
  starting transfers between devices  17.4 us (47%)
  waiting for transfers between devices  10.1 us (27%)
  Pallas kernels  8.81 us (24%)
  other arithmetic  0.77 us (2%)
    ppermute x17, starting transfers between devices, swap(): return lax.ppermute(array, axis, [(i, i ^ mask) for i in range(size)])  17.4 us
    ppermute x17, waiting for transfers between devices, swap(): return lax.ppermute(array, axis, [(i, i ^ mask) for i in range(size)])  10.1 us
    pallas_call x1, Pallas kernels, body(): pl.pallas_call(functools.partial(kernel, cols, order, shard, pos_count, l...  8.81 us
  transfers between devices with their start and end apart: 17, of which 11 were waited for; matrix products, arithmetic and copies ran while one was open for 2% of the time, Pallas kernels for 0%

profile of v8, /device:TPU:0, one launch (start us, length us, event | category | flops | bytes accessed | tf_op | source)
XLA Modules:
  0.0 37.2 jit_solution(13738450538677328809)
XLA Ops:
  0.0 3.0 %collective-permute-start = (bf16[32,1024]{1,0:T(8,128)(2,1)}, bf16[32,1024]{1,0:T(8,128)(2,1)S(1)}, u32[]{:S(2)}, u32[]{:S(2)}) collective-permute-start(bf16[32,1024]{1,0:T(8,128)(2,1)} %param.3), channel_id=1, source_target_pairs={{0,8},{4,12},{8,0},{12,4},{16,24},{20,28},{24,16},{28,20},{1,9},{5... | collective-permute-start | bytes 196616 | tf_op jit(solution)/shard_map/ppermute | solution.py:217
  3.0 2.6 %collective-permute-start.6 = (s32[4,128]{1,0:T(4,128)}, s32[4,128]{1,0:T(4,128)S(1)}, u32[]{:S(2)}, u32[]{:S(2)}) collective-permute-start(s32[4,128]{1,0:T(4,128)} %bitcast.5), channel_id=1, source_target_pairs={{0,16},{4,20},{8,24},{12,28},{16,0},{20,4},{24,8},{28,12},{1,17},{... | collective-permute-start | bytes 6152 | tf_op jit(solution)/shard_map/ppermute | solution.py:217
  5.6 0.3 collective-permute-start.1
  6.0 2.5 %collective-permute-start.2 = (bf16[32,1024]{1,0:T(8,128)(2,1)}, bf16[32,1024]{1,0:T(8,128)(2,1)S(1)}, u32[]{:S(2)}, u32[]{:S(2)}) collective-permute-start(bf16[32,1024]{1,0:T(8,128)(2,1)} %param.3), channel_id=1, source_target_pairs={{0,24},{4,28},{8,16},{12,20},{16,8},{20,12},{24,0},{28,4},{1,25},{... | collective-permute-start | bytes 196616 | tf_op jit(solution)/shard_map/ppermute | solution.py:217
  8.4 1.5 %collective-permute-start.3 = (bf16[32,1024]{1,0:T(8,128)(2,1)}, bf16[32,1024]{1,0:T(8,128)(2,1)S(1)}, u32[]{:S(2)}, u32[]{:S(2)}) collective-permute-start(bf16[32,1024]{1,0:T(8,128)(2,1)} %param.3), channel_id=1, source_target_pairs={{0,1},{1,0},{2,3},{3,2},{4,5},{5,4},{6,7},{7,6},{8,9},{9,8},{10,11... | collective-permute-start | bytes 196616 | tf_op jit(solution)/shard_map/ppermute | solution.py:217
  9.9 0.0 collective-permute-done.6
  9.9 1.5 %collective-permute-start.4 = (bf16[32,1024]{1,0:T(8,128)(2,1)}, bf16[32,1024]{1,0:T(8,128)(2,1)S(1)}, u32[]{:S(2)}, u32[]{:S(2)}) collective-permute-start(bf16[32,1024]{1,0:T(8,128)(2,1)} %param.3), channel_id=1, source_target_pairs={{0,2},{1,3},{2,0},{3,1},{4,6},{5,7},{6,4},{7,5},{8,10},{9,11},{10,... | collective-permute-start | bytes 196616 | tf_op jit(solution)/shard_map/ppermute | solution.py:217
  11.4 0.0 collective-permute-done
  11.4 0.5 %collective-permute-start.5 = (bf16[32,1024]{1,0:T(8,128)(2,1)}, bf16[32,1024]{1,0:T(8,128)(2,1)S(1)}, u32[]{:S(2)}, u32[]{:S(2)}) collective-permute-start(bf16[32,1024]{1,0:T(8,128)(2,1)} %param.3), channel_id=1, source_target_pairs={{0,3},{1,2},{2,1},{3,0},{4,7},{5,6},{6,5},{7,4},{8,11},{9,10},{10,... | collective-permute-start | bytes 196616 | tf_op jit(solution)/shard_map/ppermute | solution.py:217
  11.9 0.7 %pad_add_fusion.1 = s32[8,128]{1,0:T(8,128)S(1)} fusion(s32[4,128]{1,0:T(4,128)S(1)} %collective-permute-done.6, s32[4,128]{1,0:T(4,128)} %bitcast.6), kind=kLoop, calls=%fused_computation.8 | loop fusion | flops 1024 | bytes 8192 | tf_op jit(solution)/shard_map/concatenate | solution.py:231
  12.6 0.5 %collective-permute-done.1 = bf16[32,1024]{1,0:T(8,128)(2,1)S(1)} collective-permute-done((bf16[32,1024]{1,0:T(8,128)(2,1)}, bf16[32,1024]{1,0:T(8,128)(2,1)S(1)}, u32[]{:S(2)}, u32[]{:S(2)}) %collective-permute-start.1) | collective-permute-done | bytes 65568 | tf_op jit(solution)/shard_map/ppermute | solution.py:217
  13.1 0.0 collective-permute-done.2
  13.1 0.3 collective-permute-done.3
  13.5 1.4 %collective-permute-done.4 = bf16[32,1024]{1,0:T(8,128)(2,1)S(1)} collective-permute-done((bf16[32,1024]{1,0:T(8,128)(2,1)}, bf16[32,1024]{1,0:T(8,128)(2,1)S(1)}, u32[]{:S(2)}, u32[]{:S(2)}) %collective-permute-start.4) | collective-permute-done | bytes 65568 | tf_op jit(solution)/shard_map/ppermute | solution.py:217
  14.9 1.9 %collective-permute-done.5 = bf16[32,1024]{1,0:T(8,128)(2,1)S(1)} collective-permute-done((bf16[32,1024]{1,0:T(8,128)(2,1)}, bf16[32,1024]{1,0:T(8,128)(2,1)S(1)}, u32[]{:S(2)}, u32[]{:S(2)}) %collective-permute-start.5) | collective-permute-done | bytes 65568 | tf_op jit(solution)/shard_map/ppermute | solution.py:217
  16.8 0.0 copy-start.1
  16.9 0.7 %collective-permute-start.7 = (bf16[96,1024]{1,0:T(8,128)(2,1)S(1)}, bf16[96,1024]{1,0:T(8,128)(2,1)S(1)}, u32[]{:S(2)}, u32[]{:S(2)}) collective-permute-start(bf16[96,1024]{1,0:T(8,128)(2,1)S(1)} %constant_dynamic-update-slice_fusion.refs_6_), channel_id=1, source_target_pairs={{0,1},{1,0},{2,3},{3,2},{4,5},{5,4},{6,7},{7,6},{8,9},{9,8},{10,11... | collective-permute-start | bytes 589832 | tf_op jit(solution)/shard_map/ppermute | solution.py:217
  17.6 0.4 %collective-permute-start.8 = (bf16[96,1024]{1,0:T(8,128)(2,1)S(1)}, bf16[96,1024]{1,0:T(8,128)(2,1)S(1)}, u32[]{:S(2)}, u32[]{:S(2)}) collective-permute-start(bf16[96,1024]{1,0:T(8,128)(2,1)S(1)} %constant_dynamic-update-slice_fusion.refs_6_), channel_id=1, source_target_pairs={{0,2},{1,3},{2,0},{3,1},{4,6},{5,7},{6,4},{7,5},{8,10},{9,11},{10,... | collective-permute-start | bytes 589832 | tf_op jit(solution)/shard_map/ppermute | solution.py:217
  18.0 2.4 %collective-permute-start.9 = (bf16[96,1024]{1,0:T(8,128)(2,1)S(1)}, bf16[96,1024]{1,0:T(8,128)(2,1)S(1)}, u32[]{:S(2)}, u32[]{:S(2)}) collective-permute-start(bf16[96,1024]{1,0:T(8,128)(2,1)S(1)} %constant_dynamic-update-slice_fusion.refs_6_), channel_id=1, source_target_pairs={{0,3},{1,2},{2,1},{3,0},{4,7},{5,6},{6,5},{7,4},{8,11},{9,10},{10,... | collective-permute-start | bytes 589832 | tf_op jit(solution)/shard_map/ppermute | solution.py:217
  20.4 0.7 %collective-permute-start.10 = (s32[8,128]{1,0:T(8,128)S(1)}, s32[8,128]{1,0:T(8,128)S(1)}, u32[]{:S(2)}, u32[]{:S(2)}) collective-permute-start(s32[8,128]{1,0:T(8,128)S(1)} %pad_add_fusion.1), channel_id=1, source_target_pairs={{0,8},{4,12},{8,0},{12,4},{16,24},{20,28},{24,16},{28,20},{1,9},{5... | collective-permute-start | bytes 12296 | tf_op jit(solution)/shard_map/ppermute | solution.py:217
  21.1 0.0 copy-done.1
  21.2 0.1 collective-permute-start.12
  21.2 2.8 %collective-permute-done.10 = s32[8,128]{1,0:T(8,128)S(1)} collective-permute-done((s32[8,128]{1,0:T(8,128)S(1)}, s32[8,128]{1,0:T(8,128)S(1)}, u32[]{:S(2)}, u32[]{:S(2)}) %collective-permute-start.10) | collective-permute-done | bytes 4128 | tf_op jit(solution)/shard_map/ppermute | solution.py:217
  24.0 0.0 collective-permute-done.7.refs_8_
  24.0 1.8 %collective-permute-done.8.refs_10_ = bf16[96,1024]{1,0:T(8,128)(2,1)S(1)} collective-permute-done((bf16[96,1024]{1,0:T(8,128)(2,1)S(1)}, bf16[96,1024]{1,0:T(8,128)(2,1)S(1)}, u32[]{:S(2)}, u32[]{:S(2)}) %collective-permute-start.8) | collective-permute-done | bytes 196640 | tf_op jit(solution)/shard_map/ppermute | solution.py:217
  25.8 0.0 collective-permute-done.9.refs_12_
  25.8 0.0 collective-permute-start.11
  25.8 0.5 %collective-permute-start.13 = (bf16[96,1024]{1,0:T(8,128)(2,1)S(1)}, bf16[96,1024]{1,0:T(8,128)(2,1)S(1)}, u32[]{:S(2)}, u32[]{:S(2)}) collective-permute-start(bf16[96,1024]{1,0:T(8,128)(2,1)S(1)} %constant_dynamic-update-slice_fusion.refs_6_), channel_id=1, source_target_pairs={{0,4},{4,0},{8,12},{12,8},{16,20},{20,16},{24,28},{28,24},{1,5},{5... | collective-permute-start | bytes 589832 | tf_op jit(solution)/shard_map/ppermute | solution.py:217
  26.3 0.0 collective-permute-start.14
  26.3 0.5 %collective-permute-start.15 = (bf16[96,1024]{1,0:T(8,128)(2,1)S(1)}, bf16[96,1024]{1,0:T(8,128)(2,1)S(1)}, u32[]{:S(2)}, u32[]{:S(2)}) collective-permute-start(bf16[96,1024]{1,0:T(8,128)(2,1)S(1)} %collective-permute-done.8.refs_10_), channel_id=1, source_target_pairs={{0,4},{4,0},{8,12},{12,8},{16,20},{20,16},{24,28},{28,24},{1,5},{5... | collective-permute-start | bytes 589832 | tf_op jit(solution)/shard_map/ppermute | solution.py:217
  26.8 0.2 collective-permute-done.11.refs_3_
  27.0 0.2 collective-permute-start.16
  27.1 0.0 copy-start
  27.2 0.1 pad_add_fusion.2.refs_0_
  27.2 0.0 collective-permute-done.12.refs_5_
  27.2 0.2 collective-permute-done.13.refs_7_
  27.4 0.4 collective-permute-done.14.refs_9_
  27.8 0.3 collective-permute-done.15.refs_11_
  28.0 0.4 %collective-permute-done.16.refs_13_ = bf16[96,1024]{1,0:T(8,128)(2,1)S(1)} collective-permute-done((bf16[96,1024]{1,0:T(8,128)(2,1)S(1)}, bf16[96,1024]{1,0:T(8,128)(2,1)S(1)}, u32[]{:S(2)}, u32[]{:S(2)}) %collective-permute-start.16) | collective-permute-done | bytes 196640 | tf_op jit(solution)/shard_map/ppermute | solution.py:217
  28.4 0.0 copy-done
  28.4 8.8 %shard_map.37 = f32[32,1024]{1,0:T(8,128)} custom-call(s32[2]{0:T(128)S(1)} %pad_add_fusion.2.refs_0_, s32[8,128]{1,0:T(8,128)S(1)} %bitcast.4, s32[16,128]{1,0:T(8,128)S(1)} %pad_add_fusion.refs_2_, s32[16,128]{1,0:T(8,128)S(1)} %collective-permute-done.11.refs_3_, bf16[128,1024]{1,0:T(8,128)(2,1)S(1)} %constant_dynamic-update-slice_fusion.3.refs_4_, ...), custom_call_target="tpu_custom_call" | custom-call | flops 2147483648 | bytes 2097152 | tf_op jit(solution)/shard_map/pallas_call | solution.py:257
  (8 shorter events, 0.0 us)
Async XLA Ops:
  0.0 11.4 %collective-permute-start = (bf16[32,1024]{1,0:T(8,128)(2,1)}, bf16[32,1024]{1,0:T(8,128)(2,1)S(1)}, u32[]{:S(2)}, u32[]{:S(2)}) collective-permute-start(bf16[32,1024]{1,0:T(8,128)(2,1)} %param.3), channel_id=1, source_target_pairs={{0,8},{4,12},{8,0},{12,4},{16,24},{20,28},{24,16},{28,20},{1,9},{5... | collective-permute-start | bytes 196616 | tf_op jit(solution)/shard_map/ppermute | solution.py:217
  3.0 6.9 %collective-permute-start.6 = (s32[4,128]{1,0:T(4,128)}, s32[4,128]{1,0:T(4,128)S(1)}, u32[]{:S(2)}, u32[]{:S(2)}) collective-permute-start(s32[4,128]{1,0:T(4,128)} %bitcast.5), channel_id=1, source_target_pairs={{0,16},{4,20},{8,24},{12,28},{16,0},{20,4},{24,8},{28,12},{1,17},{... | collective-permute-start | bytes 6152 | tf_op jit(solution)/shard_map/ppermute | solution.py:217
  5.6 7.5 %collective-permute-start.1 = (bf16[32,1024]{1,0:T(8,128)(2,1)}, bf16[32,1024]{1,0:T(8,128)(2,1)S(1)}, u32[]{:S(2)}, u32[]{:S(2)}) collective-permute-start(bf16[32,1024]{1,0:T(8,128)(2,1)} %param.3), channel_id=1, source_target_pairs={{0,16},{4,20},{8,24},{12,28},{16,0},{20,4},{24,8},{28,12},{1,17},{... | collective-permute-start | bytes 196616 | tf_op jit(solution)/shard_map/ppermute | solution.py:217
  6.0 7.2 %collective-permute-start.2 = (bf16[32,1024]{1,0:T(8,128)(2,1)}, bf16[32,1024]{1,0:T(8,128)(2,1)S(1)}, u32[]{:S(2)}, u32[]{:S(2)}) collective-permute-start(bf16[32,1024]{1,0:T(8,128)(2,1)} %param.3), channel_id=1, source_target_pairs={{0,24},{4,28},{8,16},{12,20},{16,8},{20,12},{24,0},{28,4},{1,25},{... | collective-permute-start | bytes 196616 | tf_op jit(solution)/shard_map/ppermute | solution.py:217
  8.4 5.0 %collective-permute-start.3 = (bf16[32,1024]{1,0:T(8,128)(2,1)}, bf16[32,1024]{1,0:T(8,128)(2,1)S(1)}, u32[]{:S(2)}, u32[]{:S(2)}) collective-permute-start(bf16[32,1024]{1,0:T(8,128)(2,1)} %param.3), channel_id=1, source_target_pairs={{0,1},{1,0},{2,3},{3,2},{4,5},{5,4},{6,7},{7,6},{8,9},{9,8},{10,11... | collective-permute-start | bytes 196616 | tf_op jit(solution)/shard_map/ppermute | solution.py:217
  9.9 5.0 %collective-permute-start.4 = (bf16[32,1024]{1,0:T(8,128)(2,1)}, bf16[32,1024]{1,0:T(8,128)(2,1)S(1)}, u32[]{:S(2)}, u32[]{:S(2)}) collective-permute-start(bf16[32,1024]{1,0:T(8,128)(2,1)} %param.3), channel_id=1, source_target_pairs={{0,2},{1,3},{2,0},{3,1},{4,6},{5,7},{6,4},{7,5},{8,10},{9,11},{10,... | collective-permute-start | bytes 196616 | tf_op jit(solution)/shard_map/ppermute | solution.py:217
  11.4 5.4 %collective-permute-start.5 = (bf16[32,1024]{1,0:T(8,128)(2,1)}, bf16[32,1024]{1,0:T(8,128)(2,1)S(1)}, u32[]{:S(2)}, u32[]{:S(2)}) collective-permute-start(bf16[32,1024]{1,0:T(8,128)(2,1)} %param.3), channel_id=1, source_target_pairs={{0,3},{1,2},{2,1},{3,0},{4,7},{5,6},{6,5},{7,4},{8,11},{9,10},{10,... | collective-permute-start | bytes 196616 | tf_op jit(solution)/shard_map/ppermute | solution.py:217
  16.8 4.3 %copy-start.1 = (bf16[32,1024]{1,0:T(8,128)(2,1)S(1)}, bf16[32,1024]{1,0:T(8,128)(2,1)}, u32[]{:S(2)}) copy-start(bf16[32,1024]{1,0:T(8,128)(2,1)} %param.3) | copy-start | bytes 196612
  16.9 7.2 %collective-permute-start.7 = (bf16[96,1024]{1,0:T(8,128)(2,1)S(1)}, bf16[96,1024]{1,0:T(8,128)(2,1)S(1)}, u32[]{:S(2)}, u32[]{:S(2)}) collective-permute-start(bf16[96,1024]{1,0:T(8,128)(2,1)S(1)} %constant_dynamic-update-slice_fusion.refs_6_), channel_id=1, source_target_pairs={{0,1},{1,0},{2,3},{3,2},{4,5},{5,4},{6,7},{7,6},{8,9},{9,8},{10,11... | collective-permute-start | bytes 589832 | tf_op jit(solution)/shard_map/ppermute | solution.py:217
  17.6 8.2 %collective-permute-start.8 = (bf16[96,1024]{1,0:T(8,128)(2,1)S(1)}, bf16[96,1024]{1,0:T(8,128)(2,1)S(1)}, u32[]{:S(2)}, u32[]{:S(2)}) collective-permute-start(bf16[96,1024]{1,0:T(8,128)(2,1)S(1)} %constant_dynamic-update-slice_fusion.refs_6_), channel_id=1, source_target_pairs={{0,2},{1,3},{2,0},{3,1},{4,6},{5,7},{6,4},{7,5},{8,10},{9,11},{10,... | collective-permute-start | bytes 589832 | tf_op jit(solution)/shard_map/ppermute | solution.py:217
  18.0 7.8 %collective-permute-start.9 = (bf16[96,1024]{1,0:T(8,128)(2,1)S(1)}, bf16[96,1024]{1,0:T(8,128)(2,1)S(1)}, u32[]{:S(2)}, u32[]{:S(2)}) collective-permute-start(bf16[96,1024]{1,0:T(8,128)(2,1)S(1)} %constant_dynamic-update-slice_fusion.refs_6_), channel_id=1, source_target_pairs={{0,3},{1,2},{2,1},{3,0},{4,7},{5,6},{6,5},{7,4},{8,11},{9,10},{10,... | collective-permute-start | bytes 589832 | tf_op jit(solution)/shard_map/ppermute | solution.py:217
  20.4 3.6 %collective-permute-start.10 = (s32[8,128]{1,0:T(8,128)S(1)}, s32[8,128]{1,0:T(8,128)S(1)}, u32[]{:S(2)}, u32[]{:S(2)}) collective-permute-start(s32[8,128]{1,0:T(8,128)S(1)} %pad_add_fusion.1), channel_id=1, source_target_pairs={{0,8},{4,12},{8,0},{12,4},{16,24},{20,28},{24,16},{28,20},{1,9},{5... | collective-permute-start | bytes 12296 | tf_op jit(solution)/shard_map/ppermute | solution.py:217
  21.2 6.1 %collective-permute-start.12 = (bf16[128,1024]{1,0:T(8,128)(2,1)S(1)}, bf16[128,1024]{1,0:T(8,128)(2,1)S(1)}, u32[]{:S(2)}, u32[]{:S(2)}) collective-permute-start(bf16[128,1024]{1,0:T(8,128)(2,1)S(1)} %constant_dynamic-update-slice_fusion.3.refs_4_), channel_id=1, source_target_pairs={{0,4},{4,0},{8,12},{12,8},{16,20},{20,16},{24,28},{28,24},{1,5},{5... | collective-permute-start | bytes 786440 | tf_op jit(solution)/shard_map/ppermute | solution.py:217
  25.8 1.2 %collective-permute-start.11 = (s32[16,128]{1,0:T(8,128)S(1)}, s32[16,128]{1,0:T(8,128)S(1)}, u32[]{:S(2)}, u32[]{:S(2)}) collective-permute-start(s32[16,128]{1,0:T(8,128)S(1)} %pad_add_fusion.refs_2_), channel_id=1, source_target_pairs={{0,4},{4,0},{8,12},{12,8},{16,20},{20,16},{24,28},{28,24},{1,5},{5... | collective-permute-start | bytes 24584 | tf_op jit(solution)/shard_map/ppermute | solution.py:217
  25.8 1.6 %collective-permute-start.13 = (bf16[96,1024]{1,0:T(8,128)(2,1)S(1)}, bf16[96,1024]{1,0:T(8,128)(2,1)S(1)}, u32[]{:S(2)}, u32[]{:S(2)}) collective-permute-start(bf16[96,1024]{1,0:T(8,128)(2,1)S(1)} %constant_dynamic-update-slice_fusion.refs_6_), channel_id=1, source_target_pairs={{0,4},{4,0},{8,12},{12,8},{16,20},{20,16},{24,28},{28,24},{1,5},{5... | collective-permute-start | bytes 589832 | tf_op jit(solution)/shard_map/ppermute | solution.py:217
  26.3 1.4 %collective-permute-start.14 = (bf16[96,1024]{1,0:T(8,128)(2,1)S(1)}, bf16[96,1024]{1,0:T(8,128)(2,1)S(1)}, u32[]{:S(2)}, u32[]{:S(2)}) collective-permute-start(bf16[96,1024]{1,0:T(8,128)(2,1)S(1)} %collective-permute-done.7.refs_8_), channel_id=1, source_target_pairs={{0,4},{4,0},{8,12},{12,8},{16,20},{20,16},{24,28},{28,24},{1,5},{5... | collective-permute-start | bytes 589832 | tf_op jit(solution)/shard_map/ppermute | solution.py:217
  26.3 1.7 %collective-permute-start.15 = (bf16[96,1024]{1,0:T(8,128)(2,1)S(1)}, bf16[96,1024]{1,0:T(8,128)(2,1)S(1)}, u32[]{:S(2)}, u32[]{:S(2)}) collective-permute-start(bf16[96,1024]{1,0:T(8,128)(2,1)S(1)} %collective-permute-done.8.refs_10_), channel_id=1, source_target_pairs={{0,4},{4,0},{8,12},{12,8},{16,20},{20,16},{24,28},{28,24},{1,5},{5... | collective-permute-start | bytes 589832 | tf_op jit(solution)/shard_map/ppermute | solution.py:217
  27.0 1.4 %collective-permute-start.16 = (bf16[96,1024]{1,0:T(8,128)(2,1)S(1)}, bf16[96,1024]{1,0:T(8,128)(2,1)S(1)}, u32[]{:S(2)}, u32[]{:S(2)}) collective-permute-start(bf16[96,1024]{1,0:T(8,128)(2,1)S(1)} %collective-permute-done.9.refs_12_), channel_id=1, source_target_pairs={{0,4},{4,0},{8,12},{12,8},{16,20},{20,16},{24,28},{28,24},{1,5},{5... | collective-permute-start | bytes 589832 | tf_op jit(solution)/shard_map/ppermute | solution.py:217
  27.1 1.3 %copy-start = (s32[1024]{0:T(1024)S(1)}, s32[1024]{0:T(1024)}, u32[]{:S(2)}) copy-start(s32[1024]{0:T(1024)} %param.5) | copy-start | bytes 12292

commit v9 on v8

--- a/solution.py
+++ b/solution.py
@@ -10,10 +10,6 @@
 logistic_sharpness = 0.02
 half_scale = 0.5 / logistic_sharpness
 masked = -1e30
-
-
-def fold_rows(values):
-    return jnp.sum(values.reshape(values.shape[0] // 8, 8, values.shape[1]), axis=0)
 
 
 def lookup(table_ref, ids):
@@ -27,6 +23,7 @@
 
 
 def kernel(cols, order, shard, pos_count, lane_block, layout, *refs):
+    levels = len(order)
     place_ref, table_ref = refs[:2]
     ids_refs = refs[2:4]
     pieces = refs[4 : 4 + len(layout)]
@@ -42,11 +39,13 @@
             embed_ref[slot * shard : (slot + 1) * shard, :] = piece[spot * shard : (spot + 1) * shard, :]
 
     group = cols * shard
-    for line in range(2 * len(order)):
+    for line in range(2 * levels):
         for begin in range(0, group, 128):
-            level = order.index(line // 2) * pos_count
-            ids = ids_refs[line % 2][level : level + pos_count, begin : begin + 128]
-            ids = jnp.concatenate([ids, ids], axis=0)
+            ids_ref = ids_refs[line % 2]
+            size = ids_ref.shape[0] // levels
+            at = order.index(line // 2) * size
+            ids = ids_ref[at : at + size, begin : begin + 128]
+            ids = jnp.concatenate([ids] * (8 // size), axis=0)
             found = lookup(table_ref, ids) ^ me
             lane = lax.broadcasted_iota(jnp.int32, found.shape, 1)
             found = jnp.take_along_axis(found, lane ^ (my_col % 128), axis=1)
@@ -91,12 +90,18 @@
         for half in range(pair):
             for part in range(row_chunk // 32):
                 scores = score_ref[buffer, pl.ds(row + part * 32, 32), half * 128 : (half + 1) * 128]
+                scores = scores.reshape(4, 8, 128)
                 for m in range(pos_count):
-                    at = (half * pos_count + m) * 2
-                    bent = jnp.tanh(scores - pos[half][m])
-                    sums[at] = sums[at] + fold_rows(bent)
-                    sums[at + 1] = sums[at + 1] + fold_rows(bent * bent)
+                    at = half * pos_count + m
+                    bent = jnp.tanh(scores - pos[at][None])
+                    sums[2 * at] = sums[2 * at] + jnp.sum(bent, axis=0)
+                    sums[2 * at + 1] = sums[2 * at + 1] + jnp.sum(bent * bent, axis=0)
         return tuple(sums)
+
+    def over_chunks(step, have):
+        if chunks == 1:
+            return step(0, have)
+        return lax.fori_loop(0, chunks, step, have)
 
     chunks = total // row_chunk
     nothing = (jnp.zeros((8, 128), jnp.float32),) * (pair * pos_count)
@@ -110,51 +115,26 @@
         sub = lax.broadcasted_iota(jnp.int32, (8, 128), 0)
         pos = []
         for half in range(pair):
-            targets = target_ref[:, pl.ds(pl.multiple_of(start + half * 128, 128), 128)]
-            parts = picked[half * pos_count : (half + 1) * pos_count]
-            pos.append(
-                tuple(
-                    jnp.sum(
-                        jnp.where(sub == (targets[m : m + 1, :] & 7), parts[m], 0.0),
-                        axis=0,
-                        keepdims=True,
-                    )
-                    for m in range(pos_count)
-                )
-            )
+            lanes = pl.ds(pl.multiple_of(start + half * 128, 128), 128)
+            own_ref[:, lanes] = score_ref[buffer, 0:shard, half * 128 : (half + 1) * 128]
+            for m in range(pos_count):
+                hit = sub == (target_ref[m : m + 1, lanes] & 7)
+                spot = jnp.where(hit, picked[half * pos_count + m], 0.0)
+                spot = jnp.sum(spot, axis=0, keepdims=True)
+                stat_ref[m : m + 1, lanes] = spot
+                pos.append(jnp.broadcast_to(spot, (8, 128)))
         return tuple(pos)
 
-    def finish(start, buffer, pos, sums):
-        factor = 1.0 / (pos_count * total)
+    def finish(start, sums):
         for half in range(pair):
             lanes = pl.ds(pl.multiple_of(start + half * 128, 128), 128)
-            spot = pos[half]
-            ranks = []
-            slopes = []
             for m in range(pos_count):
                 at = (half * pos_count + m) * 2
-                ranks.append(0.5 + 0.5 * (total + jnp.sum(sums[at], axis=0, keepdims=True)))
-                slopes.append(0.25 * (total - jnp.sum(sums[at + 1], axis=0, keepdims=True)))
-            own_ref[:, lanes] = score_ref[buffer, 0:shard, half * 128 : (half + 1) * 128]
-            pulls = [-factor / ranks[m] for m in range(pos_count)]
-            for m in range(pos_count):
-                prank = 1.0
-                pulled = 0.0
-                for q in range(pos_count):
-                    if q != m:
-                        bent = jnp.tanh(spot[q] - spot[m])
-                        prank = prank + 0.5 * (1.0 + bent)
-                        pulled = pulled + (pulls[q] - pulls[m]) * (0.25 * (1.0 - bent * bent))
-                weight = prank / (ranks[m] * ranks[m]) * (factor / logistic_sharpness)
-                extra = pulled / logistic_sharpness - weight * slopes[m]
-                stat_ref[m : m + 1, lanes] = spot[m]
-                stat_ref[8 + m : 9 + m, lanes] = 0.25 * weight
-                stat_ref[16 + m : 17 + m, lanes] = extra
+                stat_ref[8 + m : 9 + m, lanes] = jnp.sum(sums[at], axis=0, keepdims=True)
+                stat_ref[16 + m : 17 + m, lanes] = jnp.sum(sums[at + 1], axis=0, keepdims=True)
 
     first = embed_ref[0:lane_block, :]
-    picked = lax.fori_loop(
-        0, chunks, lambda chunk, have: score_chunk(first, 0, 0, chunk, have), nothing
-    )
+    picked = over_chunks(lambda chunk, have: score_chunk(first, 0, 0, chunk, have), nothing)
 
     def block_step(block, pos):
         start = pl.multiple_of(block * lane_block, lane_block)
@@ -167,16 +147,32 @@
             picked = score_chunk(anchors, following, 1 - buffer, chunk, picked)
             return picked, rank_chunk(pos, buffer, chunk, sums)
 
-        picked, sums = lax.fori_loop(0, chunks, both, (nothing, zero))
-        finish(start, buffer, pos, sums)
+        picked, sums = over_chunks(both, (nothing, zero))
+        finish(start, sums)
         return split(following, 1 - buffer, picked)
 
     last = total // lane_block - 1
     pos = lax.fori_loop(0, last, block_step, split(0, 0, picked))
-    sums = lax.fori_loop(
-        0, chunks, lambda chunk, have: rank_chunk(pos, last % 2, chunk, have), zero
-    )
-    finish(last * lane_block, last % 2, pos, sums)
+    sums = over_chunks(lambda chunk, have: rank_chunk(pos, last % 2, chunk, have), zero)
+    finish(last * lane_block, sums)
+
+    def turned(values, steps):
+        return jnp.concatenate([values[steps:], values[:steps]], axis=0)
+
+    spot = stat_ref[0:pos_count, :]
+    ranks = 0.5 + 0.5 * (total + stat_ref[8 : 8 + pos_count, :])
+    slopes = 0.25 * (total - stat_ref[16 : 16 + pos_count, :])
+    factor = 1.0 / (pos_count * total)
+    pulls = -factor / ranks
+    prank = 1.0
+    pulled = 0.0
+    for steps in range(1, pos_count):
+        bent = jnp.tanh(turned(spot, steps) - spot)
+        prank = prank + 0.5 * (1.0 + bent)
+        pulled = pulled + (turned(pulls, steps) - pulls) * (0.25 * (1.0 - bent * bent))
+    weight = prank / (ranks * ranks) * (factor / logistic_sharpness)
+    stat_ref[8 : 8 + pos_count, :] = 0.25 * weight
+    stat_ref[16 : 16 + pos_count, :] = pulled / logistic_sharpness - weight * slopes
 
     scores = own_ref[...]
     lane = lax.broadcasted_iota(jnp.int32, (shard, total), 1)
@@ -219,9 +215,8 @@
     def join(parts):
         return parts[0] if len(parts) == 1 else jnp.concatenate(parts, axis=0)
 
-    bits = [1 << b for b in reversed(range(levels.bit_length() - 1))]
     order = [0]
-    steps = list(bits)
+    steps = [1 << b for b in reversed(range(levels.bit_length() - 1))]
 
     def spread(ids):
         if not steps:
@@ -231,24 +226,27 @@
         return jnp.concatenate([ids, swap(ids, "row", 2 * bit)], axis=0)
 
     line = [swap(embed, "row", 2 * d) for d in range(1, levels)]
-    mine = {0: embed}
-    mine.update({p: swap(embed, "col", p) for p in range(1, cols)})
-    ids = spread(positives.T)
-    line, mine, ids = lax.optimization_barrier((line, mine, ids))
+    near = jnp.concatenate([embed, jnp.zeros(((cols - 1) * shard, width), embed.dtype)], axis=0)
+    near = lax.optimization_barrier(near)
+    mine = [swap(near[:shard], "col", p) for p in range(1, cols)]
+    ids = positives.T
+    line, mine, near, ids = lax.optimization_barrier((line, mine, near, ids))
     tall = join(line)
 
     plane = {0: tall}
     plane.update({p: swap(tall, "col", p) for p in range(1, cols)})
+    for p in range(1, cols):
+        near = lax.dynamic_update_slice(near, mine[p - 1], (p * shard, 0))
     while steps:
         ids = spread(ids)
-    plane, ids = lax.optimization_barrier((plane, ids))
+    near, tall, ids = lax.optimization_barrier((near, tall, ids))
+    other = [swap(near, "row", 1), swap(tall, "row", 1)]
 
     ids = (ids, swap(ids, "row", 1))
-    near = join([mine[p] for p in range(cols)])
-    pieces = [near, swap(near, "row", 1)]
+    pieces = [near, other[0]]
     layout = [[c * cols + p for p in range(cols)] for c in range(2)]
     for p in range(cols):
-        for c, part in enumerate((plane[p], swap(plane[p], "row", 1))):
+        for c, part in enumerate((plane[p], swap(plane[p], "row", 1) if p else other[1])):
             pieces.append(part)
             layout.append([(d * 2 + c) * cols + p for d in range(1, levels)])
 

time: 37.4 us -> 37.9 us (1.013)
  waiting for transfers between devices: 10.1 us -> 11.3 us
  local copies, waits for them, and re-layouts: 0.05 us -> 0.97 us
  other arithmetic: 0.77 us -> 0.09 us
  Pallas kernels: 8.81 us -> 8.14 us
    ppermute x17, waiting for transfers between devices: 10.1 us -> 11.3 us  [swap(): return lax.ppermute(array, axis, [(i, i ^ mask) for i in range(size)])]
    concatenate x0 -> x1, local copies, waits for them, and re-layouts: none -> 0.92 us  [body(): jnp.concatenate([embed, jnp.zeros(((cols - 1) * shard, width), embed.dtyp...]
    concatenate x2, other arithmetic: 0.69 us -> 0.02 us  [spread(): return jnp.concatenate([ids, swap(ids, 'row', 2 * bit)], axis=0)]
    pallas_call x1, Pallas kernels: 8.81 us -> 8.14 us  [body(): pl.pallas_call(functools.partial(kernel, cols, order, shard, pos_count, l...]
  transfers between devices with their start and end apart: 17 -> 17, of which waited for: 11 -> 10; matrix products, arithmetic and copies ran while one was open for 2% -> 3% of each run, Pallas kernels for 0% -> 0%
where the time goes in v9:
time: 37.9 us; the launch traced here: 37.7 us
  starting transfers between devices  17.2 us (45%)
  waiting for transfers between devices  11.3 us (30%)
  Pallas kernels  8.14 us (21%)
  local copies, waits for them, and re-layouts  0.97 us (3%)
    ppermute x17, starting transfers between devices, swap(): return lax.ppermute(array, axis, [(i, i ^ mask) for i in range(size)])  17.2 us
    ppermute x17, waiting for transfers between devices, swap(): return lax.ppermute(array, axis, [(i, i ^ mask) for i in range(size)])  11.3 us
    pallas_call x1, Pallas kernels, body(): pl.pallas_call(functools.partial(kernel, cols, order, shard, pos_count, l...  8.14 us
    concatenate x1, local copies, waits for them, and re-layouts, body(): jnp.concatenate([embed, jnp.zeros(((cols - 1) * shard, width), embed.dtyp...  0.92 us
  transfers between devices with their start and end apart: 17, of which 10 were waited for; matrix products, arithmetic and copies ran while one was open for 3% of the time, Pallas kernels for 0%

profile of v9, /device:TPU:0, one launch (start us, length us, event | category | flops | bytes accessed | tf_op | source)
XLA Modules:
  0.0 37.7 jit_solution(14242951592588738246)
XLA Ops:
  0.0 4.0 %collective-permute-start.1 = (bf16[32,1024]{1,0:T(8,128)(2,1)}, bf16[32,1024]{1,0:T(8,128)(2,1)S(1)}, u32[]{:S(2)}, u32[]{:S(2)}) collective-permute-start(bf16[32,1024]{1,0:T(8,128)(2,1)} %param.3), channel_id=1, source_target_pairs={{0,16},{4,20},{8,24},{12,28},{16,0},{20,4},{24,8},{28,12},{1,17},{... | collective-permute-start | bytes 196616 | tf_op jit(solution)/shard_map/ppermute | solution.py:213
  4.0 1.6 %collective-permute-start = (bf16[32,1024]{1,0:T(8,128)(2,1)}, bf16[32,1024]{1,0:T(8,128)(2,1)S(1)}, u32[]{:S(2)}, u32[]{:S(2)}) collective-permute-start(bf16[32,1024]{1,0:T(8,128)(2,1)} %param.3), channel_id=1, source_target_pairs={{0,8},{4,12},{8,0},{12,4},{16,24},{20,28},{24,16},{28,20},{1,9},{5... | collective-permute-start | bytes 196616 | tf_op jit(solution)/shard_map/ppermute | solution.py:213
  5.6 0.0 collective-permute-start.2
  5.6 0.9 %concatenate.13 = bf16[128,1024]{1,0:T(8,128)(2,1)S(1)} pad(bf16[32,1024]{1,0:T(8,128)(2,1)} %param.3, bf16[]{:T(256)} %constant.8.clone.1), padding=0_96x0_0 | pad | bytes 327682 | tf_op jit(solution)/shard_map/concatenate | solution.py:229
  6.6 2.7 %collective-permute-start.5 = (bf16[32,1024]{1,0:T(8,128)(2,1)S(1)}, bf16[32,1024]{1,0:T(8,128)(2,1)S(1)}, u32[]{:S(2)}, u32[]{:S(2)}) collective-permute-start(bf16[32,1024]{1,0:T(8,128)(2,1)S(1)} %slice.6), channel_id=1, source_target_pairs={{0,3},{1,2},{2,1},{3,0},{4,7},{5,6},{6,5},{7,4},{8,11},{9,10},{10,... | collective-permute-start | bytes 196616 | tf_op jit(solution)/shard_map/ppermute | solution.py:213
  9.3 0.5 %collective-permute-start.4 = (bf16[32,1024]{1,0:T(8,128)(2,1)S(1)}, bf16[32,1024]{1,0:T(8,128)(2,1)S(1)}, u32[]{:S(2)}, u32[]{:S(2)}) collective-permute-start(bf16[32,1024]{1,0:T(8,128)(2,1)S(1)} %slice.6), channel_id=1, source_target_pairs={{0,2},{1,3},{2,0},{3,1},{4,6},{5,7},{6,4},{7,5},{8,10},{9,11},{10,... | collective-permute-start | bytes 196616 | tf_op jit(solution)/shard_map/ppermute | solution.py:213
  9.8 0.0 collective-permute-done.1
  9.8 0.3 collective-permute-start.3
  10.1 0.0 collective-permute-done
  10.1 1.8 %collective-permute-done.2 = bf16[32,1024]{1,0:T(8,128)(2,1)S(1)} collective-permute-done((bf16[32,1024]{1,0:T(8,128)(2,1)}, bf16[32,1024]{1,0:T(8,128)(2,1)S(1)}, u32[]{:S(2)}, u32[]{:S(2)}) %collective-permute-start.2) | collective-permute-done | bytes 65568 | tf_op jit(solution)/shard_map/ppermute | solution.py:213
  11.9 0.0 collective-permute-done.5
  11.9 1.6 %collective-permute-done.4 = bf16[32,1024]{1,0:T(8,128)(2,1)S(1)} collective-permute-done((bf16[32,1024]{1,0:T(8,128)(2,1)S(1)}, bf16[32,1024]{1,0:T(8,128)(2,1)S(1)}, u32[]{:S(2)}, u32[]{:S(2)}) %collective-permute-start.4) | collective-permute-done | bytes 65568 | tf_op jit(solution)/shard_map/ppermute | solution.py:213
  13.5 0.5 %collective-permute-done.3 = bf16[32,1024]{1,0:T(8,128)(2,1)S(1)} collective-permute-done((bf16[32,1024]{1,0:T(8,128)(2,1)S(1)}, bf16[32,1024]{1,0:T(8,128)(2,1)S(1)}, u32[]{:S(2)}, u32[]{:S(2)}) %collective-permute-start.3) | collective-permute-done | bytes 65568 | tf_op jit(solution)/shard_map/ppermute | solution.py:213
  14.1 0.0 copy-start.1
  14.1 1.6 %collective-permute-start.15 = (bf16[96,1024]{1,0:T(8,128)(2,1)S(1)}, bf16[96,1024]{1,0:T(8,128)(2,1)S(1)}, u32[]{:S(2)}, u32[]{:S(2)}) collective-permute-start(bf16[96,1024]{1,0:T(8,128)(2,1)S(1)} %constant_dynamic-update-slice_fusion.refs_6_), channel_id=1, source_target_pairs={{0,3},{1,2},{2,1},{3,0},{4,7},{5,6},{6,5},{7,4},{8,11},{9,10},{10,... | collective-permute-start | bytes 589832 | tf_op jit(solution)/shard_map/ppermute | solution.py:213
  15.6 0.4 collective-permute-start.13
  16.0 1.6 %collective-permute-start.11 = (bf16[96,1024]{1,0:T(8,128)(2,1)S(1)}, bf16[96,1024]{1,0:T(8,128)(2,1)S(1)}, u32[]{:S(2)}, u32[]{:S(2)}) collective-permute-start(bf16[96,1024]{1,0:T(8,128)(2,1)S(1)} %constant_dynamic-update-slice_fusion.refs_6_), channel_id=1, source_target_pairs={{0,1},{1,0},{2,3},{3,2},{4,5},{5,4},{6,7},{7,6},{8,9},{9,8},{10,11... | collective-permute-start | bytes 589832 | tf_op jit(solution)/shard_map/ppermute | solution.py:213
  17.6 0.0 copy-done.1
  17.6 1.7 %collective-permute-start.6 = (s32[4,128]{1,0:T(4,128)S(1)}, s32[4,128]{1,0:T(4,128)S(1)}, u32[]{:S(2)}, u32[]{:S(2)}) collective-permute-start(s32[4,128]{1,0:T(4,128)S(1)} %bitcast.5), channel_id=1, source_target_pairs={{0,16},{4,20},{8,24},{12,28},{16,0},{20,4},{24,8},{28,12},{1,17},{... | collective-permute-start | bytes 6152 | tf_op jit(solution)/shard_map/ppermute | solution.py:213
  19.3 2.8 %collective-permute-done.6 = s32[4,128]{1,0:T(4,128)S(1)} collective-permute-done((s32[4,128]{1,0:T(4,128)S(1)}, s32[4,128]{1,0:T(4,128)S(1)}, u32[]{:S(2)}, u32[]{:S(2)}) %collective-permute-start.6) | collective-permute-done | bytes 2080 | tf_op jit(solution)/shard_map/ppermute | solution.py:213
  22.1 1.2 %collective-permute-start.7 = (s32[8,128]{1,0:T(8,128)S(1)}, s32[8,128]{1,0:T(8,128)S(1)}, u32[]{:S(2)}, u32[]{:S(2)}) collective-permute-start(s32[8,128]{1,0:T(8,128)S(1)} %pad_add_fusion.1), channel_id=1, source_target_pairs={{0,8},{4,12},{8,0},{12,4},{16,24},{20,28},{24,16},{28,20},{1,9},{5... | collective-permute-start | bytes 12296 | tf_op jit(solution)/shard_map/ppermute | solution.py:213
  23.4 2.4 %collective-permute-done.7 = s32[8,128]{1,0:T(8,128)S(1)} collective-permute-done((s32[8,128]{1,0:T(8,128)S(1)}, s32[8,128]{1,0:T(8,128)S(1)}, u32[]{:S(2)}, u32[]{:S(2)}) %collective-permute-start.7) | collective-permute-done | bytes 4128 | tf_op jit(solution)/shard_map/ppermute | solution.py:213
  25.7 0.0 collective-permute-start.9
  25.8 0.5 %collective-permute-start.8 = (s32[16,128]{1,0:T(8,128)S(1)}, s32[16,128]{1,0:T(8,128)S(1)}, u32[]{:S(2)}, u32[]{:S(2)}) collective-permute-start(s32[16,128]{1,0:T(8,128)S(1)} %pad_add_fusion.refs_2_), channel_id=1, source_target_pairs={{0,4},{4,0},{8,12},{12,8},{16,20},{20,16},{24,28},{28,24},{1,5},{5... | collective-permute-start | bytes 24584 | tf_op jit(solution)/shard_map/ppermute | solution.py:213
  26.3 1.0 %collective-permute-done.8.refs_3_ = s32[16,128]{1,0:T(8,128)S(1)} collective-permute-done((s32[16,128]{1,0:T(8,128)S(1)}, s32[16,128]{1,0:T(8,128)S(1)}, u32[]{:S(2)}, u32[]{:S(2)}) %collective-permute-start.8) | collective-permute-done | bytes 8224 | tf_op jit(solution)/shard_map/ppermute | solution.py:213
  27.3 0.1 collective-permute-start.10
  27.4 0.0 collective-permute-done.15.refs_12_
  27.4 0.4 collective-permute-start.16
  27.8 0.0 collective-permute-done.13.refs_10_
  27.8 0.1 collective-permute-start.14
  27.9 0.0 collective-permute-done.11.refs_8_
  28.0 0.4 collective-permute-start.12
  28.3 0.0 copy-start
  28.3 0.1 pad_add_fusion.2.refs_0_
  28.4 0.3 collective-permute-done.10.refs_7_
  28.7 0.0 collective-permute-done.9.refs_5_
  28.7 0.3 collective-permute-done.16.refs_13_
  29.0 0.3 collective-permute-done.14.refs_11_
  29.3 0.3 collective-permute-done.12.refs_9_
  29.6 0.0 copy-done
  29.6 8.1 %shard_map.37 = f32[32,1024]{1,0:T(8,128)} custom-call(s32[2]{0:T(128)S(1)} %pad_add_fusion.2.refs_0_, s32[8,128]{1,0:T(8,128)S(1)} %bitcast.4, s32[16,128]{1,0:T(8,128)S(1)} %pad_add_fusion.refs_2_, s32[16,128]{1,0:T(8,128)S(1)} %collective-permute-done.8.refs_3_, bf16[128,1024]{1,0:T(8,128)(2,1)S(1)} %constant_dynamic-update-slice_fusion.3.refs_4_, ...), custom_call_target="tpu_custom_call" | custom-call | flops 2147483648 | bytes 2097152 | tf_op jit(solution)/shard_map/pallas_call | solution.py:255
  (9 shorter events, 0.1 us)
Async XLA Ops:
  0.0 9.8 %collective-permute-start.1 = (bf16[32,1024]{1,0:T(8,128)(2,1)}, bf16[32,1024]{1,0:T(8,128)(2,1)S(1)}, u32[]{:S(2)}, u32[]{:S(2)}) collective-permute-start(bf16[32,1024]{1,0:T(8,128)(2,1)} %param.3), channel_id=1, source_target_pairs={{0,16},{4,20},{8,24},{12,28},{16,0},{20,4},{24,8},{28,12},{1,17},{... | collective-permute-start | bytes 196616 | tf_op jit(solution)/shard_map/ppermute | solution.py:213
  4.0 6.1 %collective-permute-start = (bf16[32,1024]{1,0:T(8,128)(2,1)}, bf16[32,1024]{1,0:T(8,128)(2,1)S(1)}, u32[]{:S(2)}, u32[]{:S(2)}) collective-permute-start(bf16[32,1024]{1,0:T(8,128)(2,1)} %param.3), channel_id=1, source_target_pairs={{0,8},{4,12},{8,0},{12,4},{16,24},{20,28},{24,16},{28,20},{1,9},{5... | collective-permute-start | bytes 196616 | tf_op jit(solution)/shard_map/ppermute | solution.py:213
  5.6 6.3 %collective-permute-start.2 = (bf16[32,1024]{1,0:T(8,128)(2,1)}, bf16[32,1024]{1,0:T(8,128)(2,1)S(1)}, u32[]{:S(2)}, u32[]{:S(2)}) collective-permute-start(bf16[32,1024]{1,0:T(8,128)(2,1)} %param.3), channel_id=1, source_target_pairs={{0,24},{4,28},{8,16},{12,20},{16,8},{20,12},{24,0},{28,4},{1,25},{... | collective-permute-start | bytes 196616 | tf_op jit(solution)/shard_map/ppermute | solution.py:213
  6.6 5.3 %collective-permute-start.5 = (bf16[32,1024]{1,0:T(8,128)(2,1)S(1)}, bf16[32,1024]{1,0:T(8,128)(2,1)S(1)}, u32[]{:S(2)}, u32[]{:S(2)}) collective-permute-start(bf16[32,1024]{1,0:T(8,128)(2,1)S(1)} %slice.6), channel_id=1, source_target_pairs={{0,3},{1,2},{2,1},{3,0},{4,7},{5,6},{6,5},{7,4},{8,11},{9,10},{10,... | collective-permute-start | bytes 196616 | tf_op jit(solution)/shard_map/ppermute | solution.py:213
  9.3 4.3 %collective-permute-start.4 = (bf16[32,1024]{1,0:T(8,128)(2,1)S(1)}, bf16[32,1024]{1,0:T(8,128)(2,1)S(1)}, u32[]{:S(2)}, u32[]{:S(2)}) collective-permute-start(bf16[32,1024]{1,0:T(8,128)(2,1)S(1)} %slice.6), channel_id=1, source_target_pairs={{0,2},{1,3},{2,0},{3,1},{4,6},{5,7},{6,4},{7,5},{8,10},{9,11},{10,... | collective-permute-start | bytes 196616 | tf_op jit(solution)/shard_map/ppermute | solution.py:213
  9.8 4.3 %collective-permute-start.3 = (bf16[32,1024]{1,0:T(8,128)(2,1)S(1)}, bf16[32,1024]{1,0:T(8,128)(2,1)S(1)}, u32[]{:S(2)}, u32[]{:S(2)}) collective-permute-start(bf16[32,1024]{1,0:T(8,128)(2,1)S(1)} %slice.6), channel_id=1, source_target_pairs={{0,1},{1,0},{2,3},{3,2},{4,5},{5,4},{6,7},{7,6},{8,9},{9,8},{10,11... | collective-permute-start | bytes 196616 | tf_op jit(solution)/shard_map/ppermute | solution.py:213
  14.1 3.6 %copy-start.1 = (s32[128,4]{0,1:T(4,128)S(1)}, s32[128,4]{0,1:T(4,128)}, u32[]{:S(2)}) copy-start(s32[128,4]{0,1:T(4,128)} %param.4) | copy-start | bytes 6148
  14.1 13.4 %collective-permute-start.15 = (bf16[96,1024]{1,0:T(8,128)(2,1)S(1)}, bf16[96,1024]{1,0:T(8,128)(2,1)S(1)}, u32[]{:S(2)}, u32[]{:S(2)}) collective-permute-start(bf16[96,1024]{1,0:T(8,128)(2,1)S(1)} %constant_dynamic-update-slice_fusion.refs_6_), channel_id=1, source_target_pairs={{0,3},{1,2},{2,1},{3,0},{4,7},{5,6},{6,5},{7,4},{8,11},{9,10},{10,... | collective-permute-start | bytes 589832 | tf_op jit(solution)/shard_map/ppermute | solution.py:213
  15.6 12.2 %collective-permute-start.13 = (bf16[96,1024]{1,0:T(8,128)(2,1)S(1)}, bf16[96,1024]{1,0:T(8,128)(2,1)S(1)}, u32[]{:S(2)}, u32[]{:S(2)}) collective-permute-start(bf16[96,1024]{1,0:T(8,128)(2,1)S(1)} %constant_dynamic-update-slice_fusion.refs_6_), channel_id=1, source_target_pairs={{0,2},{1,3},{2,0},{3,1},{4,6},{5,7},{6,4},{7,5},{8,10},{9,11},{10,... | collective-permute-start | bytes 589832 | tf_op jit(solution)/shard_map/ppermute | solution.py:213
  16.0 11.9 %collective-permute-start.11 = (bf16[96,1024]{1,0:T(8,128)(2,1)S(1)}, bf16[96,1024]{1,0:T(8,128)(2,1)S(1)}, u32[]{:S(2)}, u32[]{:S(2)}) collective-permute-start(bf16[96,1024]{1,0:T(8,128)(2,1)S(1)} %constant_dynamic-update-slice_fusion.refs_6_), channel_id=1, source_target_pairs={{0,1},{1,0},{2,3},{3,2},{4,5},{5,4},{6,7},{7,6},{8,9},{9,8},{10,11... | collective-permute-start | bytes 589832 | tf_op jit(solution)/shard_map/ppermute | solution.py:213
  17.6 4.5 %collective-permute-start.6 = (s32[4,128]{1,0:T(4,128)S(1)}, s32[4,128]{1,0:T(4,128)S(1)}, u32[]{:S(2)}, u32[]{:S(2)}) collective-permute-start(s32[4,128]{1,0:T(4,128)S(1)} %bitcast.5), channel_id=1, source_target_pairs={{0,16},{4,20},{8,24},{12,28},{16,0},{20,4},{24,8},{28,12},{1,17},{... | collective-permute-start | bytes 6152 | tf_op jit(solution)/shard_map/ppermute | solution.py:213
  22.1 3.6 %collective-permute-start.7 = (s32[8,128]{1,0:T(8,128)S(1)}, s32[8,128]{1,0:T(8,128)S(1)}, u32[]{:S(2)}, u32[]{:S(2)}) collective-permute-start(s32[8,128]{1,0:T(8,128)S(1)} %pad_add_fusion.1), channel_id=1, source_target_pairs={{0,8},{4,12},{8,0},{12,4},{16,24},{20,28},{24,16},{28,20},{1,9},{5... | collective-permute-start | bytes 12296 | tf_op jit(solution)/shard_map/ppermute | solution.py:213
  25.7 3.0 %collective-permute-start.9 = (bf16[128,1024]{1,0:T(8,128)(2,1)S(1)}, bf16[128,1024]{1,0:T(8,128)(2,1)S(1)}, u32[]{:S(2)}, u32[]{:S(2)}) collective-permute-start(bf16[128,1024]{1,0:T(8,128)(2,1)S(1)} %constant_dynamic-update-slice_fusion.3.refs_4_), channel_id=1, source_target_pairs={{0,4},{4,0},{8,12},{12,8},{16,20},{20,16},{24,28},{28,24},{1,5},{5... | collective-permute-start | bytes 786440 | tf_op jit(solution)/shard_map/ppermute | solution.py:213
  25.8 1.5 %collective-permute-start.8 = (s32[16,128]{1,0:T(8,128)S(1)}, s32[16,128]{1,0:T(8,128)S(1)}, u32[]{:S(2)}, u32[]{:S(2)}) collective-permute-start(s32[16,128]{1,0:T(8,128)S(1)} %pad_add_fusion.refs_2_), channel_id=1, source_target_pairs={{0,4},{4,0},{8,12},{12,8},{16,20},{20,16},{24,28},{28,24},{1,5},{5... | collective-permute-start | bytes 24584 | tf_op jit(solution)/shard_map/ppermute | solution.py:213
  27.3 1.4 %collective-permute-start.10 = (bf16[96,1024]{1,0:T(8,128)(2,1)S(1)}, bf16[96,1024]{1,0:T(8,128)(2,1)S(1)}, u32[]{:S(2)}, u32[]{:S(2)}) collective-permute-start(bf16[96,1024]{1,0:T(8,128)(2,1)S(1)} %constant_dynamic-update-slice_fusion.refs_6_), channel_id=1, source_target_pairs={{0,4},{4,0},{8,12},{12,8},{16,20},{20,16},{24,28},{28,24},{1,5},{5... | collective-permute-start | bytes 589832 | tf_op jit(solution)/shard_map/ppermute | solution.py:213
  27.4 1.6 %collective-permute-start.16 = (bf16[96,1024]{1,0:T(8,128)(2,1)S(1)}, bf16[96,1024]{1,0:T(8,128)(2,1)S(1)}, u32[]{:S(2)}, u32[]{:S(2)}) collective-permute-start(bf16[96,1024]{1,0:T(8,128)(2,1)S(1)} %collective-permute-done.15.refs_12_), channel_id=1, source_target_pairs={{0,4},{4,0},{8,12},{12,8},{16,20},{20,16},{24,28},{28,24},{1,5},{5... | collective-permute-start | bytes 589832 | tf_op jit(solution)/shard_map/ppermute | solution.py:213
  27.8 1.5 %collective-permute-start.14 = (bf16[96,1024]{1,0:T(8,128)(2,1)S(1)}, bf16[96,1024]{1,0:T(8,128)(2,1)S(1)}, u32[]{:S(2)}, u32[]{:S(2)}) collective-permute-start(bf16[96,1024]{1,0:T(8,128)(2,1)S(1)} %collective-permute-done.13.refs_10_), channel_id=1, source_target_pairs={{0,4},{4,0},{8,12},{12,8},{16,20},{20,16},{24,28},{28,24},{1,5},{5... | collective-permute-start | bytes 589832 | tf_op jit(solution)/shard_map/ppermute | solution.py:213
  28.0 1.6 %collective-permute-start.12 = (bf16[96,1024]{1,0:T(8,128)(2,1)S(1)}, bf16[96,1024]{1,0:T(8,128)(2,1)S(1)}, u32[]{:S(2)}, u32[]{:S(2)}) collective-permute-start(bf16[96,1024]{1,0:T(8,128)(2,1)S(1)} %collective-permute-done.11.refs_8_), channel_id=1, source_target_pairs={{0,4},{4,0},{8,12},{12,8},{16,20},{20,16},{24,28},{28,24},{1,5},{5... | collective-permute-start | bytes 589832 | tf_op jit(solution)/shard_map/ppermute | solution.py:213
  28.3 1.3 %copy-start = (s32[1024]{0:T(1024)S(1)}, s32[1024]{0:T(1024)}, u32[]{:S(2)}) copy-start(s32[1024]{0:T(1024)} %param.5) | copy-start | bytes 12292

commit v10 on v9

--- a/solution.py
+++ b/solution.py
@@ -63,25 +63,13 @@
         score_ref[buffer, pl.ds(row, row_chunk), :] = scores
         picked = list(picked)
         for half in range(pair):
-            lanes = slice(half * 128, (half + 1) * 128)
-            for m in range(pos_count):
-                target = jnp.broadcast_to(
-                    target_ref[m : m + 1, pl.ds(pl.multiple_of(start + half * 128, 128), 128)],
-                    (8, 128),
-                )
-                odd = [(target & (8 << b)) != 0 for b in range(3)]
-                near = (target - row) >> 6
-                at = half * pos_count + m
-                for step in range(row_chunk // 64):
-                    tiles = [
-                        scores[step * 64 + k * 8 : step * 64 + (k + 1) * 8, lanes] for k in range(8)
-                    ]
-                    for b in range(3):
-                        tiles = [
-                            jnp.where(odd[b], tiles[2 * k + 1], tiles[2 * k])
-                            for k in range(len(tiles) // 2)
-                        ]
-                    picked[at] = jnp.where(near == step, tiles[0], picked[at])
+            targets = target_ref[:, pl.ds(pl.multiple_of(start + half * 128, 128), 128)]
+            near = (targets - row) >> 3
+            sub = targets & 7
+            for step in range(row_chunk // 8):
+                tile = scores[step * 8 : (step + 1) * 8, half * 128 : (half + 1) * 128]
+                tile = jnp.take_along_axis(tile, sub, axis=0)
+                picked[half] = jnp.where(near == step, tile, picked[half])
         return tuple(picked)
 
     def rank_chunk(pos, buffer, chunk, sums):
@@ -104,7 +92,7 @@
         return lax.fori_loop(0, chunks, step, have)
 
     chunks = total // row_chunk
-    nothing = (jnp.zeros((8, 128), jnp.float32),) * (pair * pos_count)
+    nothing = (jnp.zeros((8, 128), jnp.float32),) * pair
     zero = (jnp.zeros((8, 128), jnp.float32),) * (2 * pos_count * pair)
 
     def split(start, buffer, picked):
@@ -112,17 +100,13 @@
         index = lax.broadcasted_iota(jnp.int32, (lane_block, lane_block), 0)
         lane = lax.broadcasted_iota(jnp.int32, (lane_block, lane_block), 1)
         score_ref[inside] = jnp.where(index == lane, masked, score_ref[inside])
-        sub = lax.broadcasted_iota(jnp.int32, (8, 128), 0)
         pos = []
         for half in range(pair):
             lanes = pl.ds(pl.multiple_of(start + half * 128, 128), 128)
             own_ref[:, lanes] = score_ref[buffer, 0:shard, half * 128 : (half + 1) * 128]
+            stat_ref[0:8, lanes] = picked[half]
             for m in range(pos_count):
-                hit = sub == (target_ref[m : m + 1, lanes] & 7)
-                spot = jnp.where(hit, picked[half * pos_count + m], 0.0)
-                spot = jnp.sum(spot, axis=0, keepdims=True)
-                stat_ref[m : m + 1, lanes] = spot
-                pos.append(jnp.broadcast_to(spot, (8, 128)))
+                pos.append(jnp.broadcast_to(picked[half][m : m + 1, :], (8, 128)))
         return tuple(pos)
 
     def finish(start, sums):
@@ -226,29 +210,25 @@
         return jnp.concatenate([ids, swap(ids, "row", 2 * bit)], axis=0)
 
     line = [swap(embed, "row", 2 * d) for d in range(1, levels)]
-    near = jnp.concatenate([embed, jnp.zeros(((cols - 1) * shard, width), embed.dtype)], axis=0)
-    near = lax.optimization_barrier(near)
-    mine = [swap(near[:shard], "col", p) for p in range(1, cols)]
-    ids = positives.T
-    line, mine, near, ids = lax.optimization_barrier((line, mine, near, ids))
-    tall = join(line)
-
-    plane = {0: tall}
-    plane.update({p: swap(tall, "col", p) for p in range(1, cols)})
-    for p in range(1, cols):
-        near = lax.dynamic_update_slice(near, mine[p - 1], (p * shard, 0))
+    ids = spread(positives.T)
+    line, ids = lax.optimization_barrier((line, ids))
+    tall = join([embed] + line)
+
+    plane = {p: swap(tall, "col", p) for p in range(1, cols)}
     while steps:
         ids = spread(ids)
-    near, tall, ids = lax.optimization_barrier((near, tall, ids))
-    other = [swap(near, "row", 1), swap(tall, "row", 1)]
-
+    other = {0: swap(tall, "row", 1)}
     ids = (ids, swap(ids, "row", 1))
-    pieces = [near, other[0]]
-    layout = [[c * cols + p for p in range(cols)] for c in range(2)]
+    ids, plane[cols - 1] = lax.optimization_barrier((ids, plane[cols - 1]))
+
+    plane[0] = tall
+    other.update({p: swap(plane[p], "row", 1) for p in range(1, cols)})
+    pieces = []
+    layout = []
     for p in range(cols):
-        for c, part in enumerate((plane[p], swap(plane[p], "row", 1) if p else other[1])):
+        for c, part in enumerate((plane[p], other[p])):
             pieces.append(part)
-            layout.append([(d * 2 + c) * cols + p for d in range(1, levels)])
+            layout.append([(d * 2 + c) * cols + p for d in range(levels)])
 
     place = jnp.stack([lax.axis_index(axes) * shard, lax.axis_index("col") * shard])
     vmem = pl.BlockSpec(memory_space=pltpu.VMEM)

time: 37.9 us -> 35.1 us (0.926)
  starting transfers between devices: 17.2 us -> 12.7 us
  waiting for transfers between devices: 11.3 us -> 13.5 us
    ppermute x17 -> x13, starting transfers between devices: 17.2 us -> 12.7 us  [swap(): return lax.ppermute(array, axis, [(i, i ^ mask) for i in range(size)])]
    ppermute x17 -> x13, waiting for transfers between devices: 11.3 us -> 13.5 us  [swap(): return lax.ppermute(array, axis, [(i, i ^ mask) for i in range(size)])]
    concatenate x1, local copies, waits for them, and re-layouts: 0.92 us -> 0.01 us  [spread(): return jnp.concatenate([ids, swap(ids, 'row', 2 * bit)], axis=0)]
    unnamed x6 -> x8, local copies, waits for them, and re-layouts: 0.02 us -> 0.86 us
  transfers between devices with their start and end apart: 17 -> 13, of which waited for: 10 -> 10; matrix products, arithmetic and copies ran while one was open for 3% -> 3% of each run, Pallas kernels for 0% -> 0%
where the time goes in v10:
time: 35.1 us; the launch traced here: 35 us
  waiting for transfers between devices  13.5 us (38%)
  starting transfers between devices  12.7 us (36%)
  Pallas kernels  7.77 us (22%)
  local copies, waits for them, and re-layouts  0.87 us (2%)
    ppermute x13, waiting for transfers between devices, swap(): return lax.ppermute(array, axis, [(i, i ^ mask) for i in range(size)])  13.5 us
    ppermute x13, starting transfers between devices, swap(): return lax.ppermute(array, axis, [(i, i ^ mask) for i in range(size)])  12.7 us
    pallas_call x1, Pallas kernels, body(): pl.pallas_call(functools.partial(kernel, cols, order, shard, pos_count, l...  7.77 us
    unnamed x8, local copies, waits for them, and re-layouts  0.86 us
  transfers between devices with their start and end apart: 13, of which 10 were waited for; matrix products, arithmetic and copies ran while one was open for 3% of the time, Pallas kernels for 0%

profile of v10, /device:TPU:0, one launch (start us, length us, event | category | flops | bytes accessed | tf_op | source)
XLA Modules:
  0.0 35.0 jit_solution(2309566924696364365)
XLA Ops:
  0.0 4.0 %collective-permute-start.1 = (bf16[32,1024]{1,0:T(8,128)(2,1)}, bf16[32,1024]{1,0:T(8,128)(2,1)S(1)}, u32[]{:S(2)}, u32[]{:S(2)}) collective-permute-start(bf16[32,1024]{1,0:T(8,128)(2,1)} %param.3), channel_id=1, source_target_pairs={{0,16},{4,20},{8,24},{12,28},{16,0},{20,4},{24,8},{28,12},{1,17},{... | collective-permute-start | bytes 196616 | tf_op jit(solution)/shard_map/ppermute | solution.py:197
  4.0 1.6 %collective-permute-start = (bf16[32,1024]{1,0:T(8,128)(2,1)}, bf16[32,1024]{1,0:T(8,128)(2,1)S(1)}, u32[]{:S(2)}, u32[]{:S(2)}) collective-permute-start(bf16[32,1024]{1,0:T(8,128)(2,1)} %param.3), channel_id=1, source_target_pairs={{0,8},{4,12},{8,0},{12,4},{16,24},{20,28},{24,16},{28,20},{1,9},{5... | collective-permute-start | bytes 196616 | tf_op jit(solution)/shard_map/ppermute | solution.py:197
  5.6 0.0 collective-permute-start.2
  5.6 0.0 copy-start.1
  5.6 1.9 %collective-permute-start.3 = (s32[4,128]{1,0:T(4,128)}, s32[4,128]{1,0:T(4,128)S(1)}, u32[]{:S(2)}, u32[]{:S(2)}) collective-permute-start(s32[4,128]{1,0:T(4,128)} %bitcast.5), channel_id=1, source_target_pairs={{0,16},{4,20},{8,24},{12,28},{16,0},{20,4},{24,8},{28,12},{1,17},{... | collective-permute-start | bytes 6152 | tf_op jit(solution)/shard_map/ppermute | solution.py:197
  7.5 0.8 %constant_dynamic-update-slice_fusion.5 = bf16[128,1024]{1,0:T(8,128)(2,1)S(1)} fusion(bf16[32,1024]{1,0:T(8,128)(2,1)} %param.3), kind=kLoop, calls=%fused_computation.5 | loop fusion | bytes 131072
  8.4 2.3 %collective-permute-done.3 = s32[4,128]{1,0:T(4,128)S(1)} collective-permute-done((s32[4,128]{1,0:T(4,128)}, s32[4,128]{1,0:T(4,128)S(1)}, u32[]{:S(2)}, u32[]{:S(2)}) %collective-permute-start.3) | collective-permute-done | bytes 2080 | tf_op jit(solution)/shard_map/ppermute | solution.py:197
  10.7 0.0 copy-done.1
  10.7 0.0 collective-permute-done.1
  10.7 0.0 collective-permute-done
  10.8 1.1 %collective-permute-done.2 = bf16[32,1024]{1,0:T(8,128)(2,1)S(1)} collective-permute-done((bf16[32,1024]{1,0:T(8,128)(2,1)}, bf16[32,1024]{1,0:T(8,128)(2,1)S(1)}, u32[]{:S(2)}, u32[]{:S(2)}) %collective-permute-start.2) | collective-permute-done | bytes 65568 | tf_op jit(solution)/shard_map/ppermute | solution.py:197
  11.9 2.5 %collective-permute-start.6 = (bf16[128,1024]{1,0:T(8,128)(2,1)S(1)}, bf16[128,1024]{1,0:T(8,128)(2,1)S(1)}, u32[]{:S(2)}, u32[]{:S(2)}) collective-permute-start(bf16[128,1024]{1,0:T(8,128)(2,1)S(1)} %constant_dynamic-update-slice_fusion.2.refs_4_), channel_id=1, source_target_pairs={{0,3},{1,2},{2,1},{3,0},{4,7},{5,6},{6,5},{7,4},{8,11},{9,10},{10,... | collective-permute-start | bytes 786440 | tf_op jit(solution)/shard_map/ppermute | solution.py:197
  14.4 0.5 %collective-permute-start.10 = (bf16[128,1024]{1,0:T(8,128)(2,1)S(1)}, bf16[128,1024]{1,0:T(8,128)(2,1)S(1)}, u32[]{:S(2)}, u32[]{:S(2)}) collective-permute-start(bf16[128,1024]{1,0:T(8,128)(2,1)S(1)} %constant_dynamic-update-slice_fusion.2.refs_4_), channel_id=1, source_target_pairs={{0,2},{1,3},{2,0},{3,1},{4,6},{5,7},{6,4},{7,5},{8,10},{9,11},{10,... | collective-permute-start | bytes 786440 | tf_op jit(solution)/shard_map/ppermute | solution.py:197
  14.9 0.5 %collective-permute-start.8 = (bf16[128,1024]{1,0:T(8,128)(2,1)S(1)}, bf16[128,1024]{1,0:T(8,128)(2,1)S(1)}, u32[]{:S(2)}, u32[]{:S(2)}) collective-permute-start(bf16[128,1024]{1,0:T(8,128)(2,1)S(1)} %constant_dynamic-update-slice_fusion.2.refs_4_), channel_id=1, source_target_pairs={{0,1},{1,0},{2,3},{3,2},{4,5},{5,4},{6,7},{7,6},{8,9},{9,8},{10,11... | collective-permute-start | bytes 786440 | tf_op jit(solution)/shard_map/ppermute | solution.py:197
  15.5 0.6 %collective-permute-start.4 = (s32[8,128]{1,0:T(8,128)S(1)}, s32[8,128]{1,0:T(8,128)S(1)}, u32[]{:S(2)}, u32[]{:S(2)}) collective-permute-start(s32[8,128]{1,0:T(8,128)S(1)} %pad_add_fusion), channel_id=1, source_target_pairs={{0,8},{4,12},{8,0},{12,4},{16,24},{20,28},{24,16},{28,20},{1,9},{5... | collective-permute-start | bytes 12296 | tf_op jit(solution)/shard_map/ppermute | solution.py:197
  16.1 3.0 %collective-permute-done.4 = s32[8,128]{1,0:T(8,128)S(1)} collective-permute-done((s32[8,128]{1,0:T(8,128)S(1)}, s32[8,128]{1,0:T(8,128)S(1)}, u32[]{:S(2)}, u32[]{:S(2)}) %collective-permute-start.4) | collective-permute-done | bytes 4128 | tf_op jit(solution)/shard_map/ppermute | solution.py:197
  19.1 0.0 collective-permute-start.5
  19.1 0.5 %collective-permute-start.7 = (bf16[128,1024]{1,0:T(8,128)(2,1)S(1)}, bf16[128,1024]{1,0:T(8,128)(2,1)S(1)}, u32[]{:S(2)}, u32[]{:S(2)}) collective-permute-start(bf16[128,1024]{1,0:T(8,128)(2,1)S(1)} %constant_dynamic-update-slice_fusion.2.refs_4_), channel_id=1, source_target_pairs={{0,4},{4,0},{8,12},{12,8},{16,20},{20,16},{24,28},{28,24},{1,5},{5... | collective-permute-start | bytes 786440 | tf_op jit(solution)/shard_map/ppermute | solution.py:197
  19.6 0.7 %collective-permute-done.5.refs_3_ = s32[16,128]{1,0:T(8,128)S(1)} collective-permute-done((s32[16,128]{1,0:T(8,128)S(1)}, s32[16,128]{1,0:T(8,128)S(1)}, u32[]{:S(2)}, u32[]{:S(2)}) %collective-permute-start.5) | collective-permute-done | bytes 8224 | tf_op jit(solution)/shard_map/ppermute | solution.py:197
  20.3 1.9 %collective-permute-done.6.refs_10_ = bf16[128,1024]{1,0:T(8,128)(2,1)S(1)} collective-permute-done((bf16[128,1024]{1,0:T(8,128)(2,1)S(1)}, bf16[128,1024]{1,0:T(8,128)(2,1)S(1)}, u32[]{:S(2)}, u32[]{:S(2)}) %collective-permute-start.6) | collective-permute-done | bytes 262176 | tf_op jit(solution)/shard_map/ppermute | solution.py:197
  22.1 2.8 %collective-permute-done.10.refs_8_ = bf16[128,1024]{1,0:T(8,128)(2,1)S(1)} collective-permute-done((bf16[128,1024]{1,0:T(8,128)(2,1)S(1)}, bf16[128,1024]{1,0:T(8,128)(2,1)S(1)}, u32[]{:S(2)}, u32[]{:S(2)}) %collective-permute-start.10) | collective-permute-done | bytes 262176 | tf_op jit(solution)/shard_map/ppermute | solution.py:197
  24.9 0.0 collective-permute-start.11
  24.9 0.1 collective-permute-done.8.refs_6_
  25.0 0.4 %collective-permute-start.9 = (bf16[128,1024]{1,0:T(8,128)(2,1)S(1)}, bf16[128,1024]{1,0:T(8,128)(2,1)S(1)}, u32[]{:S(2)}, u32[]{:S(2)}) collective-permute-start(bf16[128,1024]{1,0:T(8,128)(2,1)S(1)} %collective-permute-done.8.refs_6_), channel_id=1, source_target_pairs={{0,4},{4,0},{8,12},{12,8},{16,20},{20,16},{24,28},{28,24},{1,5},{5... | collective-permute-start | bytes 786440 | tf_op jit(solution)/shard_map/ppermute | solution.py:197
  25.5 0.1 collective-permute-start.12
  25.6 0.0 copy-start
  25.6 0.1 pad_add_fusion.1.refs_0_
  25.6 0.0 collective-permute-done.7.refs_5_
  25.6 0.8 %collective-permute-done.11.refs_9_ = bf16[128,1024]{1,0:T(8,128)(2,1)S(1)} collective-permute-done((bf16[128,1024]{1,0:T(8,128)(2,1)S(1)}, bf16[128,1024]{1,0:T(8,128)(2,1)S(1)}, u32[]{:S(2)}, u32[]{:S(2)}) %collective-permute-start.11) | collective-permute-done | bytes 262176 | tf_op jit(solution)/shard_map/ppermute | solution.py:197
  26.5 0.4 %collective-permute-done.9.refs_7_ = bf16[128,1024]{1,0:T(8,128)(2,1)S(1)} collective-permute-done((bf16[128,1024]{1,0:T(8,128)(2,1)S(1)}, bf16[128,1024]{1,0:T(8,128)(2,1)S(1)}, u32[]{:S(2)}, u32[]{:S(2)}) %collective-permute-start.9) | collective-permute-done | bytes 262176 | tf_op jit(solution)/shard_map/ppermute | solution.py:197
  26.8 0.4 %collective-permute-done.12.refs_11_ = bf16[128,1024]{1,0:T(8,128)(2,1)S(1)} collective-permute-done((bf16[128,1024]{1,0:T(8,128)(2,1)S(1)}, bf16[128,1024]{1,0:T(8,128)(2,1)S(1)}, u32[]{:S(2)}, u32[]{:S(2)}) %collective-permute-start.12) | collective-permute-done | bytes 262176 | tf_op jit(solution)/shard_map/ppermute | solution.py:197
  27.2 0.0 copy-done
  27.2 7.8 %shard_map.37 = f32[32,1024]{1,0:T(8,128)} custom-call(s32[2]{0:T(128)S(1)} %pad_add_fusion.1.refs_0_, s32[8,128]{1,0:T(8,128)S(1)} %bitcast.4, s32[16,128]{1,0:T(8,128)S(1)} %constant_dynamic-update-slice_fusion.refs_2_, s32[16,128]{1,0:T(8,128)S(1)} %collective-permute-done.5.refs_3_, bf16[128,1024]{1,0:T(8,128)(2,1)S(1)} %constant_dynamic-update-slice_fusion.2.refs_4_, ...), custom_call_target="tpu_custom_call" | custom-call | flops 2147483648 | bytes 2097152 | tf_op jit(solution)/shard_map/pallas_call | solution.py:235
  (6 shorter events, 0.0 us)
Async XLA Ops:
  0.0 10.7 %collective-permute-start.1 = (bf16[32,1024]{1,0:T(8,128)(2,1)}, bf16[32,1024]{1,0:T(8,128)(2,1)S(1)}, u32[]{:S(2)}, u32[]{:S(2)}) collective-permute-start(bf16[32,1024]{1,0:T(8,128)(2,1)} %param.3), channel_id=1, source_target_pairs={{0,16},{4,20},{8,24},{12,28},{16,0},{20,4},{24,8},{28,12},{1,17},{... | collective-permute-start | bytes 196616 | tf_op jit(solution)/shard_map/ppermute | solution.py:197
  4.0 6.7 %collective-permute-start = (bf16[32,1024]{1,0:T(8,128)(2,1)}, bf16[32,1024]{1,0:T(8,128)(2,1)S(1)}, u32[]{:S(2)}, u32[]{:S(2)}) collective-permute-start(bf16[32,1024]{1,0:T(8,128)(2,1)} %param.3), channel_id=1, source_target_pairs={{0,8},{4,12},{8,0},{12,4},{16,24},{20,28},{24,16},{28,20},{1,9},{5... | collective-permute-start | bytes 196616 | tf_op jit(solution)/shard_map/ppermute | solution.py:197
  5.6 6.3 %collective-permute-start.2 = (bf16[32,1024]{1,0:T(8,128)(2,1)}, bf16[32,1024]{1,0:T(8,128)(2,1)S(1)}, u32[]{:S(2)}, u32[]{:S(2)}) collective-permute-start(bf16[32,1024]{1,0:T(8,128)(2,1)} %param.3), channel_id=1, source_target_pairs={{0,24},{4,28},{8,16},{12,20},{16,8},{20,12},{24,0},{28,4},{1,25},{... | collective-permute-start | bytes 196616 | tf_op jit(solution)/shard_map/ppermute | solution.py:197
  5.6 5.1 %copy-start.1 = (s32[128,4]{0,1:T(4,128)S(1)}, s32[128,4]{0,1:T(4,128)}, u32[]{:S(2)}) copy-start(s32[128,4]{0,1:T(4,128)} %param.4) | copy-start | bytes 6148
  5.6 5.1 %collective-permute-start.3 = (s32[4,128]{1,0:T(4,128)}, s32[4,128]{1,0:T(4,128)S(1)}, u32[]{:S(2)}, u32[]{:S(2)}) collective-permute-start(s32[4,128]{1,0:T(4,128)} %bitcast.5), channel_id=1, source_target_pairs={{0,16},{4,20},{8,24},{12,28},{16,0},{20,4},{24,8},{28,12},{1,17},{... | collective-permute-start | bytes 6152 | tf_op jit(solution)/shard_map/ppermute | solution.py:197
  11.9 10.2 %collective-permute-start.6 = (bf16[128,1024]{1,0:T(8,128)(2,1)S(1)}, bf16[128,1024]{1,0:T(8,128)(2,1)S(1)}, u32[]{:S(2)}, u32[]{:S(2)}) collective-permute-start(bf16[128,1024]{1,0:T(8,128)(2,1)S(1)} %constant_dynamic-update-slice_fusion.2.refs_4_), channel_id=1, source_target_pairs={{0,3},{1,2},{2,1},{3,0},{4,7},{5,6},{6,5},{7,4},{8,11},{9,10},{10,... | collective-permute-start | bytes 786440 | tf_op jit(solution)/shard_map/ppermute | solution.py:197
  14.4 10.5 %collective-permute-start.10 = (bf16[128,1024]{1,0:T(8,128)(2,1)S(1)}, bf16[128,1024]{1,0:T(8,128)(2,1)S(1)}, u32[]{:S(2)}, u32[]{:S(2)}) collective-permute-start(bf16[128,1024]{1,0:T(8,128)(2,1)S(1)} %constant_dynamic-update-slice_fusion.2.refs_4_), channel_id=1, source_target_pairs={{0,2},{1,3},{2,0},{3,1},{4,6},{5,7},{6,4},{7,5},{8,10},{9,11},{10,... | collective-permute-start | bytes 786440 | tf_op jit(solution)/shard_map/ppermute | solution.py:197
  14.9 10.1 %collective-permute-start.8 = (bf16[128,1024]{1,0:T(8,128)(2,1)S(1)}, bf16[128,1024]{1,0:T(8,128)(2,1)S(1)}, u32[]{:S(2)}, u32[]{:S(2)}) collective-permute-start(bf16[128,1024]{1,0:T(8,128)(2,1)S(1)} %constant_dynamic-update-slice_fusion.2.refs_4_), channel_id=1, source_target_pairs={{0,1},{1,0},{2,3},{3,2},{4,5},{5,4},{6,7},{7,6},{8,9},{9,8},{10,11... | collective-permute-start | bytes 786440 | tf_op jit(solution)/shard_map/ppermute | solution.py:197
  15.5 3.6 %collective-permute-start.4 = (s32[8,128]{1,0:T(8,128)S(1)}, s32[8,128]{1,0:T(8,128)S(1)}, u32[]{:S(2)}, u32[]{:S(2)}) collective-permute-start(s32[8,128]{1,0:T(8,128)S(1)} %pad_add_fusion), channel_id=1, source_target_pairs={{0,8},{4,12},{8,0},{12,4},{16,24},{20,28},{24,16},{28,20},{1,9},{5... | collective-permute-start | bytes 12296 | tf_op jit(solution)/shard_map/ppermute | solution.py:197
  19.1 1.2 %collective-permute-start.5 = (s32[16,128]{1,0:T(8,128)S(1)}, s32[16,128]{1,0:T(8,128)S(1)}, u32[]{:S(2)}, u32[]{:S(2)}) collective-permute-start(s32[16,128]{1,0:T(8,128)S(1)} %constant_dynamic-update-slice_fusion.refs_2_), channel_id=1, source_target_pairs={{0,4},{4,0},{8,12},{12,8},{16,20},{20,16},{24,28},{28,24},{1,5},{5... | collective-permute-start | bytes 24584 | tf_op jit(solution)/shard_map/ppermute | solution.py:197
  19.1 6.5 %collective-permute-start.7 = (bf16[128,1024]{1,0:T(8,128)(2,1)S(1)}, bf16[128,1024]{1,0:T(8,128)(2,1)S(1)}, u32[]{:S(2)}, u32[]{:S(2)}) collective-permute-start(bf16[128,1024]{1,0:T(8,128)(2,1)S(1)} %constant_dynamic-update-slice_fusion.2.refs_4_), channel_id=1, source_target_pairs={{0,4},{4,0},{8,12},{12,8},{16,20},{20,16},{24,28},{28,24},{1,5},{5... | collective-permute-start | bytes 786440 | tf_op jit(solution)/shard_map/ppermute | solution.py:197
  24.9 1.5 %collective-permute-start.11 = (bf16[128,1024]{1,0:T(8,128)(2,1)S(1)}, bf16[128,1024]{1,0:T(8,128)(2,1)S(1)}, u32[]{:S(2)}, u32[]{:S(2)}) collective-permute-start(bf16[128,1024]{1,0:T(8,128)(2,1)S(1)} %collective-permute-done.10.refs_8_), channel_id=1, source_target_pairs={{0,4},{4,0},{8,12},{12,8},{16,20},{20,16},{24,28},{28,24},{1,5},{5... | collective-permute-start | bytes 786440 | tf_op jit(solution)/shard_map/ppermute | solution.py:197
  25.0 1.8 %collective-permute-start.9 = (bf16[128,1024]{1,0:T(8,128)(2,1)S(1)}, bf16[128,1024]{1,0:T(8,128)(2,1)S(1)}, u32[]{:S(2)}, u32[]{:S(2)}) collective-permute-start(bf16[128,1024]{1,0:T(8,128)(2,1)S(1)} %collective-permute-done.8.refs_6_), channel_id=1, source_target_pairs={{0,4},{4,0},{8,12},{12,8},{16,20},{20,16},{24,28},{28,24},{1,5},{5... | collective-permute-start | bytes 786440 | tf_op jit(solution)/shard_map/ppermute | solution.py:197
  25.5 1.8 %collective-permute-start.12 = (bf16[128,1024]{1,0:T(8,128)(2,1)S(1)}, bf16[128,1024]{1,0:T(8,128)(2,1)S(1)}, u32[]{:S(2)}, u32[]{:S(2)}) collective-permute-start(bf16[128,1024]{1,0:T(8,128)(2,1)S(1)} %collective-permute-done.6.refs_10_), channel_id=1, source_target_pairs={{0,4},{4,0},{8,12},{12,8},{16,20},{20,16},{24,28},{28,24},{1,5},{5... | collective-permute-start | bytes 786440 | tf_op jit(solution)/shard_map/ppermute | solution.py:197
  25.6 1.7 %copy-start = (s32[1024]{0:T(1024)S(1)}, s32[1024]{0:T(1024)}, u32[]{:S(2)}) copy-start(s32[1024]{0:T(1024)} %param.5) | copy-start | bytes 12292

commit v11 on v10

--- a/solution.py
+++ b/solution.py
@@ -10,6 +10,12 @@
 logistic_sharpness = 0.02
 half_scale = 0.5 / logistic_sharpness
 masked = -1e30
+
+
+def aligned(start, size):
+    if isinstance(start, int):
+        return slice(start, start + size)
+    return pl.ds(pl.multiple_of(start, size), size)
 
 
 def lookup(table_ref, ids):
@@ -53,17 +59,17 @@
             target_ref[:, pl.ds(pl.multiple_of(start, 128), 128)] = found
 
     def score_chunk(anchors, start, buffer, chunk, picked):
-        row = pl.multiple_of(chunk * row_chunk, row_chunk)
+        row = chunk * row_chunk
         scores = half_scale * lax.dot_general(
-            embed_ref[pl.ds(row, row_chunk), :],
+            embed_ref[aligned(row, row_chunk), :],
             anchors,
             (((1,), (1,)), ((), ())),
             preferred_element_type=jnp.float32,
         )
-        score_ref[buffer, pl.ds(row, row_chunk), :] = scores
+        score_ref[buffer, aligned(row, row_chunk), :] = scores
         picked = list(picked)
         for half in range(pair):
-            targets = target_ref[:, pl.ds(pl.multiple_of(start + half * 128, 128), 128)]
+            targets = target_ref[:, aligned(start + half * 128, 128)]
             near = (targets - row) >> 3
             sub = targets & 7
             for step in range(row_chunk // 8):
@@ -73,11 +79,11 @@
         return tuple(picked)
 
     def rank_chunk(pos, buffer, chunk, sums):
-        row = pl.multiple_of(chunk * row_chunk, row_chunk)
+        row = chunk * row_chunk
         sums = list(sums)
         for half in range(pair):
             for part in range(row_chunk // 32):
-                scores = score_ref[buffer, pl.ds(row + part * 32, 32), half * 128 : (half + 1) * 128]
+                scores = score_ref[buffer, aligned(row + part * 32, 32), half * 128 : (half + 1) * 128]
                 scores = scores.reshape(4, 8, 128)
                 for m in range(pos_count):
                     at = half * pos_count + m
@@ -96,13 +102,13 @@
     zero = (jnp.zeros((8, 128), jnp.float32),) * (2 * pos_count * pair)
 
     def split(start, buffer, picked):
-        inside = (buffer, pl.ds(start, lane_block), slice(None))
+        inside = (buffer, aligned(start, lane_block), slice(None))
         index = lax.broadcasted_iota(jnp.int32, (lane_block, lane_block), 0)
         lane = lax.broadcasted_iota(jnp.int32, (lane_block, lane_block), 1)
         score_ref[inside] = jnp.where(index == lane, masked, score_ref[inside])
         pos = []
         for half in range(pair):
-            lanes = pl.ds(pl.multiple_of(start + half * 128, 128), 128)
+            lanes = aligned(start + half * 128, 128)
             own_ref[:, lanes] = score_ref[buffer, 0:shard, half * 128 : (half + 1) * 128]
             stat_ref[0:8, lanes] = picked[half]
             for m in range(pos_count):
@@ -111,7 +117,7 @@
 
     def finish(start, sums):
         for half in range(pair):
-            lanes = pl.ds(pl.multiple_of(start + half * 128, 128), 128)
+            lanes = aligned(start + half * 128, 128)
             for m in range(pos_count):
                 at = (half * pos_count + m) * 2
                 stat_ref[8 + m : 9 + m, lanes] = jnp.sum(sums[at], axis=0, keepdims=True)
@@ -121,10 +127,10 @@
     picked = over_chunks(lambda chunk, have: score_chunk(first, 0, 0, chunk, have), nothing)
 
     def block_step(block, pos):
-        start = pl.multiple_of(block * lane_block, lane_block)
-        buffer = lax.rem(block, 2)
-        following = pl.multiple_of(start + lane_block, lane_block)
-        anchors = embed_ref[pl.ds(following, lane_block), :]
+        start = block * lane_block
+        following = start + lane_block
+        buffer = block % 2
+        anchors = embed_ref[aligned(following, lane_block), :]
 
         def both(chunk, carry):
             picked, sums = carry
@@ -136,7 +142,12 @@
         return split(following, 1 - buffer, picked)
 
     last = total // lane_block - 1
-    pos = lax.fori_loop(0, last, block_step, split(0, 0, picked))
+    pos = split(0, 0, picked)
+    if chunks == 1:
+        for block in range(last):
+            pos = block_step(block, pos)
+    else:
+        pos = lax.fori_loop(0, last, block_step, pos)
     sums = over_chunks(lambda chunk, have: rank_chunk(pos, last % 2, chunk, have), zero)
     finish(last * lane_block, sums)
 
@@ -210,19 +221,25 @@
         return jnp.concatenate([ids, swap(ids, "row", 2 * bit)], axis=0)
 
     line = [swap(embed, "row", 2 * d) for d in range(1, levels)]
+    far = cols - 1
     ids = spread(positives.T)
-    line, ids = lax.optimization_barrier((line, ids))
-    tall = join([embed] + line)
-
-    plane = {p: swap(tall, "col", p) for p in range(1, cols)}
+    tall = jnp.concatenate([embed, jnp.zeros(((levels - 1) * shard, width), embed.dtype)], axis=0)
+    tall = lax.optimization_barrier(tall)
+    early = swap(tall[:shard], "col", far)
+    line, ids, early, tall = lax.optimization_barrier((line, ids, early, tall))
+    for d in range(1, levels):
+        tall = lax.dynamic_update_slice(tall, line[d - 1], (d * shard, 0))
+
+    plane = {0: tall}
+    plane.update({p: swap(tall, "col", p) for p in range(1, far)})
+    plane[far] = swap(tall[shard:], "col", far)
     while steps:
         ids = spread(ids)
-    other = {0: swap(tall, "row", 1)}
+    plane, ids, early = lax.optimization_barrier((plane, ids, early))
+
+    plane[far] = join([early, plane[far]])
     ids = (ids, swap(ids, "row", 1))
-    ids, plane[cols - 1] = lax.optimization_barrier((ids, plane[cols - 1]))
-
-    plane[0] = tall
-    other.update({p: swap(plane[p], "row", 1) for p in range(1, cols)})
+    other = {p: swap(plane[p], "row", 1) for p in range(cols)}
     pieces = []
     layout = []
     for p in range(cols):

time: 35.1 us -> 36.4 us (1.037)
  starting transfers between devices: 12.7 us -> 16.4 us
  waiting for transfers between devices: 13.5 us -> 11.4 us
  Pallas kernels: 7.77 us -> 7.28 us
    ppermute x13 -> x14, starting transfers between devices: 12.7 us -> 16.4 us  [swap(): return lax.ppermute(array, axis, [(i, i ^ mask) for i in range(size)])]
    ppermute x13 -> x14, waiting for transfers between devices: 13.5 us -> 11.4 us  [swap(): return lax.ppermute(array, axis, [(i, i ^ mask) for i in range(size)])]
    concatenate x1, local copies, waits for them, and re-layouts: 0.01 us -> 0.89 us  [body(): jnp.concatenate([embed, jnp.zeros(((levels - 1) * shard, width), embed.dt...]
    unnamed x8 -> x5, local copies, waits for them, and re-layouts: 0.86 us -> 0.02 us
    pallas_call x1, Pallas kernels: 7.77 us -> 7.28 us  [body(): pl.pallas_call(functools.partial(kernel, cols, order, shard, pos_count, l...]
  transfers between devices with their start and end apart: 13 -> 14, of which waited for: 10 -> 5; matrix products, arithmetic and copies ran while one was open for 3% -> 3% of each run, Pallas kernels for 0% -> 0%
where the time goes in v11:
time: 36.4 us; the launch traced here: 36.2 us
  starting transfers between devices  16.4 us (45%)
  waiting for transfers between devices  11.4 us (31%)
  Pallas kernels  7.28 us (20%)
  local copies, waits for them, and re-layouts  0.96 us (3%)
    ppermute x14, starting transfers between devices, swap(): return lax.ppermute(array, axis, [(i, i ^ mask) for i in range(size)])  16.4 us
    ppermute x14, waiting for transfers between devices, swap(): return lax.ppermute(array, axis, [(i, i ^ mask) for i in range(size)])  11.4 us
    pallas_call x1, Pallas kernels, body(): pl.pallas_call(functools.partial(kernel, cols, order, shard, pos_count, l...  7.28 us
    concatenate x1, local copies, waits for them, and re-layouts, body(): jnp.concatenate([embed, jnp.zeros(((levels - 1) * shard, width), embed.dt...  0.89 us
  transfers between devices with their start and end apart: 14, of which 5 were waited for; matrix products, arithmetic and copies ran while one was open for 3% of the time, Pallas kernels for 0%

profile of v11, /device:TPU:0, one launch (start us, length us, event | category | flops | bytes accessed | tf_op | source)
XLA Modules:
  0.0 36.2 jit_solution(5006987587566463819)
XLA Ops:
  0.0 4.0 %collective-permute-start.3 = (s32[4,128]{1,0:T(4,128)}, s32[4,128]{1,0:T(4,128)S(1)}, u32[]{:S(2)}, u32[]{:S(2)}) collective-permute-start(s32[4,128]{1,0:T(4,128)} %bitcast.5), channel_id=1, source_target_pairs={{0,16},{4,20},{8,24},{12,28},{16,0},{20,4},{24,8},{28,12},{1,17},{... | collective-permute-start | bytes 6152 | tf_op jit(solution)/shard_map/ppermute | solution.py:208
  4.0 0.0 collective-permute-start.1
  4.1 1.9 %collective-permute-start = (bf16[32,1024]{1,0:T(8,128)(2,1)}, bf16[32,1024]{1,0:T(8,128)(2,1)S(1)}, u32[]{:S(2)}, u32[]{:S(2)}) collective-permute-start(bf16[32,1024]{1,0:T(8,128)(2,1)} %param.3), channel_id=1, source_target_pairs={{0,8},{4,12},{8,0},{12,4},{16,24},{20,28},{24,16},{28,20},{1,9},{5... | collective-permute-start | bytes 196616 | tf_op jit(solution)/shard_map/ppermute | solution.py:208
  6.0 2.5 %collective-permute-start.2 = (bf16[32,1024]{1,0:T(8,128)(2,1)}, bf16[32,1024]{1,0:T(8,128)(2,1)S(1)}, u32[]{:S(2)}, u32[]{:S(2)}) collective-permute-start(bf16[32,1024]{1,0:T(8,128)(2,1)} %param.3), channel_id=1, source_target_pairs={{0,24},{4,28},{8,16},{12,20},{16,8},{20,12},{24,0},{28,4},{1,25},{... | collective-permute-start | bytes 196616 | tf_op jit(solution)/shard_map/ppermute | solution.py:208
  8.4 0.9 %concatenate.13 = bf16[128,1024]{1,0:T(8,128)(2,1)S(1)} pad(bf16[32,1024]{1,0:T(8,128)(2,1)} %param.3, bf16[]{:T(256)} %constant.8.clone.1), padding=0_96x0_0 | pad | bytes 327682 | tf_op jit(solution)/shard_map/concatenate | solution.py:226
  9.3 0.0 copy-start.1
  9.3 2.5 %collective-permute-start.4 = (bf16[32,1024]{1,0:T(8,128)(2,1)S(1)}, bf16[32,1024]{1,0:T(8,128)(2,1)S(1)}, u32[]{:S(2)}, u32[]{:S(2)}) collective-permute-start(bf16[32,1024]{1,0:T(8,128)(2,1)S(1)} %slice.8), channel_id=1, source_target_pairs={{0,3},{1,2},{2,1},{3,0},{4,7},{5,6},{6,5},{7,4},{8,11},{9,10},{10,... | collective-permute-start | bytes 196616 | tf_op jit(solution)/shard_map/ppermute | solution.py:208
  11.9 0.0 collective-permute-done.3
  11.9 0.0 copy-done.1
  11.9 0.0 collective-permute-done.1
  11.9 0.0 collective-permute-done
  11.9 0.8 %collective-permute-done.2 = bf16[32,1024]{1,0:T(8,128)(2,1)S(1)} collective-permute-done((bf16[32,1024]{1,0:T(8,128)(2,1)}, bf16[32,1024]{1,0:T(8,128)(2,1)S(1)}, u32[]{:S(2)}, u32[]{:S(2)}) %collective-permute-start.2) | collective-permute-done | bytes 65568 | tf_op jit(solution)/shard_map/ppermute | solution.py:208
  12.7 1.9 %collective-permute-done.4 = bf16[32,1024]{1,0:T(8,128)(2,1)S(1)} collective-permute-done((bf16[32,1024]{1,0:T(8,128)(2,1)S(1)}, bf16[32,1024]{1,0:T(8,128)(2,1)S(1)}, u32[]{:S(2)}, u32[]{:S(2)}) %collective-permute-start.4) | collective-permute-done | bytes 65568 | tf_op jit(solution)/shard_map/ppermute | solution.py:208
  14.6 1.6 %collective-permute-start.6 = (bf16[128,1024]{1,0:T(8,128)(2,1)S(1)}, bf16[128,1024]{1,0:T(8,128)(2,1)S(1)}, u32[]{:S(2)}, u32[]{:S(2)}) collective-permute-start(bf16[128,1024]{1,0:T(8,128)(2,1)S(1)} %constant_dynamic-update-slice_fusion.2.refs_4_), channel_id=1, source_target_pairs={{0,2},{1,3},{2,0},{3,1},{4,6},{5,7},{6,4},{7,5},{8,10},{9,11},{10,... | collective-permute-start | bytes 786440 | tf_op jit(solution)/shard_map/ppermute | solution.py:208
  16.2 1.5 %collective-permute-start.5 = (bf16[128,1024]{1,0:T(8,128)(2,1)S(1)}, bf16[128,1024]{1,0:T(8,128)(2,1)S(1)}, u32[]{:S(2)}, u32[]{:S(2)}) collective-permute-start(bf16[128,1024]{1,0:T(8,128)(2,1)S(1)} %constant_dynamic-update-slice_fusion.2.refs_4_), channel_id=1, source_target_pairs={{0,1},{1,0},{2,3},{3,2},{4,5},{5,4},{6,7},{7,6},{8,9},{9,8},{10,11... | collective-permute-start | bytes 786440 | tf_op jit(solution)/shard_map/ppermute | solution.py:208
  17.7 0.5 %collective-permute-start.7 = (bf16[96,1024]{1,0:T(8,128)(2,1)S(1)}, bf16[96,1024]{1,0:T(8,128)(2,1)S(1)}, u32[]{:S(2)}, u32[]{:S(2)}) collective-permute-start(bf16[96,1024]{1,0:T(8,128)(2,1)S(1)} %slice.9), channel_id=1, source_target_pairs={{0,3},{1,2},{2,1},{3,0},{4,7},{5,6},{6,5},{7,4},{8,11},{9,10},{10,... | collective-permute-start | bytes 589832 | tf_op jit(solution)/shard_map/ppermute | solution.py:208
  18.2 0.7 %collective-permute-start.8 = (s32[8,128]{1,0:T(8,128)S(1)}, s32[8,128]{1,0:T(8,128)S(1)}, u32[]{:S(2)}, u32[]{:S(2)}) collective-permute-start(s32[8,128]{1,0:T(8,128)S(1)} %pad_add_fusion.1), channel_id=1, source_target_pairs={{0,8},{4,12},{8,0},{12,4},{16,24},{20,28},{24,16},{28,20},{1,9},{5... | collective-permute-start | bytes 12296 | tf_op jit(solution)/shard_map/ppermute | solution.py:208
  18.9 2.9 %collective-permute-done.8 = s32[8,128]{1,0:T(8,128)S(1)} collective-permute-done((s32[8,128]{1,0:T(8,128)S(1)}, s32[8,128]{1,0:T(8,128)S(1)}, u32[]{:S(2)}, u32[]{:S(2)}) %collective-permute-start.8) | collective-permute-done | bytes 4128 | tf_op jit(solution)/shard_map/ppermute | solution.py:208
  21.9 4.3 %collective-permute-done.7 = bf16[96,1024]{1,0:T(8,128)(2,1)S(1)} collective-permute-done((bf16[96,1024]{1,0:T(8,128)(2,1)S(1)}, bf16[96,1024]{1,0:T(8,128)(2,1)S(1)}, u32[]{:S(2)}, u32[]{:S(2)}) %collective-permute-start.7) | collective-permute-done | bytes 196640 | tf_op jit(solution)/shard_map/ppermute | solution.py:208
  26.1 0.0 collective-permute-done.6.refs_8_
  26.1 0.0 collective-permute-done.5.refs_6_
  26.2 0.1 collective-permute-start.13
  26.3 0.5 %collective-permute-start.10 = (bf16[128,1024]{1,0:T(8,128)(2,1)S(1)}, bf16[128,1024]{1,0:T(8,128)(2,1)S(1)}, u32[]{:S(2)}, u32[]{:S(2)}) collective-permute-start(bf16[128,1024]{1,0:T(8,128)(2,1)S(1)} %constant_dynamic-update-slice_fusion.2.refs_4_), channel_id=1, source_target_pairs={{0,4},{4,0},{8,12},{12,8},{16,20},{20,16},{24,28},{28,24},{1,5},{5... | collective-permute-start | bytes 786440 | tf_op jit(solution)/shard_map/ppermute | solution.py:208
  26.8 0.1 collective-permute-start.11
  26.8 0.4 %collective-permute-start.12 = (bf16[128,1024]{1,0:T(8,128)(2,1)S(1)}, bf16[128,1024]{1,0:T(8,128)(2,1)S(1)}, u32[]{:S(2)}, u32[]{:S(2)}) collective-permute-start(bf16[128,1024]{1,0:T(8,128)(2,1)S(1)} %collective-permute-done.6.refs_8_), channel_id=1, source_target_pairs={{0,4},{4,0},{8,12},{12,8},{16,20},{20,16},{24,28},{28,24},{1,5},{5... | collective-permute-start | bytes 786440 | tf_op jit(solution)/shard_map/ppermute | solution.py:208
  27.3 0.0 copy-start
  27.3 0.1 collective-permute-start.9
  27.3 0.1 pad_add_fusion.2.refs_0_
  27.4 1.5 %collective-permute-done.9.refs_3_ = s32[16,128]{1,0:T(8,128)S(1)} collective-permute-done((s32[16,128]{1,0:T(8,128)S(1)}, s32[16,128]{1,0:T(8,128)S(1)}, u32[]{:S(2)}, u32[]{:S(2)}) %collective-permute-start.9) | collective-permute-done | bytes 8224 | tf_op jit(solution)/shard_map/ppermute | solution.py:208
  28.9 0.0 collective-permute-done.13.refs_11_
  28.9 0.0 collective-permute-done.10.refs_5_
  28.9 0.0 collective-permute-done.11.refs_7_
  28.9 0.0 collective-permute-done.12.refs_9_
  28.9 0.0 copy-done
  29.0 7.3 %shard_map.37 = f32[32,1024]{1,0:T(8,128)} custom-call(s32[2]{0:T(128)S(1)} %pad_add_fusion.2.refs_0_, s32[8,128]{1,0:T(8,128)S(1)} %bitcast.4, s32[16,128]{1,0:T(8,128)S(1)} %pad_add_fusion.refs_2_, s32[16,128]{1,0:T(8,128)S(1)} %collective-permute-done.9.refs_3_, bf16[128,1024]{1,0:T(8,128)(2,1)S(1)} %constant_dynamic-update-slice_fusion.2.refs_4_, ...), custom_call_target="tpu_custom_call" | custom-call | flops 2147483648 | bytes 2097152 | tf_op jit(solution)/shard_map/pallas_call | solution.py:252
  (9 shorter events, 0.1 us)
Async XLA Ops:
  0.0 11.9 %collective-permute-start.3 = (s32[4,128]{1,0:T(4,128)}, s32[4,128]{1,0:T(4,128)S(1)}, u32[]{:S(2)}, u32[]{:S(2)}) collective-permute-start(s32[4,128]{1,0:T(4,128)} %bitcast.5), channel_id=1, source_target_pairs={{0,16},{4,20},{8,24},{12,28},{16,0},{20,4},{24,8},{28,12},{1,17},{... | collective-permute-start | bytes 6152 | tf_op jit(solution)/shard_map/ppermute | solution.py:208
  4.0 7.8 %collective-permute-start.1 = (bf16[32,1024]{1,0:T(8,128)(2,1)}, bf16[32,1024]{1,0:T(8,128)(2,1)S(1)}, u32[]{:S(2)}, u32[]{:S(2)}) collective-permute-start(bf16[32,1024]{1,0:T(8,128)(2,1)} %param.3), channel_id=1, source_target_pairs={{0,16},{4,20},{8,24},{12,28},{16,0},{20,4},{24,8},{28,12},{1,17},{... | collective-permute-start | bytes 196616 | tf_op jit(solution)/shard_map/ppermute | solution.py:208
  4.1 7.8 %collective-permute-start = (bf16[32,1024]{1,0:T(8,128)(2,1)}, bf16[32,1024]{1,0:T(8,128)(2,1)S(1)}, u32[]{:S(2)}, u32[]{:S(2)}) collective-permute-start(bf16[32,1024]{1,0:T(8,128)(2,1)} %param.3), channel_id=1, source_target_pairs={{0,8},{4,12},{8,0},{12,4},{16,24},{20,28},{24,16},{28,20},{1,9},{5... | collective-permute-start | bytes 196616 | tf_op jit(solution)/shard_map/ppermute | solution.py:208
  6.0 6.7 %collective-permute-start.2 = (bf16[32,1024]{1,0:T(8,128)(2,1)}, bf16[32,1024]{1,0:T(8,128)(2,1)S(1)}, u32[]{:S(2)}, u32[]{:S(2)}) collective-permute-start(bf16[32,1024]{1,0:T(8,128)(2,1)} %param.3), channel_id=1, source_target_pairs={{0,24},{4,28},{8,16},{12,20},{16,8},{20,12},{24,0},{28,4},{1,25},{... | collective-permute-start | bytes 196616 | tf_op jit(solution)/shard_map/ppermute | solution.py:208
  9.3 2.5 %copy-start.1 = (s32[128,4]{0,1:T(4,128)S(1)}, s32[128,4]{0,1:T(4,128)}, u32[]{:S(2)}) copy-start(s32[128,4]{0,1:T(4,128)} %param.4) | copy-start | bytes 6148
  9.3 5.2 %collective-permute-start.4 = (bf16[32,1024]{1,0:T(8,128)(2,1)S(1)}, bf16[32,1024]{1,0:T(8,128)(2,1)S(1)}, u32[]{:S(2)}, u32[]{:S(2)}) collective-permute-start(bf16[32,1024]{1,0:T(8,128)(2,1)S(1)} %slice.8), channel_id=1, source_target_pairs={{0,3},{1,2},{2,1},{3,0},{4,7},{5,6},{6,5},{7,4},{8,11},{9,10},{10,... | collective-permute-start | bytes 196616 | tf_op jit(solution)/shard_map/ppermute | solution.py:208
  14.6 11.5 %collective-permute-start.6 = (bf16[128,1024]{1,0:T(8,128)(2,1)S(1)}, bf16[128,1024]{1,0:T(8,128)(2,1)S(1)}, u32[]{:S(2)}, u32[]{:S(2)}) collective-permute-start(bf16[128,1024]{1,0:T(8,128)(2,1)S(1)} %constant_dynamic-update-slice_fusion.2.refs_4_), channel_id=1, source_target_pairs={{0,2},{1,3},{2,0},{3,1},{4,6},{5,7},{6,4},{7,5},{8,10},{9,11},{10,... | collective-permute-start | bytes 786440 | tf_op jit(solution)/shard_map/ppermute | solution.py:208
  16.2 10.0 %collective-permute-start.5 = (bf16[128,1024]{1,0:T(8,128)(2,1)S(1)}, bf16[128,1024]{1,0:T(8,128)(2,1)S(1)}, u32[]{:S(2)}, u32[]{:S(2)}) collective-permute-start(bf16[128,1024]{1,0:T(8,128)(2,1)S(1)} %constant_dynamic-update-slice_fusion.2.refs_4_), channel_id=1, source_target_pairs={{0,1},{1,0},{2,3},{3,2},{4,5},{5,4},{6,7},{7,6},{8,9},{9,8},{10,11... | collective-permute-start | bytes 786440 | tf_op jit(solution)/shard_map/ppermute | solution.py:208
  17.7 8.4 %collective-permute-start.7 = (bf16[96,1024]{1,0:T(8,128)(2,1)S(1)}, bf16[96,1024]{1,0:T(8,128)(2,1)S(1)}, u32[]{:S(2)}, u32[]{:S(2)}) collective-permute-start(bf16[96,1024]{1,0:T(8,128)(2,1)S(1)} %slice.9), channel_id=1, source_target_pairs={{0,3},{1,2},{2,1},{3,0},{4,7},{5,6},{6,5},{7,4},{8,11},{9,10},{10,... | collective-permute-start | bytes 589832 | tf_op jit(solution)/shard_map/ppermute | solution.py:208
  18.2 3.6 %collective-permute-start.8 = (s32[8,128]{1,0:T(8,128)S(1)}, s32[8,128]{1,0:T(8,128)S(1)}, u32[]{:S(2)}, u32[]{:S(2)}) collective-permute-start(s32[8,128]{1,0:T(8,128)S(1)} %pad_add_fusion.1), channel_id=1, source_target_pairs={{0,8},{4,12},{8,0},{12,4},{16,24},{20,28},{24,16},{28,20},{1,9},{5... | collective-permute-start | bytes 12296 | tf_op jit(solution)/shard_map/ppermute | solution.py:208
  26.2 2.7 %collective-permute-start.13 = (bf16[128,1024]{1,0:T(8,128)(2,1)S(1)}, bf16[128,1024]{1,0:T(8,128)(2,1)S(1)}, u32[]{:S(2)}, u32[]{:S(2)}) collective-permute-start(bf16[128,1024]{1,0:T(8,128)(2,1)S(1)} %constant_dynamic-update-slice_fusion.refs_10_), channel_id=1, source_target_pairs={{0,4},{4,0},{8,12},{12,8},{16,20},{20,16},{24,28},{28,24},{1,5},{5... | collective-permute-start | bytes 786440 | tf_op jit(solution)/shard_map/ppermute | solution.py:208
  26.3 2.7 %collective-permute-start.10 = (bf16[128,1024]{1,0:T(8,128)(2,1)S(1)}, bf16[128,1024]{1,0:T(8,128)(2,1)S(1)}, u32[]{:S(2)}, u32[]{:S(2)}) collective-permute-start(bf16[128,1024]{1,0:T(8,128)(2,1)S(1)} %constant_dynamic-update-slice_fusion.2.refs_4_), channel_id=1, source_target_pairs={{0,4},{4,0},{8,12},{12,8},{16,20},{20,16},{24,28},{28,24},{1,5},{5... | collective-permute-start | bytes 786440 | tf_op jit(solution)/shard_map/ppermute | solution.py:208
  26.8 2.2 %collective-permute-start.11 = (bf16[128,1024]{1,0:T(8,128)(2,1)S(1)}, bf16[128,1024]{1,0:T(8,128)(2,1)S(1)}, u32[]{:S(2)}, u32[]{:S(2)}) collective-permute-start(bf16[128,1024]{1,0:T(8,128)(2,1)S(1)} %collective-permute-done.5.refs_6_), channel_id=1, source_target_pairs={{0,4},{4,0},{8,12},{12,8},{16,20},{20,16},{24,28},{28,24},{1,5},{5... | collective-permute-start | bytes 786440 | tf_op jit(solution)/shard_map/ppermute | solution.py:208
  26.8 2.1 %collective-permute-start.12 = (bf16[128,1024]{1,0:T(8,128)(2,1)S(1)}, bf16[128,1024]{1,0:T(8,128)(2,1)S(1)}, u32[]{:S(2)}, u32[]{:S(2)}) collective-permute-start(bf16[128,1024]{1,0:T(8,128)(2,1)S(1)} %collective-permute-done.6.refs_8_), channel_id=1, source_target_pairs={{0,4},{4,0},{8,12},{12,8},{16,20},{20,16},{24,28},{28,24},{1,5},{5... | collective-permute-start | bytes 786440 | tf_op jit(solution)/shard_map/ppermute | solution.py:208
  27.3 1.7 %copy-start = (s32[1024]{0:T(1024)S(1)}, s32[1024]{0:T(1024)}, u32[]{:S(2)}) copy-start(s32[1024]{0:T(1024)} %param.5) | copy-start | bytes 12292
  27.3 1.6 %collective-permute-start.9 = (s32[16,128]{1,0:T(8,128)S(1)}, s32[16,128]{1,0:T(8,128)S(1)}, u32[]{:S(2)}, u32[]{:S(2)}) collective-permute-start(s32[16,128]{1,0:T(8,128)S(1)} %pad_add_fusion.refs_2_), channel_id=1, source_target_pairs={{0,4},{4,0},{8,12},{12,8},{16,20},{20,16},{24,28},{28,24},{1,5},{5... | collective-permute-start | bytes 24584 | tf_op jit(solution)/shard_map/ppermute | solution.py:208

commit v12 on v11

--- a/solution.py
+++ b/solution.py
@@ -40,9 +40,12 @@
     pair = lane_block // 128
     row_chunk = min(1024, total)
 
-    for piece, slots in zip(pieces, layout):
-        for spot, slot in enumerate(slots):
-            embed_ref[slot * shard : (slot + 1) * shard, :] = piece[spot * shard : (spot + 1) * shard, :]
+    for piece, (c, p) in zip(pieces, layout):
+        for z in range(levels):
+            start = (((z ^ place_ref[2]) * 2 + c) * cols + p) * shard
+            embed_ref[pl.ds(pl.multiple_of(start, shard), shard), :] = piece[
+                z * shard : (z + 1) * shard, :
+            ]
 
     group = cols * shard
     for line in range(2 * levels):
@@ -220,34 +223,28 @@
         order.extend([d ^ bit for d in order])
         return jnp.concatenate([ids, swap(ids, "row", 2 * bit)], axis=0)
 
-    line = [swap(embed, "row", 2 * d) for d in range(1, levels)]
-    far = cols - 1
+    lines = [[2 * d + c for d in range(levels)] for c in range(2)]
     ids = spread(positives.T)
-    tall = jnp.concatenate([embed, jnp.zeros(((levels - 1) * shard, width), embed.dtype)], axis=0)
-    tall = lax.optimization_barrier(tall)
-    early = swap(tall[:shard], "col", far)
-    line, ids, early, tall = lax.optimization_barrier((line, ids, early, tall))
-    for d in range(1, levels):
-        tall = lax.dynamic_update_slice(tall, line[d - 1], (d * shard, 0))
+    tall = lax.all_gather(embed, "row", axis_index_groups=lines, axis=0, tiled=True)
+    tall, ids = lax.optimization_barrier((tall, ids))
 
     plane = {0: tall}
-    plane.update({p: swap(tall, "col", p) for p in range(1, far)})
-    plane[far] = swap(tall[shard:], "col", far)
+    plane.update({p: swap(tall, "col", p) for p in range(1, cols)})
     while steps:
         ids = spread(ids)
-    plane, ids, early = lax.optimization_barrier((plane, ids, early))
-
-    plane[far] = join([early, plane[far]])
+    plane, ids = lax.optimization_barrier((plane, ids))
+
     ids = (ids, swap(ids, "row", 1))
-    other = {p: swap(plane[p], "row", 1) for p in range(cols)}
     pieces = []
     layout = []
     for p in range(cols):
-        for c, part in enumerate((plane[p], other[p])):
+        for c, part in enumerate((plane[p], swap(plane[p], "row", 1))):
             pieces.append(part)
-            layout.append([(d * 2 + c) * cols + p for d in range(levels)])
-
-    place = jnp.stack([lax.axis_index(axes) * shard, lax.axis_index("col") * shard])
+            layout.append((c, p))
+
+    place = jnp.stack(
+        [lax.axis_index(axes) * shard, lax.axis_index("col") * shard, lax.axis_index("row") // 2]
+    )
     vmem = pl.BlockSpec(memory_space=pltpu.VMEM)
     return pl.pallas_call(
         functools.partial(kernel, cols, order, shard, pos_count, lane_block, layout),

time: 36.4 us -> 40.3 us (1.11)
  blocking collectives: 0 us -> 14.7 us
  starting transfers between devices: 16.4 us -> 8.62 us
  waiting for transfers between devices: 11.4 us -> 8.97 us
  local copies, waits for them, and re-layouts: 0.96 us -> 0.01 us
    all_gather x0 -> x1, blocking collectives: none -> 14.7 us  [body(): lax.all_gather(embed, 'row', axis_index_groups=lines, axis=0, tiled=True)]
    ppermute x14 -> x10, starting transfers between devices: 16.4 us -> 8.62 us  [swap(): return lax.ppermute(array, axis, [(i, i ^ mask) for i in range(size)])]
    ppermute x14 -> x10, waiting for transfers between devices: 11.4 us -> 8.97 us  [swap(): return lax.ppermute(array, axis, [(i, i ^ mask) for i in range(size)])]
    concatenate x2 -> x0, local copies, waits for them, and re-layouts: 0.91 us -> none  [the longest x1 0.89 us: body(): jnp.concatenate([embed, jnp.zeros(((levels - 1) * shard, width), embed.dt...]
  transfers between devices with their start and end apart: 14 -> 10, of which waited for: 5 -> 5; matrix products, arithmetic and copies ran while one was open for 3% -> 0% of each run, Pallas kernels for 0% -> 0%
where the time goes in v12:
time: 40.3 us; the launch traced here: 40.1 us
  blocking collectives  14.7 us (36%)
  waiting for transfers between devices  8.97 us (22%)
  starting transfers between devices  8.62 us (21%)
  Pallas kernels  7.67 us (19%)
    all_gather x1, blocking collectives, body(): lax.all_gather(embed, 'row', axis_index_groups=lines, axis=0, tiled=True)  14.7 us
    ppermute x10, waiting for transfers between devices, swap(): return lax.ppermute(array, axis, [(i, i ^ mask) for i in range(size)])  8.97 us
    ppermute x10, starting transfers between devices, swap(): return lax.ppermute(array, axis, [(i, i ^ mask) for i in range(size)])  8.62 us
    pallas_call x1, Pallas kernels, body(): pl.pallas_call(functools.partial(kernel, cols, order, shard, pos_count, l...  7.67 us
  transfers between devices with their start and end apart: 10, of which 5 were waited for; matrix products, arithmetic and copies ran while one was open for 0% of the time, Pallas kernels for 0%

profile of v12, /device:TPU:0, one launch (start us, length us, event | category | flops | bytes accessed | tf_op | source)
XLA Modules:
  0.0 40.1 jit_solution(1063152244639438218)
XLA Ops:
  0.0 0.0 copy-start.1
  0.0 4.0 %collective-permute-start = (s32[4,128]{1,0:T(4,128)}, s32[4,128]{1,0:T(4,128)S(1)}, u32[]{:S(2)}, u32[]{:S(2)}) collective-permute-start(s32[4,128]{1,0:T(4,128)} %bitcast.6), channel_id=1, source_target_pairs={{0,16},{4,20},{8,24},{12,28},{16,0},{20,4},{24,8},{28,12},{1,17},{... | collective-permute-start | bytes 6152 | tf_op jit(solution)/shard_map/ppermute | solution.py:211
  4.0 14.7 %all_gather.3.refs_4_ = bf16[128,1024]{1,0:T(8,128)(2,1)S(1)} all-gather(bf16[32,1024]{1,0:T(8,128)(2,1)} %param.3), channel_id=1, replica_groups={{0,8,16,24},{4,12,20,28},{1,9,17,25},{5,13,21,29},{2,10,18,26},{6,14,22..., dimensions={0}, use_global_device_ids=true | all-gather | bytes 327680 | tf_op jit(solution)/shard_map/all_gather | solution.py:228
  18.8 0.0 collective-permute-done
  18.8 0.0 copy-done.1
  18.8 2.5 %collective-permute-start.3 = (bf16[128,1024]{1,0:T(8,128)(2,1)S(1)}, bf16[128,1024]{1,0:T(8,128)(2,1)S(1)}, u32[]{:S(2)}, u32[]{:S(2)}) collective-permute-start(bf16[128,1024]{1,0:T(8,128)(2,1)S(1)} %all_gather.3.refs_4_), channel_id=1, source_target_pairs={{0,3},{1,2},{2,1},{3,0},{4,7},{5,6},{6,5},{7,4},{8,11},{9,10},{10,... | collective-permute-start | bytes 786440 | tf_op jit(solution)/shard_map/ppermute | solution.py:211
  21.3 0.5 %collective-permute-start.2 = (bf16[128,1024]{1,0:T(8,128)(2,1)S(1)}, bf16[128,1024]{1,0:T(8,128)(2,1)S(1)}, u32[]{:S(2)}, u32[]{:S(2)}) collective-permute-start(bf16[128,1024]{1,0:T(8,128)(2,1)S(1)} %all_gather.3.refs_4_), channel_id=1, source_target_pairs={{0,2},{1,3},{2,0},{3,1},{4,6},{5,7},{6,4},{7,5},{8,10},{9,11},{10,... | collective-permute-start | bytes 786440 | tf_op jit(solution)/shard_map/ppermute | solution.py:211
  21.8 0.5 %collective-permute-start.1 = (bf16[128,1024]{1,0:T(8,128)(2,1)S(1)}, bf16[128,1024]{1,0:T(8,128)(2,1)S(1)}, u32[]{:S(2)}, u32[]{:S(2)}) collective-permute-start(bf16[128,1024]{1,0:T(8,128)(2,1)S(1)} %all_gather.3.refs_4_), channel_id=1, source_target_pairs={{0,1},{1,0},{2,3},{3,2},{4,5},{5,4},{6,7},{7,6},{8,9},{9,8},{10,11... | collective-permute-start | bytes 786440 | tf_op jit(solution)/shard_map/ppermute | solution.py:211
  22.3 0.0 collective-permute-start.4
  22.3 3.6 %collective-permute-done.4 = s32[8,128]{1,0:T(8,128)S(1)} collective-permute-done((s32[8,128]{1,0:T(8,128)S(1)}, s32[8,128]{1,0:T(8,128)S(1)}, u32[]{:S(2)}, u32[]{:S(2)}) %collective-permute-start.4) | collective-permute-done | bytes 4128 | tf_op jit(solution)/shard_map/ppermute | solution.py:211
  25.9 0.9 %collective-permute-done.3.refs_10_ = bf16[128,1024]{1,0:T(8,128)(2,1)S(1)} collective-permute-done((bf16[128,1024]{1,0:T(8,128)(2,1)S(1)}, bf16[128,1024]{1,0:T(8,128)(2,1)S(1)}, u32[]{:S(2)}, u32[]{:S(2)}) %collective-permute-start.3) | collective-permute-done | bytes 262176 | tf_op jit(solution)/shard_map/ppermute | solution.py:211
  26.9 2.7 %collective-permute-done.2.refs_8_ = bf16[128,1024]{1,0:T(8,128)(2,1)S(1)} collective-permute-done((bf16[128,1024]{1,0:T(8,128)(2,1)S(1)}, bf16[128,1024]{1,0:T(8,128)(2,1)S(1)}, u32[]{:S(2)}, u32[]{:S(2)}) %collective-permute-start.2) | collective-permute-done | bytes 262176 | tf_op jit(solution)/shard_map/ppermute | solution.py:211
  29.6 0.1 collective-permute-done.1.refs_6_
  29.7 0.0 collective-permute-start.6
  29.7 0.5 %collective-permute-start.7 = (bf16[128,1024]{1,0:T(8,128)(2,1)S(1)}, bf16[128,1024]{1,0:T(8,128)(2,1)S(1)}, u32[]{:S(2)}, u32[]{:S(2)}) collective-permute-start(bf16[128,1024]{1,0:T(8,128)(2,1)S(1)} %collective-permute-done.1.refs_6_), channel_id=1, source_target_pairs={{0,4},{4,0},{8,12},{12,8},{16,20},{20,16},{24,28},{28,24},{1,5},{5... | collective-permute-start | bytes 786440 | tf_op jit(solution)/shard_map/ppermute | solution.py:211
  30.2 0.0 collective-permute-start.8
  30.2 0.5 %collective-permute-start.9 = (bf16[128,1024]{1,0:T(8,128)(2,1)S(1)}, bf16[128,1024]{1,0:T(8,128)(2,1)S(1)}, u32[]{:S(2)}, u32[]{:S(2)}) collective-permute-start(bf16[128,1024]{1,0:T(8,128)(2,1)S(1)} %collective-permute-done.3.refs_10_), channel_id=1, source_target_pairs={{0,4},{4,0},{8,12},{12,8},{16,20},{20,16},{24,28},{28,24},{1,5},{5... | collective-permute-start | bytes 786440 | tf_op jit(solution)/shard_map/ppermute | solution.py:211
  30.8 0.0 collective-permute-start.5
  30.8 0.0 copy-start
  30.8 0.1 pad_add_fusion.2.refs_0_
  30.8 1.6 %collective-permute-done.5.refs_3_ = s32[16,128]{1,0:T(8,128)S(1)} collective-permute-done((s32[16,128]{1,0:T(8,128)S(1)}, s32[16,128]{1,0:T(8,128)S(1)}, u32[]{:S(2)}, u32[]{:S(2)}) %collective-permute-start.5) | collective-permute-done | bytes 8224 | tf_op jit(solution)/shard_map/ppermute | solution.py:211
  32.4 0.0 collective-permute-done.6.refs_5_
  32.4 0.0 collective-permute-done.7.refs_7_
  32.4 0.0 collective-permute-done.8.refs_9_
  32.4 0.0 collective-permute-done.9.refs_11_
  32.4 0.0 copy-done
  32.4 7.7 %shard_map.37 = f32[32,1024]{1,0:T(8,128)} custom-call(s32[3]{0:T(128)S(1)} %pad_add_fusion.2.refs_0_, s32[8,128]{1,0:T(8,128)S(1)} %bitcast.5, s32[16,128]{1,0:T(8,128)S(1)} %pad_add_fusion.refs_2_, s32[16,128]{1,0:T(8,128)S(1)} %collective-permute-done.5.refs_3_, bf16[128,1024]{1,0:T(8,128)(2,1)S(1)} %all_gather.3.refs_4_, ...), custom_call_target="tpu_custom_call" | custom-call | flops 2147483648 | bytes 2097152 | tf_op jit(solution)/shard_map/pallas_call | solution.py:249
  (2 shorter events, 0.0 us)
Async XLA Ops:
  0.0 18.8 %copy-start.1 = (s32[128,4]{0,1:T(4,128)S(1)}, s32[128,4]{0,1:T(4,128)}, u32[]{:S(2)}) copy-start(s32[128,4]{0,1:T(4,128)} %param.4) | copy-start | bytes 6148
  0.0 18.8 %collective-permute-start = (s32[4,128]{1,0:T(4,128)}, s32[4,128]{1,0:T(4,128)S(1)}, u32[]{:S(2)}, u32[]{:S(2)}) collective-permute-start(s32[4,128]{1,0:T(4,128)} %bitcast.6), channel_id=1, source_target_pairs={{0,16},{4,20},{8,24},{12,28},{16,0},{20,4},{24,8},{28,12},{1,17},{... | collective-permute-start | bytes 6152 | tf_op jit(solution)/shard_map/ppermute | solution.py:211
  18.8 8.1 %collective-permute-start.3 = (bf16[128,1024]{1,0:T(8,128)(2,1)S(1)}, bf16[128,1024]{1,0:T(8,128)(2,1)S(1)}, u32[]{:S(2)}, u32[]{:S(2)}) collective-permute-start(bf16[128,1024]{1,0:T(8,128)(2,1)S(1)} %all_gather.3.refs_4_), channel_id=1, source_target_pairs={{0,3},{1,2},{2,1},{3,0},{4,7},{5,6},{6,5},{7,4},{8,11},{9,10},{10,... | collective-permute-start | bytes 786440 | tf_op jit(solution)/shard_map/ppermute | solution.py:211
  21.3 8.3 %collective-permute-start.2 = (bf16[128,1024]{1,0:T(8,128)(2,1)S(1)}, bf16[128,1024]{1,0:T(8,128)(2,1)S(1)}, u32[]{:S(2)}, u32[]{:S(2)}) collective-permute-start(bf16[128,1024]{1,0:T(8,128)(2,1)S(1)} %all_gather.3.refs_4_), channel_id=1, source_target_pairs={{0,2},{1,3},{2,0},{3,1},{4,6},{5,7},{6,4},{7,5},{8,10},{9,11},{10,... | collective-permute-start | bytes 786440 | tf_op jit(solution)/shard_map/ppermute | solution.py:211
  21.8 7.9 %collective-permute-start.1 = (bf16[128,1024]{1,0:T(8,128)(2,1)S(1)}, bf16[128,1024]{1,0:T(8,128)(2,1)S(1)}, u32[]{:S(2)}, u32[]{:S(2)}) collective-permute-start(bf16[128,1024]{1,0:T(8,128)(2,1)S(1)} %all_gather.3.refs_4_), channel_id=1, source_target_pairs={{0,1},{1,0},{2,3},{3,2},{4,5},{5,4},{6,7},{7,6},{8,9},{9,8},{10,11... | collective-permute-start | bytes 786440 | tf_op jit(solution)/shard_map/ppermute | solution.py:211
  22.3 3.6 %collective-permute-start.4 = (s32[8,128]{1,0:T(8,128)S(1)}, s32[8,128]{1,0:T(8,128)S(1)}, u32[]{:S(2)}, u32[]{:S(2)}) collective-permute-start(s32[8,128]{1,0:T(8,128)S(1)} %pad_add_fusion.1), channel_id=1, source_target_pairs={{0,8},{4,12},{8,0},{12,4},{16,24},{20,28},{24,16},{28,20},{1,9},{5... | collective-permute-start | bytes 12296 | tf_op jit(solution)/shard_map/ppermute | solution.py:211
  29.7 2.7 %collective-permute-start.6 = (bf16[128,1024]{1,0:T(8,128)(2,1)S(1)}, bf16[128,1024]{1,0:T(8,128)(2,1)S(1)}, u32[]{:S(2)}, u32[]{:S(2)}) collective-permute-start(bf16[128,1024]{1,0:T(8,128)(2,1)S(1)} %all_gather.3.refs_4_), channel_id=1, source_target_pairs={{0,4},{4,0},{8,12},{12,8},{16,20},{20,16},{24,28},{28,24},{1,5},{5... | collective-permute-start | bytes 786440 | tf_op jit(solution)/shard_map/ppermute | solution.py:211
  29.7 2.7 %collective-permute-start.7 = (bf16[128,1024]{1,0:T(8,128)(2,1)S(1)}, bf16[128,1024]{1,0:T(8,128)(2,1)S(1)}, u32[]{:S(2)}, u32[]{:S(2)}) collective-permute-start(bf16[128,1024]{1,0:T(8,128)(2,1)S(1)} %collective-permute-done.1.refs_6_), channel_id=1, source_target_pairs={{0,4},{4,0},{8,12},{12,8},{16,20},{20,16},{24,28},{28,24},{1,5},{5... | collective-permute-start | bytes 786440 | tf_op jit(solution)/shard_map/ppermute | solution.py:211
  30.2 2.2 %collective-permute-start.8 = (bf16[128,1024]{1,0:T(8,128)(2,1)S(1)}, bf16[128,1024]{1,0:T(8,128)(2,1)S(1)}, u32[]{:S(2)}, u32[]{:S(2)}) collective-permute-start(bf16[128,1024]{1,0:T(8,128)(2,1)S(1)} %collective-permute-done.2.refs_8_), channel_id=1, source_target_pairs={{0,4},{4,0},{8,12},{12,8},{16,20},{20,16},{24,28},{28,24},{1,5},{5... | collective-permute-start | bytes 786440 | tf_op jit(solution)/shard_map/ppermute | solution.py:211
  30.2 2.2 %collective-permute-start.9 = (bf16[128,1024]{1,0:T(8,128)(2,1)S(1)}, bf16[128,1024]{1,0:T(8,128)(2,1)S(1)}, u32[]{:S(2)}, u32[]{:S(2)}) collective-permute-start(bf16[128,1024]{1,0:T(8,128)(2,1)S(1)} %collective-permute-done.3.refs_10_), channel_id=1, source_target_pairs={{0,4},{4,0},{8,12},{12,8},{16,20},{20,16},{24,28},{28,24},{1,5},{5... | collective-permute-start | bytes 786440 | tf_op jit(solution)/shard_map/ppermute | solution.py:211
  30.8 1.6 %collective-permute-start.5 = (s32[16,128]{1,0:T(8,128)S(1)}, s32[16,128]{1,0:T(8,128)S(1)}, u32[]{:S(2)}, u32[]{:S(2)}) collective-permute-start(s32[16,128]{1,0:T(8,128)S(1)} %pad_add_fusion.refs_2_), channel_id=1, source_target_pairs={{0,4},{4,0},{8,12},{12,8},{16,20},{20,16},{24,28},{28,24},{1,5},{5... | collective-permute-start | bytes 24584 | tf_op jit(solution)/shard_map/ppermute | solution.py:211
  30.8 1.7 %copy-start = (s32[1024]{0:T(1024)S(1)}, s32[1024]{0:T(1024)}, u32[]{:S(2)}) copy-start(s32[1024]{0:T(1024)} %param.5) | copy-start | bytes 12292

commit v13 on v11

--- a/solution.py
+++ b/solution.py
@@ -33,7 +33,7 @@
     place_ref, table_ref = refs[:2]
     ids_refs = refs[2:4]
     pieces = refs[4 : 4 + len(layout)]
-    out_ref, embed_ref, score_ref, own_ref, target_ref, stat_ref = refs[4 + len(layout) :]
+    out_ref, embed_ref, score_ref, own_ref, target_ref, stat_ref, column_ref = refs[4 + len(layout) :]
     total = embed_ref.shape[0]
     me = place_ref[0]
     my_col = place_ref[1]
@@ -115,6 +115,11 @@
                 pos.append(jnp.broadcast_to(picked[half][m : m + 1, :], (8, 128)))
         return tuple(pos)
 
+    factor = 1.0 / (pos_count * total)
+
+    def turned(values, steps):
+        return jnp.concatenate([values[steps:], values[:steps]], axis=0)
+
     def finish(start, sums):
         for half in range(pair):
             lanes = aligned(start + half * 128, 128)
@@ -122,9 +127,53 @@
                 at = (half * pos_count + m) * 2
                 stat_ref[8 + m : 9 + m, lanes] = jnp.sum(sums[at], axis=0, keepdims=True)
                 stat_ref[16 + m : 17 + m, lanes] = jnp.sum(sums[at + 1], axis=0, keepdims=True)
+        lanes = aligned(start, lane_block)
+        spot = stat_ref[0:pos_count, lanes]
+        ranks = 0.5 + 0.5 * (total + stat_ref[8 : 8 + pos_count, lanes])
+        slopes = 0.25 * (total - stat_ref[16 : 16 + pos_count, lanes])
+        pulls = -factor / ranks
+        prank = 1.0
+        pulled = 0.0
+        for steps in range(1, pos_count):
+            bent = jnp.tanh(turned(spot, steps) - spot)
+            prank = prank + 0.5 * (1.0 + bent)
+            pulled = pulled + (turned(pulls, steps) - pulls) * (0.25 * (1.0 - bent * bent))
+        weight = prank / (ranks * ranks) * (factor / logistic_sharpness)
+        stat_ref[8 : 8 + pos_count, lanes] = 0.25 * weight
+        stat_ref[16 : 16 + pos_count, lanes] = pulled / logistic_sharpness - weight * slopes
+
+    def keep_own():
+        rows = [stat_ref[:, 0:128], target_ref[:, 0:128].astype(jnp.float32)]
+        column_ref[:, 0:32] = jnp.transpose(jnp.concatenate(rows, axis=0))[0:shard, :]
+
+    def contribute(start, fresh):
+        lanes = aligned(start, lane_block)
+        scores = own_ref[:, lanes]
+        lane = lax.broadcasted_iota(jnp.int32, (shard, lane_block), 1) + start
+        line = lax.broadcasted_iota(jnp.int32, (shard, lane_block), 0)
+        grads = [jnp.zeros((shard, lane_block), jnp.float32) for _ in range(2)]
+
+        def column(k):
+            return column_ref[:, k : k + 1]
+
+        for m in range(pos_count):
+            bent = jnp.tanh(scores - stat_ref[m : m + 1, lanes])
+            grads[0] = grads[0] + stat_ref[8 + m : 9 + m, lanes] * (1.0 - bent * bent)
+            bent = jnp.tanh(scores - column(m))
+            grads[1] = grads[1] + column(8 + m) * (1.0 - bent * bent)
+        for m in range(pos_count):
+            found = line == target_ref[m : m + 1, lanes]
+            grads[0] = grads[0] + jnp.where(found, stat_ref[16 + m : 17 + m, lanes], 0.0)
+            found = lane == column(24 + m).astype(jnp.int32)
+            grads[1] = grads[1] + jnp.where(found, column(16 + m), 0.0)
+        both = jnp.concatenate(grads, axis=0).astype(jnp.bfloat16)
+        part = jnp.dot(both, embed_ref[lanes, :], preferred_element_type=jnp.float32)
+        part = part[:shard, :] + part[shard:, :]
+        out_ref[...] = part if fresh else out_ref[...] + part
 
     first = embed_ref[0:lane_block, :]
     picked = over_chunks(lambda chunk, have: score_chunk(first, 0, 0, chunk, have), nothing)
+    last = total // lane_block - 1
 
     def block_step(block, pos):
         start = block * lane_block
@@ -139,58 +188,21 @@
 
         picked, sums = over_chunks(both, (nothing, zero))
         finish(start, sums)
-        return split(following, 1 - buffer, picked)
-
-    last = total // lane_block - 1
-    pos = split(0, 0, picked)
+        pos = split(following, 1 - buffer, picked)
+        if isinstance(block, int) and block == 0:
+            keep_own()
+        contribute(start, isinstance(block, int) and block == 0)
+        return pos
+
+    pos = block_step(0, split(0, 0, picked))
     if chunks == 1:
-        for block in range(last):
+        for block in range(1, last):
             pos = block_step(block, pos)
     else:
-        pos = lax.fori_loop(0, last, block_step, pos)
+        pos = lax.fori_loop(1, last, block_step, pos)
     sums = over_chunks(lambda chunk, have: rank_chunk(pos, last % 2, chunk, have), zero)
     finish(last * lane_block, sums)
-
-    def turned(values, steps):
-        return jnp.concatenate([values[steps:], values[:steps]], axis=0)
-
-    spot = stat_ref[0:pos_count, :]
-    ranks = 0.5 + 0.5 * (total + stat_ref[8 : 8 + pos_count, :])
-    slopes = 0.25 * (total - stat_ref[16 : 16 + pos_count, :])
-    factor = 1.0 / (pos_count * total)
-    pulls = -factor / ranks
-    prank = 1.0
-    pulled = 0.0
-    for steps in range(1, pos_count):
-        bent = jnp.tanh(turned(spot, steps) - spot)
-        prank = prank + 0.5 * (1.0 + bent)
-        pulled = pulled + (turned(pulls, steps) - pulls) * (0.25 * (1.0 - bent * bent))
-    weight = prank / (ranks * ranks) * (factor / logistic_sharpness)
-    stat_ref[8 : 8 + pos_count, :] = 0.25 * weight
-    stat_ref[16 : 16 + pos_count, :] = pulled / logistic_sharpness - weight * slopes
-
-    scores = own_ref[...]
-    lane = lax.broadcasted_iota(jnp.int32, (shard, total), 1)
-    line = lax.broadcasted_iota(jnp.int32, (shard, total), 0)
-    columns = jnp.transpose(
-        jnp.concatenate(
-            [stat_ref[:, 0:128], target_ref[:, 0:128].astype(jnp.float32)], axis=0
-        )
-    )[0:shard, :]
-    grads = [jnp.zeros((shard, total), jnp.float32) for _ in range(2)]
-    for m in range(pos_count):
-        bent = jnp.tanh(scores - stat_ref[m : m + 1, :])
-        grads[0] = grads[0] + stat_ref[8 + m : 9 + m, :] * (1.0 - bent * bent)
-        bent = jnp.tanh(scores - columns[:, m : m + 1])
-        grads[1] = grads[1] + columns[:, 8 + m : 9 + m] * (1.0 - bent * bent)
-    for m in range(pos_count):
-        found = line == target_ref[m : m + 1, :]
-        grads[0] = grads[0] + jnp.where(found, stat_ref[16 + m : 17 + m, :], 0.0)
-        found = lane == columns[:, 24 + m : 25 + m].astype(jnp.int32)
-        grads[1] = grads[1] + jnp.where(found, columns[:, 16 + m : 17 + m], 0.0)
-    both = jnp.concatenate(grads, axis=0).astype(jnp.bfloat16)
-    product = jnp.dot(both, embed_ref[...], preferred_element_type=jnp.float32)
-    out_ref[...] = product[:shard, :] + product[shard:, :]
+    contribute(last * lane_block, False)
 
 
 def body(embed, positives, placement):
@@ -221,29 +233,21 @@
         return jnp.concatenate([ids, swap(ids, "row", 2 * bit)], axis=0)
 
     line = [swap(embed, "row", 2 * d) for d in range(1, levels)]
-    far = cols - 1
     ids = spread(positives.T)
-    tall = jnp.concatenate([embed, jnp.zeros(((levels - 1) * shard, width), embed.dtype)], axis=0)
-    tall = lax.optimization_barrier(tall)
-    early = swap(tall[:shard], "col", far)
-    line, ids, early, tall = lax.optimization_barrier((line, ids, early, tall))
-    for d in range(1, levels):
-        tall = lax.dynamic_update_slice(tall, line[d - 1], (d * shard, 0))
+    line, ids = lax.optimization_barrier((line, ids))
+    tall = join([embed] + line)
 
     plane = {0: tall}
-    plane.update({p: swap(tall, "col", p) for p in range(1, far)})
-    plane[far] = swap(tall[shard:], "col", far)
+    plane.update({p: swap(tall, "col", p) for p in range(1, cols)})
     while steps:
         ids = spread(ids)
-    plane, ids, early = lax.optimization_barrier((plane, ids, early))
-
-    plane[far] = join([early, plane[far]])
+    plane, ids = lax.optimization_barrier((plane, ids))
+
     ids = (ids, swap(ids, "row", 1))
-    other = {p: swap(plane[p], "row", 1) for p in range(cols)}
     pieces = []
     layout = []
     for p in range(cols):
-        for c, part in enumerate((plane[p], other[p])):
+        for c, part in enumerate((plane[p], swap(plane[p], "row", 1))):
             pieces.append(part)
             layout.append([(d * 2 + c) * cols + p for d in range(levels)])
 
@@ -260,6 +264,7 @@
             pltpu.VMEM((shard, total), jnp.float32),
             pltpu.VMEM((8, total), jnp.int32),
             pltpu.VMEM((24, total), jnp.float32),
+            pltpu.VMEM((shard, 128), jnp.float32),
         ],
         compiler_params=pltpu.CompilerParams(vmem_limit_bytes=4 * total * width + 8 * total * lane_block + (16 << 20)),
         cost_estimate=pl.CostEstimate(

time: 36.4 us -> 35.9 us (0.986)
  starting transfers between devices: 16.4 us -> 12.7 us
  waiting for transfers between devices: 11.4 us -> 14 us
  Pallas kernels: 7.28 us -> 7.95 us
    ppermute x14 -> x13, starting transfers between devices: 16.4 us -> 12.7 us  [swap(): return lax.ppermute(array, axis, [(i, i ^ mask) for i in range(size)])]
    ppermute x14 -> x13, waiting for transfers between devices: 11.4 us -> 14 us  [swap(): return lax.ppermute(array, axis, [(i, i ^ mask) for i in range(size)])]
    concatenate x1 -> x0, local copies, waits for them, and re-layouts: 0.89 us -> none  [body(): jnp.concatenate([embed, jnp.zeros(((levels - 1) * shard, width), embed.dt...]
    unnamed x5 -> x7, local copies, waits for them, and re-layouts: 0.02 us -> 0.86 us
    pallas_call x1, Pallas kernels: 7.28 us -> 7.95 us  [body(): pl.pallas_call(functools.partial(kernel, cols, order, shard, pos_count, l...]
  transfers between devices with their start and end apart: 14 -> 13, of which waited for: 5 -> 7; matrix products, arithmetic and copies ran while one was open for 3% -> 3% of each run, Pallas kernels for 0% -> 0%
where the time goes in v13:
time: 35.9 us; the launch traced here: 35.7 us
  waiting for transfers between devices  14 us (39%)
  starting transfers between devices  12.7 us (35%)
  Pallas kernels  7.95 us (22%)
  local copies, waits for them, and re-layouts  0.87 us (2%)
    ppermute x13, waiting for transfers between devices, swap(): return lax.ppermute(array, axis, [(i, i ^ mask) for i in range(size)])  14 us
    ppermute x13, starting transfers between devices, swap(): return lax.ppermute(array, axis, [(i, i ^ mask) for i in range(size)])  12.7 us
    pallas_call x1, Pallas kernels, body(): pl.pallas_call(functools.partial(kernel, cols, order, shard, pos_count, l...  7.95 us
    unnamed x7, local copies, waits for them, and re-layouts  0.86 us
  transfers between devices with their start and end apart: 13, of which 7 were waited for; matrix products, arithmetic and copies ran while one was open for 3% of the time, Pallas kernels for 0%

profile of v13, /device:TPU:0, one launch (start us, length us, event | category | flops | bytes accessed | tf_op | source)
XLA Modules:
  0.0 35.7 jit_solution(932743107077931227)
XLA Ops:
  0.0 4.0 %collective-permute-start.1 = (bf16[32,1024]{1,0:T(8,128)(2,1)}, bf16[32,1024]{1,0:T(8,128)(2,1)S(1)}, u32[]{:S(2)}, u32[]{:S(2)}) collective-permute-start(bf16[32,1024]{1,0:T(8,128)(2,1)} %param.3), channel_id=1, source_target_pairs={{0,16},{4,20},{8,24},{12,28},{16,0},{20,4},{24,8},{28,12},{1,17},{... | collective-permute-start | bytes 196616 | tf_op jit(solution)/shard_map/ppermute | solution.py:220
  4.0 1.6 %collective-permute-start = (bf16[32,1024]{1,0:T(8,128)(2,1)}, bf16[32,1024]{1,0:T(8,128)(2,1)S(1)}, u32[]{:S(2)}, u32[]{:S(2)}) collective-permute-start(bf16[32,1024]{1,0:T(8,128)(2,1)} %param.3), channel_id=1, source_target_pairs={{0,8},{4,12},{8,0},{12,4},{16,24},{20,28},{24,16},{28,20},{1,9},{5... | collective-permute-start | bytes 196616 | tf_op jit(solution)/shard_map/ppermute | solution.py:220
  5.6 0.0 collective-permute-start.2
  5.6 0.0 copy-start.1
  5.6 1.9 %collective-permute-start.3 = (s32[4,128]{1,0:T(4,128)}, s32[4,128]{1,0:T(4,128)S(1)}, u32[]{:S(2)}, u32[]{:S(2)}) collective-permute-start(s32[4,128]{1,0:T(4,128)} %bitcast.5), channel_id=1, source_target_pairs={{0,16},{4,20},{8,24},{12,28},{16,0},{20,4},{24,8},{28,12},{1,17},{... | collective-permute-start | bytes 6152 | tf_op jit(solution)/shard_map/ppermute | solution.py:220
  7.5 0.8 %constant_dynamic-update-slice_fusion.3 = bf16[128,1024]{1,0:T(8,128)(2,1)S(1)} fusion(bf16[32,1024]{1,0:T(8,128)(2,1)} %param.3), kind=kLoop, calls=%fused_computation.3 | loop fusion | bytes 131072
  8.4 2.3 %collective-permute-done.3 = s32[4,128]{1,0:T(4,128)S(1)} collective-permute-done((s32[4,128]{1,0:T(4,128)}, s32[4,128]{1,0:T(4,128)S(1)}, u32[]{:S(2)}, u32[]{:S(2)}) %collective-permute-start.3) | collective-permute-done | bytes 2080 | tf_op jit(solution)/shard_map/ppermute | solution.py:220
  10.7 0.0 copy-done.1
  10.7 0.0 collective-permute-done.1
  10.7 0.0 collective-permute-done
  10.8 1.1 %collective-permute-done.2 = bf16[32,1024]{1,0:T(8,128)(2,1)S(1)} collective-permute-done((bf16[32,1024]{1,0:T(8,128)(2,1)}, bf16[32,1024]{1,0:T(8,128)(2,1)S(1)}, u32[]{:S(2)}, u32[]{:S(2)}) %collective-permute-start.2) | collective-permute-done | bytes 65568 | tf_op jit(solution)/shard_map/ppermute | solution.py:220
  11.9 2.5 %collective-permute-start.6 = (bf16[128,1024]{1,0:T(8,128)(2,1)S(1)}, bf16[128,1024]{1,0:T(8,128)(2,1)S(1)}, u32[]{:S(2)}, u32[]{:S(2)}) collective-permute-start(bf16[128,1024]{1,0:T(8,128)(2,1)S(1)} %constant_dynamic-update-slice_fusion.refs_4_), channel_id=1, source_target_pairs={{0,3},{1,2},{2,1},{3,0},{4,7},{5,6},{6,5},{7,4},{8,11},{9,10},{10,... | collective-permute-start | bytes 786440 | tf_op jit(solution)/shard_map/ppermute | solution.py:220
  14.4 0.5 %collective-permute-start.5 = (bf16[128,1024]{1,0:T(8,128)(2,1)S(1)}, bf16[128,1024]{1,0:T(8,128)(2,1)S(1)}, u32[]{:S(2)}, u32[]{:S(2)}) collective-permute-start(bf16[128,1024]{1,0:T(8,128)(2,1)S(1)} %constant_dynamic-update-slice_fusion.refs_4_), channel_id=1, source_target_pairs={{0,2},{1,3},{2,0},{3,1},{4,6},{5,7},{6,4},{7,5},{8,10},{9,11},{10,... | collective-permute-start | bytes 786440 | tf_op jit(solution)/shard_map/ppermute | solution.py:220
  14.9 0.5 %collective-permute-start.4 = (bf16[128,1024]{1,0:T(8,128)(2,1)S(1)}, bf16[128,1024]{1,0:T(8,128)(2,1)S(1)}, u32[]{:S(2)}, u32[]{:S(2)}) collective-permute-start(bf16[128,1024]{1,0:T(8,128)(2,1)S(1)} %constant_dynamic-update-slice_fusion.refs_4_), channel_id=1, source_target_pairs={{0,1},{1,0},{2,3},{3,2},{4,5},{5,4},{6,7},{7,6},{8,9},{9,8},{10,11... | collective-permute-start | bytes 786440 | tf_op jit(solution)/shard_map/ppermute | solution.py:220
  15.5 0.6 %collective-permute-start.7 = (s32[8,128]{1,0:T(8,128)S(1)}, s32[8,128]{1,0:T(8,128)S(1)}, u32[]{:S(2)}, u32[]{:S(2)}) collective-permute-start(s32[8,128]{1,0:T(8,128)S(1)} %pad_add_fusion.1), channel_id=1, source_target_pairs={{0,8},{4,12},{8,0},{12,4},{16,24},{20,28},{24,16},{28,20},{1,9},{5... | collective-permute-start | bytes 12296 | tf_op jit(solution)/shard_map/ppermute | solution.py:220
  16.1 3.0 %collective-permute-done.7 = s32[8,128]{1,0:T(8,128)S(1)} collective-permute-done((s32[8,128]{1,0:T(8,128)S(1)}, s32[8,128]{1,0:T(8,128)S(1)}, u32[]{:S(2)}, u32[]{:S(2)}) %collective-permute-start.7) | collective-permute-done | bytes 4128 | tf_op jit(solution)/shard_map/ppermute | solution.py:220
  19.1 3.0 %collective-permute-done.6.refs_10_ = bf16[128,1024]{1,0:T(8,128)(2,1)S(1)} collective-permute-done((bf16[128,1024]{1,0:T(8,128)(2,1)S(1)}, bf16[128,1024]{1,0:T(8,128)(2,1)S(1)}, u32[]{:S(2)}, u32[]{:S(2)}) %collective-permute-start.6) | collective-permute-done | bytes 262176 | tf_op jit(solution)/shard_map/ppermute | solution.py:220
  22.1 2.8 %collective-permute-done.5.refs_8_ = bf16[128,1024]{1,0:T(8,128)(2,1)S(1)} collective-permute-done((bf16[128,1024]{1,0:T(8,128)(2,1)S(1)}, bf16[128,1024]{1,0:T(8,128)(2,1)S(1)}, u32[]{:S(2)}, u32[]{:S(2)}) %collective-permute-start.5) | collective-permute-done | bytes 262176 | tf_op jit(solution)/shard_map/ppermute | solution.py:220
  24.9 0.1 collective-permute-done.4.refs_6_
  25.0 0.0 collective-permute-start.9
  25.0 0.5 %collective-permute-start.10 = (bf16[128,1024]{1,0:T(8,128)(2,1)S(1)}, bf16[128,1024]{1,0:T(8,128)(2,1)S(1)}, u32[]{:S(2)}, u32[]{:S(2)}) collective-permute-start(bf16[128,1024]{1,0:T(8,128)(2,1)S(1)} %collective-permute-done.4.refs_6_), channel_id=1, source_target_pairs={{0,4},{4,0},{8,12},{12,8},{16,20},{20,16},{24,28},{28,24},{1,5},{5... | collective-permute-start | bytes 786440 | tf_op jit(solution)/shard_map/ppermute | solution.py:220
  25.6 0.0 collective-permute-start.11
  25.6 0.5 %collective-permute-start.12 = (bf16[128,1024]{1,0:T(8,128)(2,1)S(1)}, bf16[128,1024]{1,0:T(8,128)(2,1)S(1)}, u32[]{:S(2)}, u32[]{:S(2)}) collective-permute-start(bf16[128,1024]{1,0:T(8,128)(2,1)S(1)} %collective-permute-done.6.refs_10_), channel_id=1, source_target_pairs={{0,4},{4,0},{8,12},{12,8},{16,20},{20,16},{24,28},{28,24},{1,5},{5... | collective-permute-start | bytes 786440 | tf_op jit(solution)/shard_map/ppermute | solution.py:220
  26.1 0.0 copy-start
  26.1 0.0 collective-permute-start.8
  26.1 0.1 pad_add_fusion.2.refs_0_
  26.1 1.6 %collective-permute-done.8.refs_3_ = s32[16,128]{1,0:T(8,128)S(1)} collective-permute-done((s32[16,128]{1,0:T(8,128)S(1)}, s32[16,128]{1,0:T(8,128)S(1)}, u32[]{:S(2)}, u32[]{:S(2)}) %collective-permute-start.8) | collective-permute-done | bytes 8224 | tf_op jit(solution)/shard_map/ppermute | solution.py:220
  27.7 0.0 collective-permute-done.9.refs_5_
  27.7 0.0 collective-permute-done.10.refs_7_
  27.7 0.0 collective-permute-done.11.refs_9_
  27.7 0.0 collective-permute-done.12.refs_11_
  27.7 0.0 copy-done
  27.7 8.0 %shard_map.37 = f32[32,1024]{1,0:T(8,128)} custom-call(s32[2]{0:T(128)S(1)} %pad_add_fusion.2.refs_0_, s32[8,128]{1,0:T(8,128)S(1)} %bitcast.4, s32[16,128]{1,0:T(8,128)S(1)} %pad_add_fusion.refs_2_, s32[16,128]{1,0:T(8,128)S(1)} %collective-permute-done.8.refs_3_, bf16[128,1024]{1,0:T(8,128)(2,1)S(1)} %constant_dynamic-update-slice_fusion.refs_4_, ...), custom_call_target="tpu_custom_call" | custom-call | flops 2147483648 | bytes 2097152 | tf_op jit(solution)/shard_map/pallas_call | solution.py:256
  (5 shorter events, 0.0 us)
Async XLA Ops:
  0.0 10.7 %collective-permute-start.1 = (bf16[32,1024]{1,0:T(8,128)(2,1)}, bf16[32,1024]{1,0:T(8,128)(2,1)S(1)}, u32[]{:S(2)}, u32[]{:S(2)}) collective-permute-start(bf16[32,1024]{1,0:T(8,128)(2,1)} %param.3), channel_id=1, source_target_pairs={{0,16},{4,20},{8,24},{12,28},{16,0},{20,4},{24,8},{28,12},{1,17},{... | collective-permute-start | bytes 196616 | tf_op jit(solution)/shard_map/ppermute | solution.py:220
  4.0 6.7 %collective-permute-start = (bf16[32,1024]{1,0:T(8,128)(2,1)}, bf16[32,1024]{1,0:T(8,128)(2,1)S(1)}, u32[]{:S(2)}, u32[]{:S(2)}) collective-permute-start(bf16[32,1024]{1,0:T(8,128)(2,1)} %param.3), channel_id=1, source_target_pairs={{0,8},{4,12},{8,0},{12,4},{16,24},{20,28},{24,16},{28,20},{1,9},{5... | collective-permute-start | bytes 196616 | tf_op jit(solution)/shard_map/ppermute | solution.py:220
  5.6 6.3 %collective-permute-start.2 = (bf16[32,1024]{1,0:T(8,128)(2,1)}, bf16[32,1024]{1,0:T(8,128)(2,1)S(1)}, u32[]{:S(2)}, u32[]{:S(2)}) collective-permute-start(bf16[32,1024]{1,0:T(8,128)(2,1)} %param.3), channel_id=1, source_target_pairs={{0,24},{4,28},{8,16},{12,20},{16,8},{20,12},{24,0},{28,4},{1,25},{... | collective-permute-start | bytes 196616 | tf_op jit(solution)/shard_map/ppermute | solution.py:220
  5.6 5.1 %copy-start.1 = (s32[128,4]{0,1:T(4,128)S(1)}, s32[128,4]{0,1:T(4,128)}, u32[]{:S(2)}) copy-start(s32[128,4]{0,1:T(4,128)} %param.4) | copy-start | bytes 6148
  5.6 5.1 %collective-permute-start.3 = (s32[4,128]{1,0:T(4,128)}, s32[4,128]{1,0:T(4,128)S(1)}, u32[]{:S(2)}, u32[]{:S(2)}) collective-permute-start(s32[4,128]{1,0:T(4,128)} %bitcast.5), channel_id=1, source_target_pairs={{0,16},{4,20},{8,24},{12,28},{16,0},{20,4},{24,8},{28,12},{1,17},{... | collective-permute-start | bytes 6152 | tf_op jit(solution)/shard_map/ppermute | solution.py:220
  11.9 10.2 %collective-permute-start.6 = (bf16[128,1024]{1,0:T(8,128)(2,1)S(1)}, bf16[128,1024]{1,0:T(8,128)(2,1)S(1)}, u32[]{:S(2)}, u32[]{:S(2)}) collective-permute-start(bf16[128,1024]{1,0:T(8,128)(2,1)S(1)} %constant_dynamic-update-slice_fusion.refs_4_), channel_id=1, source_target_pairs={{0,3},{1,2},{2,1},{3,0},{4,7},{5,6},{6,5},{7,4},{8,11},{9,10},{10,... | collective-permute-start | bytes 786440 | tf_op jit(solution)/shard_map/ppermute | solution.py:220
  14.4 10.5 %collective-permute-start.5 = (bf16[128,1024]{1,0:T(8,128)(2,1)S(1)}, bf16[128,1024]{1,0:T(8,128)(2,1)S(1)}, u32[]{:S(2)}, u32[]{:S(2)}) collective-permute-start(bf16[128,1024]{1,0:T(8,128)(2,1)S(1)} %constant_dynamic-update-slice_fusion.refs_4_), channel_id=1, source_target_pairs={{0,2},{1,3},{2,0},{3,1},{4,6},{5,7},{6,4},{7,5},{8,10},{9,11},{10,... | collective-permute-start | bytes 786440 | tf_op jit(solution)/shard_map/ppermute | solution.py:220
  14.9 10.1 %collective-permute-start.4 = (bf16[128,1024]{1,0:T(8,128)(2,1)S(1)}, bf16[128,1024]{1,0:T(8,128)(2,1)S(1)}, u32[]{:S(2)}, u32[]{:S(2)}) collective-permute-start(bf16[128,1024]{1,0:T(8,128)(2,1)S(1)} %constant_dynamic-update-slice_fusion.refs_4_), channel_id=1, source_target_pairs={{0,1},{1,0},{2,3},{3,2},{4,5},{5,4},{6,7},{7,6},{8,9},{9,8},{10,11... | collective-permute-start | bytes 786440 | tf_op jit(solution)/shard_map/ppermute | solution.py:220
  15.5 3.6 %collective-permute-start.7 = (s32[8,128]{1,0:T(8,128)S(1)}, s32[8,128]{1,0:T(8,128)S(1)}, u32[]{:S(2)}, u32[]{:S(2)}) collective-permute-start(s32[8,128]{1,0:T(8,128)S(1)} %pad_add_fusion.1), channel_id=1, source_target_pairs={{0,8},{4,12},{8,0},{12,4},{16,24},{20,28},{24,16},{28,20},{1,9},{5... | collective-permute-start | bytes 12296 | tf_op jit(solution)/shard_map/ppermute | solution.py:220
  25.0 2.7 %collective-permute-start.9 = (bf16[128,1024]{1,0:T(8,128)(2,1)S(1)}, bf16[128,1024]{1,0:T(8,128)(2,1)S(1)}, u32[]{:S(2)}, u32[]{:S(2)}) collective-permute-start(bf16[128,1024]{1,0:T(8,128)(2,1)S(1)} %constant_dynamic-update-slice_fusion.refs_4_), channel_id=1, source_target_pairs={{0,4},{4,0},{8,12},{12,8},{16,20},{20,16},{24,28},{28,24},{1,5},{5... | collective-permute-start | bytes 786440 | tf_op jit(solution)/shard_map/ppermute | solution.py:220
  25.0 2.7 %collective-permute-start.10 = (bf16[128,1024]{1,0:T(8,128)(2,1)S(1)}, bf16[128,1024]{1,0:T(8,128)(2,1)S(1)}, u32[]{:S(2)}, u32[]{:S(2)}) collective-permute-start(bf16[128,1024]{1,0:T(8,128)(2,1)S(1)} %collective-permute-done.4.refs_6_), channel_id=1, source_target_pairs={{0,4},{4,0},{8,12},{12,8},{16,20},{20,16},{24,28},{28,24},{1,5},{5... | collective-permute-start | bytes 786440 | tf_op jit(solution)/shard_map/ppermute | solution.py:220
  25.6 2.2 %collective-permute-start.11 = (bf16[128,1024]{1,0:T(8,128)(2,1)S(1)}, bf16[128,1024]{1,0:T(8,128)(2,1)S(1)}, u32[]{:S(2)}, u32[]{:S(2)}) collective-permute-start(bf16[128,1024]{1,0:T(8,128)(2,1)S(1)} %collective-permute-done.5.refs_8_), channel_id=1, source_target_pairs={{0,4},{4,0},{8,12},{12,8},{16,20},{20,16},{24,28},{28,24},{1,5},{5... | collective-permute-start | bytes 786440 | tf_op jit(solution)/shard_map/ppermute | solution.py:220
  25.6 2.2 %collective-permute-start.12 = (bf16[128,1024]{1,0:T(8,128)(2,1)S(1)}, bf16[128,1024]{1,0:T(8,128)(2,1)S(1)}, u32[]{:S(2)}, u32[]{:S(2)}) collective-permute-start(bf16[128,1024]{1,0:T(8,128)(2,1)S(1)} %collective-permute-done.6.refs_10_), channel_id=1, source_target_pairs={{0,4},{4,0},{8,12},{12,8},{16,20},{20,16},{24,28},{28,24},{1,5},{5... | collective-permute-start | bytes 786440 | tf_op jit(solution)/shard_map/ppermute | solution.py:220
  26.1 1.7 %copy-start = (s32[1024]{0:T(1024)S(1)}, s32[1024]{0:T(1024)}, u32[]{:S(2)}) copy-start(s32[1024]{0:T(1024)} %param.5) | copy-start | bytes 12292
  26.1 1.6 %collective-permute-start.8 = (s32[16,128]{1,0:T(8,128)S(1)}, s32[16,128]{1,0:T(8,128)S(1)}, u32[]{:S(2)}, u32[]{:S(2)}) collective-permute-start(s32[16,128]{1,0:T(8,128)S(1)} %pad_add_fusion.refs_2_), channel_id=1, source_target_pairs={{0,4},{4,0},{8,12},{12,8},{16,20},{20,16},{24,28},{28,24},{1,5},{5... | collective-permute-start | bytes 24584 | tf_op jit(solution)/shard_map/ppermute | solution.py:220

commit v14 on v11

--- a/solution.py
+++ b/solution.py
@@ -38,7 +38,8 @@
     me = place_ref[0]
     my_col = place_ref[1]
     pair = lane_block // 128
-    row_chunk = min(1024, total)
+    small = total <= 1024
+    row_chunk = min(512, total)
 
     for piece, slots in zip(pieces, layout):
         for spot, slot in enumerate(slots):
@@ -93,9 +94,11 @@
         return tuple(sums)
 
     def over_chunks(step, have):
-        if chunks == 1:
-            return step(0, have)
-        return lax.fori_loop(0, chunks, step, have)
+        if not small:
+            return lax.fori_loop(0, chunks, step, have)
+        for chunk in range(chunks):
+            have = step(chunk, have)
+        return have
 
     chunks = total // row_chunk
     nothing = (jnp.zeros((8, 128), jnp.float32),) * pair
@@ -143,7 +146,7 @@
 
     last = total // lane_block - 1
     pos = split(0, 0, picked)
-    if chunks == 1:
+    if small:
         for block in range(last):
             pos = block_step(block, pos)
     else:
@@ -221,25 +224,19 @@
         return jnp.concatenate([ids, swap(ids, "row", 2 * bit)], axis=0)
 
     line = [swap(embed, "row", 2 * d) for d in range(1, levels)]
-    far = cols - 1
     ids = spread(positives.T)
-    tall = jnp.concatenate([embed, jnp.zeros(((levels - 1) * shard, width), embed.dtype)], axis=0)
-    tall = lax.optimization_barrier(tall)
-    early = swap(tall[:shard], "col", far)
-    line, ids, early, tall = lax.optimization_barrier((line, ids, early, tall))
-    for d in range(1, levels):
-        tall = lax.dynamic_update_slice(tall, line[d - 1], (d * shard, 0))
-
-    plane = {0: tall}
-    plane.update({p: swap(tall, "col", p) for p in range(1, far)})
-    plane[far] = swap(tall[shard:], "col", far)
+    line, ids = lax.optimization_barrier((line, ids))
+    tall = join([embed] + line)
+
+    plane = {p: swap(tall, "col", p) for p in range(1, cols)}
     while steps:
         ids = spread(ids)
-    plane, ids, early = lax.optimization_barrier((plane, ids, early))
-
-    plane[far] = join([early, plane[far]])
+    here, ids = lax.optimization_barrier((tall, ids))
+    other = {0: swap(here, "row", 1)}
     ids = (ids, swap(ids, "row", 1))
-    other = {p: swap(plane[p], "row", 1) for p in range(cols)}
+
+    plane[0] = tall
+    other.update({p: swap(plane[p], "row", 1) for p in range(1, cols)})
     pieces = []
     layout = []
     for p in range(cols):

time: 36.4 us -> 34.3 us (0.942)
  starting transfers between devices: 16.4 us -> 12.2 us
  waiting for transfers between devices: 11.4 us -> 13.6 us
    ppermute x14 -> x13, starting transfers between devices: 16.4 us -> 12.2 us  [swap(): return lax.ppermute(array, axis, [(i, i ^ mask) for i in range(size)])]
    ppermute x14 -> x13, waiting for transfers between devices: 11.4 us -> 13.6 us  [swap(): return lax.ppermute(array, axis, [(i, i ^ mask) for i in range(size)])]
    concatenate x1 -> x0, local copies, waits for them, and re-layouts: 0.89 us -> none  [body(): jnp.concatenate([embed, jnp.zeros(((levels - 1) * shard, width), embed.dt...]
    unnamed x5 -> x7, local copies, waits for them, and re-layouts: 0.02 us -> 0.86 us
  transfers between devices with their start and end apart: 14 -> 13, of which waited for: 5 -> 7; matrix products, arithmetic and copies ran while one was open for 3% -> 3% of each run, Pallas kernels for 0% -> 0%
where the time goes in v14:
time: 34.3 us; the launch traced here: 34.1 us
  waiting for transfers between devices  13.6 us (40%)
  starting transfers between devices  12.2 us (36%)
  Pallas kernels  7.22 us (21%)
  local copies, waits for them, and re-layouts  0.87 us (3%)
    ppermute x13, waiting for transfers between devices, swap(): return lax.ppermute(array, axis, [(i, i ^ mask) for i in range(size)])  13.6 us
    ppermute x13, starting transfers between devices, swap(): return lax.ppermute(array, axis, [(i, i ^ mask) for i in range(size)])  12.2 us
    pallas_call x1, Pallas kernels, body(): pl.pallas_call(functools.partial(kernel, cols, order, shard, pos_count, l...  7.22 us
    unnamed x7, local copies, waits for them, and re-layouts  0.86 us
  transfers between devices with their start and end apart: 13, of which 7 were waited for; matrix products, arithmetic and copies ran while one was open for 3% of the time, Pallas kernels for 0%

profile of v14, /device:TPU:0, one launch (start us, length us, event | category | flops | bytes accessed | tf_op | source)
XLA Modules:
  0.0 34.1 jit_solution(376395951248588544)
XLA Ops:
  0.0 4.0 %collective-permute-start.1 = (bf16[32,1024]{1,0:T(8,128)(2,1)}, bf16[32,1024]{1,0:T(8,128)(2,1)S(1)}, u32[]{:S(2)}, u32[]{:S(2)}) collective-permute-start(bf16[32,1024]{1,0:T(8,128)(2,1)} %param.3), channel_id=1, source_target_pairs={{0,16},{4,20},{8,24},{12,28},{16,0},{20,4},{24,8},{28,12},{1,17},{... | collective-permute-start | bytes 196616 | tf_op jit(solution)/shard_map/ppermute | solution.py:211
  4.0 1.6 %collective-permute-start = (bf16[32,1024]{1,0:T(8,128)(2,1)}, bf16[32,1024]{1,0:T(8,128)(2,1)S(1)}, u32[]{:S(2)}, u32[]{:S(2)}) collective-permute-start(bf16[32,1024]{1,0:T(8,128)(2,1)} %param.3), channel_id=1, source_target_pairs={{0,8},{4,12},{8,0},{12,4},{16,24},{20,28},{24,16},{28,20},{1,9},{5... | collective-permute-start | bytes 196616 | tf_op jit(solution)/shard_map/ppermute | solution.py:211
  5.6 0.0 collective-permute-start.2
  5.6 0.0 copy-start.1
  5.6 1.9 %collective-permute-start.3 = (s32[4,128]{1,0:T(4,128)}, s32[4,128]{1,0:T(4,128)S(1)}, u32[]{:S(2)}, u32[]{:S(2)}) collective-permute-start(s32[4,128]{1,0:T(4,128)} %bitcast.5), channel_id=1, source_target_pairs={{0,16},{4,20},{8,24},{12,28},{16,0},{20,4},{24,8},{28,12},{1,17},{... | collective-permute-start | bytes 6152 | tf_op jit(solution)/shard_map/ppermute | solution.py:211
  7.5 0.8 %constant_dynamic-update-slice_fusion.3 = bf16[128,1024]{1,0:T(8,128)(2,1)S(1)} fusion(bf16[32,1024]{1,0:T(8,128)(2,1)} %param.3), kind=kLoop, calls=%fused_computation.3 | loop fusion | bytes 131072
  8.4 2.3 %collective-permute-done.3 = s32[4,128]{1,0:T(4,128)S(1)} collective-permute-done((s32[4,128]{1,0:T(4,128)}, s32[4,128]{1,0:T(4,128)S(1)}, u32[]{:S(2)}, u32[]{:S(2)}) %collective-permute-start.3) | collective-permute-done | bytes 2080 | tf_op jit(solution)/shard_map/ppermute | solution.py:211
  10.7 0.0 copy-done.1
  10.7 0.0 collective-permute-done.1
  10.7 0.0 collective-permute-done
  10.8 1.1 %collective-permute-done.2 = bf16[32,1024]{1,0:T(8,128)(2,1)S(1)} collective-permute-done((bf16[32,1024]{1,0:T(8,128)(2,1)}, bf16[32,1024]{1,0:T(8,128)(2,1)S(1)}, u32[]{:S(2)}, u32[]{:S(2)}) %collective-permute-start.2) | collective-permute-done | bytes 65568 | tf_op jit(solution)/shard_map/ppermute | solution.py:211
  11.9 2.5 %collective-permute-start.11 = (bf16[128,1024]{1,0:T(8,128)(2,1)S(1)}, bf16[128,1024]{1,0:T(8,128)(2,1)S(1)}, u32[]{:S(2)}, u32[]{:S(2)}) collective-permute-start(bf16[128,1024]{1,0:T(8,128)(2,1)S(1)} %constant_dynamic-update-slice_fusion.refs_4_), channel_id=1, source_target_pairs={{0,3},{1,2},{2,1},{3,0},{4,7},{5,6},{6,5},{7,4},{8,11},{9,10},{10,... | collective-permute-start | bytes 786440 | tf_op jit(solution)/shard_map/ppermute | solution.py:211
  14.4 0.5 %collective-permute-start.9 = (bf16[128,1024]{1,0:T(8,128)(2,1)S(1)}, bf16[128,1024]{1,0:T(8,128)(2,1)S(1)}, u32[]{:S(2)}, u32[]{:S(2)}) collective-permute-start(bf16[128,1024]{1,0:T(8,128)(2,1)S(1)} %constant_dynamic-update-slice_fusion.refs_4_), channel_id=1, source_target_pairs={{0,2},{1,3},{2,0},{3,1},{4,6},{5,7},{6,4},{7,5},{8,10},{9,11},{10,... | collective-permute-start | bytes 786440 | tf_op jit(solution)/shard_map/ppermute | solution.py:211
  14.9 0.5 %collective-permute-start.7 = (bf16[128,1024]{1,0:T(8,128)(2,1)S(1)}, bf16[128,1024]{1,0:T(8,128)(2,1)S(1)}, u32[]{:S(2)}, u32[]{:S(2)}) collective-permute-start(bf16[128,1024]{1,0:T(8,128)(2,1)S(1)} %constant_dynamic-update-slice_fusion.refs_4_), channel_id=1, source_target_pairs={{0,1},{1,0},{2,3},{3,2},{4,5},{5,4},{6,7},{7,6},{8,9},{9,8},{10,11... | collective-permute-start | bytes 786440 | tf_op jit(solution)/shard_map/ppermute | solution.py:211
  15.5 0.6 %collective-permute-start.4 = (s32[8,128]{1,0:T(8,128)S(1)}, s32[8,128]{1,0:T(8,128)S(1)}, u32[]{:S(2)}, u32[]{:S(2)}) collective-permute-start(s32[8,128]{1,0:T(8,128)S(1)} %pad_add_fusion.1), channel_id=1, source_target_pairs={{0,8},{4,12},{8,0},{12,4},{16,24},{20,28},{24,16},{28,20},{1,9},{5... | collective-permute-start | bytes 12296 | tf_op jit(solution)/shard_map/ppermute | solution.py:211
  16.1 3.0 %collective-permute-done.4 = s32[8,128]{1,0:T(8,128)S(1)} collective-permute-done((s32[8,128]{1,0:T(8,128)S(1)}, s32[8,128]{1,0:T(8,128)S(1)}, u32[]{:S(2)}, u32[]{:S(2)}) %collective-permute-start.4) | collective-permute-done | bytes 4128 | tf_op jit(solution)/shard_map/ppermute | solution.py:211
  19.1 0.0 collective-permute-start.6
  19.1 3.0 %collective-permute-done.11.refs_10_ = bf16[128,1024]{1,0:T(8,128)(2,1)S(1)} collective-permute-done((bf16[128,1024]{1,0:T(8,128)(2,1)S(1)}, bf16[128,1024]{1,0:T(8,128)(2,1)S(1)}, u32[]{:S(2)}, u32[]{:S(2)}) %collective-permute-start.11) | collective-permute-done | bytes 262176 | tf_op jit(solution)/shard_map/ppermute | solution.py:211
  22.1 0.0 collective-permute-start.12
  22.1 2.8 %collective-permute-done.9.refs_8_ = bf16[128,1024]{1,0:T(8,128)(2,1)S(1)} collective-permute-done((bf16[128,1024]{1,0:T(8,128)(2,1)S(1)}, bf16[128,1024]{1,0:T(8,128)(2,1)S(1)}, u32[]{:S(2)}, u32[]{:S(2)}) %collective-permute-start.9) | collective-permute-done | bytes 262176 | tf_op jit(solution)/shard_map/ppermute | solution.py:211
  24.9 0.0 collective-permute-start.10
  24.9 0.1 collective-permute-done.7.refs_6_
  25.0 0.4 %collective-permute-start.8 = (bf16[128,1024]{1,0:T(8,128)(2,1)S(1)}, bf16[128,1024]{1,0:T(8,128)(2,1)S(1)}, u32[]{:S(2)}, u32[]{:S(2)}) collective-permute-start(bf16[128,1024]{1,0:T(8,128)(2,1)S(1)} %collective-permute-done.7.refs_6_), channel_id=1, source_target_pairs={{0,4},{4,0},{8,12},{12,8},{16,20},{20,16},{24,28},{28,24},{1,5},{5... | collective-permute-start | bytes 786440 | tf_op jit(solution)/shard_map/ppermute | solution.py:211
  25.5 0.0 copy-start
  25.5 0.1 collective-permute-start.5
  25.6 0.1 pad_add_fusion.2.refs_0_
  25.6 1.2 %collective-permute-done.5.refs_3_ = s32[16,128]{1,0:T(8,128)S(1)} collective-permute-done((s32[16,128]{1,0:T(8,128)S(1)}, s32[16,128]{1,0:T(8,128)S(1)}, u32[]{:S(2)}, u32[]{:S(2)}) %collective-permute-start.5) | collective-permute-done | bytes 8224 | tf_op jit(solution)/shard_map/ppermute | solution.py:211
  26.9 0.0 collective-permute-done.6.refs_5_
  26.9 0.0 collective-permute-done.12.refs_11_
  26.9 0.0 collective-permute-done.10.refs_9_
  26.9 0.0 collective-permute-done.8.refs_7_
  26.9 0.0 copy-done
  26.9 7.2 %shard_map.37 = f32[32,1024]{1,0:T(8,128)} custom-call(s32[2]{0:T(128)S(1)} %pad_add_fusion.2.refs_0_, s32[8,128]{1,0:T(8,128)S(1)} %bitcast.4, s32[16,128]{1,0:T(8,128)S(1)} %pad_add_fusion.refs_2_, s32[16,128]{1,0:T(8,128)S(1)} %collective-permute-done.5.refs_3_, bf16[128,1024]{1,0:T(8,128)(2,1)S(1)} %constant_dynamic-update-slice_fusion.refs_4_, ...), custom_call_target="tpu_custom_call" | custom-call | flops 2147483648 | bytes 2097152 | tf_op jit(solution)/shard_map/pallas_call | solution.py:249
  (5 shorter events, 0.0 us)
Async XLA Ops:
  0.0 10.7 %collective-permute-start.1 = (bf16[32,1024]{1,0:T(8,128)(2,1)}, bf16[32,1024]{1,0:T(8,128)(2,1)S(1)}, u32[]{:S(2)}, u32[]{:S(2)}) collective-permute-start(bf16[32,1024]{1,0:T(8,128)(2,1)} %param.3), channel_id=1, source_target_pairs={{0,16},{4,20},{8,24},{12,28},{16,0},{20,4},{24,8},{28,12},{1,17},{... | collective-permute-start | bytes 196616 | tf_op jit(solution)/shard_map/ppermute | solution.py:211
  4.0 6.7 %collective-permute-start = (bf16[32,1024]{1,0:T(8,128)(2,1)}, bf16[32,1024]{1,0:T(8,128)(2,1)S(1)}, u32[]{:S(2)}, u32[]{:S(2)}) collective-permute-start(bf16[32,1024]{1,0:T(8,128)(2,1)} %param.3), channel_id=1, source_target_pairs={{0,8},{4,12},{8,0},{12,4},{16,24},{20,28},{24,16},{28,20},{1,9},{5... | collective-permute-start | bytes 196616 | tf_op jit(solution)/shard_map/ppermute | solution.py:211
  5.6 6.3 %collective-permute-start.2 = (bf16[32,1024]{1,0:T(8,128)(2,1)}, bf16[32,1024]{1,0:T(8,128)(2,1)S(1)}, u32[]{:S(2)}, u32[]{:S(2)}) collective-permute-start(bf16[32,1024]{1,0:T(8,128)(2,1)} %param.3), channel_id=1, source_target_pairs={{0,24},{4,28},{8,16},{12,20},{16,8},{20,12},{24,0},{28,4},{1,25},{... | collective-permute-start | bytes 196616 | tf_op jit(solution)/shard_map/ppermute | solution.py:211
  5.6 5.1 %copy-start.1 = (s32[128,4]{0,1:T(4,128)S(1)}, s32[128,4]{0,1:T(4,128)}, u32[]{:S(2)}) copy-start(s32[128,4]{0,1:T(4,128)} %param.4) | copy-start | bytes 6148
  5.6 5.1 %collective-permute-start.3 = (s32[4,128]{1,0:T(4,128)}, s32[4,128]{1,0:T(4,128)S(1)}, u32[]{:S(2)}, u32[]{:S(2)}) collective-permute-start(s32[4,128]{1,0:T(4,128)} %bitcast.5), channel_id=1, source_target_pairs={{0,16},{4,20},{8,24},{12,28},{16,0},{20,4},{24,8},{28,12},{1,17},{... | collective-permute-start | bytes 6152 | tf_op jit(solution)/shard_map/ppermute | solution.py:211
  11.9 10.2 %collective-permute-start.11 = (bf16[128,1024]{1,0:T(8,128)(2,1)S(1)}, bf16[128,1024]{1,0:T(8,128)(2,1)S(1)}, u32[]{:S(2)}, u32[]{:S(2)}) collective-permute-start(bf16[128,1024]{1,0:T(8,128)(2,1)S(1)} %constant_dynamic-update-slice_fusion.refs_4_), channel_id=1, source_target_pairs={{0,3},{1,2},{2,1},{3,0},{4,7},{5,6},{6,5},{7,4},{8,11},{9,10},{10,... | collective-permute-start | bytes 786440 | tf_op jit(solution)/shard_map/ppermute | solution.py:211
  14.4 10.5 %collective-permute-start.9 = (bf16[128,1024]{1,0:T(8,128)(2,1)S(1)}, bf16[128,1024]{1,0:T(8,128)(2,1)S(1)}, u32[]{:S(2)}, u32[]{:S(2)}) collective-permute-start(bf16[128,1024]{1,0:T(8,128)(2,1)S(1)} %constant_dynamic-update-slice_fusion.refs_4_), channel_id=1, source_target_pairs={{0,2},{1,3},{2,0},{3,1},{4,6},{5,7},{6,4},{7,5},{8,10},{9,11},{10,... | collective-permute-start | bytes 786440 | tf_op jit(solution)/shard_map/ppermute | solution.py:211
  14.9 10.1 %collective-permute-start.7 = (bf16[128,1024]{1,0:T(8,128)(2,1)S(1)}, bf16[128,1024]{1,0:T(8,128)(2,1)S(1)}, u32[]{:S(2)}, u32[]{:S(2)}) collective-permute-start(bf16[128,1024]{1,0:T(8,128)(2,1)S(1)} %constant_dynamic-update-slice_fusion.refs_4_), channel_id=1, source_target_pairs={{0,1},{1,0},{2,3},{3,2},{4,5},{5,4},{6,7},{7,6},{8,9},{9,8},{10,11... | collective-permute-start | bytes 786440 | tf_op jit(solution)/shard_map/ppermute | solution.py:211
  15.5 3.6 %collective-permute-start.4 = (s32[8,128]{1,0:T(8,128)S(1)}, s32[8,128]{1,0:T(8,128)S(1)}, u32[]{:S(2)}, u32[]{:S(2)}) collective-permute-start(s32[8,128]{1,0:T(8,128)S(1)} %pad_add_fusion.1), channel_id=1, source_target_pairs={{0,8},{4,12},{8,0},{12,4},{16,24},{20,28},{24,16},{28,20},{1,9},{5... | collective-permute-start | bytes 12296 | tf_op jit(solution)/shard_map/ppermute | solution.py:211
  19.1 7.8 %collective-permute-start.6 = (bf16[128,1024]{1,0:T(8,128)(2,1)S(1)}, bf16[128,1024]{1,0:T(8,128)(2,1)S(1)}, u32[]{:S(2)}, u32[]{:S(2)}) collective-permute-start(bf16[128,1024]{1,0:T(8,128)(2,1)S(1)} %constant_dynamic-update-slice_fusion.refs_4_), channel_id=1, source_target_pairs={{0,4},{4,0},{8,12},{12,8},{16,20},{20,16},{24,28},{28,24},{1,5},{5... | collective-permute-start | bytes 786440 | tf_op jit(solution)/shard_map/ppermute | solution.py:211
  22.1 4.7 %collective-permute-start.12 = (bf16[128,1024]{1,0:T(8,128)(2,1)S(1)}, bf16[128,1024]{1,0:T(8,128)(2,1)S(1)}, u32[]{:S(2)}, u32[]{:S(2)}) collective-permute-start(bf16[128,1024]{1,0:T(8,128)(2,1)S(1)} %collective-permute-done.11.refs_10_), channel_id=1, source_target_pairs={{0,4},{4,0},{8,12},{12,8},{16,20},{20,16},{24,28},{28,24},{1,5},{5... | collective-permute-start | bytes 786440 | tf_op jit(solution)/shard_map/ppermute | solution.py:211
  24.9 1.9 %collective-permute-start.10 = (bf16[128,1024]{1,0:T(8,128)(2,1)S(1)}, bf16[128,1024]{1,0:T(8,128)(2,1)S(1)}, u32[]{:S(2)}, u32[]{:S(2)}) collective-permute-start(bf16[128,1024]{1,0:T(8,128)(2,1)S(1)} %collective-permute-done.9.refs_8_), channel_id=1, source_target_pairs={{0,4},{4,0},{8,12},{12,8},{16,20},{20,16},{24,28},{28,24},{1,5},{5... | collective-permute-start | bytes 786440 | tf_op jit(solution)/shard_map/ppermute | solution.py:211
  25.0 1.8 %collective-permute-start.8 = (bf16[128,1024]{1,0:T(8,128)(2,1)S(1)}, bf16[128,1024]{1,0:T(8,128)(2,1)S(1)}, u32[]{:S(2)}, u32[]{:S(2)}) collective-permute-start(bf16[128,1024]{1,0:T(8,128)(2,1)S(1)} %collective-permute-done.7.refs_6_), channel_id=1, source_target_pairs={{0,4},{4,0},{8,12},{12,8},{16,20},{20,16},{24,28},{28,24},{1,5},{5... | collective-permute-start | bytes 786440 | tf_op jit(solution)/shard_map/ppermute | solution.py:211
  25.5 1.4 %copy-start = (s32[1024]{0:T(1024)S(1)}, s32[1024]{0:T(1024)}, u32[]{:S(2)}) copy-start(s32[1024]{0:T(1024)} %param.5) | copy-start | bytes 12292
  25.5 1.4 %collective-permute-start.5 = (s32[16,128]{1,0:T(8,128)S(1)}, s32[16,128]{1,0:T(8,128)S(1)}, u32[]{:S(2)}, u32[]{:S(2)}) collective-permute-start(s32[16,128]{1,0:T(8,128)S(1)} %pad_add_fusion.refs_2_), channel_id=1, source_target_pairs={{0,4},{4,0},{8,12},{12,8},{16,20},{20,16},{24,28},{28,24},{1,5},{5... | collective-permute-start | bytes 24584 | tf_op jit(solution)/shard_map/ppermute | solution.py:211

commit v15 on v14

--- a/solution.py
+++ b/solution.py
@@ -64,7 +64,7 @@
         scores = half_scale * lax.dot_general(
             embed_ref[aligned(row, row_chunk), :],
             anchors,
-            (((1,), (1,)), ((), ())),
+            (((1,), (0,)), ((), ())),
             preferred_element_type=jnp.float32,
         )
         score_ref[buffer, aligned(row, row_chunk), :] = scores
@@ -126,14 +126,14 @@
                 stat_ref[8 + m : 9 + m, lanes] = jnp.sum(sums[at], axis=0, keepdims=True)
                 stat_ref[16 + m : 17 + m, lanes] = jnp.sum(sums[at + 1], axis=0, keepdims=True)
 
-    first = embed_ref[0:lane_block, :]
+    first = jnp.transpose(embed_ref[0:lane_block, :])
     picked = over_chunks(lambda chunk, have: score_chunk(first, 0, 0, chunk, have), nothing)
 
     def block_step(block, pos):
         start = block * lane_block
         following = start + lane_block
         buffer = block % 2
-        anchors = embed_ref[aligned(following, lane_block), :]
+        anchors = jnp.transpose(embed_ref[aligned(following, lane_block), :])
 
         def both(chunk, carry):
             picked, sums = carry
@@ -223,10 +223,13 @@
         order.extend([d ^ bit for d in order])
         return jnp.concatenate([ids, swap(ids, "row", 2 * bit)], axis=0)
 
-    line = [swap(embed, "row", 2 * d) for d in range(1, levels)]
+    line = {d: swap(embed, "row", 2 * d) for d in range(1, levels)}
+    far = levels - 1
+    ranking = [far // 2 + 1, far] + [d for d in range(1, far) if d != far // 2 + 1]
     ids = spread(positives.T)
-    line, ids = lax.optimization_barrier((line, ids))
-    tall = join([embed] + line)
+    parts, ids = lax.optimization_barrier(([line[d] for d in ranking], ids))
+    line = dict(zip(ranking, parts))
+    tall = join([embed] + [line[d] for d in range(1, levels)])
 
     plane = {p: swap(tall, "col", p) for p in range(1, cols)}
     while steps:

time: 34.3 us -> 34.8 us (1.015)
  starting transfers between devices: 12.2 us -> 13.6 us
  waiting for transfers between devices: 13.6 us -> 12.8 us
    ppermute x13, starting transfers between devices: 12.2 us -> 13.6 us  [swap(): return lax.ppermute(array, axis, [(i, i ^ mask) for i in range(size)])]
    ppermute x13, waiting for transfers between devices: 13.6 us -> 12.8 us  [swap(): return lax.ppermute(array, axis, [(i, i ^ mask) for i in range(size)])]
  transfers between devices with their start and end apart: 13 -> 13, of which waited for: 7 -> 6; matrix products, arithmetic and copies ran while one was open for 3% -> 3% of each run, Pallas kernels for 0% -> 0%
where the time goes in v15:
time: 34.8 us; the launch traced here: 34.6 us
  starting transfers between devices  13.6 us (39%)
  waiting for transfers between devices  12.8 us (37%)
  Pallas kernels  7.21 us (21%)
  local copies, waits for them, and re-layouts  0.87 us (2%)
    ppermute x13, starting transfers between devices, swap(): return lax.ppermute(array, axis, [(i, i ^ mask) for i in range(size)])  13.6 us
    ppermute x13, waiting for transfers between devices, swap(): return lax.ppermute(array, axis, [(i, i ^ mask) for i in range(size)])  12.8 us
    pallas_call x1, Pallas kernels, body(): pl.pallas_call(functools.partial(kernel, cols, order, shard, pos_count, l...  7.21 us
    unnamed x7, local copies, waits for them, and re-layouts  0.86 us
  transfers between devices with their start and end apart: 13, of which 6 were waited for; matrix products, arithmetic and copies ran while one was open for 3% of the time, Pallas kernels for 0%

profile of v15, /device:TPU:0, one launch (start us, length us, event | category | flops | bytes accessed | tf_op | source)
XLA Modules:
  0.0 34.6 jit_solution(427167452311766679)
XLA Ops:
  0.0 5.0 %collective-permute-start.1 = (bf16[32,1024]{1,0:T(8,128)(2,1)}, bf16[32,1024]{1,0:T(8,128)(2,1)S(1)}, u32[]{:S(2)}, u32[]{:S(2)}) collective-permute-start(bf16[32,1024]{1,0:T(8,128)(2,1)} %param.3), channel_id=1, source_target_pairs={{0,24},{4,28},{8,16},{12,20},{16,8},{20,12},{24,0},{28,4},{1,25},{... | collective-permute-start | bytes 196616 | tf_op jit(solution)/shard_map/ppermute | solution.py:211
  5.0 0.0 collective-permute-start
  5.1 0.6 %collective-permute-start.2 = (bf16[32,1024]{1,0:T(8,128)(2,1)}, bf16[32,1024]{1,0:T(8,128)(2,1)S(1)}, u32[]{:S(2)}, u32[]{:S(2)}) collective-permute-start(bf16[32,1024]{1,0:T(8,128)(2,1)} %param.3), channel_id=1, source_target_pairs={{0,8},{4,12},{8,0},{12,4},{16,24},{20,28},{24,16},{28,20},{1,9},{5... | collective-permute-start | bytes 196616 | tf_op jit(solution)/shard_map/ppermute | solution.py:211
  5.6 0.0 copy-start.1
  5.6 2.4 %collective-permute-start.3 = (s32[4,128]{1,0:T(4,128)}, s32[4,128]{1,0:T(4,128)S(1)}, u32[]{:S(2)}, u32[]{:S(2)}) collective-permute-start(s32[4,128]{1,0:T(4,128)} %bitcast.5), channel_id=1, source_target_pairs={{0,16},{4,20},{8,24},{12,28},{16,0},{20,4},{24,8},{28,12},{1,17},{... | collective-permute-start | bytes 6152 | tf_op jit(solution)/shard_map/ppermute | solution.py:211
  8.0 0.8 %constant_dynamic-update-slice_fusion.3 = bf16[128,1024]{1,0:T(8,128)(2,1)S(1)} fusion(bf16[32,1024]{1,0:T(8,128)(2,1)} %param.3), kind=kLoop, calls=%fused_computation.3 | loop fusion | bytes 131072
  8.8 2.1 %collective-permute-done.3 = s32[4,128]{1,0:T(4,128)S(1)} collective-permute-done((s32[4,128]{1,0:T(4,128)}, s32[4,128]{1,0:T(4,128)S(1)}, u32[]{:S(2)}, u32[]{:S(2)}) %collective-permute-start.3) | collective-permute-done | bytes 2080 | tf_op jit(solution)/shard_map/ppermute | solution.py:211
  10.9 0.0 copy-done.1
  10.9 0.0 collective-permute-done.1
  10.9 0.0 collective-permute-done
  11.0 0.0 collective-permute-done.2
  11.0 2.5 %collective-permute-start.11 = (bf16[128,1024]{1,0:T(8,128)(2,1)S(1)}, bf16[128,1024]{1,0:T(8,128)(2,1)S(1)}, u32[]{:S(2)}, u32[]{:S(2)}) collective-permute-start(bf16[128,1024]{1,0:T(8,128)(2,1)S(1)} %constant_dynamic-update-slice_fusion.refs_4_), channel_id=1, source_target_pairs={{0,3},{1,2},{2,1},{3,0},{4,7},{5,6},{6,5},{7,4},{8,11},{9,10},{10,... | collective-permute-start | bytes 786440 | tf_op jit(solution)/shard_map/ppermute | solution.py:211
  13.5 0.5 %collective-permute-start.9 = (bf16[128,1024]{1,0:T(8,128)(2,1)S(1)}, bf16[128,1024]{1,0:T(8,128)(2,1)S(1)}, u32[]{:S(2)}, u32[]{:S(2)}) collective-permute-start(bf16[128,1024]{1,0:T(8,128)(2,1)S(1)} %constant_dynamic-update-slice_fusion.refs_4_), channel_id=1, source_target_pairs={{0,2},{1,3},{2,0},{3,1},{4,6},{5,7},{6,4},{7,5},{8,10},{9,11},{10,... | collective-permute-start | bytes 786440 | tf_op jit(solution)/shard_map/ppermute | solution.py:211
  14.0 0.5 %collective-permute-start.7 = (bf16[128,1024]{1,0:T(8,128)(2,1)S(1)}, bf16[128,1024]{1,0:T(8,128)(2,1)S(1)}, u32[]{:S(2)}, u32[]{:S(2)}) collective-permute-start(bf16[128,1024]{1,0:T(8,128)(2,1)S(1)} %constant_dynamic-update-slice_fusion.refs_4_), channel_id=1, source_target_pairs={{0,1},{1,0},{2,3},{3,2},{4,5},{5,4},{6,7},{7,6},{8,9},{9,8},{10,11... | collective-permute-start | bytes 786440 | tf_op jit(solution)/shard_map/ppermute | solution.py:211
  14.6 1.5 %collective-permute-start.4 = (s32[8,128]{1,0:T(8,128)S(1)}, s32[8,128]{1,0:T(8,128)S(1)}, u32[]{:S(2)}, u32[]{:S(2)}) collective-permute-start(s32[8,128]{1,0:T(8,128)S(1)} %pad_add_fusion.1), channel_id=1, source_target_pairs={{0,8},{4,12},{8,0},{12,4},{16,24},{20,28},{24,16},{28,20},{1,9},{5... | collective-permute-start | bytes 12296 | tf_op jit(solution)/shard_map/ppermute | solution.py:211
  16.1 2.1 %collective-permute-done.4 = s32[8,128]{1,0:T(8,128)S(1)} collective-permute-done((s32[8,128]{1,0:T(8,128)S(1)}, s32[8,128]{1,0:T(8,128)S(1)}, u32[]{:S(2)}, u32[]{:S(2)}) %collective-permute-start.4) | collective-permute-done | bytes 4128 | tf_op jit(solution)/shard_map/ppermute | solution.py:211
  18.2 0.0 collective-permute-start.6
  18.2 3.1 %collective-permute-done.11.refs_10_ = bf16[128,1024]{1,0:T(8,128)(2,1)S(1)} collective-permute-done((bf16[128,1024]{1,0:T(8,128)(2,1)S(1)}, bf16[128,1024]{1,0:T(8,128)(2,1)S(1)}, u32[]{:S(2)}, u32[]{:S(2)}) %collective-permute-start.11) | collective-permute-done | bytes 262176 | tf_op jit(solution)/shard_map/ppermute | solution.py:211
  21.2 0.0 collective-permute-start.12
  21.2 4.2 %collective-permute-done.9.refs_8_ = bf16[128,1024]{1,0:T(8,128)(2,1)S(1)} collective-permute-done((bf16[128,1024]{1,0:T(8,128)(2,1)S(1)}, bf16[128,1024]{1,0:T(8,128)(2,1)S(1)}, u32[]{:S(2)}, u32[]{:S(2)}) %collective-permute-start.9) | collective-permute-done | bytes 262176 | tf_op jit(solution)/shard_map/ppermute | solution.py:211
  25.5 0.0 collective-permute-start.10
  25.5 0.3 collective-permute-done.7.refs_6_
  25.8 0.2 collective-permute-start.8
  26.0 0.0 copy-start
  26.0 0.3 collective-permute-start.5
  26.3 0.1 pad_add_fusion.2.refs_0_
  26.3 1.1 %collective-permute-done.5.refs_3_ = s32[16,128]{1,0:T(8,128)S(1)} collective-permute-done((s32[16,128]{1,0:T(8,128)S(1)}, s32[16,128]{1,0:T(8,128)S(1)}, u32[]{:S(2)}, u32[]{:S(2)}) %collective-permute-start.5) | collective-permute-done | bytes 8224 | tf_op jit(solution)/shard_map/ppermute | solution.py:211
  27.4 0.0 collective-permute-done.6.refs_5_
  27.4 0.0 collective-permute-done.12.refs_11_
  27.4 0.0 collective-permute-done.10.refs_9_
  27.4 0.0 collective-permute-done.8.refs_7_
  27.4 0.0 copy-done
  27.4 7.2 %shard_map.37 = f32[32,1024]{1,0:T(8,128)} custom-call(s32[2]{0:T(128)S(1)} %pad_add_fusion.2.refs_0_, s32[8,128]{1,0:T(8,128)S(1)} %bitcast.4, s32[16,128]{1,0:T(8,128)S(1)} %pad_add_fusion.refs_2_, s32[16,128]{1,0:T(8,128)S(1)} %collective-permute-done.5.refs_3_, bf16[128,1024]{1,0:T(8,128)(2,1)S(1)} %constant_dynamic-update-slice_fusion.refs_4_, ...), custom_call_target="tpu_custom_call" | custom-call | flops 2147483648 | bytes 2097152 | tf_op jit(solution)/shard_map/pallas_call | solution.py:252
  (5 shorter events, 0.0 us)
Async XLA Ops:
  0.0 10.9 %collective-permute-start.1 = (bf16[32,1024]{1,0:T(8,128)(2,1)}, bf16[32,1024]{1,0:T(8,128)(2,1)S(1)}, u32[]{:S(2)}, u32[]{:S(2)}) collective-permute-start(bf16[32,1024]{1,0:T(8,128)(2,1)} %param.3), channel_id=1, source_target_pairs={{0,24},{4,28},{8,16},{12,20},{16,8},{20,12},{24,0},{28,4},{1,25},{... | collective-permute-start | bytes 196616 | tf_op jit(solution)/shard_map/ppermute | solution.py:211
  5.0 5.9 %collective-permute-start = (bf16[32,1024]{1,0:T(8,128)(2,1)}, bf16[32,1024]{1,0:T(8,128)(2,1)S(1)}, u32[]{:S(2)}, u32[]{:S(2)}) collective-permute-start(bf16[32,1024]{1,0:T(8,128)(2,1)} %param.3), channel_id=1, source_target_pairs={{0,16},{4,20},{8,24},{12,28},{16,0},{20,4},{24,8},{28,12},{1,17},{... | collective-permute-start | bytes 196616 | tf_op jit(solution)/shard_map/ppermute | solution.py:211
  5.1 5.9 %collective-permute-start.2 = (bf16[32,1024]{1,0:T(8,128)(2,1)}, bf16[32,1024]{1,0:T(8,128)(2,1)S(1)}, u32[]{:S(2)}, u32[]{:S(2)}) collective-permute-start(bf16[32,1024]{1,0:T(8,128)(2,1)} %param.3), channel_id=1, source_target_pairs={{0,8},{4,12},{8,0},{12,4},{16,24},{20,28},{24,16},{28,20},{1,9},{5... | collective-permute-start | bytes 196616 | tf_op jit(solution)/shard_map/ppermute | solution.py:211
  5.6 5.3 %copy-start.1 = (s32[128,4]{0,1:T(4,128)S(1)}, s32[128,4]{0,1:T(4,128)}, u32[]{:S(2)}) copy-start(s32[128,4]{0,1:T(4,128)} %param.4) | copy-start | bytes 6148
  5.6 5.3 %collective-permute-start.3 = (s32[4,128]{1,0:T(4,128)}, s32[4,128]{1,0:T(4,128)S(1)}, u32[]{:S(2)}, u32[]{:S(2)}) collective-permute-start(s32[4,128]{1,0:T(4,128)} %bitcast.5), channel_id=1, source_target_pairs={{0,16},{4,20},{8,24},{12,28},{16,0},{20,4},{24,8},{28,12},{1,17},{... | collective-permute-start | bytes 6152 | tf_op jit(solution)/shard_map/ppermute | solution.py:211
  11.0 10.2 %collective-permute-start.11 = (bf16[128,1024]{1,0:T(8,128)(2,1)S(1)}, bf16[128,1024]{1,0:T(8,128)(2,1)S(1)}, u32[]{:S(2)}, u32[]{:S(2)}) collective-permute-start(bf16[128,1024]{1,0:T(8,128)(2,1)S(1)} %constant_dynamic-update-slice_fusion.refs_4_), channel_id=1, source_target_pairs={{0,3},{1,2},{2,1},{3,0},{4,7},{5,6},{6,5},{7,4},{8,11},{9,10},{10,... | collective-permute-start | bytes 786440 | tf_op jit(solution)/shard_map/ppermute | solution.py:211
  13.5 11.9 %collective-permute-start.9 = (bf16[128,1024]{1,0:T(8,128)(2,1)S(1)}, bf16[128,1024]{1,0:T(8,128)(2,1)S(1)}, u32[]{:S(2)}, u32[]{:S(2)}) collective-permute-start(bf16[128,1024]{1,0:T(8,128)(2,1)S(1)} %constant_dynamic-update-slice_fusion.refs_4_), channel_id=1, source_target_pairs={{0,2},{1,3},{2,0},{3,1},{4,6},{5,7},{6,4},{7,5},{8,10},{9,11},{10,... | collective-permute-start | bytes 786440 | tf_op jit(solution)/shard_map/ppermute | solution.py:211
  14.0 11.7 %collective-permute-start.7 = (bf16[128,1024]{1,0:T(8,128)(2,1)S(1)}, bf16[128,1024]{1,0:T(8,128)(2,1)S(1)}, u32[]{:S(2)}, u32[]{:S(2)}) collective-permute-start(bf16[128,1024]{1,0:T(8,128)(2,1)S(1)} %constant_dynamic-update-slice_fusion.refs_4_), channel_id=1, source_target_pairs={{0,1},{1,0},{2,3},{3,2},{4,5},{5,4},{6,7},{7,6},{8,9},{9,8},{10,11... | collective-permute-start | bytes 786440 | tf_op jit(solution)/shard_map/ppermute | solution.py:211
  14.6 3.6 %collective-permute-start.4 = (s32[8,128]{1,0:T(8,128)S(1)}, s32[8,128]{1,0:T(8,128)S(1)}, u32[]{:S(2)}, u32[]{:S(2)}) collective-permute-start(s32[8,128]{1,0:T(8,128)S(1)} %pad_add_fusion.1), channel_id=1, source_target_pairs={{0,8},{4,12},{8,0},{12,4},{16,24},{20,28},{24,16},{28,20},{1,9},{5... | collective-permute-start | bytes 12296 | tf_op jit(solution)/shard_map/ppermute | solution.py:211
  18.2 9.2 %collective-permute-start.6 = (bf16[128,1024]{1,0:T(8,128)(2,1)S(1)}, bf16[128,1024]{1,0:T(8,128)(2,1)S(1)}, u32[]{:S(2)}, u32[]{:S(2)}) collective-permute-start(bf16[128,1024]{1,0:T(8,128)(2,1)S(1)} %constant_dynamic-update-slice_fusion.refs_4_), channel_id=1, source_target_pairs={{0,4},{4,0},{8,12},{12,8},{16,20},{20,16},{24,28},{28,24},{1,5},{5... | collective-permute-start | bytes 786440 | tf_op jit(solution)/shard_map/ppermute | solution.py:211
  21.2 6.2 %collective-permute-start.12 = (bf16[128,1024]{1,0:T(8,128)(2,1)S(1)}, bf16[128,1024]{1,0:T(8,128)(2,1)S(1)}, u32[]{:S(2)}, u32[]{:S(2)}) collective-permute-start(bf16[128,1024]{1,0:T(8,128)(2,1)S(1)} %collective-permute-done.11.refs_10_), channel_id=1, source_target_pairs={{0,4},{4,0},{8,12},{12,8},{16,20},{20,16},{24,28},{28,24},{1,5},{5... | collective-permute-start | bytes 786440 | tf_op jit(solution)/shard_map/ppermute | solution.py:211
  25.5 1.9 %collective-permute-start.10 = (bf16[128,1024]{1,0:T(8,128)(2,1)S(1)}, bf16[128,1024]{1,0:T(8,128)(2,1)S(1)}, u32[]{:S(2)}, u32[]{:S(2)}) collective-permute-start(bf16[128,1024]{1,0:T(8,128)(2,1)S(1)} %collective-permute-done.9.refs_8_), channel_id=1, source_target_pairs={{0,4},{4,0},{8,12},{12,8},{16,20},{20,16},{24,28},{28,24},{1,5},{5... | collective-permute-start | bytes 786440 | tf_op jit(solution)/shard_map/ppermute | solution.py:211
  25.8 1.7 %collective-permute-start.8 = (bf16[128,1024]{1,0:T(8,128)(2,1)S(1)}, bf16[128,1024]{1,0:T(8,128)(2,1)S(1)}, u32[]{:S(2)}, u32[]{:S(2)}) collective-permute-start(bf16[128,1024]{1,0:T(8,128)(2,1)S(1)} %collective-permute-done.7.refs_6_), channel_id=1, source_target_pairs={{0,4},{4,0},{8,12},{12,8},{16,20},{20,16},{24,28},{28,24},{1,5},{5... | collective-permute-start | bytes 786440 | tf_op jit(solution)/shard_map/ppermute | solution.py:211
  26.0 1.4 %copy-start = (s32[1024]{0:T(1024)S(1)}, s32[1024]{0:T(1024)}, u32[]{:S(2)}) copy-start(s32[1024]{0:T(1024)} %param.5) | copy-start | bytes 12292
  26.0 1.4 %collective-permute-start.5 = (s32[16,128]{1,0:T(8,128)S(1)}, s32[16,128]{1,0:T(8,128)S(1)}, u32[]{:S(2)}, u32[]{:S(2)}) collective-permute-start(s32[16,128]{1,0:T(8,128)S(1)} %pad_add_fusion.refs_2_), channel_id=1, source_target_pairs={{0,4},{4,0},{8,12},{12,8},{16,20},{20,16},{24,28},{28,24},{1,5},{5... | collective-permute-start | bytes 24584 | tf_op jit(solution)/shard_map/ppermute | solution.py:211

commit v16 on v15

--- a/solution.py
+++ b/solution.py
@@ -64,7 +64,7 @@
         scores = half_scale * lax.dot_general(
             embed_ref[aligned(row, row_chunk), :],
             anchors,
-            (((1,), (0,)), ((), ())),
+            (((1,), (1,)), ((), ())),
             preferred_element_type=jnp.float32,
         )
         score_ref[buffer, aligned(row, row_chunk), :] = scores
@@ -126,14 +126,14 @@
                 stat_ref[8 + m : 9 + m, lanes] = jnp.sum(sums[at], axis=0, keepdims=True)
                 stat_ref[16 + m : 17 + m, lanes] = jnp.sum(sums[at + 1], axis=0, keepdims=True)
 
-    first = jnp.transpose(embed_ref[0:lane_block, :])
+    first = embed_ref[0:lane_block, :]
     picked = over_chunks(lambda chunk, have: score_chunk(first, 0, 0, chunk, have), nothing)
 
     def block_step(block, pos):
         start = block * lane_block
         following = start + lane_block
         buffer = block % 2
-        anchors = jnp.transpose(embed_ref[aligned(following, lane_block), :])
+        anchors = embed_ref[aligned(following, lane_block), :]
 
         def both(chunk, carry):
             picked, sums = carry
@@ -226,20 +226,25 @@
     line = {d: swap(embed, "row", 2 * d) for d in range(1, levels)}
     far = levels - 1
     ranking = [far // 2 + 1, far] + [d for d in range(1, far) if d != far // 2 + 1]
-    ids = spread(positives.T)
+    corner = cols - 1
+    early = swap(embed, "col", corner)
+    ids = positives.T
+    ids = spread(ids)
     parts, ids = lax.optimization_barrier(([line[d] for d in ranking], ids))
     line = dict(zip(ranking, parts))
     tall = join([embed] + [line[d] for d in range(1, levels)])
 
-    plane = {p: swap(tall, "col", p) for p in range(1, cols)}
+    plane = {0: tall}
+    plane.update({p: swap(tall, "col", p) for p in range(1, corner)})
+    beyond = {d: swap(early, "row", 2 * d) for d in range(1, levels)}
     while steps:
         ids = spread(ids)
+    plane[corner] = join([early] + [beyond[d] for d in range(1, levels)])
+
     here, ids = lax.optimization_barrier((tall, ids))
     other = {0: swap(here, "row", 1)}
+    other.update({p: swap(plane[p], "row", 1) for p in range(1, cols)})
     ids = (ids, swap(ids, "row", 1))
-
-    plane[0] = tall
-    other.update({p: swap(plane[p], "row", 1) for p in range(1, cols)})
     pieces = []
     layout = []
     for p in range(cols):

time: 34.8 us -> 34 us (0.977)
  waiting for transfers between devices: 12.8 us -> 6.25 us
  starting transfers between devices: 13.6 us -> 19.3 us
    ppermute x13 -> x16, waiting for transfers between devices: 12.8 us -> 6.25 us  [swap(): return lax.ppermute(array, axis, [(i, i ^ mask) for i in range(size)])]
    ppermute x13 -> x16, starting transfers between devices: 13.6 us -> 19.3 us  [swap(): return lax.ppermute(array, axis, [(i, i ^ mask) for i in range(size)])]
    unnamed x7 -> x10, local copies, waits for them, and re-layouts: 0.86 us -> 0.88 us
  transfers between devices with their start and end apart: 13 -> 16, of which waited for: 6 -> 5; matrix products, arithmetic and copies ran while one was open for 3% -> 3% of each run, Pallas kernels for 0% -> 0%
where the time goes in v16:
time: 34 us; the launch traced here: 33.9 us
  starting transfers between devices  19.3 us (57%)
  Pallas kernels  7.22 us (21%)
  waiting for transfers between devices  6.25 us (18%)
  local copies, waits for them, and re-layouts  0.89 us (3%)
    ppermute x16, starting transfers between devices, swap(): return lax.ppermute(array, axis, [(i, i ^ mask) for i in range(size)])  19.3 us
    pallas_call x1, Pallas kernels, body(): pl.pallas_call(functools.partial(kernel, cols, order, shard, pos_count, l...  7.22 us
    ppermute x16, waiting for transfers between devices, swap(): return lax.ppermute(array, axis, [(i, i ^ mask) for i in range(size)])  6.25 us
    unnamed x10, local copies, waits for them, and re-layouts  0.88 us
  transfers between devices with their start and end apart: 16, of which 5 were waited for; matrix products, arithmetic and copies ran while one was open for 3% of the time, Pallas kernels for 0%

profile of v16, /device:TPU:0, one launch (start us, length us, event | category | flops | bytes accessed | tf_op | source)
XLA Modules:
  0.0 33.9 jit_solution(12836100388664374444)
XLA Ops:
  0.0 3.0 %collective-permute-start.2 = (bf16[32,1024]{1,0:T(8,128)(2,1)}, bf16[32,1024]{1,0:T(8,128)(2,1)S(1)}, u32[]{:S(2)}, u32[]{:S(2)}) collective-permute-start(bf16[32,1024]{1,0:T(8,128)(2,1)} %param.3), channel_id=1, source_target_pairs={{0,8},{4,12},{8,0},{12,4},{16,24},{20,28},{24,16},{28,20},{1,9},{5... | collective-permute-start | bytes 196616 | tf_op jit(solution)/shard_map/ppermute | solution.py:211
  3.0 2.5 %collective-permute-start.1 = (bf16[32,1024]{1,0:T(8,128)(2,1)}, bf16[32,1024]{1,0:T(8,128)(2,1)S(1)}, u32[]{:S(2)}, u32[]{:S(2)}) collective-permute-start(bf16[32,1024]{1,0:T(8,128)(2,1)} %param.3), channel_id=1, source_target_pairs={{0,24},{4,28},{8,16},{12,20},{16,8},{20,12},{24,0},{28,4},{1,25},{... | collective-permute-start | bytes 196616 | tf_op jit(solution)/shard_map/ppermute | solution.py:211
  5.5 0.1 collective-permute-start
  5.6 2.4 %collective-permute-start.11 = (bf16[32,1024]{1,0:T(8,128)(2,1)}, bf16[32,1024]{1,0:T(8,128)(2,1)S(1)}, u32[]{:S(2)}, u32[]{:S(2)}) collective-permute-start(bf16[32,1024]{1,0:T(8,128)(2,1)} %param.3), channel_id=1, source_target_pairs={{0,3},{1,2},{2,1},{3,0},{4,7},{5,6},{6,5},{7,4},{8,11},{9,10},{10,... | collective-permute-start | bytes 196616 | tf_op jit(solution)/shard_map/ppermute | solution.py:211
  8.1 0.0 copy-start.1
  8.1 2.8 %collective-permute-start.3 = (s32[4,128]{1,0:T(4,128)}, s32[4,128]{1,0:T(4,128)S(1)}, u32[]{:S(2)}, u32[]{:S(2)}) collective-permute-start(s32[4,128]{1,0:T(4,128)} %bitcast.5), channel_id=1, source_target_pairs={{0,16},{4,20},{8,24},{12,28},{16,0},{20,4},{24,8},{28,12},{1,17},{... | collective-permute-start | bytes 6152 | tf_op jit(solution)/shard_map/ppermute | solution.py:211
  10.9 0.8 %constant_dynamic-update-slice_fusion.3 = bf16[128,1024]{1,0:T(8,128)(2,1)S(1)} fusion(bf16[32,1024]{1,0:T(8,128)(2,1)} %param.3), kind=kLoop, calls=%fused_computation.3 | loop fusion | bytes 131072
  11.7 1.0 %collective-permute-done.3 = s32[4,128]{1,0:T(4,128)S(1)} collective-permute-done((s32[4,128]{1,0:T(4,128)}, s32[4,128]{1,0:T(4,128)S(1)}, u32[]{:S(2)}, u32[]{:S(2)}) %collective-permute-start.3) | collective-permute-done | bytes 2080 | tf_op jit(solution)/shard_map/ppermute | solution.py:211
  12.8 0.0 copy-done.1
  12.8 0.0 collective-permute-done.2
  12.8 0.0 collective-permute-done.1
  12.8 0.0 collective-permute-done
  12.8 1.1 %collective-permute-start.9 = (bf16[128,1024]{1,0:T(8,128)(2,1)S(1)}, bf16[128,1024]{1,0:T(8,128)(2,1)S(1)}, u32[]{:S(2)}, u32[]{:S(2)}) collective-permute-start(bf16[128,1024]{1,0:T(8,128)(2,1)S(1)} %constant_dynamic-update-slice_fusion.refs_4_), channel_id=1, source_target_pairs={{0,2},{1,3},{2,0},{3,1},{4,6},{5,7},{6,4},{7,5},{8,10},{9,11},{10,... | collective-permute-start | bytes 786440 | tf_op jit(solution)/shard_map/ppermute | solution.py:211
  13.9 1.5 %collective-permute-start.7 = (bf16[128,1024]{1,0:T(8,128)(2,1)S(1)}, bf16[128,1024]{1,0:T(8,128)(2,1)S(1)}, u32[]{:S(2)}, u32[]{:S(2)}) collective-permute-start(bf16[128,1024]{1,0:T(8,128)(2,1)S(1)} %constant_dynamic-update-slice_fusion.refs_4_), channel_id=1, source_target_pairs={{0,1},{1,0},{2,3},{3,2},{4,5},{5,4},{6,7},{7,6},{8,9},{9,8},{10,11... | collective-permute-start | bytes 786440 | tf_op jit(solution)/shard_map/ppermute | solution.py:211
  15.4 0.4 %collective-permute-start.4 = (s32[8,128]{1,0:T(8,128)S(1)}, s32[8,128]{1,0:T(8,128)S(1)}, u32[]{:S(2)}, u32[]{:S(2)}) collective-permute-start(s32[8,128]{1,0:T(8,128)S(1)} %pad_add_fusion.1), channel_id=1, source_target_pairs={{0,8},{4,12},{8,0},{12,4},{16,24},{20,28},{24,16},{28,20},{1,9},{5... | collective-permute-start | bytes 12296 | tf_op jit(solution)/shard_map/ppermute | solution.py:211
  15.9 0.0 collective-permute-done.11
  15.9 2.5 %collective-permute-start.14 = (bf16[32,1024]{1,0:T(8,128)(2,1)S(1)}, bf16[32,1024]{1,0:T(8,128)(2,1)S(1)}, u32[]{:S(2)}, u32[]{:S(2)}) collective-permute-start(bf16[32,1024]{1,0:T(8,128)(2,1)S(1)} %collective-permute-done.11), channel_id=1, source_target_pairs={{0,24},{4,28},{8,16},{12,20},{16,8},{20,12},{24,0},{28,4},{1,25},{... | collective-permute-start | bytes 196616 | tf_op jit(solution)/shard_map/ppermute | solution.py:211
  18.3 0.6 %collective-permute-start.13 = (bf16[32,1024]{1,0:T(8,128)(2,1)S(1)}, bf16[32,1024]{1,0:T(8,128)(2,1)S(1)}, u32[]{:S(2)}, u32[]{:S(2)}) collective-permute-start(bf16[32,1024]{1,0:T(8,128)(2,1)S(1)} %collective-permute-done.11), channel_id=1, source_target_pairs={{0,16},{4,20},{8,24},{12,28},{16,0},{20,4},{24,8},{28,12},{1,17},{... | collective-permute-start | bytes 196616 | tf_op jit(solution)/shard_map/ppermute | solution.py:211
  18.9 0.1 collective-permute-done.4
  19.0 1.3 %collective-permute-start.12 = (bf16[32,1024]{1,0:T(8,128)(2,1)S(1)}, bf16[32,1024]{1,0:T(8,128)(2,1)S(1)}, u32[]{:S(2)}, u32[]{:S(2)}) collective-permute-start(bf16[32,1024]{1,0:T(8,128)(2,1)S(1)} %collective-permute-done.11), channel_id=1, source_target_pairs={{0,8},{4,12},{8,0},{12,4},{16,24},{20,28},{24,16},{28,20},{1,9},{5... | collective-permute-start | bytes 196616 | tf_op jit(solution)/shard_map/ppermute | solution.py:211
  20.3 3.1 %collective-permute-done.12 = bf16[32,1024]{1,0:T(8,128)(2,1)S(1)} collective-permute-done((bf16[32,1024]{1,0:T(8,128)(2,1)S(1)}, bf16[32,1024]{1,0:T(8,128)(2,1)S(1)}, u32[]{:S(2)}, u32[]{:S(2)}) %collective-permute-start.12) | collective-permute-done | bytes 65568 | tf_op jit(solution)/shard_map/ppermute | solution.py:211
  23.4 0.0 collective-permute-start.6
  23.4 0.8 %collective-permute-done.13 = bf16[32,1024]{1,0:T(8,128)(2,1)S(1)} collective-permute-done((bf16[32,1024]{1,0:T(8,128)(2,1)S(1)}, bf16[32,1024]{1,0:T(8,128)(2,1)S(1)}, u32[]{:S(2)}, u32[]{:S(2)}) %collective-permute-start.13) | collective-permute-done | bytes 65568 | tf_op jit(solution)/shard_map/ppermute | solution.py:211
  24.2 0.0 collective-permute-done.14
  24.2 0.1 collective-permute-start.15
  24.3 0.0 collective-permute-done.9.refs_8_
  24.3 0.5 %collective-permute-start.10 = (bf16[128,1024]{1,0:T(8,128)(2,1)S(1)}, bf16[128,1024]{1,0:T(8,128)(2,1)S(1)}, u32[]{:S(2)}, u32[]{:S(2)}) collective-permute-start(bf16[128,1024]{1,0:T(8,128)(2,1)S(1)} %collective-permute-done.9.refs_8_), channel_id=1, source_target_pairs={{0,4},{4,0},{8,12},{12,8},{16,20},{20,16},{24,28},{28,24},{1,5},{5... | collective-permute-start | bytes 786440 | tf_op jit(solution)/shard_map/ppermute | solution.py:211
  24.8 0.0 collective-permute-done.7.refs_6_
  24.8 0.1 collective-permute-start.8
  24.9 0.0 copy-start
  24.9 0.4 %collective-permute-start.5 = (s32[16,128]{1,0:T(8,128)S(1)}, s32[16,128]{1,0:T(8,128)S(1)}, u32[]{:S(2)}, u32[]{:S(2)}) collective-permute-start(s32[16,128]{1,0:T(8,128)S(1)} %pad_add_fusion.refs_2_), channel_id=1, source_target_pairs={{0,4},{4,0},{8,12},{12,8},{16,20},{20,16},{24,28},{28,24},{1,5},{5... | collective-permute-start | bytes 24584 | tf_op jit(solution)/shard_map/ppermute | solution.py:211
  25.3 0.1 pad_add_fusion.2.refs_0_
  25.4 1.2 %collective-permute-done.5.refs_3_ = s32[16,128]{1,0:T(8,128)S(1)} collective-permute-done((s32[16,128]{1,0:T(8,128)S(1)}, s32[16,128]{1,0:T(8,128)S(1)}, u32[]{:S(2)}, u32[]{:S(2)}) %collective-permute-start.5) | collective-permute-done | bytes 8224 | tf_op jit(solution)/shard_map/ppermute | solution.py:211
  26.6 0.0 collective-permute-done.6.refs_5_
  26.6 0.0 collective-permute-done.15.refs_11_
  26.6 0.0 collective-permute-done.10.refs_9_
  26.6 0.0 collective-permute-done.8.refs_7_
  26.6 0.0 copy-done
  26.6 7.2 %shard_map.37 = f32[32,1024]{1,0:T(8,128)} custom-call(s32[2]{0:T(128)S(1)} %pad_add_fusion.2.refs_0_, s32[8,128]{1,0:T(8,128)S(1)} %bitcast.4, s32[16,128]{1,0:T(8,128)S(1)} %pad_add_fusion.refs_2_, s32[16,128]{1,0:T(8,128)S(1)} %collective-permute-done.5.refs_3_, bf16[128,1024]{1,0:T(8,128)(2,1)S(1)} %constant_dynamic-update-slice_fusion.refs_4_, ...), custom_call_target="tpu_custom_call" | custom-call | flops 2147483648 | bytes 2097152 | tf_op jit(solution)/shard_map/pallas_call | solution.py:257
  (9 shorter events, 0.1 us)
Async XLA Ops:
  0.0 12.8 %collective-permute-start.2 = (bf16[32,1024]{1,0:T(8,128)(2,1)}, bf16[32,1024]{1,0:T(8,128)(2,1)S(1)}, u32[]{:S(2)}, u32[]{:S(2)}) collective-permute-start(bf16[32,1024]{1,0:T(8,128)(2,1)} %param.3), channel_id=1, source_target_pairs={{0,8},{4,12},{8,0},{12,4},{16,24},{20,28},{24,16},{28,20},{1,9},{5... | collective-permute-start | bytes 196616 | tf_op jit(solution)/shard_map/ppermute | solution.py:211
  3.0 9.8 %collective-permute-start.1 = (bf16[32,1024]{1,0:T(8,128)(2,1)}, bf16[32,1024]{1,0:T(8,128)(2,1)S(1)}, u32[]{:S(2)}, u32[]{:S(2)}) collective-permute-start(bf16[32,1024]{1,0:T(8,128)(2,1)} %param.3), channel_id=1, source_target_pairs={{0,24},{4,28},{8,16},{12,20},{16,8},{20,12},{24,0},{28,4},{1,25},{... | collective-permute-start | bytes 196616 | tf_op jit(solution)/shard_map/ppermute | solution.py:211
  5.5 7.3 %collective-permute-start = (bf16[32,1024]{1,0:T(8,128)(2,1)}, bf16[32,1024]{1,0:T(8,128)(2,1)S(1)}, u32[]{:S(2)}, u32[]{:S(2)}) collective-permute-start(bf16[32,1024]{1,0:T(8,128)(2,1)} %param.3), channel_id=1, source_target_pairs={{0,16},{4,20},{8,24},{12,28},{16,0},{20,4},{24,8},{28,12},{1,17},{... | collective-permute-start | bytes 196616 | tf_op jit(solution)/shard_map/ppermute | solution.py:211
  5.6 10.2 %collective-permute-start.11 = (bf16[32,1024]{1,0:T(8,128)(2,1)}, bf16[32,1024]{1,0:T(8,128)(2,1)S(1)}, u32[]{:S(2)}, u32[]{:S(2)}) collective-permute-start(bf16[32,1024]{1,0:T(8,128)(2,1)} %param.3), channel_id=1, source_target_pairs={{0,3},{1,2},{2,1},{3,0},{4,7},{5,6},{6,5},{7,4},{8,11},{9,10},{10,... | collective-permute-start | bytes 196616 | tf_op jit(solution)/shard_map/ppermute | solution.py:211
  8.1 4.7 %copy-start.1 = (s32[128,4]{0,1:T(4,128)S(1)}, s32[128,4]{0,1:T(4,128)}, u32[]{:S(2)}) copy-start(s32[128,4]{0,1:T(4,128)} %param.4) | copy-start | bytes 6148
  8.1 4.7 %collective-permute-start.3 = (s32[4,128]{1,0:T(4,128)}, s32[4,128]{1,0:T(4,128)S(1)}, u32[]{:S(2)}, u32[]{:S(2)}) collective-permute-start(s32[4,128]{1,0:T(4,128)} %bitcast.5), channel_id=1, source_target_pairs={{0,16},{4,20},{8,24},{12,28},{16,0},{20,4},{24,8},{28,12},{1,17},{... | collective-permute-start | bytes 6152 | tf_op jit(solution)/shard_map/ppermute | solution.py:211
  12.8 11.5 %collective-permute-start.9 = (bf16[128,1024]{1,0:T(8,128)(2,1)S(1)}, bf16[128,1024]{1,0:T(8,128)(2,1)S(1)}, u32[]{:S(2)}, u32[]{:S(2)}) collective-permute-start(bf16[128,1024]{1,0:T(8,128)(2,1)S(1)} %constant_dynamic-update-slice_fusion.refs_4_), channel_id=1, source_target_pairs={{0,2},{1,3},{2,0},{3,1},{4,6},{5,7},{6,4},{7,5},{8,10},{9,11},{10,... | collective-permute-start | bytes 786440 | tf_op jit(solution)/shard_map/ppermute | solution.py:211
  13.9 10.9 %collective-permute-start.7 = (bf16[128,1024]{1,0:T(8,128)(2,1)S(1)}, bf16[128,1024]{1,0:T(8,128)(2,1)S(1)}, u32[]{:S(2)}, u32[]{:S(2)}) collective-permute-start(bf16[128,1024]{1,0:T(8,128)(2,1)S(1)} %constant_dynamic-update-slice_fusion.refs_4_), channel_id=1, source_target_pairs={{0,1},{1,0},{2,3},{3,2},{4,5},{5,4},{6,7},{7,6},{8,9},{9,8},{10,11... | collective-permute-start | bytes 786440 | tf_op jit(solution)/shard_map/ppermute | solution.py:211
  15.4 3.6 %collective-permute-start.4 = (s32[8,128]{1,0:T(8,128)S(1)}, s32[8,128]{1,0:T(8,128)S(1)}, u32[]{:S(2)}, u32[]{:S(2)}) collective-permute-start(s32[8,128]{1,0:T(8,128)S(1)} %pad_add_fusion.1), channel_id=1, source_target_pairs={{0,8},{4,12},{8,0},{12,4},{16,24},{20,28},{24,16},{28,20},{1,9},{5... | collective-permute-start | bytes 12296 | tf_op jit(solution)/shard_map/ppermute | solution.py:211
  15.9 8.4 %collective-permute-start.14 = (bf16[32,1024]{1,0:T(8,128)(2,1)S(1)}, bf16[32,1024]{1,0:T(8,128)(2,1)S(1)}, u32[]{:S(2)}, u32[]{:S(2)}) collective-permute-start(bf16[32,1024]{1,0:T(8,128)(2,1)S(1)} %collective-permute-done.11), channel_id=1, source_target_pairs={{0,24},{4,28},{8,16},{12,20},{16,8},{20,12},{24,0},{28,4},{1,25},{... | collective-permute-start | bytes 196616 | tf_op jit(solution)/shard_map/ppermute | solution.py:211
  18.3 5.9 %collective-permute-start.13 = (bf16[32,1024]{1,0:T(8,128)(2,1)S(1)}, bf16[32,1024]{1,0:T(8,128)(2,1)S(1)}, u32[]{:S(2)}, u32[]{:S(2)}) collective-permute-start(bf16[32,1024]{1,0:T(8,128)(2,1)S(1)} %collective-permute-done.11), channel_id=1, source_target_pairs={{0,16},{4,20},{8,24},{12,28},{16,0},{20,4},{24,8},{28,12},{1,17},{... | collective-permute-start | bytes 196616 | tf_op jit(solution)/shard_map/ppermute | solution.py:211
  19.0 4.4 %collective-permute-start.12 = (bf16[32,1024]{1,0:T(8,128)(2,1)S(1)}, bf16[32,1024]{1,0:T(8,128)(2,1)S(1)}, u32[]{:S(2)}, u32[]{:S(2)}) collective-permute-start(bf16[32,1024]{1,0:T(8,128)(2,1)S(1)} %collective-permute-done.11), channel_id=1, source_target_pairs={{0,8},{4,12},{8,0},{12,4},{16,24},{20,28},{24,16},{28,20},{1,9},{5... | collective-permute-start | bytes 196616 | tf_op jit(solution)/shard_map/ppermute | solution.py:211
  23.4 3.2 %collective-permute-start.6 = (bf16[128,1024]{1,0:T(8,128)(2,1)S(1)}, bf16[128,1024]{1,0:T(8,128)(2,1)S(1)}, u32[]{:S(2)}, u32[]{:S(2)}) collective-permute-start(bf16[128,1024]{1,0:T(8,128)(2,1)S(1)} %constant_dynamic-update-slice_fusion.refs_4_), channel_id=1, source_target_pairs={{0,4},{4,0},{8,12},{12,8},{16,20},{20,16},{24,28},{28,24},{1,5},{5... | collective-permute-start | bytes 786440 | tf_op jit(solution)/shard_map/ppermute | solution.py:211
  24.2 2.4 %collective-permute-start.15 = (bf16[128,1024]{1,0:T(8,128)(2,1)S(1)}, bf16[128,1024]{1,0:T(8,128)(2,1)S(1)}, u32[]{:S(2)}, u32[]{:S(2)}) collective-permute-start(bf16[128,1024]{1,0:T(8,128)(2,1)S(1)} %constant_dynamic-update-slice_fusion.4.refs_10_), channel_id=1, source_target_pairs={{0,4},{4,0},{8,12},{12,8},{16,20},{20,16},{24,28},{28,24},{1,5},{5... | collective-permute-start | bytes 786440 | tf_op jit(solution)/shard_map/ppermute | solution.py:211
  24.3 2.3 %collective-permute-start.10 = (bf16[128,1024]{1,0:T(8,128)(2,1)S(1)}, bf16[128,1024]{1,0:T(8,128)(2,1)S(1)}, u32[]{:S(2)}, u32[]{:S(2)}) collective-permute-start(bf16[128,1024]{1,0:T(8,128)(2,1)S(1)} %collective-permute-done.9.refs_8_), channel_id=1, source_target_pairs={{0,4},{4,0},{8,12},{12,8},{16,20},{20,16},{24,28},{28,24},{1,5},{5... | collective-permute-start | bytes 786440 | tf_op jit(solution)/shard_map/ppermute | solution.py:211
  24.8 1.8 %collective-permute-start.8 = (bf16[128,1024]{1,0:T(8,128)(2,1)S(1)}, bf16[128,1024]{1,0:T(8,128)(2,1)S(1)}, u32[]{:S(2)}, u32[]{:S(2)}) collective-permute-start(bf16[128,1024]{1,0:T(8,128)(2,1)S(1)} %collective-permute-done.7.refs_6_), channel_id=1, source_target_pairs={{0,4},{4,0},{8,12},{12,8},{16,20},{20,16},{24,28},{28,24},{1,5},{5... | collective-permute-start | bytes 786440 | tf_op jit(solution)/shard_map/ppermute | solution.py:211
  24.9 1.7 %copy-start = (s32[1024]{0:T(1024)S(1)}, s32[1024]{0:T(1024)}, u32[]{:S(2)}) copy-start(s32[1024]{0:T(1024)} %param.5) | copy-start | bytes 12292
  24.9 1.7 %collective-permute-start.5 = (s32[16,128]{1,0:T(8,128)S(1)}, s32[16,128]{1,0:T(8,128)S(1)}, u32[]{:S(2)}, u32[]{:S(2)}) collective-permute-start(s32[16,128]{1,0:T(8,128)S(1)} %pad_add_fusion.refs_2_), channel_id=1, source_target_pairs={{0,4},{4,0},{8,12},{12,8},{16,20},{20,16},{24,28},{28,24},{1,5},{5... | collective-permute-start | bytes 24584 | tf_op jit(solution)/shard_map/ppermute | solution.py:211

commit v17 on v16

--- a/solution.py
+++ b/solution.py
@@ -28,12 +28,10 @@
     return found
 
 
-def kernel(cols, order, shard, pos_count, lane_block, layout, *refs):
-    levels = len(order)
+def kernel(cols, shard, pos_count, lane_block, layout, *refs):
     place_ref, table_ref = refs[:2]
-    ids_refs = refs[2:4]
-    pieces = refs[4 : 4 + len(layout)]
-    out_ref, embed_ref, score_ref, own_ref, target_ref, stat_ref = refs[4 + len(layout) :]
+    pieces = refs[2 : 2 + len(layout)]
+    out_ref, embed_ref, score_ref, own_ref, target_ref, stat_ref = refs[2 + len(layout) :]
     total = embed_ref.shape[0]
     me = place_ref[0]
     my_col = place_ref[1]
@@ -41,23 +39,25 @@
     small = total <= 1024
     row_chunk = min(512, total)
 
+    width = embed_ref.shape[1]
+    group = cols * shard
     for piece, slots in zip(pieces, layout):
         for spot, slot in enumerate(slots):
-            embed_ref[slot * shard : (slot + 1) * shard, :] = piece[spot * shard : (spot + 1) * shard, :]
-
-    group = cols * shard
-    for line in range(2 * levels):
-        for begin in range(0, group, 128):
-            ids_ref = ids_refs[line % 2]
-            size = ids_ref.shape[0] // levels
-            at = order.index(line // 2) * size
-            ids = ids_ref[at : at + size, begin : begin + 128]
-            ids = jnp.concatenate([ids] * (8 // size), axis=0)
-            found = lookup(table_ref, ids) ^ me
-            lane = lax.broadcasted_iota(jnp.int32, found.shape, 1)
-            found = jnp.take_along_axis(found, lane ^ (my_col % 128), axis=1)
-            start = line * group + (begin ^ (my_col - my_col % 128))
-            target_ref[:, pl.ds(pl.multiple_of(start, 128), 128)] = found
+            rows = slice(spot * shard, (spot + 1) * shard)
+            embed_ref[slot * shard : (slot + 1) * shard, :] = piece[rows, 0:width]
+            if piece.shape[1] == width:
+                continue
+            tail = piece[rows, width : width + 128].astype(jnp.float32).astype(jnp.int32)
+            for begin in range(0, group, 128):
+                lines = [k * (group // 128) + begin // 128 for k in range(2 * pos_count)]
+                parts = jnp.concatenate([tail[k : k + 1, :] for k in lines], axis=0)
+                ids = parts[0:pos_count] * 256 + parts[pos_count : 2 * pos_count]
+                ids = jnp.concatenate([ids] * (8 // pos_count), axis=0)
+                found = lookup(table_ref, ids) ^ me
+                lane = lax.broadcasted_iota(jnp.int32, found.shape, 1)
+                found = jnp.take_along_axis(found, lane ^ (my_col % 128), axis=1)
+                start = slot // cols * group + (begin ^ (my_col - my_col % 128))
+                target_ref[:, pl.ds(pl.multiple_of(start, 128), 128)] = found
 
     def score_chunk(anchors, start, buffer, chunk, picked):
         row = chunk * row_chunk
@@ -213,38 +213,27 @@
     def join(parts):
         return parts[0] if len(parts) == 1 else jnp.concatenate(parts, axis=0)
 
-    order = [0]
-    steps = [1 << b for b in reversed(range(levels.bit_length() - 1))]
-
-    def spread(ids):
-        if not steps:
-            return ids
-        bit = steps.pop(0)
-        order.extend([d ^ bit for d in order])
-        return jnp.concatenate([ids, swap(ids, "row", 2 * bit)], axis=0)
-
     line = {d: swap(embed, "row", 2 * d) for d in range(1, levels)}
     far = levels - 1
-    ranking = [far // 2 + 1, far] + [d for d in range(1, far) if d != far // 2 + 1]
+    middle = far // 2 + 1
+    ranking = [middle, far] + [d for d in range(1, far) if d != middle]
     corner = cols - 1
     early = swap(embed, "col", corner)
-    ids = positives.T
-    ids = spread(ids)
-    parts, ids = lax.optimization_barrier(([line[d] for d in ranking], ids))
+    parts = lax.optimization_barrier([line[d] for d in ranking])
     line = dict(zip(ranking, parts))
     tall = join([embed] + [line[d] for d in range(1, levels)])
+
+    ids = positives.T
+    ids = jnp.concatenate([ids // 256, ids % 256], axis=0).astype(jnp.bfloat16).reshape(-1, 128)
+    ids = jnp.concatenate([ids, jnp.zeros((shard - ids.shape[0], 128), ids.dtype)], axis=0)
+    early = jnp.concatenate([early, ids], axis=1)
 
     plane = {0: tall}
     plane.update({p: swap(tall, "col", p) for p in range(1, corner)})
     beyond = {d: swap(early, "row", 2 * d) for d in range(1, levels)}
-    while steps:
-        ids = spread(ids)
     plane[corner] = join([early] + [beyond[d] for d in range(1, levels)])
 
-    here, ids = lax.optimization_barrier((tall, ids))
-    other = {0: swap(here, "row", 1)}
-    other.update({p: swap(plane[p], "row", 1) for p in range(1, cols)})
-    ids = (ids, swap(ids, "row", 1))
+    other = {p: swap(plane[p], "row", 1) for p in range(cols)}
     pieces = []
     layout = []
     for p in range(cols):
@@ -255,9 +244,9 @@
     place = jnp.stack([lax.axis_index(axes) * shard, lax.axis_index("col") * shard])
     vmem = pl.BlockSpec(memory_space=pltpu.VMEM)
     return pl.pallas_call(
-        functools.partial(kernel, cols, order, shard, pos_count, lane_block, layout),
+        functools.partial(kernel, cols, shard, pos_count, lane_block, layout),
         out_shape=jax.ShapeDtypeStruct((shard, width), jnp.float32),
-        in_specs=[pl.BlockSpec(memory_space=pltpu.SMEM)] + [vmem] * (3 + len(pieces)),
+        in_specs=[pl.BlockSpec(memory_space=pltpu.SMEM)] + [vmem] * (1 + len(pieces)),
         out_specs=vmem,
         scratch_shapes=[
             pltpu.VMEM((total, width), jnp.bfloat16),
@@ -275,7 +264,6 @@
     )(
         place.astype(jnp.int32),
         placement.reshape(-1, 128),
-        *ids,
         *pieces,
     )
 

time: 34 us -> 32.3 us (0.950)
  starting transfers between devices: 19.3 us -> 16.1 us
  waiting for transfers between devices: 6.25 us -> 7.74 us
    ppermute x16 -> x13, starting transfers between devices: 19.3 us -> 16.1 us  [swap(): return lax.ppermute(array, axis, [(i, i ^ mask) for i in range(size)])]
    ppermute x16 -> x13, waiting for transfers between devices: 6.25 us -> 7.74 us  [swap(): return lax.ppermute(array, axis, [(i, i ^ mask) for i in range(size)])]
    unnamed x10 -> x7, local copies, waits for them, and re-layouts: 0.88 us -> 0.9 us
  transfers between devices with their start and end apart: 16 -> 13, of which waited for: 5 -> 5; matrix products, arithmetic and copies ran while one was open for 3% -> 3% of each run, Pallas kernels for 0% -> 0%
where the time goes in v17:
time: 32.3 us; the launch traced here: 32.2 us
  starting transfers between devices  16.1 us (50%)
  waiting for transfers between devices  7.74 us (24%)
  Pallas kernels  7.22 us (22%)
  local copies, waits for them, and re-layouts  0.9 us (3%)
    ppermute x13, starting transfers between devices, swap(): return lax.ppermute(array, axis, [(i, i ^ mask) for i in range(size)])  16.1 us
    ppermute x13, waiting for transfers between devices, swap(): return lax.ppermute(array, axis, [(i, i ^ mask) for i in range(size)])  7.74 us
    pallas_call x1, Pallas kernels, body(): pl.pallas_call(functools.partial(kernel, cols, shard, pos_count, lane_blo...  7.22 us
    unnamed x7, local copies, waits for them, and re-layouts  0.9 us
  transfers between devices with their start and end apart: 13, of which 5 were waited for; matrix products, arithmetic and copies ran while one was open for 3% of the time, Pallas kernels for 0%

profile of v17, /device:TPU:0, one launch (start us, length us, event | category | flops | bytes accessed | tf_op | source)
XLA Modules:
  0.0 32.2 jit_solution(1526275320007657182)
XLA Ops:
  0.0 0.0 copy-start.1
  0.0 3.0 %collective-permute-start.2 = (bf16[32,1024]{1,0:T(8,128)(2,1)}, bf16[32,1024]{1,0:T(8,128)(2,1)S(1)}, u32[]{:S(2)}, u32[]{:S(2)}) collective-permute-start(bf16[32,1024]{1,0:T(8,128)(2,1)} %param.3), channel_id=1, source_target_pairs={{0,8},{4,12},{8,0},{12,4},{16,24},{20,28},{24,16},{28,20},{1,9},{5... | collective-permute-start | bytes 196616 | tf_op jit(solution)/shard_map/ppermute | solution.py:211
  3.0 2.5 %collective-permute-start.1 = (bf16[32,1024]{1,0:T(8,128)(2,1)}, bf16[32,1024]{1,0:T(8,128)(2,1)S(1)}, u32[]{:S(2)}, u32[]{:S(2)}) collective-permute-start(bf16[32,1024]{1,0:T(8,128)(2,1)} %param.3), channel_id=1, source_target_pairs={{0,24},{4,28},{8,16},{12,20},{16,8},{20,12},{24,0},{28,4},{1,25},{... | collective-permute-start | bytes 196616 | tf_op jit(solution)/shard_map/ppermute | solution.py:211
  5.5 0.1 collective-permute-start
  5.6 2.4 %collective-permute-start.8 = (bf16[32,1024]{1,0:T(8,128)(2,1)}, bf16[32,1024]{1,0:T(8,128)(2,1)S(1)}, u32[]{:S(2)}, u32[]{:S(2)}) collective-permute-start(bf16[32,1024]{1,0:T(8,128)(2,1)} %param.3), channel_id=1, source_target_pairs={{0,3},{1,2},{2,1},{3,0},{4,7},{5,6},{6,5},{7,4},{8,11},{9,10},{10,... | collective-permute-start | bytes 196616 | tf_op jit(solution)/shard_map/ppermute | solution.py:211
  8.1 0.9 %constant_dynamic-update-slice_fusion.3 = bf16[128,1024]{1,0:T(8,128)(2,1)S(1)} fusion(bf16[32,1024]{1,0:T(8,128)(2,1)} %param.3), kind=kLoop, calls=%fused_computation.8 | loop fusion | bytes 131072
  8.9 0.0 copy-done.1
  9.0 2.0 %collective-permute-done.8 = bf16[32,1024]{1,0:T(8,128)(2,1)S(1)} collective-permute-done((bf16[32,1024]{1,0:T(8,128)(2,1)}, bf16[32,1024]{1,0:T(8,128)(2,1)S(1)}, u32[]{:S(2)}, u32[]{:S(2)}) %collective-permute-start.8) | collective-permute-done | bytes 65568 | tf_op jit(solution)/shard_map/ppermute | solution.py:211
  11.0 2.9 %collective-permute-start.11 = (bf16[32,1152]{1,0:T(8,128)(2,1)S(1)}, bf16[32,1152]{1,0:T(8,128)(2,1)S(1)}, u32[]{:S(2)}, u32[]{:S(2)}) collective-permute-start(bf16[32,1152]{1,0:T(8,128)(2,1)S(1)} %pad_maximum_fusion.1), channel_id=1, source_target_pairs={{0,24},{4,28},{8,16},{12,20},{16,8},{20,12},{24,0},{28,4},{1,25},{... | collective-permute-start | bytes 221192 | tf_op jit(solution)/shard_map/ppermute | solution.py:211
  13.9 0.3 %collective-permute-start.10 = (bf16[32,1152]{1,0:T(8,128)(2,1)S(1)}, bf16[32,1152]{1,0:T(8,128)(2,1)S(1)}, u32[]{:S(2)}, u32[]{:S(2)}) collective-permute-start(bf16[32,1152]{1,0:T(8,128)(2,1)S(1)} %pad_maximum_fusion.1), channel_id=1, source_target_pairs={{0,16},{4,20},{8,24},{12,28},{16,0},{20,4},{24,8},{28,12},{1,17},{... | collective-permute-start | bytes 221192 | tf_op jit(solution)/shard_map/ppermute | solution.py:211
  14.3 0.0 collective-permute-done.2
  14.3 1.1 %collective-permute-start.9 = (bf16[32,1152]{1,0:T(8,128)(2,1)S(1)}, bf16[32,1152]{1,0:T(8,128)(2,1)S(1)}, u32[]{:S(2)}, u32[]{:S(2)}) collective-permute-start(bf16[32,1152]{1,0:T(8,128)(2,1)S(1)} %pad_maximum_fusion.1), channel_id=1, source_target_pairs={{0,8},{4,12},{8,0},{12,4},{16,24},{20,28},{24,16},{28,20},{1,9},{5... | collective-permute-start | bytes 221192 | tf_op jit(solution)/shard_map/ppermute | solution.py:211
  15.4 0.0 collective-permute-done.1
  15.4 0.0 collective-permute-done
  15.4 1.6 %collective-permute-start.6 = (bf16[128,1024]{1,0:T(8,128)(2,1)S(1)}, bf16[128,1024]{1,0:T(8,128)(2,1)S(1)}, u32[]{:S(2)}, u32[]{:S(2)}) collective-permute-start(bf16[128,1024]{1,0:T(8,128)(2,1)S(1)} %constant_dynamic-update-slice_fusion.refs_2_), channel_id=1, source_target_pairs={{0,2},{1,3},{2,0},{3,1},{4,6},{5,7},{6,4},{7,5},{8,10},{9,11},{10,... | collective-permute-start | bytes 786440 | tf_op jit(solution)/shard_map/ppermute | solution.py:211
  17.0 1.5 %collective-permute-start.4 = (bf16[128,1024]{1,0:T(8,128)(2,1)S(1)}, bf16[128,1024]{1,0:T(8,128)(2,1)S(1)}, u32[]{:S(2)}, u32[]{:S(2)}) collective-permute-start(bf16[128,1024]{1,0:T(8,128)(2,1)S(1)} %constant_dynamic-update-slice_fusion.refs_2_), channel_id=1, source_target_pairs={{0,1},{1,0},{2,3},{3,2},{4,5},{5,4},{6,7},{7,6},{8,9},{9,8},{10,11... | collective-permute-start | bytes 786440 | tf_op jit(solution)/shard_map/ppermute | solution.py:211
  18.5 0.0 collective-permute-done.11
  18.5 1.3 %collective-permute-done.10 = bf16[32,1152]{1,0:T(8,128)(2,1)S(1)} collective-permute-done((bf16[32,1152]{1,0:T(8,128)(2,1)S(1)}, bf16[32,1152]{1,0:T(8,128)(2,1)S(1)}, u32[]{:S(2)}, u32[]{:S(2)}) %collective-permute-start.10) | collective-permute-done | bytes 73760 | tf_op jit(solution)/shard_map/ppermute | solution.py:211
  19.9 0.0 collective-permute-done.9
  19.9 0.1 collective-permute-start.12
  20.0 0.5 %collective-permute-start.3 = (bf16[128,1024]{1,0:T(8,128)(2,1)S(1)}, bf16[128,1024]{1,0:T(8,128)(2,1)S(1)}, u32[]{:S(2)}, u32[]{:S(2)}) collective-permute-start(bf16[128,1024]{1,0:T(8,128)(2,1)S(1)} %constant_dynamic-update-slice_fusion.refs_2_), channel_id=1, source_target_pairs={{0,4},{4,0},{8,12},{12,8},{16,20},{20,16},{24,28},{28,24},{1,5},{5... | collective-permute-start | bytes 786440 | tf_op jit(solution)/shard_map/ppermute | solution.py:211
  20.5 1.4 %collective-permute-done.6.refs_6_ = bf16[128,1024]{1,0:T(8,128)(2,1)S(1)} collective-permute-done((bf16[128,1024]{1,0:T(8,128)(2,1)S(1)}, bf16[128,1024]{1,0:T(8,128)(2,1)S(1)}, u32[]{:S(2)}, u32[]{:S(2)}) %collective-permute-start.6) | collective-permute-done | bytes 262176 | tf_op jit(solution)/shard_map/ppermute | solution.py:211
  21.9 0.0 collective-permute-start.7
  21.9 1.5 %collective-permute-done.4.refs_4_ = bf16[128,1024]{1,0:T(8,128)(2,1)S(1)} collective-permute-done((bf16[128,1024]{1,0:T(8,128)(2,1)S(1)}, bf16[128,1024]{1,0:T(8,128)(2,1)S(1)}, u32[]{:S(2)}, u32[]{:S(2)}) %collective-permute-start.4) | collective-permute-done | bytes 262176 | tf_op jit(solution)/shard_map/ppermute | solution.py:211
  23.4 0.0 collective-permute-start.5
  23.4 0.0 copy-start
  23.4 0.1 pad_add_fusion.refs_0_
  23.5 0.0 collective-permute-done.3.refs_3_
  23.5 0.0 collective-permute-done.12.refs_9_
  23.5 0.0 collective-permute-done.7.refs_7_
  23.5 1.4 %collective-permute-done.5.refs_5_ = bf16[128,1024]{1,0:T(8,128)(2,1)S(1)} collective-permute-done((bf16[128,1024]{1,0:T(8,128)(2,1)S(1)}, bf16[128,1024]{1,0:T(8,128)(2,1)S(1)}, u32[]{:S(2)}, u32[]{:S(2)}) %collective-permute-start.5) | collective-permute-done | bytes 262176 | tf_op jit(solution)/shard_map/ppermute | solution.py:211
  24.9 0.0 copy-done
  24.9 7.2 %shard_map.37 = f32[32,1024]{1,0:T(8,128)} custom-call(s32[2]{0:T(128)S(1)} %pad_add_fusion.refs_0_, s32[8,128]{1,0:T(8,128)S(1)} %bitcast.25, bf16[128,1024]{1,0:T(8,128)(2,1)S(1)} %constant_dynamic-update-slice_fusion.refs_2_, bf16[128,1024]{1,0:T(8,128)(2,1)S(1)} %collective-permute-done.3.refs_3_, bf16[128,1024]{1,0:T(8,128)(2,1)S(1)} %collective-permute-done.4.refs_4_, ...), custom_call_target="tpu_custom_call" | custom-call | flops 2147483648 | bytes 2097152 | tf_op jit(solution)/shard_map/pallas_call | solution.py:246
  (7 shorter events, 0.1 us)
Async XLA Ops:
  0.0 8.9 %copy-start.1 = (s32[128,4]{0,1:T(4,128)S(1)}, s32[128,4]{0,1:T(4,128)}, u32[]{:S(2)}) copy-start(s32[128,4]{0,1:T(4,128)} %param.4) | copy-start | bytes 6148
  0.0 14.3 %collective-permute-start.2 = (bf16[32,1024]{1,0:T(8,128)(2,1)}, bf16[32,1024]{1,0:T(8,128)(2,1)S(1)}, u32[]{:S(2)}, u32[]{:S(2)}) collective-permute-start(bf16[32,1024]{1,0:T(8,128)(2,1)} %param.3), channel_id=1, source_target_pairs={{0,8},{4,12},{8,0},{12,4},{16,24},{20,28},{24,16},{28,20},{1,9},{5... | collective-permute-start | bytes 196616 | tf_op jit(solution)/shard_map/ppermute | solution.py:211
  3.0 12.4 %collective-permute-start.1 = (bf16[32,1024]{1,0:T(8,128)(2,1)}, bf16[32,1024]{1,0:T(8,128)(2,1)S(1)}, u32[]{:S(2)}, u32[]{:S(2)}) collective-permute-start(bf16[32,1024]{1,0:T(8,128)(2,1)} %param.3), channel_id=1, source_target_pairs={{0,24},{4,28},{8,16},{12,20},{16,8},{20,12},{24,0},{28,4},{1,25},{... | collective-permute-start | bytes 196616 | tf_op jit(solution)/shard_map/ppermute | solution.py:211
  5.5 9.9 %collective-permute-start = (bf16[32,1024]{1,0:T(8,128)(2,1)}, bf16[32,1024]{1,0:T(8,128)(2,1)S(1)}, u32[]{:S(2)}, u32[]{:S(2)}) collective-permute-start(bf16[32,1024]{1,0:T(8,128)(2,1)} %param.3), channel_id=1, source_target_pairs={{0,16},{4,20},{8,24},{12,28},{16,0},{20,4},{24,8},{28,12},{1,17},{... | collective-permute-start | bytes 196616 | tf_op jit(solution)/shard_map/ppermute | solution.py:211
  5.6 5.4 %collective-permute-start.8 = (bf16[32,1024]{1,0:T(8,128)(2,1)}, bf16[32,1024]{1,0:T(8,128)(2,1)S(1)}, u32[]{:S(2)}, u32[]{:S(2)}) collective-permute-start(bf16[32,1024]{1,0:T(8,128)(2,1)} %param.3), channel_id=1, source_target_pairs={{0,3},{1,2},{2,1},{3,0},{4,7},{5,6},{6,5},{7,4},{8,11},{9,10},{10,... | collective-permute-start | bytes 196616 | tf_op jit(solution)/shard_map/ppermute | solution.py:211
  11.0 7.5 %collective-permute-start.11 = (bf16[32,1152]{1,0:T(8,128)(2,1)S(1)}, bf16[32,1152]{1,0:T(8,128)(2,1)S(1)}, u32[]{:S(2)}, u32[]{:S(2)}) collective-permute-start(bf16[32,1152]{1,0:T(8,128)(2,1)S(1)} %pad_maximum_fusion.1), channel_id=1, source_target_pairs={{0,24},{4,28},{8,16},{12,20},{16,8},{20,12},{24,0},{28,4},{1,25},{... | collective-permute-start | bytes 221192 | tf_op jit(solution)/shard_map/ppermute | solution.py:211
  13.9 5.9 %collective-permute-start.10 = (bf16[32,1152]{1,0:T(8,128)(2,1)S(1)}, bf16[32,1152]{1,0:T(8,128)(2,1)S(1)}, u32[]{:S(2)}, u32[]{:S(2)}) collective-permute-start(bf16[32,1152]{1,0:T(8,128)(2,1)S(1)} %pad_maximum_fusion.1), channel_id=1, source_target_pairs={{0,16},{4,20},{8,24},{12,28},{16,0},{20,4},{24,8},{28,12},{1,17},{... | collective-permute-start | bytes 221192 | tf_op jit(solution)/shard_map/ppermute | solution.py:211
  14.3 5.6 %collective-permute-start.9 = (bf16[32,1152]{1,0:T(8,128)(2,1)S(1)}, bf16[32,1152]{1,0:T(8,128)(2,1)S(1)}, u32[]{:S(2)}, u32[]{:S(2)}) collective-permute-start(bf16[32,1152]{1,0:T(8,128)(2,1)S(1)} %pad_maximum_fusion.1), channel_id=1, source_target_pairs={{0,8},{4,12},{8,0},{12,4},{16,24},{20,28},{24,16},{28,20},{1,9},{5... | collective-permute-start | bytes 221192 | tf_op jit(solution)/shard_map/ppermute | solution.py:211
  15.4 6.4 %collective-permute-start.6 = (bf16[128,1024]{1,0:T(8,128)(2,1)S(1)}, bf16[128,1024]{1,0:T(8,128)(2,1)S(1)}, u32[]{:S(2)}, u32[]{:S(2)}) collective-permute-start(bf16[128,1024]{1,0:T(8,128)(2,1)S(1)} %constant_dynamic-update-slice_fusion.refs_2_), channel_id=1, source_target_pairs={{0,2},{1,3},{2,0},{3,1},{4,6},{5,7},{6,4},{7,5},{8,10},{9,11},{10,... | collective-permute-start | bytes 786440 | tf_op jit(solution)/shard_map/ppermute | solution.py:211
  17.0 6.4 %collective-permute-start.4 = (bf16[128,1024]{1,0:T(8,128)(2,1)S(1)}, bf16[128,1024]{1,0:T(8,128)(2,1)S(1)}, u32[]{:S(2)}, u32[]{:S(2)}) collective-permute-start(bf16[128,1024]{1,0:T(8,128)(2,1)S(1)} %constant_dynamic-update-slice_fusion.refs_2_), channel_id=1, source_target_pairs={{0,1},{1,0},{2,3},{3,2},{4,5},{5,4},{6,7},{7,6},{8,9},{9,8},{10,11... | collective-permute-start | bytes 786440 | tf_op jit(solution)/shard_map/ppermute | solution.py:211
  19.9 3.6 %collective-permute-start.12 = (bf16[128,1152]{1,0:T(8,128)(2,1)S(1)}, bf16[128,1152]{1,0:T(8,128)(2,1)S(1)}, u32[]{:S(2)}, u32[]{:S(2)}) collective-permute-start(bf16[128,1152]{1,0:T(8,128)(2,1)S(1)} %pad_maximum_fusion.refs_8_), channel_id=1, source_target_pairs={{0,4},{4,0},{8,12},{12,8},{16,20},{20,16},{24,28},{28,24},{1,5},{5... | collective-permute-start | bytes 884744 | tf_op jit(solution)/shard_map/ppermute | solution.py:211
  20.0 3.5 %collective-permute-start.3 = (bf16[128,1024]{1,0:T(8,128)(2,1)S(1)}, bf16[128,1024]{1,0:T(8,128)(2,1)S(1)}, u32[]{:S(2)}, u32[]{:S(2)}) collective-permute-start(bf16[128,1024]{1,0:T(8,128)(2,1)S(1)} %constant_dynamic-update-slice_fusion.refs_2_), channel_id=1, source_target_pairs={{0,4},{4,0},{8,12},{12,8},{16,20},{20,16},{24,28},{28,24},{1,5},{5... | collective-permute-start | bytes 786440 | tf_op jit(solution)/shard_map/ppermute | solution.py:211
  21.9 1.6 %collective-permute-start.7 = (bf16[128,1024]{1,0:T(8,128)(2,1)S(1)}, bf16[128,1024]{1,0:T(8,128)(2,1)S(1)}, u32[]{:S(2)}, u32[]{:S(2)}) collective-permute-start(bf16[128,1024]{1,0:T(8,128)(2,1)S(1)} %collective-permute-done.6.refs_6_), channel_id=1, source_target_pairs={{0,4},{4,0},{8,12},{12,8},{16,20},{20,16},{24,28},{28,24},{1,5},{5... | collective-permute-start | bytes 786440 | tf_op jit(solution)/shard_map/ppermute | solution.py:211
  23.4 1.5 %collective-permute-start.5 = (bf16[128,1024]{1,0:T(8,128)(2,1)S(1)}, bf16[128,1024]{1,0:T(8,128)(2,1)S(1)}, u32[]{:S(2)}, u32[]{:S(2)}) collective-permute-start(bf16[128,1024]{1,0:T(8,128)(2,1)S(1)} %collective-permute-done.4.refs_4_), channel_id=1, source_target_pairs={{0,4},{4,0},{8,12},{12,8},{16,20},{20,16},{24,28},{28,24},{1,5},{5... | collective-permute-start | bytes 786440 | tf_op jit(solution)/shard_map/ppermute | solution.py:211
  23.4 1.5 %copy-start = (s32[1024]{0:T(1024)S(1)}, s32[1024]{0:T(1024)}, u32[]{:S(2)}) copy-start(s32[1024]{0:T(1024)} %param.5) | copy-start | bytes 12292

commit v18 on v17

--- a/solution.py
+++ b/solution.py
@@ -231,6 +231,11 @@
     plane = {0: tall}
     plane.update({p: swap(tall, "col", p) for p in range(1, corner)})
     beyond = {d: swap(early, "row", 2 * d) for d in range(1, levels)}
+    near = [p for p in range(1, corner)]
+    tied = lax.optimization_barrier((plane[near[0]], [plane[p] for p in near[1:]], [beyond[d] for d in ranking]))
+    plane[near[0]] = tied[0]
+    plane.update(zip(near[1:], tied[1]))
+    beyond = dict(zip(ranking, tied[2]))
     plane[corner] = join([early] + [beyond[d] for d in range(1, levels)])
 
     other = {p: swap(plane[p], "row", 1) for p in range(cols)}

time: 32.3 us -> 35.2 us (1.090)
  waiting for transfers between devices: 7.74 us -> 11 us
    ppermute x13, waiting for transfers between devices: 7.74 us -> 11 us  [swap(): return lax.ppermute(array, axis, [(i, i ^ mask) for i in range(size)])]
  transfers between devices with their start and end apart: 13 -> 13, of which waited for: 5 -> 8; matrix products, arithmetic and copies ran while one was open for 3% -> 3% of each run, Pallas kernels for 0% -> 0%
where the time goes in v18:
time: 35.2 us; the launch traced here: 35.1 us
  starting transfers between devices  15.8 us (45%)
  waiting for transfers between devices  11 us (31%)
  Pallas kernels  7.21 us (20%)
  local copies, waits for them, and re-layouts  0.9 us (3%)
    ppermute x13, starting transfers between devices, swap(): return lax.ppermute(array, axis, [(i, i ^ mask) for i in range(size)])  15.8 us
    ppermute x13, waiting for transfers between devices, swap(): return lax.ppermute(array, axis, [(i, i ^ mask) for i in range(size)])  11 us
    pallas_call x1, Pallas kernels, body(): pl.pallas_call(functools.partial(kernel, cols, shard, pos_count, lane_blo...  7.21 us
    unnamed x7, local copies, waits for them, and re-layouts  0.9 us
  transfers between devices with their start and end apart: 13, of which 8 were waited for; matrix products, arithmetic and copies ran while one was open for 3% of the time, Pallas kernels for 0%

profile of v18, /device:TPU:0, one launch (start us, length us, event | category | flops | bytes accessed | tf_op | source)
XLA Modules:
  0.0 35.1 jit_solution(1536284522616006726)
XLA Ops:
  0.0 0.0 copy-start.1
  0.0 3.0 %collective-permute-start.2 = (bf16[32,1024]{1,0:T(8,128)(2,1)}, bf16[32,1024]{1,0:T(8,128)(2,1)S(1)}, u32[]{:S(2)}, u32[]{:S(2)}) collective-permute-start(bf16[32,1024]{1,0:T(8,128)(2,1)} %param.3), channel_id=1, source_target_pairs={{0,8},{4,12},{8,0},{12,4},{16,24},{20,28},{24,16},{28,20},{1,9},{5... | collective-permute-start | bytes 196616 | tf_op jit(solution)/shard_map/ppermute | solution.py:211
  3.0 2.5 %collective-permute-start.1 = (bf16[32,1024]{1,0:T(8,128)(2,1)}, bf16[32,1024]{1,0:T(8,128)(2,1)S(1)}, u32[]{:S(2)}, u32[]{:S(2)}) collective-permute-start(bf16[32,1024]{1,0:T(8,128)(2,1)} %param.3), channel_id=1, source_target_pairs={{0,24},{4,28},{8,16},{12,20},{16,8},{20,12},{24,0},{28,4},{1,25},{... | collective-permute-start | bytes 196616 | tf_op jit(solution)/shard_map/ppermute | solution.py:211
  5.5 0.1 collective-permute-start
  5.6 2.4 %collective-permute-start.6 = (bf16[32,1024]{1,0:T(8,128)(2,1)}, bf16[32,1024]{1,0:T(8,128)(2,1)S(1)}, u32[]{:S(2)}, u32[]{:S(2)}) collective-permute-start(bf16[32,1024]{1,0:T(8,128)(2,1)} %param.3), channel_id=1, source_target_pairs={{0,3},{1,2},{2,1},{3,0},{4,7},{5,6},{6,5},{7,4},{8,11},{9,10},{10,... | collective-permute-start | bytes 196616 | tf_op jit(solution)/shard_map/ppermute | solution.py:211
  8.1 0.9 %constant_dynamic-update-slice_fusion.3 = bf16[128,1024]{1,0:T(8,128)(2,1)S(1)} fusion(bf16[32,1024]{1,0:T(8,128)(2,1)} %param.3), kind=kLoop, calls=%fused_computation.8 | loop fusion | bytes 131072
  8.9 0.0 copy-done.1
  9.0 0.0 collective-permute-done.2
  9.0 1.1 %collective-permute-done.1 = bf16[32,1024]{1,0:T(8,128)(2,1)S(1)} collective-permute-done((bf16[32,1024]{1,0:T(8,128)(2,1)}, bf16[32,1024]{1,0:T(8,128)(2,1)S(1)}, u32[]{:S(2)}, u32[]{:S(2)}) %collective-permute-start.1) | collective-permute-done | bytes 65568 | tf_op jit(solution)/shard_map/ppermute | solution.py:211
  10.1 2.1 %collective-permute-done = bf16[32,1024]{1,0:T(8,128)(2,1)S(1)} collective-permute-done((bf16[32,1024]{1,0:T(8,128)(2,1)}, bf16[32,1024]{1,0:T(8,128)(2,1)S(1)}, u32[]{:S(2)}, u32[]{:S(2)}) %collective-permute-start) | collective-permute-done | bytes 65568 | tf_op jit(solution)/shard_map/ppermute | solution.py:211
  12.2 1.6 %collective-permute-start.5 = (bf16[128,1024]{1,0:T(8,128)(2,1)S(1)}, bf16[128,1024]{1,0:T(8,128)(2,1)S(1)}, u32[]{:S(2)}, u32[]{:S(2)}) collective-permute-start(bf16[128,1024]{1,0:T(8,128)(2,1)S(1)} %constant_dynamic-update-slice_fusion.refs_2_), channel_id=1, source_target_pairs={{0,2},{1,3},{2,0},{3,1},{4,6},{5,7},{6,4},{7,5},{8,10},{9,11},{10,... | collective-permute-start | bytes 786440 | tf_op jit(solution)/shard_map/ppermute | solution.py:211
  13.8 1.5 %collective-permute-start.4 = (bf16[128,1024]{1,0:T(8,128)(2,1)S(1)}, bf16[128,1024]{1,0:T(8,128)(2,1)S(1)}, u32[]{:S(2)}, u32[]{:S(2)}) collective-permute-start(bf16[128,1024]{1,0:T(8,128)(2,1)S(1)} %constant_dynamic-update-slice_fusion.refs_2_), channel_id=1, source_target_pairs={{0,1},{1,0},{2,3},{3,2},{4,5},{5,4},{6,7},{7,6},{8,9},{9,8},{10,11... | collective-permute-start | bytes 786440 | tf_op jit(solution)/shard_map/ppermute | solution.py:211
  15.3 0.0 collective-permute-done.6
  15.3 0.1 collective-permute-start.9
  15.4 2.5 %collective-permute-start.8 = (bf16[32,1152]{1,0:T(8,128)(2,1)S(1)}, bf16[32,1152]{1,0:T(8,128)(2,1)S(1)}, u32[]{:S(2)}, u32[]{:S(2)}) collective-permute-start(bf16[32,1152]{1,0:T(8,128)(2,1)S(1)} %pad_maximum_fusion.1), channel_id=1, source_target_pairs={{0,24},{4,28},{8,16},{12,20},{16,8},{20,12},{24,0},{28,4},{1,25},{... | collective-permute-start | bytes 221192 | tf_op jit(solution)/shard_map/ppermute | solution.py:211
  17.8 1.0 %collective-permute-start.7 = (bf16[32,1152]{1,0:T(8,128)(2,1)S(1)}, bf16[32,1152]{1,0:T(8,128)(2,1)S(1)}, u32[]{:S(2)}, u32[]{:S(2)}) collective-permute-start(bf16[32,1152]{1,0:T(8,128)(2,1)S(1)} %pad_maximum_fusion.1), channel_id=1, source_target_pairs={{0,16},{4,20},{8,24},{12,28},{16,0},{20,4},{24,8},{28,12},{1,17},{... | collective-permute-start | bytes 221192 | tf_op jit(solution)/shard_map/ppermute | solution.py:211
  18.9 2.0 %collective-permute-done.9 = bf16[32,1152]{1,0:T(8,128)(2,1)S(1)} collective-permute-done((bf16[32,1152]{1,0:T(8,128)(2,1)S(1)}, bf16[32,1152]{1,0:T(8,128)(2,1)S(1)}, u32[]{:S(2)}, u32[]{:S(2)}) %collective-permute-start.9) | collective-permute-done | bytes 73760 | tf_op jit(solution)/shard_map/ppermute | solution.py:211
  20.9 1.5 %collective-permute-done.8 = bf16[32,1152]{1,0:T(8,128)(2,1)S(1)} collective-permute-done((bf16[32,1152]{1,0:T(8,128)(2,1)S(1)}, bf16[32,1152]{1,0:T(8,128)(2,1)S(1)}, u32[]{:S(2)}, u32[]{:S(2)}) %collective-permute-start.8) | collective-permute-done | bytes 73760 | tf_op jit(solution)/shard_map/ppermute | solution.py:211
  22.4 2.6 %collective-permute-done.7 = bf16[32,1152]{1,0:T(8,128)(2,1)S(1)} collective-permute-done((bf16[32,1152]{1,0:T(8,128)(2,1)S(1)}, bf16[32,1152]{1,0:T(8,128)(2,1)S(1)}, u32[]{:S(2)}, u32[]{:S(2)}) %collective-permute-start.7) | collective-permute-done | bytes 73760 | tf_op jit(solution)/shard_map/ppermute | solution.py:211
  25.0 0.0 collective-permute-done.5.refs_6_
  25.0 0.0 collective-permute-done.4.refs_4_
  25.1 0.1 collective-permute-start.12
  25.2 0.5 %collective-permute-start.3 = (bf16[128,1024]{1,0:T(8,128)(2,1)S(1)}, bf16[128,1024]{1,0:T(8,128)(2,1)S(1)}, u32[]{:S(2)}, u32[]{:S(2)}) collective-permute-start(bf16[128,1024]{1,0:T(8,128)(2,1)S(1)} %constant_dynamic-update-slice_fusion.refs_2_), channel_id=1, source_target_pairs={{0,4},{4,0},{8,12},{12,8},{16,20},{20,16},{24,28},{28,24},{1,5},{5... | collective-permute-start | bytes 786440 | tf_op jit(solution)/shard_map/ppermute | solution.py:211
  25.7 0.1 collective-permute-start.10
  25.7 0.4 %collective-permute-start.11 = (bf16[128,1024]{1,0:T(8,128)(2,1)S(1)}, bf16[128,1024]{1,0:T(8,128)(2,1)S(1)}, u32[]{:S(2)}, u32[]{:S(2)}) collective-permute-start(bf16[128,1024]{1,0:T(8,128)(2,1)S(1)} %collective-permute-done.5.refs_6_), channel_id=1, source_target_pairs={{0,4},{4,0},{8,12},{12,8},{16,20},{20,16},{24,28},{28,24},{1,5},{5... | collective-permute-start | bytes 786440 | tf_op jit(solution)/shard_map/ppermute | solution.py:211
  26.2 0.0 copy-start
  26.2 0.1 pad_add_fusion.refs_0_
  26.2 0.9 %collective-permute-done.3.refs_3_ = bf16[128,1024]{1,0:T(8,128)(2,1)S(1)} collective-permute-done((bf16[128,1024]{1,0:T(8,128)(2,1)S(1)}, bf16[128,1024]{1,0:T(8,128)(2,1)S(1)}, u32[]{:S(2)}, u32[]{:S(2)}) %collective-permute-start.3) | collective-permute-done | bytes 262176 | tf_op jit(solution)/shard_map/ppermute | solution.py:211
  27.1 0.4 %collective-permute-done.10.refs_5_ = bf16[128,1024]{1,0:T(8,128)(2,1)S(1)} collective-permute-done((bf16[128,1024]{1,0:T(8,128)(2,1)S(1)}, bf16[128,1024]{1,0:T(8,128)(2,1)S(1)}, u32[]{:S(2)}, u32[]{:S(2)}) %collective-permute-start.10) | collective-permute-done | bytes 262176 | tf_op jit(solution)/shard_map/ppermute | solution.py:211
  27.5 0.4 %collective-permute-done.11.refs_7_ = bf16[128,1024]{1,0:T(8,128)(2,1)S(1)} collective-permute-done((bf16[128,1024]{1,0:T(8,128)(2,1)S(1)}, bf16[128,1024]{1,0:T(8,128)(2,1)S(1)}, u32[]{:S(2)}, u32[]{:S(2)}) %collective-permute-start.11) | collective-permute-done | bytes 262176 | tf_op jit(solution)/shard_map/ppermute | solution.py:211
  27.9 0.0 collective-permute-done.12.refs_9_
  27.9 0.0 copy-done
  27.9 7.2 %shard_map.37 = f32[32,1024]{1,0:T(8,128)} custom-call(s32[2]{0:T(128)S(1)} %pad_add_fusion.refs_0_, s32[8,128]{1,0:T(8,128)S(1)} %bitcast.25, bf16[128,1024]{1,0:T(8,128)(2,1)S(1)} %constant_dynamic-update-slice_fusion.refs_2_, bf16[128,1024]{1,0:T(8,128)(2,1)S(1)} %collective-permute-done.3.refs_3_, bf16[128,1024]{1,0:T(8,128)(2,1)S(1)} %collective-permute-done.4.refs_4_, ...), custom_call_target="tpu_custom_call" | custom-call | flops 2147483648 | bytes 2097152 | tf_op jit(solution)/shard_map/pallas_call | solution.py:251
  (7 shorter events, 0.1 us)
Async XLA Ops:
  0.0 8.9 %copy-start.1 = (s32[128,4]{0,1:T(4,128)S(1)}, s32[128,4]{0,1:T(4,128)}, u32[]{:S(2)}) copy-start(s32[128,4]{0,1:T(4,128)} %param.4) | copy-start | bytes 6148
  0.0 9.0 %collective-permute-start.2 = (bf16[32,1024]{1,0:T(8,128)(2,1)}, bf16[32,1024]{1,0:T(8,128)(2,1)S(1)}, u32[]{:S(2)}, u32[]{:S(2)}) collective-permute-start(bf16[32,1024]{1,0:T(8,128)(2,1)} %param.3), channel_id=1, source_target_pairs={{0,8},{4,12},{8,0},{12,4},{16,24},{20,28},{24,16},{28,20},{1,9},{5... | collective-permute-start | bytes 196616 | tf_op jit(solution)/shard_map/ppermute | solution.py:211
  3.0 7.1 %collective-permute-start.1 = (bf16[32,1024]{1,0:T(8,128)(2,1)}, bf16[32,1024]{1,0:T(8,128)(2,1)S(1)}, u32[]{:S(2)}, u32[]{:S(2)}) collective-permute-start(bf16[32,1024]{1,0:T(8,128)(2,1)} %param.3), channel_id=1, source_target_pairs={{0,24},{4,28},{8,16},{12,20},{16,8},{20,12},{24,0},{28,4},{1,25},{... | collective-permute-start | bytes 196616 | tf_op jit(solution)/shard_map/ppermute | solution.py:211
  5.5 6.7 %collective-permute-start = (bf16[32,1024]{1,0:T(8,128)(2,1)}, bf16[32,1024]{1,0:T(8,128)(2,1)S(1)}, u32[]{:S(2)}, u32[]{:S(2)}) collective-permute-start(bf16[32,1024]{1,0:T(8,128)(2,1)} %param.3), channel_id=1, source_target_pairs={{0,16},{4,20},{8,24},{12,28},{16,0},{20,4},{24,8},{28,12},{1,17},{... | collective-permute-start | bytes 196616 | tf_op jit(solution)/shard_map/ppermute | solution.py:211
  5.6 9.7 %collective-permute-start.6 = (bf16[32,1024]{1,0:T(8,128)(2,1)}, bf16[32,1024]{1,0:T(8,128)(2,1)S(1)}, u32[]{:S(2)}, u32[]{:S(2)}) collective-permute-start(bf16[32,1024]{1,0:T(8,128)(2,1)} %param.3), channel_id=1, source_target_pairs={{0,3},{1,2},{2,1},{3,0},{4,7},{5,6},{6,5},{7,4},{8,11},{9,10},{10,... | collective-permute-start | bytes 196616 | tf_op jit(solution)/shard_map/ppermute | solution.py:211
  12.2 12.8 %collective-permute-start.5 = (bf16[128,1024]{1,0:T(8,128)(2,1)S(1)}, bf16[128,1024]{1,0:T(8,128)(2,1)S(1)}, u32[]{:S(2)}, u32[]{:S(2)}) collective-permute-start(bf16[128,1024]{1,0:T(8,128)(2,1)S(1)} %constant_dynamic-update-slice_fusion.refs_2_), channel_id=1, source_target_pairs={{0,2},{1,3},{2,0},{3,1},{4,6},{5,7},{6,4},{7,5},{8,10},{9,11},{10,... | collective-permute-start | bytes 786440 | tf_op jit(solution)/shard_map/ppermute | solution.py:211
  13.8 11.3 %collective-permute-start.4 = (bf16[128,1024]{1,0:T(8,128)(2,1)S(1)}, bf16[128,1024]{1,0:T(8,128)(2,1)S(1)}, u32[]{:S(2)}, u32[]{:S(2)}) collective-permute-start(bf16[128,1024]{1,0:T(8,128)(2,1)S(1)} %constant_dynamic-update-slice_fusion.refs_2_), channel_id=1, source_target_pairs={{0,1},{1,0},{2,3},{3,2},{4,5},{5,4},{6,7},{7,6},{8,9},{9,8},{10,11... | collective-permute-start | bytes 786440 | tf_op jit(solution)/shard_map/ppermute | solution.py:211
  15.3 5.6 %collective-permute-start.9 = (bf16[32,1152]{1,0:T(8,128)(2,1)S(1)}, bf16[32,1152]{1,0:T(8,128)(2,1)S(1)}, u32[]{:S(2)}, u32[]{:S(2)}) collective-permute-start(bf16[32,1152]{1,0:T(8,128)(2,1)S(1)} %pad_maximum_fusion.1), channel_id=1, source_target_pairs={{0,8},{4,12},{8,0},{12,4},{16,24},{20,28},{24,16},{28,20},{1,9},{5... | collective-permute-start | bytes 221192 | tf_op jit(solution)/shard_map/ppermute | solution.py:211
  15.4 7.0 %collective-permute-start.8 = (bf16[32,1152]{1,0:T(8,128)(2,1)S(1)}, bf16[32,1152]{1,0:T(8,128)(2,1)S(1)}, u32[]{:S(2)}, u32[]{:S(2)}) collective-permute-start(bf16[32,1152]{1,0:T(8,128)(2,1)S(1)} %pad_maximum_fusion.1), channel_id=1, source_target_pairs={{0,24},{4,28},{8,16},{12,20},{16,8},{20,12},{24,0},{28,4},{1,25},{... | collective-permute-start | bytes 221192 | tf_op jit(solution)/shard_map/ppermute | solution.py:211
  17.8 7.2 %collective-permute-start.7 = (bf16[32,1152]{1,0:T(8,128)(2,1)S(1)}, bf16[32,1152]{1,0:T(8,128)(2,1)S(1)}, u32[]{:S(2)}, u32[]{:S(2)}) collective-permute-start(bf16[32,1152]{1,0:T(8,128)(2,1)S(1)} %pad_maximum_fusion.1), channel_id=1, source_target_pairs={{0,16},{4,20},{8,24},{12,28},{16,0},{20,4},{24,8},{28,12},{1,17},{... | collective-permute-start | bytes 221192 | tf_op jit(solution)/shard_map/ppermute | solution.py:211
  25.1 2.8 %collective-permute-start.12 = (bf16[128,1152]{1,0:T(8,128)(2,1)S(1)}, bf16[128,1152]{1,0:T(8,128)(2,1)S(1)}, u32[]{:S(2)}, u32[]{:S(2)}) collective-permute-start(bf16[128,1152]{1,0:T(8,128)(2,1)S(1)} %pad_maximum_fusion.refs_8_), channel_id=1, source_target_pairs={{0,4},{4,0},{8,12},{12,8},{16,20},{20,16},{24,28},{28,24},{1,5},{5... | collective-permute-start | bytes 884744 | tf_op jit(solution)/shard_map/ppermute | solution.py:211
  25.2 1.9 %collective-permute-start.3 = (bf16[128,1024]{1,0:T(8,128)(2,1)S(1)}, bf16[128,1024]{1,0:T(8,128)(2,1)S(1)}, u32[]{:S(2)}, u32[]{:S(2)}) collective-permute-start(bf16[128,1024]{1,0:T(8,128)(2,1)S(1)} %constant_dynamic-update-slice_fusion.refs_2_), channel_id=1, source_target_pairs={{0,4},{4,0},{8,12},{12,8},{16,20},{20,16},{24,28},{28,24},{1,5},{5... | collective-permute-start | bytes 786440 | tf_op jit(solution)/shard_map/ppermute | solution.py:211
  25.7 1.8 %collective-permute-start.10 = (bf16[128,1024]{1,0:T(8,128)(2,1)S(1)}, bf16[128,1024]{1,0:T(8,128)(2,1)S(1)}, u32[]{:S(2)}, u32[]{:S(2)}) collective-permute-start(bf16[128,1024]{1,0:T(8,128)(2,1)S(1)} %collective-permute-done.4.refs_4_), channel_id=1, source_target_pairs={{0,4},{4,0},{8,12},{12,8},{16,20},{20,16},{24,28},{28,24},{1,5},{5... | collective-permute-start | bytes 786440 | tf_op jit(solution)/shard_map/ppermute | solution.py:211
  25.7 2.1 %collective-permute-start.11 = (bf16[128,1024]{1,0:T(8,128)(2,1)S(1)}, bf16[128,1024]{1,0:T(8,128)(2,1)S(1)}, u32[]{:S(2)}, u32[]{:S(2)}) collective-permute-start(bf16[128,1024]{1,0:T(8,128)(2,1)S(1)} %collective-permute-done.5.refs_6_), channel_id=1, source_target_pairs={{0,4},{4,0},{8,12},{12,8},{16,20},{20,16},{24,28},{28,24},{1,5},{5... | collective-permute-start | bytes 786440 | tf_op jit(solution)/shard_map/ppermute | solution.py:211
  26.2 1.7 %copy-start = (s32[1024]{0:T(1024)S(1)}, s32[1024]{0:T(1024)}, u32[]{:S(2)}) copy-start(s32[1024]{0:T(1024)} %param.5) | copy-start | bytes 12292

commit v19 on v17

--- a/solution.py
+++ b/solution.py
@@ -219,8 +219,9 @@
     ranking = [middle, far] + [d for d in range(1, far) if d != middle]
     corner = cols - 1
     early = swap(embed, "col", corner)
-    parts = lax.optimization_barrier([line[d] for d in ranking])
-    line = dict(zip(ranking, parts))
+    parts = lax.optimization_barrier([line[middle], line[far], early] + [line[d] for d in ranking[2:]])
+    early_after = parts.pop(2)
+    line = dict(zip([middle, far] + ranking[2:], parts))
     tall = join([embed] + [line[d] for d in range(1, levels)])
 
     ids = positives.T
@@ -231,7 +232,8 @@
     plane = {0: tall}
     plane.update({p: swap(tall, "col", p) for p in range(1, corner)})
     beyond = {d: swap(early, "row", 2 * d) for d in range(1, levels)}
-    plane[corner] = join([early] + [beyond[d] for d in range(1, levels)])
+    corner_rows = jnp.concatenate([early_after, ids], axis=1)
+    plane[corner] = join([corner_rows] + [beyond[d] for d in range(1, levels)])
 
     other = {p: swap(plane[p], "row", 1) for p in range(cols)}
     pieces = []

time: 32.3 us -> 32.1 us (level)
  starting transfers between devices: 16.1 us -> 14.4 us
  waiting for transfers between devices: 7.74 us -> 9.17 us
    ppermute x13, starting transfers between devices: 16.1 us -> 14.4 us  [swap(): return lax.ppermute(array, axis, [(i, i ^ mask) for i in range(size)])]
    ppermute x13, waiting for transfers between devices: 7.74 us -> 9.17 us  [swap(): return lax.ppermute(array, axis, [(i, i ^ mask) for i in range(size)])]
  transfers between devices with their start and end apart: 13 -> 13, of which waited for: 5 -> 6; matrix products, arithmetic and copies ran while one was open for 3% -> 3% of each run, Pallas kernels for 0% -> 0%
where the time goes in v19:
time: 32.1 us; the launch traced here: 31.9 us
  starting transfers between devices  14.4 us (45%)
  waiting for transfers between devices  9.17 us (29%)
  Pallas kernels  7.21 us (22%)
  local copies, waits for them, and re-layouts  0.9 us (3%)
    ppermute x13, starting transfers between devices, swap(): return lax.ppermute(array, axis, [(i, i ^ mask) for i in range(size)])  14.4 us
    ppermute x13, waiting for transfers between devices, swap(): return lax.ppermute(array, axis, [(i, i ^ mask) for i in range(size)])  9.17 us
    pallas_call x1, Pallas kernels, body(): pl.pallas_call(functools.partial(kernel, cols, shard, pos_count, lane_blo...  7.21 us
    unnamed x7, local copies, waits for them, and re-layouts  0.9 us
  transfers between devices with their start and end apart: 13, of which 6 were waited for; matrix products, arithmetic and copies ran while one was open for 3% of the time, Pallas kernels for 0%

profile of v19, /device:TPU:0, one launch (start us, length us, event | category | flops | bytes accessed | tf_op | source)
XLA Modules:
  0.0 31.9 jit_solution(9556210425071232439)
XLA Ops:
  0.0 0.0 copy-start.1
  0.0 3.9 %collective-permute-start.2 = (bf16[32,1024]{1,0:T(8,128)(2,1)}, bf16[32,1024]{1,0:T(8,128)(2,1)S(1)}, u32[]{:S(2)}, u32[]{:S(2)}) collective-permute-start(bf16[32,1024]{1,0:T(8,128)(2,1)} %param.3), channel_id=1, source_target_pairs={{0,3},{1,2},{2,1},{3,0},{4,7},{5,6},{6,5},{7,4},{8,11},{9,10},{10,... | collective-permute-start | bytes 196616 | tf_op jit(solution)/shard_map/ppermute | solution.py:211
  3.9 3.6 %collective-permute-start.1 = (bf16[32,1024]{1,0:T(8,128)(2,1)}, bf16[32,1024]{1,0:T(8,128)(2,1)S(1)}, u32[]{:S(2)}, u32[]{:S(2)}) collective-permute-start(bf16[32,1024]{1,0:T(8,128)(2,1)} %param.3), channel_id=1, source_target_pairs={{0,24},{4,28},{8,16},{12,20},{16,8},{20,12},{24,0},{28,4},{1,25},{... | collective-permute-start | bytes 196616 | tf_op jit(solution)/shard_map/ppermute | solution.py:211
  7.5 0.0 collective-permute-start
  7.5 0.8 %collective-permute-start.3 = (bf16[32,1024]{1,0:T(8,128)(2,1)}, bf16[32,1024]{1,0:T(8,128)(2,1)S(1)}, u32[]{:S(2)}, u32[]{:S(2)}) collective-permute-start(bf16[32,1024]{1,0:T(8,128)(2,1)} %param.3), channel_id=1, source_target_pairs={{0,8},{4,12},{8,0},{12,4},{16,24},{20,28},{24,16},{28,20},{1,9},{5... | collective-permute-start | bytes 196616 | tf_op jit(solution)/shard_map/ppermute | solution.py:211
  8.3 0.9 %constant_dynamic-update-slice_fusion.3 = bf16[128,1024]{1,0:T(8,128)(2,1)S(1)} fusion(bf16[32,1024]{1,0:T(8,128)(2,1)} %param.3), kind=kLoop, calls=%fused_computation.8 | loop fusion | bytes 131072
  9.2 0.0 copy-done.1
  9.2 0.0 collective-permute-done.2
  9.2 3.7 %collective-permute-start.11 = (bf16[32,1152]{1,0:T(8,128)(2,1)S(1)}, bf16[32,1152]{1,0:T(8,128)(2,1)S(1)}, u32[]{:S(2)}, u32[]{:S(2)}) collective-permute-start(bf16[32,1152]{1,0:T(8,128)(2,1)S(1)} %pad_maximum_fusion.1), channel_id=1, source_target_pairs={{0,24},{4,28},{8,16},{12,20},{16,8},{20,12},{24,0},{28,4},{1,25},{... | collective-permute-start | bytes 221192 | tf_op jit(solution)/shard_map/ppermute | solution.py:211
  12.9 0.0 collective-permute-start.10
  12.9 0.0 collective-permute-done.1
  12.9 0.8 %collective-permute-start.9 = (bf16[32,1152]{1,0:T(8,128)(2,1)S(1)}, bf16[32,1152]{1,0:T(8,128)(2,1)S(1)}, u32[]{:S(2)}, u32[]{:S(2)}) collective-permute-start(bf16[32,1152]{1,0:T(8,128)(2,1)S(1)} %pad_maximum_fusion.1), channel_id=1, source_target_pairs={{0,8},{4,12},{8,0},{12,4},{16,24},{20,28},{24,16},{28,20},{1,9},{5... | collective-permute-start | bytes 221192 | tf_op jit(solution)/shard_map/ppermute | solution.py:211
  13.7 2.5 %collective-permute-done = bf16[32,1024]{1,0:T(8,128)(2,1)S(1)} collective-permute-done((bf16[32,1024]{1,0:T(8,128)(2,1)}, bf16[32,1024]{1,0:T(8,128)(2,1)S(1)}, u32[]{:S(2)}, u32[]{:S(2)}) %collective-permute-start) | collective-permute-done | bytes 65568 | tf_op jit(solution)/shard_map/ppermute | solution.py:211
  16.2 0.0 collective-permute-done.3
  16.2 0.6 %collective-permute-start.7 = (bf16[128,1024]{1,0:T(8,128)(2,1)S(1)}, bf16[128,1024]{1,0:T(8,128)(2,1)S(1)}, u32[]{:S(2)}, u32[]{:S(2)}) collective-permute-start(bf16[128,1024]{1,0:T(8,128)(2,1)S(1)} %constant_dynamic-update-slice_fusion.refs_2_), channel_id=1, source_target_pairs={{0,2},{1,3},{2,0},{3,1},{4,6},{5,7},{6,4},{7,5},{8,10},{9,11},{10,... | collective-permute-start | bytes 786440 | tf_op jit(solution)/shard_map/ppermute | solution.py:211
  16.8 0.5 %collective-permute-start.5 = (bf16[128,1024]{1,0:T(8,128)(2,1)S(1)}, bf16[128,1024]{1,0:T(8,128)(2,1)S(1)}, u32[]{:S(2)}, u32[]{:S(2)}) collective-permute-start(bf16[128,1024]{1,0:T(8,128)(2,1)S(1)} %constant_dynamic-update-slice_fusion.refs_2_), channel_id=1, source_target_pairs={{0,1},{1,0},{2,3},{3,2},{4,5},{5,4},{6,7},{7,6},{8,9},{9,8},{10,11... | collective-permute-start | bytes 786440 | tf_op jit(solution)/shard_map/ppermute | solution.py:211
  17.3 0.0 collective-permute-done.11
  17.3 2.1 %collective-permute-done.10 = bf16[32,1152]{1,0:T(8,128)(2,1)S(1)} collective-permute-done((bf16[32,1152]{1,0:T(8,128)(2,1)S(1)}, bf16[32,1152]{1,0:T(8,128)(2,1)S(1)}, u32[]{:S(2)}, u32[]{:S(2)}) %collective-permute-start.10) | collective-permute-done | bytes 73760 | tf_op jit(solution)/shard_map/ppermute | solution.py:211
  19.4 0.0 collective-permute-done.9
  19.4 0.1 collective-permute-start.12
  19.5 0.5 %collective-permute-start.4 = (bf16[128,1024]{1,0:T(8,128)(2,1)S(1)}, bf16[128,1024]{1,0:T(8,128)(2,1)S(1)}, u32[]{:S(2)}, u32[]{:S(2)}) collective-permute-start(bf16[128,1024]{1,0:T(8,128)(2,1)S(1)} %constant_dynamic-update-slice_fusion.refs_2_), channel_id=1, source_target_pairs={{0,4},{4,0},{8,12},{12,8},{16,20},{20,16},{24,28},{28,24},{1,5},{5... | collective-permute-start | bytes 786440 | tf_op jit(solution)/shard_map/ppermute | solution.py:211
  20.0 2.7 %collective-permute-done.7.refs_6_ = bf16[128,1024]{1,0:T(8,128)(2,1)S(1)} collective-permute-done((bf16[128,1024]{1,0:T(8,128)(2,1)S(1)}, bf16[128,1024]{1,0:T(8,128)(2,1)S(1)}, u32[]{:S(2)}, u32[]{:S(2)}) %collective-permute-start.7) | collective-permute-done | bytes 262176 | tf_op jit(solution)/shard_map/ppermute | solution.py:211
  22.6 0.0 collective-permute-start.8
  22.7 0.5 %collective-permute-done.5.refs_4_ = bf16[128,1024]{1,0:T(8,128)(2,1)S(1)} collective-permute-done((bf16[128,1024]{1,0:T(8,128)(2,1)S(1)}, bf16[128,1024]{1,0:T(8,128)(2,1)S(1)}, u32[]{:S(2)}, u32[]{:S(2)}) %collective-permute-start.5) | collective-permute-done | bytes 262176 | tf_op jit(solution)/shard_map/ppermute | solution.py:211
  23.2 0.0 collective-permute-start.6
  23.2 0.0 copy-start
  23.2 0.1 pad_add_fusion.refs_0_
  23.2 0.0 collective-permute-done.4.refs_3_
  23.2 0.0 collective-permute-done.12.refs_9_
  23.2 0.9 %collective-permute-done.8.refs_7_ = bf16[128,1024]{1,0:T(8,128)(2,1)S(1)} collective-permute-done((bf16[128,1024]{1,0:T(8,128)(2,1)S(1)}, bf16[128,1024]{1,0:T(8,128)(2,1)S(1)}, u32[]{:S(2)}, u32[]{:S(2)}) %collective-permute-start.8) | collective-permute-done | bytes 262176 | tf_op jit(solution)/shard_map/ppermute | solution.py:211
  24.2 0.5 %collective-permute-done.6.refs_5_ = bf16[128,1024]{1,0:T(8,128)(2,1)S(1)} collective-permute-done((bf16[128,1024]{1,0:T(8,128)(2,1)S(1)}, bf16[128,1024]{1,0:T(8,128)(2,1)S(1)}, u32[]{:S(2)}, u32[]{:S(2)}) %collective-permute-start.6) | collective-permute-done | bytes 262176 | tf_op jit(solution)/shard_map/ppermute | solution.py:211
  24.7 0.0 copy-done
  24.7 7.2 %shard_map.37 = f32[32,1024]{1,0:T(8,128)} custom-call(s32[2]{0:T(128)S(1)} %pad_add_fusion.refs_0_, s32[8,128]{1,0:T(8,128)S(1)} %bitcast.25, bf16[128,1024]{1,0:T(8,128)(2,1)S(1)} %constant_dynamic-update-slice_fusion.refs_2_, bf16[128,1024]{1,0:T(8,128)(2,1)S(1)} %collective-permute-done.4.refs_3_, bf16[128,1024]{1,0:T(8,128)(2,1)S(1)} %collective-permute-done.5.refs_4_, ...), custom_call_target="tpu_custom_call" | custom-call | flops 2147483648 | bytes 2097152 | tf_op jit(solution)/shard_map/pallas_call | solution.py:248
  (7 shorter events, 0.1 us)
Async XLA Ops:
  0.0 9.2 %copy-start.1 = (s32[128,4]{0,1:T(4,128)S(1)}, s32[128,4]{0,1:T(4,128)}, u32[]{:S(2)}) copy-start(s32[128,4]{0,1:T(4,128)} %param.4) | copy-start | bytes 6148
  0.0 9.2 %collective-permute-start.2 = (bf16[32,1024]{1,0:T(8,128)(2,1)}, bf16[32,1024]{1,0:T(8,128)(2,1)S(1)}, u32[]{:S(2)}, u32[]{:S(2)}) collective-permute-start(bf16[32,1024]{1,0:T(8,128)(2,1)} %param.3), channel_id=1, source_target_pairs={{0,3},{1,2},{2,1},{3,0},{4,7},{5,6},{6,5},{7,4},{8,11},{9,10},{10,... | collective-permute-start | bytes 196616 | tf_op jit(solution)/shard_map/ppermute | solution.py:211
  3.9 9.0 %collective-permute-start.1 = (bf16[32,1024]{1,0:T(8,128)(2,1)}, bf16[32,1024]{1,0:T(8,128)(2,1)S(1)}, u32[]{:S(2)}, u32[]{:S(2)}) collective-permute-start(bf16[32,1024]{1,0:T(8,128)(2,1)} %param.3), channel_id=1, source_target_pairs={{0,24},{4,28},{8,16},{12,20},{16,8},{20,12},{24,0},{28,4},{1,25},{... | collective-permute-start | bytes 196616 | tf_op jit(solution)/shard_map/ppermute | solution.py:211
  7.5 8.7 %collective-permute-start = (bf16[32,1024]{1,0:T(8,128)(2,1)}, bf16[32,1024]{1,0:T(8,128)(2,1)S(1)}, u32[]{:S(2)}, u32[]{:S(2)}) collective-permute-start(bf16[32,1024]{1,0:T(8,128)(2,1)} %param.3), channel_id=1, source_target_pairs={{0,16},{4,20},{8,24},{12,28},{16,0},{20,4},{24,8},{28,12},{1,17},{... | collective-permute-start | bytes 196616 | tf_op jit(solution)/shard_map/ppermute | solution.py:211
  7.5 8.7 %collective-permute-start.3 = (bf16[32,1024]{1,0:T(8,128)(2,1)}, bf16[32,1024]{1,0:T(8,128)(2,1)S(1)}, u32[]{:S(2)}, u32[]{:S(2)}) collective-permute-start(bf16[32,1024]{1,0:T(8,128)(2,1)} %param.3), channel_id=1, source_target_pairs={{0,8},{4,12},{8,0},{12,4},{16,24},{20,28},{24,16},{28,20},{1,9},{5... | collective-permute-start | bytes 196616 | tf_op jit(solution)/shard_map/ppermute | solution.py:211
  9.2 8.1 %collective-permute-start.11 = (bf16[32,1152]{1,0:T(8,128)(2,1)S(1)}, bf16[32,1152]{1,0:T(8,128)(2,1)S(1)}, u32[]{:S(2)}, u32[]{:S(2)}) collective-permute-start(bf16[32,1152]{1,0:T(8,128)(2,1)S(1)} %pad_maximum_fusion.1), channel_id=1, source_target_pairs={{0,24},{4,28},{8,16},{12,20},{16,8},{20,12},{24,0},{28,4},{1,25},{... | collective-permute-start | bytes 221192 | tf_op jit(solution)/shard_map/ppermute | solution.py:211
  12.9 6.5 %collective-permute-start.10 = (bf16[32,1152]{1,0:T(8,128)(2,1)S(1)}, bf16[32,1152]{1,0:T(8,128)(2,1)S(1)}, u32[]{:S(2)}, u32[]{:S(2)}) collective-permute-start(bf16[32,1152]{1,0:T(8,128)(2,1)S(1)} %pad_maximum_fusion.1), channel_id=1, source_target_pairs={{0,16},{4,20},{8,24},{12,28},{16,0},{20,4},{24,8},{28,12},{1,17},{... | collective-permute-start | bytes 221192 | tf_op jit(solution)/shard_map/ppermute | solution.py:211
  12.9 6.5 %collective-permute-start.9 = (bf16[32,1152]{1,0:T(8,128)(2,1)S(1)}, bf16[32,1152]{1,0:T(8,128)(2,1)S(1)}, u32[]{:S(2)}, u32[]{:S(2)}) collective-permute-start(bf16[32,1152]{1,0:T(8,128)(2,1)S(1)} %pad_maximum_fusion.1), channel_id=1, source_target_pairs={{0,8},{4,12},{8,0},{12,4},{16,24},{20,28},{24,16},{28,20},{1,9},{5... | collective-permute-start | bytes 221192 | tf_op jit(solution)/shard_map/ppermute | solution.py:211
  16.2 6.4 %collective-permute-start.7 = (bf16[128,1024]{1,0:T(8,128)(2,1)S(1)}, bf16[128,1024]{1,0:T(8,128)(2,1)S(1)}, u32[]{:S(2)}, u32[]{:S(2)}) collective-permute-start(bf16[128,1024]{1,0:T(8,128)(2,1)S(1)} %constant_dynamic-update-slice_fusion.refs_2_), channel_id=1, source_target_pairs={{0,2},{1,3},{2,0},{3,1},{4,6},{5,7},{6,4},{7,5},{8,10},{9,11},{10,... | collective-permute-start | bytes 786440 | tf_op jit(solution)/shard_map/ppermute | solution.py:211
  16.8 6.4 %collective-permute-start.5 = (bf16[128,1024]{1,0:T(8,128)(2,1)S(1)}, bf16[128,1024]{1,0:T(8,128)(2,1)S(1)}, u32[]{:S(2)}, u32[]{:S(2)}) collective-permute-start(bf16[128,1024]{1,0:T(8,128)(2,1)S(1)} %constant_dynamic-update-slice_fusion.refs_2_), channel_id=1, source_target_pairs={{0,1},{1,0},{2,3},{3,2},{4,5},{5,4},{6,7},{7,6},{8,9},{9,8},{10,11... | collective-permute-start | bytes 786440 | tf_op jit(solution)/shard_map/ppermute | solution.py:211
  19.4 3.8 %collective-permute-start.12 = (bf16[128,1152]{1,0:T(8,128)(2,1)S(1)}, bf16[128,1152]{1,0:T(8,128)(2,1)S(1)}, u32[]{:S(2)}, u32[]{:S(2)}) collective-permute-start(bf16[128,1152]{1,0:T(8,128)(2,1)S(1)} %pad_maximum_fusion.refs_8_), channel_id=1, source_target_pairs={{0,4},{4,0},{8,12},{12,8},{16,20},{20,16},{24,28},{28,24},{1,5},{5... | collective-permute-start | bytes 884744 | tf_op jit(solution)/shard_map/ppermute | solution.py:211
  19.5 3.7 %collective-permute-start.4 = (bf16[128,1024]{1,0:T(8,128)(2,1)S(1)}, bf16[128,1024]{1,0:T(8,128)(2,1)S(1)}, u32[]{:S(2)}, u32[]{:S(2)}) collective-permute-start(bf16[128,1024]{1,0:T(8,128)(2,1)S(1)} %constant_dynamic-update-slice_fusion.refs_2_), channel_id=1, source_target_pairs={{0,4},{4,0},{8,12},{12,8},{16,20},{20,16},{24,28},{28,24},{1,5},{5... | collective-permute-start | bytes 786440 | tf_op jit(solution)/shard_map/ppermute | solution.py:211
  22.6 1.5 %collective-permute-start.8 = (bf16[128,1024]{1,0:T(8,128)(2,1)S(1)}, bf16[128,1024]{1,0:T(8,128)(2,1)S(1)}, u32[]{:S(2)}, u32[]{:S(2)}) collective-permute-start(bf16[128,1024]{1,0:T(8,128)(2,1)S(1)} %collective-permute-done.7.refs_6_), channel_id=1, source_target_pairs={{0,4},{4,0},{8,12},{12,8},{16,20},{20,16},{24,28},{28,24},{1,5},{5... | collective-permute-start | bytes 786440 | tf_op jit(solution)/shard_map/ppermute | solution.py:211
  23.2 1.5 %collective-permute-start.6 = (bf16[128,1024]{1,0:T(8,128)(2,1)S(1)}, bf16[128,1024]{1,0:T(8,128)(2,1)S(1)}, u32[]{:S(2)}, u32[]{:S(2)}) collective-permute-start(bf16[128,1024]{1,0:T(8,128)(2,1)S(1)} %collective-permute-done.5.refs_4_), channel_id=1, source_target_pairs={{0,4},{4,0},{8,12},{12,8},{16,20},{20,16},{24,28},{28,24},{1,5},{5... | collective-permute-start | bytes 786440 | tf_op jit(solution)/shard_map/ppermute | solution.py:211
  23.2 1.5 %copy-start = (s32[1024]{0:T(1024)S(1)}, s32[1024]{0:T(1024)}, u32[]{:S(2)}) copy-start(s32[1024]{0:T(1024)} %param.5) | copy-start | bytes 12292

commit v20 on v19

--- a/solution.py
+++ b/solution.py
@@ -219,7 +219,11 @@
     ranking = [middle, far] + [d for d in range(1, far) if d != middle]
     corner = cols - 1
     early = swap(embed, "col", corner)
-    parts = lax.optimization_barrier([line[middle], line[far], early] + [line[d] for d in ranking[2:]])
+    early_first, again = lax.optimization_barrier((early, embed))
+    mine = {p: swap(again, "col", p) for p in range(1, corner)}
+    parts, mine = lax.optimization_barrier(
+        ([line[middle], line[far], early] + [line[d] for d in ranking[2:]], mine)
+    )
     early_after = parts.pop(2)
     line = dict(zip([middle, far] + ranking[2:], parts))
     tall = join([embed] + [line[d] for d in range(1, levels)])
@@ -227,10 +231,10 @@
     ids = positives.T
     ids = jnp.concatenate([ids // 256, ids % 256], axis=0).astype(jnp.bfloat16).reshape(-1, 128)
     ids = jnp.concatenate([ids, jnp.zeros((shard - ids.shape[0], 128), ids.dtype)], axis=0)
-    early = jnp.concatenate([early, ids], axis=1)
+    early = jnp.concatenate([early_first, ids], axis=1)
 
     plane = {0: tall}
-    plane.update({p: swap(tall, "col", p) for p in range(1, corner)})
+    plane.update({p: join([mine[p], swap(tall[shard:], "col", p)]) for p in range(1, corner)})
     beyond = {d: swap(early, "row", 2 * d) for d in range(1, levels)}
     corner_rows = jnp.concatenate([early_after, ids], axis=1)
     plane[corner] = join([corner_rows] + [beyond[d] for d in range(1, levels)])

time: 32.1 us -> 32.1 us (level)
  waiting for transfers between devices: 9.17 us -> 7.26 us
  starting transfers between devices: 14.4 us -> 16.2 us
    ppermute x13 -> x15, waiting for transfers between devices: 9.17 us -> 7.26 us  [swap(): return lax.ppermute(array, axis, [(i, i ^ mask) for i in range(size)])]
    ppermute x13 -> x15, starting transfers between devices: 14.4 us -> 16.2 us  [swap(): return lax.ppermute(array, axis, [(i, i ^ mask) for i in range(size)])]
    unnamed x7 -> x11, local copies, waits for them, and re-layouts: 0.9 us -> 0.92 us
  transfers between devices with their start and end apart: 13 -> 15, of which waited for: 6 -> 7; matrix products, arithmetic and copies ran while one was open for 3% -> 3% of each run, Pallas kernels for 0% -> 0%
where the time goes in v20:
time: 32.1 us; the launch traced here: 31.9 us
  starting transfers between devices  16.2 us (50%)
  waiting for transfers between devices  7.26 us (23%)
  Pallas kernels  7.21 us (22%)
  local copies, waits for them, and re-layouts  0.96 us (3%)
    ppermute x15, starting transfers between devices, swap(): return lax.ppermute(array, axis, [(i, i ^ mask) for i in range(size)])  16.2 us
    ppermute x15, waiting for transfers between devices, swap(): return lax.ppermute(array, axis, [(i, i ^ mask) for i in range(size)])  7.26 us
    pallas_call x1, Pallas kernels, body(): pl.pallas_call(functools.partial(kernel, cols, shard, pos_count, lane_blo...  7.21 us
    unnamed x11, local copies, waits for them, and re-layouts  0.92 us
  transfers between devices with their start and end apart: 15, of which 7 were waited for; matrix products, arithmetic and copies ran while one was open for 3% of the time, Pallas kernels for 0%

profile of v20, /device:TPU:0, one launch (start us, length us, event | category | flops | bytes accessed | tf_op | source)
XLA Modules:
  0.0 31.9 jit_solution(15402096425915654127)
XLA Ops:
  0.0 0.0 copy-start.1
  0.0 0.0 copy-start.2
  0.0 3.0 %collective-permute-start.3 = (bf16[32,1024]{1,0:T(8,128)(2,1)}, bf16[32,1024]{1,0:T(8,128)(2,1)S(1)}, u32[]{:S(2)}, u32[]{:S(2)}) collective-permute-start(bf16[32,1024]{1,0:T(8,128)(2,1)} %param.3), channel_id=1, source_target_pairs={{0,8},{4,12},{8,0},{12,4},{16,24},{20,28},{24,16},{28,20},{1,9},{5... | collective-permute-start | bytes 196616 | tf_op jit(solution)/shard_map/ppermute | solution.py:211
  3.0 2.4 %collective-permute-start.2 = (bf16[32,1024]{1,0:T(8,128)(2,1)}, bf16[32,1024]{1,0:T(8,128)(2,1)S(1)}, u32[]{:S(2)}, u32[]{:S(2)}) collective-permute-start(bf16[32,1024]{1,0:T(8,128)(2,1)} %param.3), channel_id=1, source_target_pairs={{0,3},{1,2},{2,1},{3,0},{4,7},{5,6},{6,5},{7,4},{8,11},{9,10},{10,... | collective-permute-start | bytes 196616 | tf_op jit(solution)/shard_map/ppermute | solution.py:211
  5.5 2.5 %collective-permute-start.1 = (bf16[32,1024]{1,0:T(8,128)(2,1)}, bf16[32,1024]{1,0:T(8,128)(2,1)S(1)}, u32[]{:S(2)}, u32[]{:S(2)}) collective-permute-start(bf16[32,1024]{1,0:T(8,128)(2,1)} %param.3), channel_id=1, source_target_pairs={{0,24},{4,28},{8,16},{12,20},{16,8},{20,12},{24,0},{28,4},{1,25},{... | collective-permute-start | bytes 196616 | tf_op jit(solution)/shard_map/ppermute | solution.py:211
  8.0 0.1 collective-permute-start
  8.1 0.9 %constant_dynamic-update-slice_fusion.3 = bf16[128,1024]{1,0:T(8,128)(2,1)S(1)} fusion(bf16[32,1024]{1,0:T(8,128)(2,1)} %param.3), kind=kLoop, calls=%fused_computation.5 | loop fusion | bytes 131072
  8.9 0.0 copy-done.2
  9.0 0.0 collective-permute-done.2
  9.0 0.0 copy-done.1
  9.0 0.9 %collective-permute-start.5 = (bf16[32,1024]{1,0:T(8,128)(2,1)S(1)}, bf16[32,1024]{1,0:T(8,128)(2,1)S(1)}, u32[]{:S(2)}, u32[]{:S(2)}) collective-permute-start(bf16[32,1024]{1,0:T(8,128)(2,1)S(1)} %copy-done.1), channel_id=1, source_target_pairs={{0,2},{1,3},{2,0},{3,1},{4,6},{5,7},{6,4},{7,5},{8,10},{9,11},{10,... | collective-permute-start | bytes 196616 | tf_op jit(solution)/shard_map/ppermute | solution.py:211
  9.9 1.5 %collective-permute-start.4 = (bf16[32,1024]{1,0:T(8,128)(2,1)S(1)}, bf16[32,1024]{1,0:T(8,128)(2,1)S(1)}, u32[]{:S(2)}, u32[]{:S(2)}) collective-permute-start(bf16[32,1024]{1,0:T(8,128)(2,1)S(1)} %copy-done.1), channel_id=1, source_target_pairs={{0,1},{1,0},{2,3},{3,2},{4,5},{5,4},{6,7},{7,6},{8,9},{9,8},{10,11... | collective-permute-start | bytes 196616 | tf_op jit(solution)/shard_map/ppermute | solution.py:211
  11.4 0.0 collective-permute-done.3
  11.4 2.5 %collective-permute-start.13 = (bf16[32,1152]{1,0:T(8,128)(2,1)S(1)}, bf16[32,1152]{1,0:T(8,128)(2,1)S(1)}, u32[]{:S(2)}, u32[]{:S(2)}) collective-permute-start(bf16[32,1152]{1,0:T(8,128)(2,1)S(1)} %pad_maximum_fusion.1), channel_id=1, source_target_pairs={{0,24},{4,28},{8,16},{12,20},{16,8},{20,12},{24,0},{28,4},{1,25},{... | collective-permute-start | bytes 221192 | tf_op jit(solution)/shard_map/ppermute | solution.py:211
  14.0 0.0 collective-permute-done.1
  14.0 1.2 %collective-permute-start.12 = (bf16[32,1152]{1,0:T(8,128)(2,1)S(1)}, bf16[32,1152]{1,0:T(8,128)(2,1)S(1)}, u32[]{:S(2)}, u32[]{:S(2)}) collective-permute-start(bf16[32,1152]{1,0:T(8,128)(2,1)S(1)} %pad_maximum_fusion.1), channel_id=1, source_target_pairs={{0,16},{4,20},{8,24},{12,28},{16,0},{20,4},{24,8},{28,12},{1,17},{... | collective-permute-start | bytes 221192 | tf_op jit(solution)/shard_map/ppermute | solution.py:211
  15.2 1.2 %collective-permute-done = bf16[32,1024]{1,0:T(8,128)(2,1)S(1)} collective-permute-done((bf16[32,1024]{1,0:T(8,128)(2,1)}, bf16[32,1024]{1,0:T(8,128)(2,1)S(1)}, u32[]{:S(2)}, u32[]{:S(2)}) %collective-permute-start) | collective-permute-done | bytes 65568 | tf_op jit(solution)/shard_map/ppermute | solution.py:211
  16.4 0.0 collective-permute-start.11
  16.4 0.0 collective-permute-done.5
  16.4 0.0 collective-permute-done.4
  16.4 0.6 %collective-permute-start.9 = (bf16[96,1024]{1,0:T(8,128)(2,1)S(1)}, bf16[96,1024]{1,0:T(8,128)(2,1)S(1)}, u32[]{:S(2)}, u32[]{:S(2)}) collective-permute-start(bf16[96,1024]{1,0:T(8,128)(2,1)S(1)} %get-tuple-element.21), channel_id=1, source_target_pairs={{0,2},{1,3},{2,0},{3,1},{4,6},{5,7},{6,4},{7,5},{8,10},{9,11},{10,... | collective-permute-start | bytes 589832 | tf_op jit(solution)/shard_map/ppermute | solution.py:211
  17.0 0.7 %collective-permute-start.7 = (bf16[96,1024]{1,0:T(8,128)(2,1)S(1)}, bf16[96,1024]{1,0:T(8,128)(2,1)S(1)}, u32[]{:S(2)}, u32[]{:S(2)}) collective-permute-start(bf16[96,1024]{1,0:T(8,128)(2,1)S(1)} %get-tuple-element.21), channel_id=1, source_target_pairs={{0,1},{1,0},{2,3},{3,2},{4,5},{5,4},{6,7},{7,6},{8,9},{9,8},{10,11... | collective-permute-start | bytes 589832 | tf_op jit(solution)/shard_map/ppermute | solution.py:211
  17.7 0.6 %collective-permute-done.13 = bf16[32,1152]{1,0:T(8,128)(2,1)S(1)} collective-permute-done((bf16[32,1152]{1,0:T(8,128)(2,1)S(1)}, bf16[32,1152]{1,0:T(8,128)(2,1)S(1)}, u32[]{:S(2)}, u32[]{:S(2)}) %collective-permute-start.13) | collective-permute-done | bytes 73760 | tf_op jit(solution)/shard_map/ppermute | solution.py:211
  18.3 0.0 collective-permute-start.6
  18.3 2.3 %collective-permute-done.12 = bf16[32,1152]{1,0:T(8,128)(2,1)S(1)} collective-permute-done((bf16[32,1152]{1,0:T(8,128)(2,1)S(1)}, bf16[32,1152]{1,0:T(8,128)(2,1)S(1)}, u32[]{:S(2)}, u32[]{:S(2)}) %collective-permute-start.12) | collective-permute-done | bytes 73760 | tf_op jit(solution)/shard_map/ppermute | solution.py:211
  20.7 0.7 %collective-permute-done.11 = bf16[32,1152]{1,0:T(8,128)(2,1)S(1)} collective-permute-done((bf16[32,1152]{1,0:T(8,128)(2,1)S(1)}, bf16[32,1152]{1,0:T(8,128)(2,1)S(1)}, u32[]{:S(2)}, u32[]{:S(2)}) %collective-permute-start.11) | collective-permute-done | bytes 73760 | tf_op jit(solution)/shard_map/ppermute | solution.py:211
  21.4 0.1 collective-permute-start.14
  21.5 1.2 %collective-permute-done.7 = bf16[96,1024]{1,0:T(8,128)(2,1)S(1)} collective-permute-done((bf16[96,1024]{1,0:T(8,128)(2,1)S(1)}, bf16[96,1024]{1,0:T(8,128)(2,1)S(1)}, u32[]{:S(2)}, u32[]{:S(2)}) %collective-permute-start.7) | collective-permute-done | bytes 196640 | tf_op jit(solution)/shard_map/ppermute | solution.py:211
  22.7 0.1 collective-permute-start.8
  22.8 0.0 collective-permute-done.9
  22.8 0.5 %collective-permute-start.10 = (bf16[128,1024]{1,0:T(8,128)(2,1)S(1)}, bf16[128,1024]{1,0:T(8,128)(2,1)S(1)}, u32[]{:S(2)}, u32[]{:S(2)}) collective-permute-start(bf16[128,1024]{1,0:T(8,128)(2,1)S(1)} %constant_dynamic-update-slice_fusion.9.refs_6_), channel_id=1, source_target_pairs={{0,4},{4,0},{8,12},{12,8},{16,20},{20,16},{24,28},{28,24},{1,5},{5... | collective-permute-start | bytes 786440 | tf_op jit(solution)/shard_map/ppermute | solution.py:211
  23.4 0.0 copy-start
  23.4 0.1 pad_add_fusion.refs_0_
  23.4 0.0 collective-permute-done.6.refs_3_
  23.4 0.0 collective-permute-done.14.refs_9_
  23.5 0.9 %collective-permute-done.8.refs_5_ = bf16[128,1024]{1,0:T(8,128)(2,1)S(1)} collective-permute-done((bf16[128,1024]{1,0:T(8,128)(2,1)S(1)}, bf16[128,1024]{1,0:T(8,128)(2,1)S(1)}, u32[]{:S(2)}, u32[]{:S(2)}) %collective-permute-start.8) | collective-permute-done | bytes 262176 | tf_op jit(solution)/shard_map/ppermute | solution.py:211
  24.3 0.4 %collective-permute-done.10.refs_7_ = bf16[128,1024]{1,0:T(8,128)(2,1)S(1)} collective-permute-done((bf16[128,1024]{1,0:T(8,128)(2,1)S(1)}, bf16[128,1024]{1,0:T(8,128)(2,1)S(1)}, u32[]{:S(2)}, u32[]{:S(2)}) %collective-permute-start.10) | collective-permute-done | bytes 262176 | tf_op jit(solution)/shard_map/ppermute | solution.py:211
  24.7 0.0 copy-done
  24.7 7.2 %shard_map.37 = f32[32,1024]{1,0:T(8,128)} custom-call(s32[2]{0:T(128)S(1)} %pad_add_fusion.refs_0_, s32[8,128]{1,0:T(8,128)S(1)} %bitcast.25, bf16[128,1024]{1,0:T(8,128)(2,1)S(1)} %get-tuple-element.22.refs_2_, bf16[128,1024]{1,0:T(8,128)(2,1)S(1)} %collective-permute-done.6.refs_3_, bf16[128,1024]{1,0:T(8,128)(2,1)S(1)} %constant_dynamic-update-slice_fusion.7.refs_4_, ...), custom_call_target="tpu_custom_call" | custom-call | flops 2147483648 | bytes 2097152 | tf_op jit(solution)/shard_map/pallas_call | solution.py:252
  (11 shorter events, 0.1 us)
Async XLA Ops:
  0.0 9.0 %copy-start.1 = (bf16[32,1024]{1,0:T(8,128)(2,1)S(1)}, bf16[32,1024]{1,0:T(8,128)(2,1)}, u32[]{:S(2)}) copy-start(bf16[32,1024]{1,0:T(8,128)(2,1)} %param.3) | copy-start | bytes 196612
  0.0 8.9 %copy-start.2 = (s32[128,4]{0,1:T(4,128)S(1)}, s32[128,4]{0,1:T(4,128)}, u32[]{:S(2)}) copy-start(s32[128,4]{0,1:T(4,128)} %param.4) | copy-start | bytes 6148
  0.0 11.4 %collective-permute-start.3 = (bf16[32,1024]{1,0:T(8,128)(2,1)}, bf16[32,1024]{1,0:T(8,128)(2,1)S(1)}, u32[]{:S(2)}, u32[]{:S(2)}) collective-permute-start(bf16[32,1024]{1,0:T(8,128)(2,1)} %param.3), channel_id=1, source_target_pairs={{0,8},{4,12},{8,0},{12,4},{16,24},{20,28},{24,16},{28,20},{1,9},{5... | collective-permute-start | bytes 196616 | tf_op jit(solution)/shard_map/ppermute | solution.py:211
  3.0 6.0 %collective-permute-start.2 = (bf16[32,1024]{1,0:T(8,128)(2,1)}, bf16[32,1024]{1,0:T(8,128)(2,1)S(1)}, u32[]{:S(2)}, u32[]{:S(2)}) collective-permute-start(bf16[32,1024]{1,0:T(8,128)(2,1)} %param.3), channel_id=1, source_target_pairs={{0,3},{1,2},{2,1},{3,0},{4,7},{5,6},{6,5},{7,4},{8,11},{9,10},{10,... | collective-permute-start | bytes 196616 | tf_op jit(solution)/shard_map/ppermute | solution.py:211
  5.5 8.5 %collective-permute-start.1 = (bf16[32,1024]{1,0:T(8,128)(2,1)}, bf16[32,1024]{1,0:T(8,128)(2,1)S(1)}, u32[]{:S(2)}, u32[]{:S(2)}) collective-permute-start(bf16[32,1024]{1,0:T(8,128)(2,1)} %param.3), channel_id=1, source_target_pairs={{0,24},{4,28},{8,16},{12,20},{16,8},{20,12},{24,0},{28,4},{1,25},{... | collective-permute-start | bytes 196616 | tf_op jit(solution)/shard_map/ppermute | solution.py:211
  8.0 8.4 %collective-permute-start = (bf16[32,1024]{1,0:T(8,128)(2,1)}, bf16[32,1024]{1,0:T(8,128)(2,1)S(1)}, u32[]{:S(2)}, u32[]{:S(2)}) collective-permute-start(bf16[32,1024]{1,0:T(8,128)(2,1)} %param.3), channel_id=1, source_target_pairs={{0,16},{4,20},{8,24},{12,28},{16,0},{20,4},{24,8},{28,12},{1,17},{... | collective-permute-start | bytes 196616 | tf_op jit(solution)/shard_map/ppermute | solution.py:211
  9.0 7.4 %collective-permute-start.5 = (bf16[32,1024]{1,0:T(8,128)(2,1)S(1)}, bf16[32,1024]{1,0:T(8,128)(2,1)S(1)}, u32[]{:S(2)}, u32[]{:S(2)}) collective-permute-start(bf16[32,1024]{1,0:T(8,128)(2,1)S(1)} %copy-done.1), channel_id=1, source_target_pairs={{0,2},{1,3},{2,0},{3,1},{4,6},{5,7},{6,4},{7,5},{8,10},{9,11},{10,... | collective-permute-start | bytes 196616 | tf_op jit(solution)/shard_map/ppermute | solution.py:211
  9.9 6.5 %collective-permute-start.4 = (bf16[32,1024]{1,0:T(8,128)(2,1)S(1)}, bf16[32,1024]{1,0:T(8,128)(2,1)S(1)}, u32[]{:S(2)}, u32[]{:S(2)}) collective-permute-start(bf16[32,1024]{1,0:T(8,128)(2,1)S(1)} %copy-done.1), channel_id=1, source_target_pairs={{0,1},{1,0},{2,3},{3,2},{4,5},{5,4},{6,7},{7,6},{8,9},{9,8},{10,11... | collective-permute-start | bytes 196616 | tf_op jit(solution)/shard_map/ppermute | solution.py:211
  11.4 6.9 %collective-permute-start.13 = (bf16[32,1152]{1,0:T(8,128)(2,1)S(1)}, bf16[32,1152]{1,0:T(8,128)(2,1)S(1)}, u32[]{:S(2)}, u32[]{:S(2)}) collective-permute-start(bf16[32,1152]{1,0:T(8,128)(2,1)S(1)} %pad_maximum_fusion.1), channel_id=1, source_target_pairs={{0,24},{4,28},{8,16},{12,20},{16,8},{20,12},{24,0},{28,4},{1,25},{... | collective-permute-start | bytes 221192 | tf_op jit(solution)/shard_map/ppermute | solution.py:211
  14.0 6.7 %collective-permute-start.12 = (bf16[32,1152]{1,0:T(8,128)(2,1)S(1)}, bf16[32,1152]{1,0:T(8,128)(2,1)S(1)}, u32[]{:S(2)}, u32[]{:S(2)}) collective-permute-start(bf16[32,1152]{1,0:T(8,128)(2,1)S(1)} %pad_maximum_fusion.1), channel_id=1, source_target_pairs={{0,16},{4,20},{8,24},{12,28},{16,0},{20,4},{24,8},{28,12},{1,17},{... | collective-permute-start | bytes 221192 | tf_op jit(solution)/shard_map/ppermute | solution.py:211
  16.4 5.0 %collective-permute-start.11 = (bf16[32,1152]{1,0:T(8,128)(2,1)S(1)}, bf16[32,1152]{1,0:T(8,128)(2,1)S(1)}, u32[]{:S(2)}, u32[]{:S(2)}) collective-permute-start(bf16[32,1152]{1,0:T(8,128)(2,1)S(1)} %pad_maximum_fusion.1), channel_id=1, source_target_pairs={{0,8},{4,12},{8,0},{12,4},{16,24},{20,28},{24,16},{28,20},{1,9},{5... | collective-permute-start | bytes 221192 | tf_op jit(solution)/shard_map/ppermute | solution.py:211
  16.4 6.3 %collective-permute-start.9 = (bf16[96,1024]{1,0:T(8,128)(2,1)S(1)}, bf16[96,1024]{1,0:T(8,128)(2,1)S(1)}, u32[]{:S(2)}, u32[]{:S(2)}) collective-permute-start(bf16[96,1024]{1,0:T(8,128)(2,1)S(1)} %get-tuple-element.21), channel_id=1, source_target_pairs={{0,2},{1,3},{2,0},{3,1},{4,6},{5,7},{6,4},{7,5},{8,10},{9,11},{10,... | collective-permute-start | bytes 589832 | tf_op jit(solution)/shard_map/ppermute | solution.py:211
  17.0 5.7 %collective-permute-start.7 = (bf16[96,1024]{1,0:T(8,128)(2,1)S(1)}, bf16[96,1024]{1,0:T(8,128)(2,1)S(1)}, u32[]{:S(2)}, u32[]{:S(2)}) collective-permute-start(bf16[96,1024]{1,0:T(8,128)(2,1)S(1)} %get-tuple-element.21), channel_id=1, source_target_pairs={{0,1},{1,0},{2,3},{3,2},{4,5},{5,4},{6,7},{7,6},{8,9},{9,8},{10,11... | collective-permute-start | bytes 589832 | tf_op jit(solution)/shard_map/ppermute | solution.py:211
  18.3 5.1 %collective-permute-start.6 = (bf16[128,1024]{1,0:T(8,128)(2,1)S(1)}, bf16[128,1024]{1,0:T(8,128)(2,1)S(1)}, u32[]{:S(2)}, u32[]{:S(2)}) collective-permute-start(bf16[128,1024]{1,0:T(8,128)(2,1)S(1)} %get-tuple-element.22.refs_2_), channel_id=1, source_target_pairs={{0,4},{4,0},{8,12},{12,8},{16,20},{20,16},{24,28},{28,24},{1,5},{5... | collective-permute-start | bytes 786440 | tf_op jit(solution)/shard_map/ppermute | solution.py:211
  21.4 2.0 %collective-permute-start.14 = (bf16[128,1152]{1,0:T(8,128)(2,1)S(1)}, bf16[128,1152]{1,0:T(8,128)(2,1)S(1)}, u32[]{:S(2)}, u32[]{:S(2)}) collective-permute-start(bf16[128,1152]{1,0:T(8,128)(2,1)S(1)} %pad_maximum_fusion.refs_8_), channel_id=1, source_target_pairs={{0,4},{4,0},{8,12},{12,8},{16,20},{20,16},{24,28},{28,24},{1,5},{5... | collective-permute-start | bytes 884744 | tf_op jit(solution)/shard_map/ppermute | solution.py:211
  22.7 1.6 %collective-permute-start.8 = (bf16[128,1024]{1,0:T(8,128)(2,1)S(1)}, bf16[128,1024]{1,0:T(8,128)(2,1)S(1)}, u32[]{:S(2)}, u32[]{:S(2)}) collective-permute-start(bf16[128,1024]{1,0:T(8,128)(2,1)S(1)} %constant_dynamic-update-slice_fusion.7.refs_4_), channel_id=1, source_target_pairs={{0,4},{4,0},{8,12},{12,8},{16,20},{20,16},{24,28},{28,24},{1,5},{5... | collective-permute-start | bytes 786440 | tf_op jit(solution)/shard_map/ppermute | solution.py:211
  22.8 1.9 %collective-permute-start.10 = (bf16[128,1024]{1,0:T(8,128)(2,1)S(1)}, bf16[128,1024]{1,0:T(8,128)(2,1)S(1)}, u32[]{:S(2)}, u32[]{:S(2)}) collective-permute-start(bf16[128,1024]{1,0:T(8,128)(2,1)S(1)} %constant_dynamic-update-slice_fusion.9.refs_6_), channel_id=1, source_target_pairs={{0,4},{4,0},{8,12},{12,8},{16,20},{20,16},{24,28},{28,24},{1,5},{5... | collective-permute-start | bytes 786440 | tf_op jit(solution)/shard_map/ppermute | solution.py:211
  23.4 1.3 %copy-start = (s32[1024]{0:T(1024)S(1)}, s32[1024]{0:T(1024)}, u32[]{:S(2)}) copy-start(s32[1024]{0:T(1024)} %param.5) | copy-start | bytes 12292
